TPU v7x, 32 devices: a whole 2x2x4 slice. The times are simulated.
32 devices in a mesh: group: 4 (over x, core), replica: 8 (over z, y).
Axes of the slice: x: 2, y: 2, z: 4, core: 2. Of those that a mesh axis runs over, the one named last changes fastest.
Arguments:
- tokens: bfloat16 [32768, 960], P(('group', 'replica')), may hold values from -6 to 6
- segments: int32 [64, 512], P(('group', 'replica')), may hold values from 0 to 3, never falling along the last dimension, each value on 1 to 256 neighbouring positions
- query_weight: bfloat16 [960, 960], P('group'), may hold values from -0.1875 to 0.1875
- key_weight: bfloat16 [960, 320], P('group'), may hold values from -0.1875 to 0.1875
- value_weight: bfloat16 [960, 320], P('group'), may hold values from -0.1875 to 0.1875
- output_weight: bfloat16 [960, 960], P('group'), may hold values from -0.75 to 0.75
- w_gate: bfloat16 [960, 2560], P('group'), may hold values from -0.1875 to 0.1875
- w_up: bfloat16 [960, 2560], P('group'), may hold values from -0.1875 to 0.1875
- w_down: bfloat16 [2560, 960], P('group'), may hold values from -0.125 to 0.125
- attn_gain: bfloat16 [960], P('group'), may hold values from 0.5 to 1.5
- ffn_gain: bfloat16 [960], P('group'), may hold values from 0.5 to 1.5
- cotangent: bfloat16 [32768, 960], P(('group', 'replica')), may hold values from -6 to 6
Outputs:
- output: bfloat16 [32768, 960], P(('group', 'replica'))
- grad_tokens: bfloat16 [32768, 960], P(('group', 'replica'))
- grad_query: float32 [960, 960], P('group')
- grad_key: float32 [960, 320], P('group')
- grad_value: float32 [960, 320], P('group')
- grad_out: float32 [960, 960], P('group')
- grad_gate: float32 [960, 2560], P('group')
- grad_up: float32 [960, 2560], P('group')
- grad_down: float32 [2560, 960], P('group')
- grad_attn_gain: float32 [960], P('group')
- grad_ffn_gain: float32 [960], P('group')
Inputs may be any that keep to these rules, and one draw needn't show every extreme that they name: `segments`: along each sequence of 512 tokens the ids never fall; equal ids mark one document of at most 256 tokens.
All inputs are finite; a program needn't handle non-finite values.
Results may differ from a plain program's by a relative error of at most 0.017.
Values may be sent and summed in bfloat16 or wider, within the bound.
No kernel may reach another device: no remote copies, remote signals or barrier semaphores. Data moves between devices by JAX's collectives and lax.ppermute only.
A program may use at most 256 MiB of HBM per device.

v0:
```python
import jax
import jax.numpy as jnp
from jax import lax
from jax.sharding import PartitionSpec as P

D = 960
QUERY_HEADS = 15
KEY_VALUE_HEADS = 5
HEAD_WIDTH = 64


EPS = 1e-05
THETA = 100000.0


def norm_forward(value, gain):
    inverse = lax.rsqrt(jnp.mean(value * value, axis=-1, keepdims=True) + EPS)
    normal = value * inverse
    return (normal * gain, normal, inverse)


def norm_backward(grad_out, normal, inverse, gain):
    grad_gain = jnp.sum(grad_out * normal, axis=0)
    scaled = grad_out * gain
    grad_in = inverse * (scaled - normal * jnp.mean(scaled * normal, axis=-1, keepdims=True))
    return (grad_in, grad_gain)


def rotate(value, cosine, sine):
    half = HEAD_WIDTH // 2
    return value * cosine + jnp.concatenate([-value[..., half:], value[..., :half]], axis=-1) * sine


def unrotate(grad, cosine, sine):
    half = HEAD_WIDTH // 2
    turned = grad * sine
    return grad * cosine + jnp.concatenate([turned[..., half:], -turned[..., :half]], axis=-1)


def tables(segments):
    length = segments.shape[1]
    index = jnp.arange(length, dtype=jnp.int32)
    same = segments[:, :, None] == segments[:, None, :]
    start = jnp.min(jnp.where(same, index[None, None, :], length), axis=-1)
    position = (index[None, :] - start).astype(jnp.float32)
    allowed = same & (index[:, None] >= index[None, :])[None]
    half = HEAD_WIDTH // 2
    freq = THETA ** (-(jnp.arange(half, dtype=jnp.float32) * 2.0 / HEAD_WIDTH))
    angle = position.reshape(-1)[:, None] * freq
    cosine = jnp.concatenate([jnp.cos(angle), jnp.cos(angle)], axis=-1)[:, None, :]
    sine = jnp.concatenate([jnp.sin(angle), jnp.sin(angle)], axis=-1)[:, None, :]
    return (allowed, cosine, sine)


def masked_scores(grouped, key_rows, allowed):
    scores = jnp.einsum(
        "sikgd,sjkd->skgij", grouped, key_rows, preferred_element_type=jnp.float32
    ) * HEAD_WIDTH ** (-0.5)
    return jnp.where(allowed[:, None, None], scores, -1e30)


def per_device(
    tokens,
    segments,
    query_weight,
    key_weight,
    value_weight,
    output_weight,
    w_gate,
    w_up,
    w_down,
    attn_gain,
    ffn_gain,
    cotangent,
):
    token_count = segments.shape[0]
    length = segments.shape[1]
    rows = tokens.shape[0]
    share = QUERY_HEADS // KEY_VALUE_HEADS
    fwd = (
        lax.all_gather(query_weight, "group", axis=0, tiled=True),
        lax.all_gather(key_weight, "group", axis=0, tiled=True),
        lax.all_gather(value_weight, "group", axis=0, tiled=True),
        lax.all_gather(output_weight, "group", axis=0, tiled=True),
        lax.all_gather(w_gate, "group", axis=0, tiled=True),
        lax.all_gather(w_up, "group", axis=0, tiled=True),
        lax.all_gather(w_down, "group", axis=0, tiled=True),
        lax.all_gather(attn_gain, "group", axis=0, tiled=True),
        lax.all_gather(ffn_gain, "group", axis=0, tiled=True),
    )
    (
        full_query,
        full_key,
        full_value,
        full_out,
        full_gate,
        full_up,
        full_down,
        gain_attn,
        gain_ffn,
    ) = fwd
    allowed, cosine, sine = tables(segments)
    inputs = tokens.astype(jnp.float32)
    normed_one, normal_one, inverse_one = norm_forward(inputs, gain_attn.astype(jnp.float32))
    hidden_input = normed_one.astype(jnp.bfloat16)
    query_rows = jnp.dot(hidden_input, full_query, preferred_element_type=jnp.float32).reshape(
        rows, QUERY_HEADS, HEAD_WIDTH
    )
    keys_raw = jnp.dot(hidden_input, full_key, preferred_element_type=jnp.float32).reshape(
        rows, KEY_VALUE_HEADS, HEAD_WIDTH
    )
    values_raw = jnp.dot(hidden_input, full_value, preferred_element_type=jnp.float32)
    grouped = (
        rotate(query_rows, cosine, sine)
        .astype(jnp.bfloat16)
        .reshape(token_count, length, KEY_VALUE_HEADS, share, HEAD_WIDTH)
    )
    key_rows = (
        rotate(keys_raw, cosine, sine)
        .astype(jnp.bfloat16)
        .reshape(token_count, length, KEY_VALUE_HEADS, HEAD_WIDTH)
    )
    value_rows = values_raw.astype(jnp.bfloat16).reshape(
        token_count, length, KEY_VALUE_HEADS, HEAD_WIDTH
    )
    scores = masked_scores(grouped, key_rows, allowed)
    top = jnp.max(scores, axis=-1, keepdims=True)
    logsum = top + jnp.log(jnp.sum(jnp.exp(scores - top), axis=-1, keepdims=True))
    probs_low = jnp.exp(scores - logsum).astype(jnp.bfloat16)
    attended_rows = jnp.einsum(
        "skgij,sjkd->sikgd", probs_low, value_rows, preferred_element_type=jnp.float32
    )
    attended_rows = attended_rows.reshape(rows, D).astype(jnp.bfloat16)
    middle = inputs + jnp.dot(attended_rows, full_out, preferred_element_type=jnp.float32)
    normed_two, normal_two, inverse_two = norm_forward(middle, gain_ffn.astype(jnp.float32))
    hidden_two = normed_two.astype(jnp.bfloat16)
    gate = jnp.dot(hidden_two, full_gate, preferred_element_type=jnp.float32)
    up_part = jnp.dot(hidden_two, full_up, preferred_element_type=jnp.float32)
    sigma = jax.nn.sigmoid(gate)
    inner = (gate * sigma * up_part).astype(jnp.bfloat16)
    result = middle + jnp.dot(inner, full_down, preferred_element_type=jnp.float32)
    again = (
        lax.all_gather(query_weight, "group", axis=0, tiled=True),
        lax.all_gather(key_weight, "group", axis=0, tiled=True),
        lax.all_gather(value_weight, "group", axis=0, tiled=True),
        lax.all_gather(output_weight, "group", axis=0, tiled=True),
        lax.all_gather(w_gate, "group", axis=0, tiled=True),
        lax.all_gather(w_up, "group", axis=0, tiled=True),
        lax.all_gather(w_down, "group", axis=0, tiled=True),
        lax.all_gather(attn_gain, "group", axis=0, tiled=True),
        lax.all_gather(ffn_gain, "group", axis=0, tiled=True),
    )
    (
        full_query,
        full_key,
        full_value,
        full_out,
        full_gate,
        full_up,
        full_down,
        gain_attn,
        gain_ffn,
    ) = again
    grad_down = jnp.einsum("nf,nd->fd", inner, cotangent, preferred_element_type=jnp.float32)
    grad_inner = jnp.einsum("nd,fd->nf", cotangent, full_down, preferred_element_type=jnp.float32)
    grad_gate_in = (grad_inner * up_part * sigma * (1.0 + gate * (1.0 - sigma))).astype(
        jnp.bfloat16
    )
    grad_up_in = (grad_inner * gate * sigma).astype(jnp.bfloat16)
    grad_gate = jnp.einsum(
        "nd,nf->df", hidden_two, grad_gate_in, preferred_element_type=jnp.float32
    )
    grad_up = jnp.einsum("nd,nf->df", hidden_two, grad_up_in, preferred_element_type=jnp.float32)
    grad_hidden_two = jnp.einsum(
        "nf,df->nd", grad_gate_in, full_gate, preferred_element_type=jnp.float32
    )
    grad_hidden_two = grad_hidden_two + jnp.einsum(
        "nf,df->nd", grad_up_in, full_up, preferred_element_type=jnp.float32
    )
    grad_mid_norm, grad_gain_ffn = norm_backward(
        grad_hidden_two, normal_two, inverse_two, gain_ffn.astype(jnp.float32)
    )
    grad_middle = cotangent.astype(jnp.float32) + grad_mid_norm
    grad_branch = grad_middle.astype(jnp.bfloat16)
    grad_out = jnp.einsum(
        "ne,nd->ed", attended_rows, grad_branch, preferred_element_type=jnp.float32
    )
    grad_att = jnp.einsum("nd,ed->ne", grad_branch, full_out, preferred_element_type=jnp.float32)
    grad_att = grad_att.astype(jnp.bfloat16).reshape(
        token_count, length, KEY_VALUE_HEADS, share, HEAD_WIDTH
    )
    scores = masked_scores(grouped, key_rows, allowed)
    probs = jnp.exp(scores - logsum)
    probs_low = probs.astype(jnp.bfloat16)
    grad_probs = jnp.einsum(
        "sikgd,sjkd->skgij", grad_att, value_rows, preferred_element_type=jnp.float32
    )
    inner_sum = jnp.sum(probs * grad_probs, axis=-1, keepdims=True)
    grad_scores = (probs * (grad_probs - inner_sum)).astype(jnp.bfloat16)
    grad_qr = jnp.einsum(
        "skgij,sjkd->sikgd", grad_scores, key_rows, preferred_element_type=jnp.float32
    ) * HEAD_WIDTH ** (-0.5)
    grad_kr = jnp.einsum(
        "skgij,sikgd->sjkd", grad_scores, grouped, preferred_element_type=jnp.float32
    ) * HEAD_WIDTH ** (-0.5)
    grad_vals = jnp.einsum(
        "skgij,sikgd->sjkd", probs_low, grad_att, preferred_element_type=jnp.float32
    )
    grad_q = (
        unrotate(grad_qr.reshape(rows, QUERY_HEADS, HEAD_WIDTH), cosine, sine)
        .reshape(rows, D)
        .astype(jnp.bfloat16)
    )
    grad_k = (
        unrotate(grad_kr.reshape(rows, KEY_VALUE_HEADS, HEAD_WIDTH), cosine, sine)
        .reshape(rows, KEY_VALUE_HEADS * HEAD_WIDTH)
        .astype(jnp.bfloat16)
    )
    grad_v = grad_vals.reshape(rows, KEY_VALUE_HEADS * HEAD_WIDTH).astype(jnp.bfloat16)
    grad_query = jnp.einsum("nd,ne->de", hidden_input, grad_q, preferred_element_type=jnp.float32)
    grad_key = jnp.einsum("nd,ne->de", hidden_input, grad_k, preferred_element_type=jnp.float32)
    grad_value = jnp.einsum("nd,ne->de", hidden_input, grad_v, preferred_element_type=jnp.float32)
    grad_hidden = jnp.einsum("ne,de->nd", grad_q, full_query, preferred_element_type=jnp.float32)
    grad_hidden = grad_hidden + jnp.einsum(
        "ne,de->nd", grad_k, full_key, preferred_element_type=jnp.float32
    )
    grad_hidden = grad_hidden + jnp.einsum(
        "ne,de->nd", grad_v, full_value, preferred_element_type=jnp.float32
    )
    grad_in_norm, grad_gain_attn = norm_backward(
        grad_hidden, normal_one, inverse_one, gain_attn.astype(jnp.float32)
    )
    grad_inputs = grad_middle + grad_in_norm
    owned = (
        lax.psum_scatter(
            grad_query.astype(jnp.bfloat16), "group", scatter_dimension=0, tiled=True
        ).astype(jnp.float32),
        lax.psum_scatter(
            grad_key.astype(jnp.bfloat16), "group", scatter_dimension=0, tiled=True
        ).astype(jnp.float32),
        lax.psum_scatter(
            grad_value.astype(jnp.bfloat16), "group", scatter_dimension=0, tiled=True
        ).astype(jnp.float32),
        lax.psum_scatter(
            grad_out.astype(jnp.bfloat16), "group", scatter_dimension=0, tiled=True
        ).astype(jnp.float32),
        lax.psum_scatter(
            grad_gate.astype(jnp.bfloat16), "group", scatter_dimension=0, tiled=True
        ).astype(jnp.float32),
        lax.psum_scatter(
            grad_up.astype(jnp.bfloat16), "group", scatter_dimension=0, tiled=True
        ).astype(jnp.float32),
        lax.psum_scatter(
            grad_down.astype(jnp.bfloat16), "group", scatter_dimension=0, tiled=True
        ).astype(jnp.float32),
        lax.psum_scatter(
            grad_gain_attn.astype(jnp.bfloat16), "group", scatter_dimension=0, tiled=True
        ).astype(jnp.float32),
        lax.psum_scatter(
            grad_gain_ffn.astype(jnp.bfloat16), "group", scatter_dimension=0, tiled=True
        ).astype(jnp.float32),
    )
    summed = lax.psum(
        (owned[0], owned[1], owned[2], owned[3], owned[4], owned[5], owned[6], owned[7], owned[8]),
        "replica",
    )
    final = tuple(summed)
    return (result.astype(jnp.bfloat16), grad_inputs.astype(jnp.bfloat16)) + final


def solution(mesh):
    return jax.shard_map(
        per_device,
        mesh=mesh,
        in_specs=(
            P(("group", "replica"), None),
            P(("group", "replica"), None),
            P("group", None),
            P("group", None),
            P("group", None),
            P("group", None),
            P("group", None),
            P("group", None),
            P("group", None),
            P("group"),
            P("group"),
            P(("group", "replica"), None),
        ),
        out_specs=(
            P(("group", "replica"), None),
            P(("group", "replica"), None),
            P("group", None),
            P("group", None),
            P("group", None),
            P("group", None),
            P("group", None),
            P("group", None),
            P("group", None),
            P("group"),
            P("group"),
        ),
        check_vma=False,
    )
```

profile of v0, /device:TPU:0, one launch (start us, length us, event | category | flops | bytes accessed | tf_op | source)
XLA Modules:
  0.0 955.5 jit_solution(16804725038905116287)
XLA Ops:
  12.6 8.3 all-reduce.6
  23.0 2.9 multiply_cosine_fusion.1
  26.6 1.2 compare_and_fusion
  27.9 9.2 all-gather.1
  37.6 1.4 reshape.203
  39.0 8.0 all-gather
  48.0 1.8 convolution_convert_fusion.6
  49.8 2.6 reshape.184
  52.4 3.1 fusion.70
  55.5 3.2 reshape.185
  58.7 2.2 slice_negate_fusion.3
  60.9 2.5 concatenate.39
  63.4 1.4 concatenate.40
  64.8 1.3 pad_maximum_fusion.2
  66.8 2.9 fusion.58
  69.8 6.1 fusion.67
  76.0 6.3 reshape.187
  82.2 4.7 slice_negate_fusion.1
  87.0 4.4 concatenate.43
  91.4 3.9 concatenate.44
  95.2 5.5 fusion.21
  100.8 14.2 %fusion.75 = (f32[2,5,3,512]{3,2,1,0:T(4,128)S(1)}, f32[2,5,3,512,512]{3,4,2,1,0:T(8,128)}) fusion(bf16[2,512,5,3,64]{1,0,4,3,2:T(2,128)(2,1)S(1)} %fusion.21, bf16[2,512,5,64,1]{1,0,3,2,4:T(2,128)(2,1)S(1)} %fusion.58, pred[2,512,512]{1,2,0:T(8,128)(4,1)S(1)} %copy-done.12), kind=kOutput, calls=%fused_computation.114 | convolution fusion | flops 1030210560 | bytes 34664448 | tf_op jit(solution)/shard_map/sikgd,sjkd->skgij/dot_general | solution.py:56
  115.0 12.8 %exponential_reduce_fusion = f32[2,5,3,512]{3,2,1,0:T(4,128)S(1)} fusion(f32[2,5,3,512,512]{3,4,2,1,0:T(8,128)} %get-tuple-element.48, f32[2,5,3,512]{3,2,1,0:T(4,128)S(1)} %get-tuple-element.47), kind=kLoop, calls=%fused_computation.7 | loop fusion | flops 15713280 | bytes 31580160 | tf_op jit(solution)/shard_map/reduce_sum | solution.py:128
  127.8 13.0 %convert_bitcast_fusion = bf16[2,512,5,3,64]{1,4,3,2,0:T(8,128)(2,1)S(1)} fusion(f32[2,5,3,512,512]{3,4,2,1,0:T(8,128)} %get-tuple-element.48, f32[2,5,3,512]{3,2,1,0:T(4,128)S(1)} %log_add_fusion, bf16[2,512,5,64,1]{1,0,3,2,4:T(2,128)(2,1)S(1)} %bitcast.148), kind=kOutput, calls=%fused_computation.54 | convolution fusion | flops 1023344640 | bytes 34140160 | tf_op jit(solution)/shard_map/skgij,sjkd->sikgd/dot_general | solution.py:130
  140.8 2.0 copy.59
  142.9 1.8 copy.98
  144.7 4.6 multiply_reduce_fusion.2
  149.3 2.0 copy-done.5
  151.7 1.2 copy-done.25
  153.0 10.5 %fusion.77 = f32[1024,2560]{1,0:T(8,128)} fusion(bf16[1024,960]{0,1:T(8,128)(2,1)S(1)} %multiply_convert_fusion.3, bf16[960,2560]{1,0:T(8,128)(2,1)} %all-gather.14.cloned.1.call-done), kind=kOutput, calls=%fused_computation.116 | convolution fusion | flops 5033164800 | bytes 17367040 | tf_op jit(solution)/shard_map/dot_general | solution.py:138
  163.5 10.7 %fusion.76 = f32[1024,2560]{1,0:T(8,128)} fusion(bf16[1024,960]{0,1:T(8,128)(2,1)} %copy-done.25, bf16[960,2560]{1,0:T(8,128)(2,1)} %all-gather.12.cloned.1.call-done), kind=kOutput, calls=%fused_computation.115 | convolution fusion | flops 5033164800 | bytes 17367040 | tf_op jit(solution)/shard_map/dot_general | solution.py:137
  174.2 5.4 all-gather.16.cloned.1.call-done
  179.5 19.4 %multiply_convert_fusion = (bf16[1024,2560]{1,0:T(8,128)(2,1)}, bf16[1024,2560]{1,0:T(8,128)(2,1)}, bf16[1024,2560]{1,0:T(8,128)(2,1)}) fusion(f32[1024,2560]{1,0:T(8,128)} %fusion.76, f32[1024,2560]{1,0:T(8,128)} %fusion.77, bf16[1024,960]{0,1:T(8,128)(2,1)S(1)} %copy-done.24, bf16[2560,960]{0,1:T(8,128)(2,1)} %all-gather.16.cloned.1.call-done), kind=kOutput, calls=%fused_computation.9 | convolution fusion | flops 5075107840 | bytes 43581440 | tf_op jit(solution)/shard_map/nd,fd->nf/dot_general | solution.py:165
  198.9 9.2 fusion.78
  208.2 8.8 multiply_reduce_fusion
  218.0 1.9 copy-done.8
  219.9 3.5 convolution_convert_fusion.3
  223.4 4.8 reshape.189
  228.2 12.6 %fusion.51 = bf16[2,512,5,64]{1,3,2,0:T(8,128)(2,1)S(1)} fusion(f32[2,5,3,512,512]{3,4,2,1,0:T(8,128)} %get-tuple-element.48, f32[2,5,3,512]{3,2,1,0:T(4,128)S(1)} %log_add_fusion, bf16[2,512,5,3,64]{1,0,4,3,2:T(2,128)(2,1)S(1)} %reshape.189), kind=kOutput, calls=%fused_computation.79 | convolution fusion | flops 1022689280 | bytes 34140160 | tf_op jit(solution)/shard_map/skgij,sikgd->sjkd/dot_general | solution.py:206
  240.8 24.1 %fusion = (f32[2,5,3,512]{3,2,1,0:T(4,128)S(1)}, f32[2,5,512,512,3]{3,2,4,1,0:T(8,128)}) fusion(f32[2,5,3,512,512]{3,4,2,1,0:T(8,128)} %get-tuple-element.48, f32[2,5,3,512]{3,2,1,0:T(4,128)S(1)} %log_add_fusion, bf16[2,512,5,3,64]{1,0,4,3,2:T(2,128)(2,1)S(1)} %reshape.189, bf16[2,512,5,64,1]{1,0,3,2,4:T(2,128)(2,1)S(1)} %bitcast.149), kind=kOutput, calls=%fused_computation.2 | convolution fusion | flops 1030210560 | bytes 65658880 | tf_op jit(solution)/shard_map/sikgd,sjkd->skgij/dot_general | solution.py:195
  268.8 27.1 %fusion.2 = bf16[2,5,3,512,512]{3,4,2,1,0:T(8,128)(2,1)} fusion(f32[2,5,512,512,3]{3,2,4,1,0:T(8,128)} %get-tuple-element.53, f32[2,5,3,512,512]{3,4,2,1,0:T(8,128)} %get-tuple-element.48, f32[2,5,3,512]{3,2,1,0:T(4,128)S(1)} %get-tuple-element.52, f32[2,5,3,512]{3,2,1,0:T(4,128)S(1)} %log_add_fusion), kind=kLoop, calls=%fused_computation.4 | loop fusion | flops 31457280 | bytes 78766080 | tf_op jit(solution)/shard_map/convert_element_type | solution.py:199
  295.9 10.3 %fusion.40 = f32[2,5,64,512]{3,2,1,0:T(8,128)S(1)} fusion(bf16[2,5,3,512,512]{3,4,2,1,0:T(8,128)(2,1)} %fusion.2, bf16[2,512,5,3,64]{1,0,4,3,2:T(2,128)(2,1)S(1)} %copy-done.1), kind=kOutput, calls=%fused_computation.67 | convolution fusion | flops 1006960640 | bytes 19005440 | tf_op jit(solution)/shard_map/skgij,sikgd->sjkd/dot_general | solution.py:203
  311.6 6.3 convolution_convert_fusion.4
  318.2 8.4 multiply_bitcast_fusion
  326.6 4.9 copy.64
  331.5 6.3 reshape.191
  337.8 3.2 copy.99
  344.0 1.3 copy-done.22
  345.3 3.5 convolution_convert_fusion.5
  349.3 9.8 %convolution_convert_fusion = bf16[2560,960]{0,1:T(8,128)(2,1)} fusion(bf16[1024,960]{0,1:T(8,128)(2,1)} %param.23, bf16[1024,2560]{1,0:T(8,128)(2,1)} %get-tuple-element.30), kind=kOutput, calls=%fused_computation.20 | convolution fusion | flops 5035622400 | bytes 12124160 | tf_op jit(solution)/shard_map/nf,nd->fd/dot_general | solution.py:164
  359.0 7.9 copy.95
  367.0 9.8 %convolution_convert_fusion.2 = bf16[960,2560]{1,0:T(8,128)(2,1)} fusion(bf16[1024,960]{0,1:T(8,128)(2,1)} %copy-done.25, bf16[1024,2560]{1,0:T(8,128)(2,1)} %get-tuple-element.29), kind=kOutput, calls=%fused_computation.22 | convolution fusion | flops 5035622400 | bytes 12124160 | tf_op jit(solution)/shard_map/nd,nf->df/dot_general | solution.py:170
  376.9 10.0 %convolution_convert_fusion.1 = bf16[960,2560]{1,0:T(8,128)(2,1)} fusion(bf16[1024,960]{0,1:T(8,128)(2,1)} %copy-done.25, bf16[1024,2560]{1,0:T(8,128)(2,1)} %get-tuple-element.28), kind=kOutput, calls=%fused_computation.21 | convolution fusion | flops 5035622400 | bytes 12124160 | tf_op jit(solution)/shard_map/nd,nf->df/dot_general | solution.py:173
  388.0 1.2 fusion.79
  390.4 2.2 fusion.80
  392.7 3.9 fusion.18
  396.6 6.4 all-reduce.5
  403.1 5.7 fusion.17
  408.9 10.6 %add_convert_fusion = bf16[1024,960]{0,1:T(8,128)(2,1)} fusion(f32[1024,960]{0,1:T(8,128)S(1)} %copy-done.7, bf16[1024,2560]{1,0:T(8,128)(2,1)} %get-tuple-element.30, bf16[2560,960]{0,1:T(8,128)(2,1)} %all-gather.16.cloned.1.call-done), kind=kOutput, calls=%fused_computation.45 | convolution fusion | flops 5035130880 | bytes 16056320 | tf_op jit(solution)/shard_map/dot_general | solution.py:141
  421.6 34.8 %reduce-scatter.26.cloned.1.call-done = bf16[640,960]{1,0:T(8,128)(2,1)} async-done(((bf16[2560,960]{1,0:T(8,128)(2,1)}), bf16[640,960]{1,0:T(8,128)(2,1)}) %reduce-scatter.26.cloned.1.call-update) | async-done | bytes 1228816
  456.4 2.1 copy.96
  458.6 49.9 %reduce-scatter.18.cloned.1.call-done = bf16[240,2560]{1,0:T(8,128)(2,1)} async-done(((bf16[960,2560]{1,0:T(8,128)(2,1)}), bf16[240,2560]{1,0:T(8,128)(2,1)}) %reduce-scatter.18.cloned.1.call-update) | async-done | bytes 1228816 | tf_op jit(solution)/shard_map/reduce_scatter | solution.py:247
  508.5 51.7 %reduce-scatter.20.cloned.1.call-done = bf16[240,2560]{1,0:T(8,128)(2,1)} async-done(((bf16[960,2560]{1,0:T(8,128)(2,1)}), bf16[240,2560]{1,0:T(8,128)(2,1)}) %reduce-scatter.20.cloned.1.call-update) | async-done | bytes 1228816 | tf_op jit(solution)/shard_map/reduce_scatter | solution.py:250
  560.2 388.3 %all-reduce.8 = (f32[240,960]{1,0:T(8,128)}, f32[240,320]{0,1:T(8,128)}, f32[240,320]{0,1:T(8,128)}, f32[240,960]{1,0:T(8,128)}, f32[240,2560]{1,0:T(8,128)}, /*...) all-reduce(bf16[240,960]{1,0:T(8,128)(2,1)} %reduce-scatter.14.clon, ...), channel_id=1, replica_groups=mesh['group'=4,'replica'=8] {'replica'}, use_global_device_ids=true, to_apply=%region_9.10 | all-reduce | flops 2458080 | bytes 14749440 | tf_op jit(solution)/shard_map/psum | solution.py:263
  (155 shorter events, 27.9 us)
Async XLA Ops:
  7.2 3.6 copy-start.33
  7.2 4.9 copy-start.37
  7.2 5.1 copy-start.38
  7.2 13.7 %copy-start.28 = (s32[2,512]{1,0:T(2,128)S(1)}, s32[2,512]{1,0:T(2,128)}, u32[]{:S(2)}) copy-start(s32[2,512]{1,0:T(2,128)} %param.13) | copy-start | bytes 12292
  7.2 14.1 %copy-start.2 = (bf16[1024,960]{0,1:T(8,128)(2,1)S(1)}, bf16[1024,960]{0,1:T(8,128)(2,1)}, u32[]{:S(2)}) copy-start(bf16[1024,960]{0,1:T(8,128)(2,1)} %param.12) | copy-start | bytes 5898244
  7.2 62.6 %all-gather.8.cloned.1.call-start = ((), (), s32[]{:S(2)}) async-start(), calls=%async_computation.7 | async-start | bytes 2457600 | tf_op jit(solution)/shard_map/all_gather | solution.py:81
  8.0 136.7 %all-gather.10.cloned.1.call-start = ((), (), s32[]{:S(2)}) async-start(), calls=%async_computation.8 | async-start | bytes 2457600 | tf_op jit(solution)/shard_map/all_gather | solution.py:84
  8.7 19.2 %copy-start.26 = (bf16[240,320]{0,1:T(8,128)(2,1)S(1)}, bf16[240,320]{0,1:T(8,128)(2,1)}, u32[]{:S(2)}) copy-start(bf16[240,320]{0,1:T(8,128)(2,1)} %param.15) | copy-start | bytes 460804
  8.7 143.0 %all-gather.14.cloned.1.call-start = ((), (), s32[]{:S(2)}) async-start(), calls=%async_computation.10 | async-start | bytes 6144000 | tf_op jit(solution)/shard_map/all_gather | solution.py:86
  9.5 154.0 %all-gather.12.cloned.1.call-start = ((), (), s32[]{:S(2)}) async-start(), calls=%async_computation.9 | async-start | bytes 6144000 | tf_op jit(solution)/shard_map/all_gather | solution.py:85
  10.0 169.5 %all-gather.16.cloned.1.call-start = ((), (), s32[]{:S(2)}) async-start(), calls=%async_computation.11 | async-start | bytes 6144000 | tf_op jit(solution)/shard_map/all_gather | solution.py:87
  10.6 408.8 %reduce-scatter.24.cloned.1.call-start = ((), (), s32[]{:S(2)}) async-start(), calls=%async_computation.17 | async-start | bytes 921600
  10.7 28.3 %copy-start.27 = (bf16[240,320]{0,1:T(8,128)(2,1)S(1)}, bf16[240,320]{0,1:T(8,128)(2,1)}, u32[]{:S(2)}) copy-start(bf16[240,320]{0,1:T(8,128)(2,1)} %param.16) | copy-start | bytes 460804
  20.9 48.9 %copy-start.29 = (f32[960]{0:T(1024)}, f32[960]{0:T(1024)S(1)}, u32[]{:S(2)}) copy-start(f32[960]{0:T(1024)S(1)} %convert_element_type.149) | copy-start | bytes 11524
  21.7 48.1 %copy-start.31 = (f32[1024]{0:T(1024)}, f32[1024]{0:T(1024)S(1)}, u32[]{:S(2)}) copy-start(f32[1024]{0:T(1024)S(1)} %add_rsqrt_fusion.1) | copy-start | bytes 12292
  48.0 4.4 copy-start.13
  66.1 0.7 copy-start.21
  69.8 31.0 %copy-start.10 = (bf16[2,512,5,64,1]{1,0,3,2,4:T(2,128)(2,1)}, bf16[2,512,5,64,1]{1,0,3,2,4:T(2,128)(2,1)S(1)}, u32[]{:S(2)}) copy-start(bf16[2,512,5,64,1]{1,0,3,2,4:T(2,128)(2,1)S(1)} %fusion.58) | copy-start | bytes 1966084
  95.2 5.5 copy-start.12
  100.8 14.2 %copy-start = (bf16[2,512,5,3,64]{1,0,4,3,2:T(2,128)(2,1)}, bf16[2,512,5,3,64]{1,0,4,3,2:T(2,128)(2,1)S(1)}, u32[]{:S(2)}) copy-start(bf16[2,512,5,3,64]{1,0,4,3,2:T(2,128)(2,1)S(1)} %fusion.21) | copy-start | bytes 5898244
  149.3 2.0 copy-start.5
  151.7 1.3 copy-start.25
  163.5 16.0 %copy-start.24 = (bf16[1024,960]{0,1:T(8,128)(2,1)S(1)}, bf16[1024,960]{0,1:T(8,128)(2,1)}, u32[]{:S(2)}) copy-start(bf16[1024,960]{0,1:T(8,128)(2,1)} %param.23) | copy-start | bytes 5898244
  198.9 9.2 copy-start.6
  198.9 9.2 copy-start.39
  217.0 2.9 copy-start.36
  218.0 1.9 copy-start.8
  240.8 25.8 %copy-start.3 = (bf16[1024,960]{0,1:T(8,128)(2,1)S(1)}, bf16[1024,960]{0,1:T(8,128)(2,1)}, u32[]{:S(2)}) copy-start(bf16[1024,960]{0,1:T(8,128)(2,1)} %param.12) | copy-start | bytes 5898244
  240.8 25.8 %copy-start.30 = (f32[960]{0:T(1024)S(1)}, f32[960]{0:T(1024)}, u32[]{:S(2)}) copy-start(f32[960]{0:T(1024)} %copy-done.29) | copy-start | bytes 11524
  240.8 25.8 %copy-start.32 = (f32[1024]{0:T(1024)S(1)}, f32[1024]{0:T(1024)}, u32[]{:S(2)}) copy-start(f32[1024]{0:T(1024)} %copy-done.31) | copy-start | bytes 12292
  265.7 0.9 copy-start.16
  268.7 151.8 %reduce-scatter.22.cloned.1.call-start = ((), (), s32[]{:S(2)}) async-start(), calls=%async_computation.16 | async-start | bytes 921600
  268.8 27.1 %copy-start.1 = (bf16[2,512,5,3,64]{1,0,4,3,2:T(2,128)(2,1)S(1)}, bf16[2,512,5,3,64]{1,0,4,3,2:T(2,128)(2,1)}, u32[]{:S(2)}) copy-start(bf16[2,512,5,3,64]{1,0,4,3,2:T(2,128)(2,1)} %copy-done) | copy-start | bytes 5898244
  306.2 1.4 copy-start.19
  307.7 1.0 copy-start.18
  307.8 1.6 copy-start.4
  311.6 6.6 copy-start.11
  311.6 110.0 %reduce-scatter.16.cloned.1.call-start = ((), (), s32[]{:S(2)}) async-start(), calls=%async_computation.13 | async-start | bytes 2457600 | tf_op jit(solution)/shard_map/reduce_scatter | solution.py:244
  317.9 103.7 %reduce-scatter.14.cloned.1.call-start = ((), (), s32[]{:S(2)}) async-start(), calls=%async_computation.12 | async-start | bytes 2457600 | tf_op jit(solution)/shard_map/reduce_scatter | solution.py:235
  337.8 3.3 copy-start.9
  337.8 3.3 copy-start.20
  344.0 1.3 copy-start.22
  348.8 107.6 %reduce-scatter.26.cloned.1.call-start = ((), (), s32[]{:S(2)}) async-start(), calls=%async_computation.18 | async-start | bytes 6553600
  367.0 141.5 %reduce-scatter.18.cloned.1.call-start = ((), (), s32[]{:S(2)}) async-start(), calls=%async_computation.14 | async-start | bytes 6144000 | tf_op jit(solution)/shard_map/reduce_scatter | solution.py:247
  376.8 183.3 %reduce-scatter.20.cloned.1.call-start = ((), (), s32[]{:S(2)}) async-start(), calls=%async_computation.15 | async-start | bytes 6144000 | tf_op jit(solution)/shard_map/reduce_scatter | solution.py:250
  386.9 1.1 copy-start.15
  388.0 1.8 copy-start.23
  388.0 2.4 copy-start.35
  390.4 2.2 copy-start.14
  390.4 2.2 copy-start.17
  392.7 3.9 copy-start.34
  403.1 5.7 copy-start.7
Sparse Core Ops, SparseCore 0:
  9.6 26.6 all-gather.7
  37.9 21.4 all-gather.9
  60.9 38.5 all-gather.13
  100.9 38.5 all-gather.11
  140.9 38.5 all-gather.15
  268.9 22.9 reduce-scatter.23
  311.7 22.9 reduce-scatter.21
  337.8 30.6 reduce-scatter.15
  371.8 30.6 reduce-scatter.13
  405.0 51.4 reduce-scatter.25
  459.2 49.2 reduce-scatter.17
  510.9 49.2 reduce-scatter.19
where the time goes:
time: 962 us; the launch traced here: 955 us
  blocking collectives  420 us (44%)
  matrix products  220 us (23%)
  waiting for transfers between devices  145 us (15%)
  local copies, waits for them, and re-layouts  78.7 us (8%)
  other arithmetic  74.4 us (8%)
  between operations  16.5 us (2%)
    psum x1, blocking collectives, per_device(): lax.psum((owned[0], owned[1], owned[2], owned[3], owned[4], owned[5], own...  388 us
    reduce_scatter x1, waiting for transfers between devices, per_device(): lax.psum_scatter(grad_up.astype(jnp.bfloat16), 'group', scatter_dimension...  51.7 us
    reduce_scatter x1, waiting for transfers between devices, per_device(): lax.psum_scatter(grad_gate.astype(jnp.bfloat16), 'group', scatter_dimensi...  49.9 us
    unnamed x15, waiting for transfers between devices  38.1 us
    unnamed x98, local copies, waits for them, and re-layouts  33.6 us
    convert_element_type x1, other arithmetic, per_device(): grad_scores = (probs * (grad_probs - inner_sum)).astype(jnp.bfloat16)  27.1 us
    dot_general x1, matrix products, per_device(): jnp.einsum('sikgd,sjkd->skgij', grad_att, value_rows, preferred_element_t...  24.1 us
    dot_general x1, matrix products, per_device(): jnp.einsum('nd,fd->nf', cotangent, full_down, preferred_element_type=jnp....  19.4 us
  transfers between devices with their start and end apart: 12, of which 4 were waited for; matrix products, arithmetic and copies ran while one was open for 29% of the time, Pallas kernels for 0%

commit v1 on v0

v1 whole, which is shorter than its diff:
```python
import jax
import jax.numpy as jnp
from jax import lax
from jax.experimental import pallas as pl
from jax.experimental.pallas import tpu as pltpu
from jax.sharding import PartitionSpec as P

D = 960
QUERY_HEADS = 15
KEY_VALUE_HEADS = 5
HEAD_WIDTH = 64
SHARE = QUERY_HEADS // KEY_VALUE_HEADS
HALF = HEAD_WIDTH // 2
KEYS = KEY_VALUE_HEADS * HEAD_WIDTH
EPS = 1e-05
THETA = 100000.0
TILE = 256
QB = 128
GAINS = 128
WIDE = D + 2 * KEYS
CUT = 640
OWN = 240
F32 = jnp.float32
BF16 = jnp.bfloat16
MIB = 1 << 20


def dot(a, b, ca, cb):
    return lax.dot_general(a, b, (((ca,), (cb,)), ((), ())), preferred_element_type=F32)


def params(limit, grid=1):
    return pltpu.CompilerParams(
        vmem_limit_bytes=limit * MIB, dimension_semantics=("arbitrary",) * grid
    )


def cost(flops, moved, exps=0):
    return pl.CostEstimate(flops=flops, bytes_accessed=moved, transcendentals=exps)


def shaped(*shape_type):
    return [jax.ShapeDtypeStruct(s, t) for s, t in shape_type]


def norm_columns(v):
    inverse = lax.rsqrt(jnp.mean(v * v, axis=0, keepdims=True) + EPS)
    return v * inverse, inverse


def norm_columns_back(grad, normal, inverse, gain):
    scaled = grad * gain
    back = inverse * (scaled - normal * jnp.mean(scaled * normal, axis=0, keepdims=True))
    return back, jnp.sum(grad * normal, axis=1, keepdims=True)


def fixed(shape):
    return pl.BlockSpec(shape, lambda *_: (0,) * len(shape), pipeline_mode=pl.Buffered(1))


def columns(height, width):
    return pl.BlockSpec((height, width), lambda i: (0, i))


def project_kernel(x_ref, w_ref, cos_ref, sin_ref, qkv_ref, h_ref):
    gain = w_ref[:, 0:1].astype(F32)
    normal, _ = norm_columns(x_ref[...].astype(F32))
    h = (normal * gain).astype(BF16)
    h_ref[...] = h
    c, s = cos_ref[...], sin_ref[...]
    out = dot(w_ref[:, GAINS:], h, 0, 0)
    for head in range(QUERY_HEADS + KEY_VALUE_HEADS):
        at = head * HEAD_WIDTH
        a, b = out[at:at + HALF], out[at + HALF:at + HEAD_WIDTH]
        scale = HEAD_WIDTH ** -0.5 if head < QUERY_HEADS else 1.0
        qkv_ref[at:at + HALF, :] = ((a * c - b * s) * scale).astype(BF16)
        qkv_ref[at + HALF:at + HEAD_WIDTH, :] = ((b * c + a * s) * scale).astype(BF16)
    qkv_ref[D + KEYS:, :] = out[D + KEYS:].astype(BF16)


def project(x, w, cos, sin):
    rows = x.shape[1]
    return pl.pallas_call(
        project_kernel,
        grid=(rows // TILE,),
        in_specs=[columns(D, TILE), fixed(w.shape), columns(HALF, TILE), columns(HALF, TILE)],
        out_specs=[columns(WIDE, TILE), columns(D, TILE)],
        out_shape=shaped(((WIDE, rows), BF16), ((D, rows), BF16)),
        compiler_params=params(40),
        cost_estimate=cost(2 * rows * D * WIDE, rows * (2 * D + WIDE) * 2 + D * WIDE * 2),
        name="project",
    )(x, w, cos, sin)


def key_span(block):
    return max(0, QB * (block - 2)), QB * (block + 1)


def make_bias(bias_ref, segr_ref, segc_ref, length):
    for b in range(length // QB):
        lo, hi = key_span(b)
        key_at = lax.broadcasted_iota(jnp.int32, (hi - lo, QB), 0) + lo
        query_at = lax.broadcasted_iota(jnp.int32, (hi - lo, QB), 1) + b * QB
        ok = (segc_ref[lo:hi, :] == segr_ref[:, b * QB:(b + 1) * QB]) & (key_at <= query_at)
        bias_ref[b, 0:hi - lo, :] = jnp.where(ok, 0.0, -1e30)


def three(ref, kv, b):
    return jnp.concatenate(
        [
            ref[pl.ds(pl.multiple_of((kv * SHARE + i) * HEAD_WIDTH, HEAD_WIDTH), HEAD_WIDTH),
                b * QB:(b + 1) * QB]
            for i in range(SHARE)
        ],
        axis=1,
    )


def wide_bias(bias_ref, b, n):
    one = bias_ref[b, 0:n, :]
    return jnp.concatenate([one] * SHARE, axis=1)


def attend_kernel(qkv_ref, segr_ref, segc_ref, o_ref, lse_ref, bias_ref):
    length = qkv_ref.shape[1]
    make_bias(bias_ref, segr_ref.at[0], segc_ref.at[0], length)

    @pl.loop(0, KEY_VALUE_HEADS)
    def _(kv):
        k = qkv_ref[pl.ds(pl.multiple_of(D + kv * HEAD_WIDTH, HEAD_WIDTH), HEAD_WIDTH), :]
        v = qkv_ref[pl.ds(pl.multiple_of(D + KEYS + kv * HEAD_WIDTH, HEAD_WIDTH), HEAD_WIDTH), :]
        for b in range(length // QB):
            lo, hi = key_span(b)
            s = dot(k[:, lo:hi], three(qkv_ref, kv, b), 0, 0) + wide_bias(bias_ref, b, hi - lo)
            top = jnp.max(s, axis=0, keepdims=True)
            p = jnp.exp(s - top)
            total = jnp.sum(p, axis=0, keepdims=True)
            out = dot(v[:, lo:hi], p.astype(BF16), 1, 0) / total
            lse = top + jnp.log(total)
            for i in range(SHARE):
                rows = pl.ds(pl.multiple_of((kv * SHARE + i) * HEAD_WIDTH, HEAD_WIDTH), HEAD_WIDTH)
                o_ref[rows, b * QB:(b + 1) * QB] = out[:, i * QB:(i + 1) * QB].astype(BF16)
                lse_ref[kv, i:i + 1, b * QB:(b + 1) * QB] = lse[:, i * QB:(i + 1) * QB]


def attend(qkv, segments):
    seqs, length = segments.shape
    wide, rows = qkv.shape
    pairs = seqs * QUERY_HEADS * length * length
    return pl.pallas_call(
        attend_kernel,
        grid=(seqs,),
        in_specs=[
            pl.BlockSpec((wide, length), lambda i: (0, i)),
            pl.BlockSpec((1, 1, length), lambda i: (i, 0, 0)),
            pl.BlockSpec((1, length, 1), lambda i: (i, 0, 0)),
        ],
        out_specs=[
            pl.BlockSpec((D, length), lambda i: (0, i)),
            pl.BlockSpec((KEY_VALUE_HEADS, 8, length), lambda i: (0, 0, i)),
        ],
        out_shape=shaped(((D, rows), BF16), ((KEY_VALUE_HEADS, 8, rows), F32)),
        scratch_shapes=[pltpu.VMEM((length // QB, 3 * QB, QB), F32)],
        compiler_params=params(48),
        cost_estimate=cost(pairs * 256 * 2, rows * (wide + D) * 2, pairs // 2),
        name="attend",
    )(qkv, segments[:, None, :], segments[:, :, None])


def middle_kernel(x_ref, o_ref, w_ref, gain_ref, x1_ref, h_ref):
    x1 = x_ref[...].astype(F32) + dot(w_ref[...], o_ref[...], 0, 0)
    normal, _ = norm_columns(x1)
    x1_ref[...] = x1
    h_ref[...] = (normal * gain_ref[:, 1:2].astype(F32)).astype(BF16)


def middle(x, o, w, gains):
    rows = x.shape[1]
    return pl.pallas_call(
        middle_kernel,
        grid=(rows // TILE,),
        in_specs=[columns(D, TILE), columns(D, TILE), fixed(w.shape), fixed((D, GAINS))],
        out_specs=[columns(D, TILE), columns(D, TILE)],
        out_shape=shaped(((D, rows), F32), ((D, rows), BF16)),
        compiler_params=params(40),
        cost_estimate=cost(2 * rows * D * D, rows * D * 10),
        name="middle",
    )(x, o, w, gains)


def split_owners(grad, core, keep_ref, send_ref):
    for x in range(2):
        a = grad[2 * x * OWN:(2 * x + 1) * OWN]
        b = grad[(2 * x + 1) * OWN:(2 * x + 2) * OWN]
        keep_ref[x, 0] = jnp.where(core == 0, a, b).astype(BF16)
        send_ref[x, 0] = jnp.where(core == 0, b, a).astype(BF16)


def feed_forward_kernel(core_ref, h_ref, dy_ref, x1_ref, wg_ref, wu_ref, wd_ref, y_ref, dh_ref,
                        gg_keep, gg_send, gu_keep, gu_send, gd_keep, gd_send, acc_ref):
    step = pl.program_id(0)
    core = core_ref[0]

    @pl.when(step == 0)
    def _():
        acc_ref[...] = x1_ref[...]
        dh_ref[...] = jnp.zeros_like(dh_ref)

    h, dy = h_ref[...], dy_ref[...]
    gate = dot(wg_ref[...], h, 0, 0)
    up = dot(wu_ref[...], h, 0, 0)
    dhid = dot(wd_ref[...], dy, 0, 0)
    sig = jax.nn.sigmoid(gate)
    silu = gate * sig
    hid = (silu * up).astype(BF16)
    dgate = (dhid * up * (sig + silu * (1.0 - sig))).astype(BF16)
    dup = (dhid * silu).astype(BF16)
    acc_ref[...] += dot(wd_ref[...], hid, 1, 0)
    split_owners(dot(h, dgate, 1, 1), core, gg_keep, gg_send)
    split_owners(dot(h, dup, 1, 1), core, gu_keep, gu_send)
    down = dot(dy, hid, 1, 1).astype(BF16).reshape(4, OWN, CUT)

    @pl.when(step % 2 == core)
    def _():
        gd_keep[0] = down

    @pl.when(step % 2 != core)
    def _():
        gd_send[0] = down

    dh_ref[...] += dot(wg_ref[...], dgate, 1, 0) + dot(wu_ref[...], dup, 1, 0)

    @pl.when(step == pl.num_programs(0) - 1)
    def _():
        y_ref[...] = acc_ref[...].astype(BF16)


def feed_forward(core, h, dy, x1, wg, wu, wd):
    rows, hidden = h.shape[1], wg.shape[1]
    steps = hidden // CUT
    part = (2, steps, OWN, CUT)
    by_rows = pl.BlockSpec((2, 1, OWN, CUT), lambda f: (0, f, 0, 0))
    by_columns = pl.BlockSpec((1, steps, OWN, CUT), lambda f: (f // 2, 0, 0, 0))
    return pl.pallas_call(
        feed_forward_kernel,
        grid=(steps,),
        in_specs=[
            pl.BlockSpec(memory_space=pltpu.SMEM),
            fixed((D, rows)), fixed((D, rows)), fixed((D, rows)),
            columns(D, CUT), columns(D, CUT), columns(D, CUT),
        ],
        out_specs=[fixed((D, rows)), fixed((D, rows))] + [by_rows] * 4 + [by_columns] * 2,
        out_shape=shaped(((D, rows), BF16), ((D, rows), F32)) + shaped((part, BF16)) * 6,
        scratch_shapes=[pltpu.VMEM((D, rows), F32)],
        compiler_params=params(60),
        cost_estimate=cost(18 * rows * D * hidden, 16 * rows * D + 12 * D * hidden, rows * hidden),
        name="feed_forward",
    )(core, h, dy, x1, wg, wu, wd)


def branch_kernel(dh_ref, x1_ref, dy_ref, gain_ref, w_ref, dx_ref, da_ref, do_ref, gain_grad):
    gain = gain_ref[:, 1:2].astype(F32)
    normal, inverse = norm_columns(x1_ref[...])
    back, part = norm_columns_back(dh_ref[...], normal, inverse, gain)
    dx = dy_ref[...].astype(F32) + back
    da = dx.astype(BF16)
    dx_ref[...] = dx
    da_ref[...] = da
    do_ref[...] = dot(w_ref[...], da, 1, 0).astype(BF16)

    @pl.when(pl.program_id(0) == 0)
    def _():
        gain_grad[...] = part

    @pl.when(pl.program_id(0) > 0)
    def _():
        gain_grad[...] += part


def branch(dh, x1, dy, gains, w):
    rows = dh.shape[1]
    return pl.pallas_call(
        branch_kernel,
        grid=(rows // TILE,),
        in_specs=[columns(D, TILE)] * 3 + [fixed((D, GAINS)), fixed(w.shape)],
        out_specs=[columns(D, TILE)] * 3 + [pl.BlockSpec((D, 1), lambda i: (0, 0))],
        out_shape=shaped(((D, rows), F32), ((D, rows), BF16), ((D, rows), BF16), ((D, 1), F32)),
        compiler_params=params(40),
        cost_estimate=cost(2 * rows * D * D, rows * D * 18),
        name="branch",
    )(dh, x1, dy, gains, w)


def attend_back_kernel(qkv_ref, o_ref, do_ref, lse_ref, segr_ref, segc_ref, cos_ref, sin_ref,
                       out_ref, bias_ref, dk_ref, dv_ref):
    length = qkv_ref.shape[1]
    make_bias(bias_ref, segr_ref.at[0], segc_ref.at[0], length)

    def turn_back(g, c, s, at, cols):
        a, b = g[:HALF], g[HALF:]
        at = pl.multiple_of(at, HEAD_WIDTH)
        out_ref[pl.ds(at, HALF), cols] = (a * c + b * s).astype(BF16)
        out_ref[pl.ds(pl.multiple_of(at + HALF, HALF), HALF), cols] = (b * c - a * s).astype(BF16)

    @pl.loop(0, KEY_VALUE_HEADS)
    def _(kv):
        k = qkv_ref[pl.ds(pl.multiple_of(D + kv * HEAD_WIDTH, HEAD_WIDTH), HEAD_WIDTH), :]
        v = qkv_ref[pl.ds(pl.multiple_of(D + KEYS + kv * HEAD_WIDTH, HEAD_WIDTH), HEAD_WIDTH), :]
        dk_ref[...] = jnp.zeros_like(dk_ref)
        dv_ref[...] = jnp.zeros_like(dv_ref)
        for b in range(length // QB):
            lo, hi = key_span(b)
            cols = slice(b * QB, (b + 1) * QB)
            q, o, do = three(qkv_ref, kv, b), three(o_ref, kv, b), three(do_ref, kv, b)
            lse = jnp.concatenate([lse_ref[kv, i:i + 1, cols] for i in range(SHARE)], axis=1)
            inner = jnp.sum(o.astype(F32) * do.astype(F32), axis=0, keepdims=True)
            s = dot(k[:, lo:hi], q, 0, 0) + wide_bias(bias_ref, b, hi - lo)
            p = jnp.exp(s - lse)
            dp = dot(v[:, lo:hi], do, 0, 0)
            ds = (p * (dp - inner)).astype(BF16)
            dv_ref[:, lo:hi] += dot(do, p.astype(BF16), 1, 1)
            dk_ref[:, lo:hi] += dot(q, ds, 1, 1)
            dq = dot(k[:, lo:hi], ds, 1, 0) * HEAD_WIDTH ** -0.5
            for i in range(SHARE):
                turn_back(dq[:, i * QB:(i + 1) * QB], cos_ref[:, cols], sin_ref[:, cols],
                          (kv * SHARE + i) * HEAD_WIDTH, cols)
        turn_back(dk_ref[...], cos_ref[...], sin_ref[...], D + kv * HEAD_WIDTH, slice(None))
        out_ref[pl.ds(pl.multiple_of(D + KEYS + kv * HEAD_WIDTH, HEAD_WIDTH), HEAD_WIDTH), :] = (
            dv_ref[...].astype(BF16))


def attend_back(qkv, o, do, lse, segments, cos, sin):
    seqs, length = segments.shape
    wide, rows = qkv.shape
    pairs = seqs * QUERY_HEADS * length * length
    return pl.pallas_call(
        attend_back_kernel,
        grid=(seqs,),
        in_specs=[
            pl.BlockSpec((wide, length), lambda i: (0, i)),
            pl.BlockSpec((D, length), lambda i: (0, i)),
            pl.BlockSpec((D, length), lambda i: (0, i)),
            pl.BlockSpec((KEY_VALUE_HEADS, 8, length), lambda i: (0, 0, i)),
            pl.BlockSpec((1, 1, length), lambda i: (i, 0, 0)),
            pl.BlockSpec((1, length, 1), lambda i: (i, 0, 0)),
            pl.BlockSpec((HALF, length), lambda i: (0, i)),
            pl.BlockSpec((HALF, length), lambda i: (0, i)),
        ],
        out_specs=pl.BlockSpec((wide, length), lambda i: (0, i)),
        out_shape=jax.ShapeDtypeStruct((wide, rows), BF16),
        scratch_shapes=[
            pltpu.VMEM((length // QB, 3 * QB, QB), F32),
            pltpu.VMEM((HEAD_WIDTH, length), F32),
            pltpu.VMEM((HEAD_WIDTH, length), F32),
        ],
        compiler_params=params(48),
        cost_estimate=cost(pairs * 256 * 5, rows * (2 * wide + 2 * D) * 2, pairs // 2),
        name="attend_back",
    )(qkv, o, do, lse, segments[:, None, :], segments[:, :, None], cos, sin)


def weight_kernel(core_ref, h_ref, dqkv_ref, o_ref, da_ref, keep_ref, send_ref):
    core = core_ref[0]
    step = pl.program_id(0)

    @pl.when(step < 2)
    def _():
        rows = pl.ds(pl.multiple_of(step * CUT, CUT), CUT)
        split_owners(dot(h_ref[...], dqkv_ref[rows, :], 1, 1), core, keep_ref, send_ref)

    @pl.when(step == 2)
    def _():
        left = dot(h_ref[...], dqkv_ref[2 * CUT:, :], 1, 1)
        right = dot(o_ref[...], da_ref[:3 * CUT - WIDE, :], 1, 1)
        split_owners(jnp.concatenate([left, right], axis=1), core, keep_ref, send_ref)

    @pl.when(step == 3)
    def _():
        split_owners(dot(o_ref[...], da_ref[3 * CUT - WIDE:, :], 1, 1), core, keep_ref, send_ref)


def weight_grads(core, h, dqkv, o, da):
    rows = h.shape[1]
    part = pl.BlockSpec((2, 1, OWN, CUT), lambda f: (0, f, 0, 0))
    return pl.pallas_call(
        weight_kernel,
        grid=(4,),
        in_specs=[pl.BlockSpec(memory_space=pltpu.SMEM), fixed((D, rows)), fixed((WIDE, rows)),
                  fixed((D, rows)), fixed((D, rows))],
        out_specs=[part, part],
        out_shape=shaped(((2, 4, OWN, CUT), BF16)) * 2,
        compiler_params=params(40),
        cost_estimate=cost(2 * rows * D * (D + WIDE), rows * (3 * D + WIDE) * 2 + D * 5120),
        name="weight_grads",
    )(core, h, dqkv, o, da)


def inputs_kernel(x_ref, dx_ref, w_ref, dqkv_ref, out_ref, gain_grad):
    gain = w_ref[:, 0:1].astype(F32)
    dh = dot(w_ref[:, GAINS:], dqkv_ref[...], 1, 0)
    normal, inverse = norm_columns(x_ref[...].astype(F32))
    back, part = norm_columns_back(dh, normal, inverse, gain)
    out_ref[...] = (dx_ref[...] + back).astype(BF16)

    @pl.when(pl.program_id(0) == 0)
    def _():
        gain_grad[...] = part

    @pl.when(pl.program_id(0) > 0)
    def _():
        gain_grad[...] += part


def input_grads(x, dx, w, dqkv):
    rows = x.shape[1]
    return pl.pallas_call(
        inputs_kernel,
        grid=(rows // TILE,),
        in_specs=[columns(D, TILE), columns(D, TILE), fixed(w.shape), columns(WIDE, TILE)],
        out_specs=[columns(D, TILE), pl.BlockSpec((D, 1), lambda i: (0, 0))],
        out_shape=shaped(((D, rows), BF16), ((D, 1), F32)),
        compiler_params=params(40),
        cost_estimate=cost(2 * rows * D * WIDE, rows * (D * 8 + WIDE * 2) + D * WIDE * 2),
        name="input_grads",
    )(x, dx, w, dqkv)


def tables(segments):
    length = segments.shape[1]
    index = jnp.arange(length, dtype=jnp.int32)
    same = segments[:, :, None] == segments[:, None, :]
    start = jnp.min(jnp.where(same, index[None, :, None], length), axis=1)
    position = (index[None, :] - start).astype(F32).reshape(1, -1)
    freq = THETA ** (-(jnp.arange(HALF, dtype=F32) * 2.0 / HEAD_WIDTH))
    angle = freq[:, None] * position
    return jnp.cos(angle), jnp.sin(angle)


def after(value, *others):
    return lax.optimization_barrier((value,) + others)[0]


class Cube:
    def __init__(self, count):
        self.count = count
        self.dims = count.bit_length() - 1
        self.masks = [1, 2, 6] + [1 << i for i in range(3, self.dims)]
        replica, group = lax.axis_index("replica"), lax.axis_index("group")
        bits = [(replica >> i) & 1 for i in range(self.dims)]
        self.coordinate = {i: bits[i] for i in range(self.dims)}
        self.coordinate[1] = bits[1] ^ bits[2]
        self.coordinate["x"] = group >> 1
        self.coordinate["core"] = group & 1

    def swap(self, value, dim):
        if dim == "x":
            return lax.ppermute(value, "group", [(i, i ^ 2) for i in range(4)])
        if dim == "core":
            return lax.ppermute(value, "group", [(i, i ^ 1) for i in range(4)])
        mask = self.masks[dim]
        return lax.ppermute(value, "replica", [(i, i ^ mask) for i in range(self.count)])

    def ordered(self, dim, mine, other, axis):
        return jnp.where(
            self.coordinate[dim] == 0,
            jnp.concatenate([mine, other], axis=axis),
            jnp.concatenate([other, mine], axis=axis),
        )


def gather(cube, shard, axis, relay, halves):
    sibling = cube.swap(shard, "core")
    if relay is None:
        across = cube.swap(shard, "x")
    else:
        size = shard.shape[halves] // 2
        part = lax.dynamic_slice_in_dim(shard, cube.coordinate[relay] * size, size, halves)
        direct = cube.swap(part, "x")
        across = cube.ordered(relay, direct, cube.swap(direct, relay), halves)
    diagonal = cube.swap(across, "core")
    here = cube.ordered("core", shard, sibling, axis)
    there = cube.ordered("core", across, diagonal, axis)
    return cube.ordered("x", here, there, axis)


def reduce_piece(cube, keep, got, order):
    rows, wide = keep.shape[2:]
    total = keep.astype(F32) + got.astype(F32)
    total = total.reshape(2, 2, 2, rows, wide)
    cut = [d for d in order if d != "x"]
    place = {"x": 0, cut[0]: 1, cut[1]: 2}
    for dim in order:
        mine = cube.coordinate[dim]
        other = lax.dynamic_slice_in_dim(total, 1 - mine, 1, place[dim]).astype(BF16)
        own = lax.dynamic_slice_in_dim(total, mine, 1, place[dim])
        total = own + cube.swap(other, dim).astype(F32)
    low = total.astype(BF16)
    for dim in range(cube.dims):
        if dim not in cut:
            low = (low.astype(F32) + cube.swap(low, dim).astype(F32)).astype(BF16)
    for dim in reversed(cut):
        low = cube.ordered(dim, low, cube.swap(low, dim), place[dim])
    return low.reshape(4, rows, wide)


def per_device(
    tokens,
    segments,
    query_weight,
    key_weight,
    value_weight,
    output_weight,
    w_gate,
    w_up,
    w_down,
    attn_gain,
    ffn_gain,
    cotangent,
    replicas,
):
    cube = Cube(replicas)
    core = cube.coordinate["core"].astype(jnp.int32).reshape(1)
    x, dy = tokens.T, cotangent.T
    pad = jnp.zeros((attn_gain.shape[0], GAINS - 2), BF16)
    first = jnp.concatenate(
        [attn_gain[:, None], ffn_gain[:, None], pad, query_weight, key_weight, value_weight], axis=1
    )
    wqkv = gather(cube, first, 0, None, 1)
    wo = gather(cube, output_weight, 0, None, 1)
    wg = gather(cube, w_gate, 0, 0, 1)
    wu = gather(cube, w_up, 0, 1, 1)
    wd = gather(cube, w_down.T, 1, 2, 0)
    gains = wqkv[:, :GAINS]

    cos, sin = tables(segments)
    qkv, h = project(x, wqkv, cos, sin)
    o, lse = attend(qkv, segments)
    x1, h2 = middle(x, o, wo, gains)
    y, dh2, gg_keep, gg_send, gu_keep, gu_send, gd_keep, gd_send = feed_forward(
        core, h2, dy, x1, wg, wu, wd
    )
    dx1, da, do, ffn_gain_grad = branch(dh2, x1, dy, gains, wo)
    dqkv = attend_back(qkv, o, do, lse, segments, cos, sin)
    ga_keep, ga_send = weight_grads(core, h, dqkv, o, da)
    grad_x, attn_gain_grad = input_grads(x, dx1, wqkv, dqkv)

    gg = reduce_piece(cube, gg_keep, cube.swap(gg_send, "core"), ("x", 0, 1))
    gu = reduce_piece(cube, gu_keep, cube.swap(gu_send, "core"), (1, "x", 2))
    gd = reduce_piece(cube, gd_keep, cube.swap(gd_send, "core"), (2, 0, "x"))
    ga_got = cube.swap(ga_send, "core")
    orders = (("x", 0, 1), (1, "x", 2), (2, 0, "x"))
    size = OWN // len(orders)
    ga = jnp.concatenate(
        [
            reduce_piece(cube, ga_keep[:, :, i * size:(i + 1) * size],
                         ga_got[:, :, i * size:(i + 1) * size], order)
            for i, order in enumerate(orders)
        ],
        axis=1,
    )
    flat = lambda g: jnp.swapaxes(g, 0, 1).reshape(OWN, 4 * CUT).astype(F32)
    ga = flat(ga)
    both = lax.psum(jnp.concatenate([attn_gain_grad, ffn_gain_grad], axis=1), ("group", "replica"))
    both = lax.dynamic_slice_in_dim(both, lax.axis_index("group") * OWN, OWN, 0)
    return (
        y.T,
        grad_x.T,
        ga[:, :D],
        ga[:, D:D + KEYS],
        ga[:, D + KEYS:WIDE],
        ga[:, WIDE:],
        flat(gg),
        flat(gu),
        gd.reshape(D, CUT).T.astype(F32),
        both[:, 0],
        both[:, 1],
    )


def solution(mesh):
    rows = P(("group", "replica"), None)
    weight, gain = P("group", None), P("group")
    replicas = mesh.shape["replica"]
    return jax.shard_map(
        lambda *args: per_device(*args, replicas),
        mesh=mesh,
        in_specs=(rows, rows) + (weight,) * 7 + (gain, gain, rows),
        out_specs=(rows, rows) + (weight,) * 7 + (gain, gain),
        check_vma=False,
    )
```

time: 962 us -> 553 us (0.57)
  the two profiles are of different devices: /device:TPU:0 before, /device:TPU:24 now
where the time goes in v1:
time: 553 us; the launch traced here: 544 us
  waiting for transfers between devices  195 us (35%)
  Pallas kernels  149 us (27%)
  other arithmetic  57.9 us (10%)
  starting transfers between devices  56.1 us (10%)
  local copies, waits for them, and re-layouts  43.3 us (8%)
  blocking collectives  39.8 us (7%)
    ppermute x33, waiting for transfers between devices, swap(): lax.ppermute(value, 'replica', [(i, i ^ mask) for i in range(self.count)])  150 us
    pallas_call x1, Pallas kernels, feed_forward(): pl.pallas_call(feed_forward_kernel, grid=(steps,), in_specs=[pl.BlockSpec...  79.5 us
    ppermute x11, waiting for transfers between devices, swap(): return lax.ppermute(value, 'group', [(i, i ^ 2) for i in range(4)])  45.3 us
    select_n x30, other arithmetic, ordered(): jnp.where(self.coordinate[dim] == 0, jnp.concatenate([mine, other], axis=...  41.6 us
    psum x1, blocking collectives, per_device(): lax.psum(jnp.concatenate([attn_gain_grad, ffn_gain_grad], axis=1), ('grou...  39.8 us
    ppermute x33, starting transfers between devices, swap(): lax.ppermute(value, 'replica', [(i, i ^ mask) for i in range(self.count)])  39.4 us
    unnamed x90, local copies, waits for them, and re-layouts  25.3 us
    pallas_call x1, Pallas kernels, attend_back(): pl.pallas_call(attend_back_kernel, grid=(seqs,), in_specs=[pl.BlockSpec((...  19.8 us
  transfers between devices with their start and end apart: 58, of which 29 were waited for; matrix products, arithmetic and copies ran while one was open for 13% of the time, Pallas kernels for 13%

profile of v1, /device:TPU:24, one launch (start us, length us, event | category | flops | bytes accessed | tf_op | source)
XLA Modules:
  0.0 543.6 jit_solution(3137656513720299448)
XLA Ops:
  2.2 2.0 constant_dynamic-slice_fusion.1
  4.8 1.9 dynamic-slice_bitcast_fusion
  17.9 10.4 %collective-permute-done.11 = bf16[240,1280]{1,0:T(8,128)(2,1)} collective-permute-done((bf16[240,1280]{1,0:T(8,128)(2,1)}, bf16[240,1280]{1,0:T(8,128)(2,1)}, u32[]{:S(2)}, u32[]{:S(2)}) %collective-permute-start.11) | collective-permute-done | bytes 614432 | tf_op jit(solution)/shard_map/ppermute | solution.py:457
  29.8 11.7 %collective-permute-done.15 = bf16[480,640]{1,0:T(8,128)(2,1)} collective-permute-done((bf16[480,640]{1,0:T(8,128)(2,1)}, bf16[480,640]{1,0:T(8,128)(2,1)}, u32[]{:S(2)}, u32[]{:S(2)}) %collective-permute-start.15) | collective-permute-done | bytes 614432 | tf_op jit(solution)/shard_map/ppermute | solution.py:457
  42.0 1.9 maximum_select_fusion.19
  51.4 3.1 collective-permute-done.7
  54.6 13.9 %collective-permute-done.12 = bf16[240,1280]{1,0:T(8,128)(2,1)S(1)} collective-permute-done((bf16[240,1280]{1,0:T(8,128)(2,1)}, bf16[240,1280]{1,0:T(8,128)(2,1)S(1)}, u32[]{:S(2)}, u32[]{:S(2)}) %collective-permute-start.12) | collective-permute-done | bytes 614432 | tf_op jit(solution)/shard_map/ppermute | solution.py:461
  70.0 2.7 maximum_select_fusion.14
  73.2 2.7 maximum_select_fusion.15
  86.1 6.1 %project.1 = (bf16[1600,1024]{1,0:T(8,128)(2,1)S(1)}, bf16[960,1024]{1,0:T(8,128)(2,1)S(1)}) custom-call(bf16[960,1024]{1,0:T(8,128)(2,1)S(1)} %bitcast.43, bf16[960,1728]{1,0:T(8,128)(2,1)S(1)} %maximum_select_fusion.3.w_ref, f32[32,1024]{1,0:T(8,128)S(1)} %copy-done.17, f32[32,1024]{1,0:T(8,128)S(1)} %copy-done.16), custom_call_target="tpu_custom_call" | custom-call | flops 3145728000 | bytes 10280960 | tf_op jit(solution)/shard_map/project/pallas_call | solution.py:83
  93.5 13.8 %attend.1 = (bf16[960,1024]{1,0:T(8,128)(2,1)S(1)}, f32[5,8,1024]{2,1,0:T(8,128)S(1)}) custom-call(bf16[1600,1024]{1,0:T(8,128)(2,1)S(1)} %get-tuple-element.33.qkv_ref, s32[2,1,512]{2,1,0:T(1,128)S(1)} %broadcast_in_dim.39.segr_ref, s32[2,512,1]{2,1,0:T(8,128)S(1)} %copy-done.12), custom_call_target="tpu_custom_call" | custom-call | flops 4026531840 | bytes 5242880 | tf_op jit(solution)/shard_map/attend/pallas_call | solution.py:150
  107.3 5.4 middle.1
  114.0 4.1 maximum_select_fusion.7
  118.1 3.0 maximum_select_fusion.9
  121.3 3.0 maximum_select_fusion.1.wu_ref
  124.2 3.1 maximum_select_fusion.2.wd_ref
  127.3 2.8 maximum_select_fusion.5
  130.5 2.8 maximum_select_fusion.wg_ref
  133.4 79.5 %feed_forward.1 = (bf16[960,1024]{1,0:T(8,128)(2,1)}, f32[960,1024]{1,0:T(8,128)}, bf16[2,4,240,640]{3,2,1,0:T(8,128)(2,1)}, bf16[2,4,240,640]{3,2,1,0:T(8,128)(...) custom-call(s32[1]{0:T(128)} %bitcast.core_ref, ...), custom_call_target="tpu_custom_call" | custom-call | flops 45298483200 | bytes 45219840 | tf_op jit(solution)/shard_map/feed_forward/pallas_call | solution.py:244
  216.1 7.8 %branch.1 = (f32[960,1024]{1,0:T(8,128)S(1)}, bf16[960,1024]{1,0:T(8,128)(2,1)S(1)}, bf16[960,1024]{1,0:T(8,128)(2,1)S(1)}, f32[960,1]{1,0:T(8,128)S(1)}) custom-call(f32[960,1024]{1,0:T(8,128)} %get-tuple-element.38.dh_ref, f32[960,1024]{1,0:T(8,128)} %copy-done.4, bf16[960,1024]{1,0:T(8,128)(2,1)S(1)} %bitcast.47, bf16[960,128]{1,0:T(8,128)(2,1)S(1)} %slice.52.gain_ref, ...), custom_call_target="tpu_custom_call" | custom-call | flops 1887436800 | bytes 17694720 | tf_op jit(solution)/shard_map/branch/pallas_call | solution.py:282
  223.9 1.9 copy-done.2
  227.1 19.8 %attend_back.1.dqkv_ref = bf16[1600,1024]{1,0:T(8,128)(2,1)} custom-call(bf16[1600,1024]{1,0:T(8,128)(2,1)} %copy-done.22, bf16[960,1024]{1,0:T(8,128)(2,1)S(1)} %copy-done.20, bf16[960,1024]{1,0:T(8,128)(2,1)S(1)} %get-tuple-element.40.do_ref, f32[5,8,1024]{2,1,0:T(8,128)S(1)} %copy-done.26, s32[2,1,512]{2,1,0:T(1,128)S(1)} %broadcast_in_dim.39.segr_ref, ...), custom_call_target="tpu_custom_call" | custom-call | flops 10066329600 | bytes 10485760 | tf_op jit(solution)/shard_map/attend_back/pallas_call | solution.py:336
  246.9 1.9 copy-done.5
  248.9 8.6 %weight_grads.1 = (bf16[2,4,240,640]{3,2,1,0:T(8,128)(2,1)S(1)}, bf16[2,4,240,640]{3,2,1,0:T(8,128)(2,1)}) custom-call(s32[1]{0:T(128)} %bitcast.core_ref, bf16[960,1024]{1,0:T(8,128)(2,1)S(1)} %copy-done.24, bf16[1600,1024]{1,0:T(8,128)(2,1)S(1)} %copy-done.5, bf16[960,1024]{1,0:T(8,128)(2,1)S(1)} %copy-done.20, bf16[960,1024]{1,0:T(8,128)(2,1)S(1)} %get-tuple-element.44.da_ref), custom_call_target="tpu_custom_call" | custom-call | flops 5033164800 | bytes 14090240 | tf_op jit(solution)/shard_map/weight_grads/pallas_call | solution.py:385
  259.4 2.1 copy-done.3
  261.5 1.9 copy-done.6
  265.0 8.1 %input_grads.1 = (bf16[960,1024]{1,0:T(8,128)(2,1)}, f32[960,1]{1,0:T(8,128)S(1)}) custom-call(bf16[960,1024]{1,0:T(8,128)(2,1)S(1)} %bitcast.45, f32[960,1024]{1,0:T(8,128)S(1)} %copy-done.3, bf16[960,1728]{1,0:T(8,128)(2,1)S(1)} %maximum_select_fusion.3.w_ref, bf16[1600,1024]{1,0:T(8,128)(2,1)S(1)} %copy-done.6), custom_call_target="tpu_custom_call" | custom-call | flops 3145728000 | bytes 14213120 | tf_op jit(solution)/shard_map/input_grads/pallas_call | solution.py:416
  276.3 39.8 %psum.7 = f32[960,2]{0,1:T(2,128)S(1)} all-reduce(f32[960,2]{0,1:T(2,128)S(1)} %pad_maximum_fusion), channel_id=1, replica_groups=mesh['group'=4,'replica'=8] {'group','replica'}, use_global_device_ids=true, to_apply=%region_1.2 | all-reduce | flops 1920 | bytes 15360 | tf_op jit(solution)/shard_map/psum | solution.py:563
  316.8 2.9 convert_add_fusion
  321.5 2.3 convert_add_fusion.1
  325.5 2.3 convert_add_fusion.8
  327.9 2.3 collective-permute-start.19
  330.2 2.3 convert_add_fusion.2
  333.9 6.6 %collective-permute-done.19 = bf16[1,2,2,80,640]{4,3,2,1,0:T(8,128)(2,1)S(1)} collective-permute-done((bf16[1,2,2,80,640]{4,3,2,1,0:T(8,128)(2,1)S(1)}, bf16[1,2,2,80,640]{4,3,2,1,0:T(8,128)(2,1)S(1)}, u32[]{:S(2)}, u32[]{:S(2)}) %collective-permute-start.19) | collective-permute-done | bytes 409632 | tf_op jit(solution)/shard_map/ppermute | solution.py:457
  340.6 2.3 collective-permute-start.31
  343.0 43.9 %collective-permute-done.25 = bf16[2,1,2,80,640]{4,3,2,1,0:T(8,128)(2,1)S(1)} collective-permute-done((bf16[2,1,2,80,640]{4,3,2,1,0:T(8,128)(2,1)S(1)}, bf16[2,1,2,80,640]{4,3,2,1,0:T(8,128)(2,1)S(1)}, u32[]{:S(2)}, u32[]{:S(2)}) %collective-permute-start.25) | collective-permute-done | bytes 409632 | tf_op jit(solution)/shard_map/ppermute | solution.py:461
  386.9 2.3 collective-permute-start.20
  389.3 4.4 collective-permute-done.31
  393.7 2.3 collective-permute-start.26
  396.8 2.9 collective-permute-done.26
  399.8 2.1 collective-permute-done.32
  403.6 1.9 collective-permute-done.21
  411.6 4.2 collective-permute-done.22
  415.8 2.1 collective-permute-start.23
  417.9 3.1 collective-permute-done.34
  423.3 4.4 collective-permute-done.29
  428.8 4.6 collective-permute-done.24
  433.4 2.0 collective-permute-start.36
  435.9 5.1 collective-permute-done.36
  445.1 2.1 collective-permute-start.53
  447.6 9.3 %collective-permute-done.46 = bf16[1,1,2,240,640]{4,3,2,1,0:T(8,128)(2,1)S(1)} collective-permute-done((bf16[1,1,2,240,640]{4,3,2,1,0:T(8,128)(2,1)S(1)}, bf16[1,1,2,240,640]{4,3,2,1,0:T(8,128)(2,1)S(1)}, u32[]{:S(2)}, u32[]{:S(2)}) %collective-permute-start.46) | collective-permute-done | bytes 614432 | tf_op jit(solution)/shard_map/ppermute | solution.py:457
  457.1 1.9 collective-permute-start.47
  459.0 2.8 collective-permute-done.53
  462.4 9.3 %collective-permute-done.39 = bf16[1,1,2,240,640]{4,3,2,1,0:T(8,128)(2,1)S(1)} collective-permute-done((bf16[1,1,2,240,640]{4,3,2,1,0:T(8,128)(2,1)S(1)}, bf16[1,1,2,240,640]{4,3,2,1,0:T(8,128)(2,1)S(1)}, u32[]{:S(2)}, u32[]{:S(2)}) %collective-permute-start.39) | collective-permute-done | bytes 614432 | tf_op jit(solution)/shard_map/ppermute | solution.py:461
  472.5 2.1 collective-permute-start.55
  474.5 5.4 collective-permute-done.48
  480.1 2.5 collective-permute-done.40
  482.6 2.0 collective-permute-start.41
  484.6 9.6 %collective-permute-done.55 = bf16[1,1,1,240,640]{4,3,2,1,0:T(8,128)(2,1)S(1)} collective-permute-done((bf16[1,1,1,240,640]{4,3,2,1,0:T(8,128)(2,1)S(1)}, bf16[1,1,1,240,640]{4,3,2,1,0:T(8,128)(2,1)S(1)}, u32[]{:S(2)}, u32[]{:S(2)}) %collective-permute-start.55) | collective-permute-done | bytes 307232 | tf_op jit(solution)/shard_map/ppermute | solution.py:461
  494.3 3.2 collective-permute-start.56
  497.8 3.2 collective-permute-done.41
  502.5 2.0 collective-permute-start.57
  506.4 22.3 %collective-permute-done.42 = bf16[1,1,1,240,640]{4,3,2,1,0:T(8,128)(2,1)} collective-permute-done((bf16[1,1,1,240,640]{4,3,2,1,0:T(8,128)(2,1)S(1)}, bf16[1,1,1,240,640]{4,3,2,1,0:T(8,128)(2,1)}, u32[]{:S(2)}, u32[]{:S(2)}) %collective-permute-start.42) | collective-permute-done | bytes 307232 | tf_op jit(solution)/shard_map/ppermute | solution.py:461
  536.3 3.8 collective-permute-done.43
  (256 shorter events, 87.8 us)
Async XLA Ops:
  0.7 14.5 %collective-permute-start.4 = (bf16[240,960]{1,0:T(8,128)(2,1)}, bf16[240,960]{1,0:T(8,128)(2,1)}, u32[]{:S(2)}, u32[]{:S(2)}) collective-permute-start(bf16[240,960]{1,0:T(8,128)(2,1)} %param.17), channel_id=1, source_target_pairs={{0,16},{8,24},{16,0},{24,8},{1,17},{9,25},{17,1},{25,9},{2,18},{10... | collective-permute-start | bytes 1382408 | tf_op jit(solution)/shard_map/ppermute | solution.py:457
  2.2 15.2 %collective-permute-start.3 = (bf16[240,960]{1,0:T(8,128)(2,1)}, bf16[240,960]{1,0:T(8,128)(2,1)}, u32[]{:S(2)}, u32[]{:S(2)}) collective-permute-start(bf16[240,960]{1,0:T(8,128)(2,1)} %param.17), channel_id=1, source_target_pairs={{0,8},{8,0},{16,24},{24,16},{1,9},{9,1},{17,25},{25,17},{2,10},{10... | collective-permute-start | bytes 1382408 | tf_op jit(solution)/shard_map/ppermute | solution.py:459
  2.2 11.0 %copy-start.32 = (bf16[240,2560]{1,0:T(8,128)(2,1)S(1)}, bf16[240,2560]{1,0:T(8,128)(2,1)}, u32[]{:S(2)}) copy-start(bf16[240,2560]{1,0:T(8,128)(2,1)} %param.18) | copy-start | bytes 3686404
  4.3 24.1 %collective-permute-start.11 = (bf16[240,1280]{1,0:T(8,128)(2,1)}, bf16[240,1280]{1,0:T(8,128)(2,1)}, u32[]{:S(2)}, u32[]{:S(2)}) collective-permute-start(bf16[240,1280]{1,0:T(8,128)(2,1)} %constant_dynamic-slice_fusion.1), channel_id=1, source_target_pairs={{0,16},{8,24},{16,0},{24,8},{1,17},{9,25},{17,1},{25,9},{2,18},{10... | collective-permute-start | bytes 1843208 | tf_op jit(solution)/shard_map/ppermute | solution.py:457
  6.8 34.7 %collective-permute-start.15 = (bf16[480,640]{1,0:T(8,128)(2,1)}, bf16[480,640]{1,0:T(8,128)(2,1)}, u32[]{:S(2)}, u32[]{:S(2)}) collective-permute-start(bf16[480,640]{1,0:T(8,128)(2,1)} %dynamic-slice_bitcast_fusion), channel_id=1, source_target_pairs={{0,16},{8,24},{16,0},{24,8},{1,17},{9,25},{17,1},{25,9},{2,18},{10... | collective-permute-start | bytes 1843208 | tf_op jit(solution)/shard_map/ppermute | solution.py:457
  12.8 31.1 %collective-permute-start = (bf16[240,1728]{1,0:T(8,128)(2,1)S(1)}, bf16[240,1728]{1,0:T(8,128)(2,1)}, u32[]{:S(2)}, u32[]{:S(2)}) collective-permute-start(bf16[240,1728]{1,0:T(8,128)(2,1)S(1)} %concatenate.369), channel_id=1, source_target_pairs={{0,8},{8,0},{16,24},{24,16},{1,9},{9,1},{17,25},{25,17},{2,10},{10... | collective-permute-start | bytes 2488328 | tf_op jit(solution)/shard_map/ppermute | solution.py:459
  15.2 32.2 %collective-permute-start.5 = (bf16[240,960]{1,0:T(8,128)(2,1)}, bf16[240,960]{1,0:T(8,128)(2,1)S(1)}, u32[]{:S(2)}, u32[]{:S(2)}) collective-permute-start(bf16[240,960]{1,0:T(8,128)(2,1)} %collective-permute-done.4), channel_id=1, source_target_pairs={{0,8},{8,0},{16,24},{24,16},{1,9},{9,1},{17,25},{25,17},{2,10},{10... | collective-permute-start | bytes 1382408 | tf_op jit(solution)/shard_map/ppermute | solution.py:459
  17.4 58.5 %collective-permute-start.14 = (bf16[960,640]{1,0:T(8,128)(2,1)S(1)}, bf16[960,640]{1,0:T(8,128)(2,1)S(1)}, u32[]{:S(2)}, u32[]{:S(2)}) collective-permute-start(bf16[960,640]{1,0:T(8,128)(2,1)S(1)} %bitcast.65), channel_id=1, source_target_pairs={{0,8},{8,0},{16,24},{24,16},{1,9},{9,1},{17,25},{25,17},{2,10},{10... | collective-permute-start | bytes 3686408 | tf_op jit(solution)/shard_map/ppermute | solution.py:459
  28.3 26.2 %collective-permute-start.7 = (bf16[240,1280]{1,0:T(8,128)(2,1)}, bf16[240,1280]{1,0:T(8,128)(2,1)S(1)}, u32[]{:S(2)}, u32[]{:S(2)}) collective-permute-start(bf16[240,1280]{1,0:T(8,128)(2,1)} %constant_dynamic-slice_fusion.2), channel_id=1, source_target_pairs={{0,16},{8,24},{16,0},{24,8},{1,17},{9,25},{17,1},{25,9},{2,18},{10... | collective-permute-start | bytes 1843208 | tf_op jit(solution)/shard_map/ppermute | solution.py:457
  41.5 27.0 %collective-permute-start.12 = (bf16[240,1280]{1,0:T(8,128)(2,1)}, bf16[240,1280]{1,0:T(8,128)(2,1)S(1)}, u32[]{:S(2)}, u32[]{:S(2)}) collective-permute-start(bf16[240,1280]{1,0:T(8,128)(2,1)} %collective-permute-done.11), channel_id=1, source_target_pairs={{0,2},{1,3},{2,0},{3,1},{4,6},{5,7},{6,4},{7,5},{8,10},{9,11},{10,... | collective-permute-start | bytes 1843208 | tf_op jit(solution)/shard_map/ppermute | solution.py:461
  43.9 28.8 %collective-permute-start.1 = (bf16[240,1728]{1,0:T(8,128)(2,1)S(1)}, bf16[240,1728]{1,0:T(8,128)(2,1)S(1)}, u32[]{:S(2)}, u32[]{:S(2)}) collective-permute-start(bf16[240,1728]{1,0:T(8,128)(2,1)S(1)} %concatenate.369), channel_id=1, source_target_pairs={{0,16},{8,24},{16,0},{24,8},{1,17},{9,25},{17,1},{25,9},{2,18},{10... | collective-permute-start | bytes 2488328 | tf_op jit(solution)/shard_map/ppermute | solution.py:457
  47.4 25.3 %collective-permute-start.16 = (bf16[480,640]{1,0:T(8,128)(2,1)}, bf16[480,640]{1,0:T(8,128)(2,1)S(1)}, u32[]{:S(2)}, u32[]{:S(2)}) collective-permute-start(bf16[480,640]{1,0:T(8,128)(2,1)} %collective-permute-done.15), channel_id=1, source_target_pairs={{0,6},{1,7},{2,4},{3,5},{4,2},{5,3},{6,0},{7,1},{8,14},{9,15},{10,... | collective-permute-start | bytes 1843208 | tf_op jit(solution)/shard_map/ppermute | solution.py:461
  50.4 22.2 %copy-start.33 = (bf16[240,2560]{1,0:T(8,128)(2,1)S(1)}, bf16[240,2560]{1,0:T(8,128)(2,1)}, u32[]{:S(2)}) copy-start(bf16[240,2560]{1,0:T(8,128)(2,1)} %param.18) | copy-start | bytes 3686404
  51.4 55.9 %copy-start = (bf16[960,960]{1,0:T(8,128)(2,1)}, bf16[960,960]{1,0:T(8,128)(2,1)S(1)}, u32[]{:S(2)}) copy-start(bf16[960,960]{1,0:T(8,128)(2,1)S(1)} %maximum_select_fusion.10.w_ref) | copy-start | bytes 5529604
  54.6 25.4 %collective-permute-start.10 = (bf16[240,2560]{1,0:T(8,128)(2,1)S(1)}, bf16[240,2560]{1,0:T(8,128)(2,1)S(1)}, u32[]{:S(2)}, u32[]{:S(2)}) collective-permute-start(bf16[240,2560]{1,0:T(8,128)(2,1)S(1)} %copy-done.31), channel_id=1, source_target_pairs={{0,8},{8,0},{16,24},{24,16},{1,9},{9,1},{17,25},{25,17},{2,10},{10... | collective-permute-start | bytes 3686408 | tf_op jit(solution)/shard_map/ppermute | solution.py:459
  68.5 10.1 %collective-permute-start.8 = (bf16[240,1280]{1,0:T(8,128)(2,1)S(1)}, bf16[240,1280]{1,0:T(8,128)(2,1)S(1)}, u32[]{:S(2)}, u32[]{:S(2)}) collective-permute-start(bf16[240,1280]{1,0:T(8,128)(2,1)S(1)} %collective-permute-done.7), channel_id=1, source_target_pairs={{0,1},{1,0},{2,3},{3,2},{4,5},{5,4},{6,7},{7,6},{8,9},{9,8},{10,11... | collective-permute-start | bytes 1843208 | tf_op jit(solution)/shard_map/ppermute | solution.py:461
  72.7 9.5 %collective-permute-start.6 = (bf16[240,2560]{1,0:T(8,128)(2,1)S(1)}, bf16[240,2560]{1,0:T(8,128)(2,1)S(1)}, u32[]{:S(2)}, u32[]{:S(2)}) collective-permute-start(bf16[240,2560]{1,0:T(8,128)(2,1)S(1)} %copy-done.33), channel_id=1, source_target_pairs={{0,8},{8,0},{16,24},{24,16},{1,9},{9,1},{17,25},{25,17},{2,10},{10... | collective-permute-start | bytes 3686408 | tf_op jit(solution)/shard_map/ppermute | solution.py:459
  72.7 11.2 %collective-permute-start.2 = (bf16[240,1728]{1,0:T(8,128)(2,1)S(1)}, bf16[240,1728]{1,0:T(8,128)(2,1)S(1)}, u32[]{:S(2)}, u32[]{:S(2)}) collective-permute-start(bf16[240,1728]{1,0:T(8,128)(2,1)S(1)} %collective-permute-done.1), channel_id=1, source_target_pairs={{0,8},{8,0},{16,24},{24,16},{1,9},{9,1},{17,25},{25,17},{2,10},{10... | collective-permute-start | bytes 2488328 | tf_op jit(solution)/shard_map/ppermute | solution.py:459
  75.9 38.1 %collective-permute-start.13 = (bf16[240,2560]{1,0:T(8,128)(2,1)}, bf16[240,2560]{1,0:T(8,128)(2,1)}, u32[]{:S(2)}, u32[]{:S(2)}) collective-permute-start(bf16[240,2560]{1,0:T(8,128)(2,1)} %maximum_select_fusion.14), channel_id=1, source_target_pairs={{0,8},{8,0},{16,24},{24,16},{1,9},{9,1},{17,25},{25,17},{2,10},{10... | collective-permute-start | bytes 3686408 | tf_op jit(solution)/shard_map/ppermute | solution.py:459
  78.6 39.5 %collective-permute-start.17 = (bf16[960,640]{1,0:T(8,128)(2,1)}, bf16[960,640]{1,0:T(8,128)(2,1)}, u32[]{:S(2)}, u32[]{:S(2)}) collective-permute-start(bf16[960,640]{1,0:T(8,128)(2,1)} %maximum_select_fusion.15), channel_id=1, source_target_pairs={{0,8},{8,0},{16,24},{24,16},{1,9},{9,1},{17,25},{25,17},{2,10},{10... | collective-permute-start | bytes 3686408 | tf_op jit(solution)/shard_map/ppermute | solution.py:459
  80.0 47.4 %collective-permute-start.9 = (bf16[240,2560]{1,0:T(8,128)(2,1)}, bf16[240,2560]{1,0:T(8,128)(2,1)}, u32[]{:S(2)}, u32[]{:S(2)}) collective-permute-start(bf16[240,2560]{1,0:T(8,128)(2,1)} %maximum_select_fusion.13), channel_id=1, source_target_pairs={{0,8},{8,0},{16,24},{24,16},{1,9},{9,1},{17,25},{25,17},{2,10},{10... | collective-permute-start | bytes 3686408 | tf_op jit(solution)/shard_map/ppermute | solution.py:459
  93.4 13.9 %copy-start.22 = (bf16[1600,1024]{1,0:T(8,128)(2,1)}, bf16[1600,1024]{1,0:T(8,128)(2,1)S(1)}, u32[]{:S(2)}) copy-start(bf16[1600,1024]{1,0:T(8,128)(2,1)S(1)} %get-tuple-element.33.qkv_ref) | copy-start | bytes 9830404
  212.9 103.9 %collective-permute-start.51 = (bf16[2,4,240,640]{3,2,1,0:T(8,128)(2,1)}, bf16[2,4,240,640]{3,2,1,0:T(8,128)(2,1)}, u32[]{:S(2)}, u32[]{:S(2)}) collective-permute-start(bf16[2,4,240,640]{3,2,1,0:T(8,128)(2,1)} %get-tuple-element.52), channel_id=1, source_target_pairs={{0,8},{8,0},{16,24},{24,16},{1,9},{9,1},{17,25},{25,17},{2,10},{10... | collective-permute-start | bytes 7372808 | tf_op jit(solution)/shard_map/ppermute | solution.py:459
  216.1 11.0 %copy-start.26 = (f32[5,8,1024]{2,1,0:T(8,128)S(1)}, f32[5,8,1024]{2,1,0:T(8,128)}, u32[]{:S(2)}) copy-start(f32[5,8,1024]{2,1,0:T(8,128)} %copy-done.25) | copy-start | bytes 491524
  226.6 94.9 %collective-permute-start.44 = (bf16[2,4,240,640]{3,2,1,0:T(8,128)(2,1)}, bf16[2,4,240,640]{3,2,1,0:T(8,128)(2,1)}, u32[]{:S(2)}, u32[]{:S(2)}) collective-permute-start(bf16[2,4,240,640]{3,2,1,0:T(8,128)(2,1)} %get-tuple-element.50), channel_id=1, source_target_pairs={{0,8},{8,0},{16,24},{24,16},{1,9},{9,1},{17,25},{25,17},{2,10},{10... | collective-permute-start | bytes 7372808 | tf_op jit(solution)/shard_map/ppermute | solution.py:459
  227.1 19.8 %copy-start.24 = (bf16[960,1024]{1,0:T(8,128)(2,1)S(1)}, bf16[960,1024]{1,0:T(8,128)(2,1)}, u32[]{:S(2)}) copy-start(bf16[960,1024]{1,0:T(8,128)(2,1)} %copy-done.23) | copy-start | bytes 5898244
  258.9 66.2 %collective-permute-start.18 = (bf16[2,4,240,640]{3,2,1,0:T(8,128)(2,1)}, bf16[2,4,240,640]{3,2,1,0:T(8,128)(2,1)}, u32[]{:S(2)}, u32[]{:S(2)}) collective-permute-start(bf16[2,4,240,640]{3,2,1,0:T(8,128)(2,1)} %get-tuple-element.46), channel_id=1, source_target_pairs={{0,8},{8,0},{16,24},{24,16},{1,9},{9,1},{17,25},{25,17},{2,10},{10... | collective-permute-start | bytes 7372808 | tf_op jit(solution)/shard_map/ppermute | solution.py:459
  258.9 71.3 %collective-permute-start.37 = (bf16[2,4,240,640]{3,2,1,0:T(8,128)(2,1)}, bf16[2,4,240,640]{3,2,1,0:T(8,128)(2,1)}, u32[]{:S(2)}, u32[]{:S(2)}) collective-permute-start(bf16[2,4,240,640]{3,2,1,0:T(8,128)(2,1)} %get-tuple-element.48), channel_id=1, source_target_pairs={{0,8},{8,0},{16,24},{24,16},{1,9},{9,1},{17,25},{25,17},{2,10},{10... | collective-permute-start | bytes 7372808 | tf_op jit(solution)/shard_map/ppermute | solution.py:459
  319.9 124.9 %collective-permute-start.52 = (bf16[2,1,2,240,640]{4,3,2,1,0:T(8,128)(2,1)S(1)}, bf16[2,1,2,240,640]{4,3,2,1,0:T(8,128)(2,1)S(1)}, u32[]{:S(2)}, u32[]{:S(2)}) collective-permute-start(bf16[2,1,2,240,640]{4,3,2,1,0:T(8,128)(2,1)S(1)} %dynamic-slice_convert_fusion), channel_id=1, source_target_pairs={{0,6},{1,7},{2,4},{3,5},{4,2},{5,3},{6,0},{7,1},{8,14},{9,15},{10,... | collective-permute-start | bytes 3686408 | tf_op jit(solution)/shard_map/ppermute | solution.py:461
  323.9 119.9 %collective-permute-start.45 = (bf16[2,1,2,240,640]{4,3,2,1,0:T(8,128)(2,1)S(1)}, bf16[2,1,2,240,640]{4,3,2,1,0:T(8,128)(2,1)S(1)}, u32[]{:S(2)}, u32[]{:S(2)}) collective-permute-start(bf16[2,1,2,240,640]{4,3,2,1,0:T(8,128)(2,1)S(1)} %dynamic-slice_convert_fusion.1), channel_id=1, source_target_pairs={{0,2},{1,3},{2,0},{3,1},{4,6},{5,7},{6,4},{7,5},{8,10},{9,11},{10,... | collective-permute-start | bytes 3686408 | tf_op jit(solution)/shard_map/ppermute | solution.py:461
  327.9 12.7 %collective-permute-start.19 = (bf16[1,2,2,80,640]{4,3,2,1,0:T(8,128)(2,1)S(1)}, bf16[1,2,2,80,640]{4,3,2,1,0:T(8,128)(2,1)S(1)}, u32[]{:S(2)}, u32[]{:S(2)}) collective-permute-start(bf16[1,2,2,80,640]{4,3,2,1,0:T(8,128)(2,1)S(1)} %dynamic-slice_convert_fusion.8), channel_id=1, source_target_pairs={{0,16},{8,24},{16,0},{24,8},{1,17},{9,25},{17,1},{25,9},{2,18},{10... | collective-permute-start | bytes 1228808 | tf_op jit(solution)/shard_map/ppermute | solution.py:457
  332.6 114.6 %collective-permute-start.38 = (bf16[1,2,2,240,640]{4,3,2,1,0:T(8,128)(2,1)S(1)}, bf16[1,2,2,240,640]{4,3,2,1,0:T(8,128)(2,1)S(1)}, u32[]{:S(2)}, u32[]{:S(2)}) collective-permute-start(bf16[1,2,2,240,640]{4,3,2,1,0:T(8,128)(2,1)S(1)} %dynamic-slice_convert_fusion.2), channel_id=1, source_target_pairs={{0,16},{8,24},{16,0},{24,8},{1,17},{9,25},{17,1},{25,9},{2,18},{10... | collective-permute-start | bytes 3686408 | tf_op jit(solution)/shard_map/ppermute | solution.py:457
  332.7 54.2 %collective-permute-start.25 = (bf16[2,1,2,80,640]{4,3,2,1,0:T(8,128)(2,1)S(1)}, bf16[2,1,2,80,640]{4,3,2,1,0:T(8,128)(2,1)S(1)}, u32[]{:S(2)}, u32[]{:S(2)}) collective-permute-start(bf16[2,1,2,80,640]{4,3,2,1,0:T(8,128)(2,1)S(1)} %dynamic-slice_convert_fusion.7), channel_id=1, source_target_pairs={{0,2},{1,3},{2,0},{3,1},{4,6},{5,7},{6,4},{7,5},{8,10},{9,11},{10,... | collective-permute-start | bytes 1228808 | tf_op jit(solution)/shard_map/ppermute | solution.py:461
  340.6 53.1 %collective-permute-start.31 = (bf16[2,1,2,80,640]{4,3,2,1,0:T(8,128)(2,1)S(1)}, bf16[2,1,2,80,640]{4,3,2,1,0:T(8,128)(2,1)S(1)}, u32[]{:S(2)}, u32[]{:S(2)}) collective-permute-start(bf16[2,1,2,80,640]{4,3,2,1,0:T(8,128)(2,1)S(1)} %dynamic-slice_convert_fusion.6), channel_id=1, source_target_pairs={{0,6},{1,7},{2,4},{3,5},{4,2},{5,3},{6,0},{7,1},{8,14},{9,15},{10,... | collective-permute-start | bytes 1228808 | tf_op jit(solution)/shard_map/ppermute | solution.py:461
  386.9 9.2 %collective-permute-start.20 = (bf16[1,1,2,80,640]{4,3,2,1,0:T(8,128)(2,1)S(1)}, bf16[1,1,2,80,640]{4,3,2,1,0:T(8,128)(2,1)S(1)}, u32[]{:S(2)}, u32[]{:S(2)}) collective-permute-start(bf16[1,1,2,80,640]{4,3,2,1,0:T(8,128)(2,1)S(1)} %dynamic-slice_convert_fusion.14), channel_id=1, source_target_pairs={{0,1},{1,0},{2,3},{3,2},{4,5},{5,4},{6,7},{7,6},{8,9},{9,8},{10,11... | collective-permute-start | bytes 614408 | tf_op jit(solution)/shard_map/ppermute | solution.py:461
  393.7 6.0 %collective-permute-start.26 = (bf16[1,1,2,80,640]{4,3,2,1,0:T(8,128)(2,1)S(1)}, bf16[1,1,2,80,640]{4,3,2,1,0:T(8,128)(2,1)S(1)}, u32[]{:S(2)}, u32[]{:S(2)}) collective-permute-start(bf16[1,1,2,80,640]{4,3,2,1,0:T(8,128)(2,1)S(1)} %dynamic-slice_convert_fusion.13), channel_id=1, source_target_pairs={{0,16},{8,24},{16,0},{24,8},{1,17},{9,25},{17,1},{25,9},{2,18},{10... | collective-permute-start | bytes 614408 | tf_op jit(solution)/shard_map/ppermute | solution.py:457
  396.1 5.8 %collective-permute-start.32 = (bf16[2,1,1,80,640]{4,3,2,1,0:T(8,128)(2,1)S(1)}, bf16[2,1,1,80,640]{4,3,2,1,0:T(8,128)(2,1)S(1)}, u32[]{:S(2)}, u32[]{:S(2)}) collective-permute-start(bf16[2,1,1,80,640]{4,3,2,1,0:T(8,128)(2,1)S(1)} %dynamic-slice_convert_fusion.12), channel_id=1, source_target_pairs={{0,1},{1,0},{2,3},{3,2},{4,5},{5,4},{6,7},{7,6},{8,9},{9,8},{10,11... | collective-permute-start | bytes 614408 | tf_op jit(solution)/shard_map/ppermute | solution.py:461
  399.7 5.8 %collective-permute-start.21 = (bf16[1,1,1,80,640]{4,3,2,1,0:T(8,128)(2,1)S(1)}, bf16[1,1,1,80,640]{4,3,2,1,0:T(8,128)(2,1)S(1)}, u32[]{:S(2)}, u32[]{:S(2)}) collective-permute-start(bf16[1,1,1,80,640]{4,3,2,1,0:T(8,128)(2,1)S(1)} %dynamic-slice_convert_fusion.17), channel_id=1, source_target_pairs={{0,2},{1,3},{2,0},{3,1},{4,6},{5,7},{6,4},{7,5},{8,10},{9,11},{10,... | collective-permute-start | bytes 307208 | tf_op jit(solution)/shard_map/ppermute | solution.py:461
  401.9 6.5 %collective-permute-start.27 = (bf16[1,1,1,80,640]{4,3,2,1,0:T(8,128)(2,1)S(1)}, bf16[1,1,1,80,640]{4,3,2,1,0:T(8,128)(2,1)S(1)}, u32[]{:S(2)}, u32[]{:S(2)}) collective-permute-start(bf16[1,1,1,80,640]{4,3,2,1,0:T(8,128)(2,1)S(1)} %dynamic-slice_convert_fusion.16), channel_id=1, source_target_pairs={{0,6},{1,7},{2,4},{3,5},{4,2},{5,3},{6,0},{7,1},{8,14},{9,15},{10,... | collective-permute-start | bytes 307208 | tf_op jit(solution)/shard_map/ppermute | solution.py:461
  405.5 4.7 collective-permute-start.33
  408.4 7.4 %collective-permute-start.22 = (bf16[1,1,1,80,640]{4,3,2,1,0:T(8,128)(2,1)S(1)}, bf16[1,1,1,80,640]{4,3,2,1,0:T(8,128)(2,1)S(1)}, u32[]{:S(2)}, u32[]{:S(2)}) collective-permute-start(bf16[1,1,1,80,640]{4,3,2,1,0:T(8,128)(2,1)S(1)} %add_convert_fusion.11), channel_id=1, source_target_pairs={{0,6},{1,7},{2,4},{3,5},{4,2},{5,3},{6,0},{7,1},{8,14},{9,15},{10,... | collective-permute-start | bytes 307208 | tf_op jit(solution)/shard_map/ppermute | solution.py:461
  410.2 5.7 %collective-permute-start.28 = (bf16[1,1,1,80,640]{4,3,2,1,0:T(8,128)(2,1)S(1)}, bf16[1,1,1,80,640]{4,3,2,1,0:T(8,128)(2,1)S(1)}, u32[]{:S(2)}, u32[]{:S(2)}) collective-permute-start(bf16[1,1,1,80,640]{4,3,2,1,0:T(8,128)(2,1)S(1)} %add_convert_fusion.9), channel_id=1, source_target_pairs={{0,1},{1,0},{2,3},{3,2},{4,5},{5,4},{6,7},{7,6},{8,9},{9,8},{10,11... | collective-permute-start | bytes 307208 | tf_op jit(solution)/shard_map/ppermute | solution.py:461
  415.8 5.3 collective-permute-start.34
  415.8 7.1 %collective-permute-start.23 = (bf16[1,1,1,80,640]{4,3,2,1,0:T(8,128)(2,1)S(1)}, bf16[1,1,1,80,640]{4,3,2,1,0:T(8,128)(2,1)S(1)}, u32[]{:S(2)}, u32[]{:S(2)}) collective-permute-start(bf16[1,1,1,80,640]{4,3,2,1,0:T(8,128)(2,1)S(1)} %add_convert_fusion.10), channel_id=1, source_target_pairs={{0,2},{1,3},{2,0},{3,1},{4,6},{5,7},{6,4},{7,5},{8,10},{9,11},{10,... | collective-permute-start | bytes 307208 | tf_op jit(solution)/shard_map/ppermute | solution.py:461
  421.1 6.6 %collective-permute-start.29 = (bf16[1,1,1,80,640]{4,3,2,1,0:T(8,128)(2,1)S(1)}, bf16[1,1,1,80,640]{4,3,2,1,0:T(8,128)(2,1)S(1)}, u32[]{:S(2)}, u32[]{:S(2)}) collective-permute-start(bf16[1,1,1,80,640]{4,3,2,1,0:T(8,128)(2,1)S(1)} %add_convert_fusion.8), channel_id=1, source_target_pairs={{0,6},{1,7},{2,4},{3,5},{4,2},{5,3},{6,0},{7,1},{8,14},{9,15},{10,... | collective-permute-start | bytes 307208 | tf_op jit(solution)/shard_map/ppermute | solution.py:461
  422.9 5.8 %collective-permute-start.35 = (bf16[1,1,1,80,640]{4,3,2,1,0:T(8,128)(2,1)S(1)}, bf16[1,1,1,80,640]{4,3,2,1,0:T(8,128)(2,1)S(1)}, u32[]{:S(2)}, u32[]{:S(2)}) collective-permute-start(bf16[1,1,1,80,640]{4,3,2,1,0:T(8,128)(2,1)S(1)} %add_convert_fusion.6), channel_id=1, source_target_pairs={{0,1},{1,0},{2,3},{3,2},{4,5},{5,4},{6,7},{7,6},{8,9},{9,8},{10,11... | collective-permute-start | bytes 307208 | tf_op jit(solution)/shard_map/ppermute | solution.py:461
  427.6 5.8 %collective-permute-start.24 = (bf16[1,1,2,80,640]{4,3,2,1,0:T(8,128)(2,1)S(1)}, bf16[1,1,2,80,640]{4,3,2,1,0:T(8,128)(2,1)S(1)}, u32[]{:S(2)}, u32[]{:S(2)}) collective-permute-start(bf16[1,1,2,80,640]{4,3,2,1,0:T(8,128)(2,1)S(1)} %maximum_select_fusion.27), channel_id=1, source_target_pairs={{0,1},{1,0},{2,3},{3,2},{4,5},{5,4},{6,7},{7,6},{8,9},{9,8},{10,11... | collective-permute-start | bytes 614408 | tf_op jit(solution)/shard_map/ppermute | solution.py:461
  428.7 6.9 %collective-permute-start.30 = (bf16[1,1,2,80,640]{4,3,2,1,0:T(8,128)(2,1)S(1)}, bf16[1,1,2,80,640]{4,3,2,1,0:T(8,128)(2,1)S(1)}, u32[]{:S(2)}, u32[]{:S(2)}) collective-permute-start(bf16[1,1,2,80,640]{4,3,2,1,0:T(8,128)(2,1)S(1)} %maximum_select_fusion.28), channel_id=1, source_target_pairs={{0,2},{1,3},{2,0},{3,1},{4,6},{5,7},{6,4},{7,5},{8,10},{9,11},{10,... | collective-permute-start | bytes 614408 | tf_op jit(solution)/shard_map/ppermute | solution.py:461
  433.4 7.6 %collective-permute-start.36 = (bf16[1,1,2,80,640]{4,3,2,1,0:T(8,128)(2,1)S(1)}, bf16[1,1,2,80,640]{4,3,2,1,0:T(8,128)(2,1)S(1)}, u32[]{:S(2)}, u32[]{:S(2)}) collective-permute-start(bf16[1,1,2,80,640]{4,3,2,1,0:T(8,128)(2,1)S(1)} %maximum_select_fusion.29), channel_id=1, source_target_pairs={{0,6},{1,7},{2,4},{3,5},{4,2},{5,3},{6,0},{7,1},{8,14},{9,15},{10,... | collective-permute-start | bytes 614408 | tf_op jit(solution)/shard_map/ppermute | solution.py:461
  444.1 12.8 %collective-permute-start.46 = (bf16[1,1,2,240,640]{4,3,2,1,0:T(8,128)(2,1)S(1)}, bf16[1,1,2,240,640]{4,3,2,1,0:T(8,128)(2,1)S(1)}, u32[]{:S(2)}, u32[]{:S(2)}) collective-permute-start(bf16[1,1,2,240,640]{4,3,2,1,0:T(8,128)(2,1)S(1)} %dynamic-slice_convert_fusion.4), channel_id=1, source_target_pairs={{0,16},{8,24},{16,0},{24,8},{1,17},{9,25},{17,1},{25,9},{2,18},{10... | collective-permute-start | bytes 1843208 | tf_op jit(solution)/shard_map/ppermute | solution.py:457
  445.1 16.7 %collective-permute-start.53 = (bf16[2,1,1,240,640]{4,3,2,1,0:T(8,128)(2,1)S(1)}, bf16[2,1,1,240,640]{4,3,2,1,0:T(8,128)(2,1)S(1)}, u32[]{:S(2)}, u32[]{:S(2)}) collective-permute-start(bf16[2,1,1,240,640]{4,3,2,1,0:T(8,128)(2,1)S(1)} %dynamic-slice_convert_fusion.3), channel_id=1, source_target_pairs={{0,1},{1,0},{2,3},{3,2},{4,5},{5,4},{6,7},{7,6},{8,9},{9,8},{10,11... | collective-permute-start | bytes 1843208 | tf_op jit(solution)/shard_map/ppermute | solution.py:461
  447.5 24.2 %collective-permute-start.39 = (bf16[1,1,2,240,640]{4,3,2,1,0:T(8,128)(2,1)S(1)}, bf16[1,1,2,240,640]{4,3,2,1,0:T(8,128)(2,1)S(1)}, u32[]{:S(2)}, u32[]{:S(2)}) collective-permute-start(bf16[1,1,2,240,640]{4,3,2,1,0:T(8,128)(2,1)S(1)} %dynamic-slice_convert_fusion.5), channel_id=1, source_target_pairs={{0,1},{1,0},{2,3},{3,2},{4,5},{5,4},{6,7},{7,6},{8,9},{9,8},{10,11... | collective-permute-start | bytes 1843208 | tf_op jit(solution)/shard_map/ppermute | solution.py:461
  457.1 14.7 %collective-permute-start.47 = (bf16[1,1,1,240,640]{4,3,2,1,0:T(8,128)(2,1)S(1)}, bf16[1,1,1,240,640]{4,3,2,1,0:T(8,128)(2,1)S(1)}, u32[]{:S(2)}, u32[]{:S(2)}) collective-permute-start(bf16[1,1,1,240,640]{4,3,2,1,0:T(8,128)(2,1)S(1)} %dynamic-slice_convert_fusion.10), channel_id=1, source_target_pairs={{0,6},{1,7},{2,4},{3,5},{4,2},{5,3},{6,0},{7,1},{8,14},{9,15},{10,... | collective-permute-start | bytes 921608 | tf_op jit(solution)/shard_map/ppermute | solution.py:461
  462.0 10.4 %collective-permute-start.54 = (bf16[1,1,1,240,640]{4,3,2,1,0:T(8,128)(2,1)S(1)}, bf16[1,1,1,240,640]{4,3,2,1,0:T(8,128)(2,1)S(1)}, u32[]{:S(2)}, u32[]{:S(2)}) collective-permute-start(bf16[1,1,1,240,640]{4,3,2,1,0:T(8,128)(2,1)S(1)} %dynamic-slice_convert_fusion.9), channel_id=1, source_target_pairs={{0,16},{8,24},{16,0},{24,8},{1,17},{9,25},{17,1},{25,9},{2,18},{10... | collective-permute-start | bytes 921608 | tf_op jit(solution)/shard_map/ppermute | solution.py:457
  471.9 8.0 %collective-permute-start.48 = (bf16[1,1,1,240,640]{4,3,2,1,0:T(8,128)(2,1)S(1)}, bf16[1,1,1,240,640]{4,3,2,1,0:T(8,128)(2,1)S(1)}, u32[]{:S(2)}, u32[]{:S(2)}) collective-permute-start(bf16[1,1,1,240,640]{4,3,2,1,0:T(8,128)(2,1)S(1)} %add_convert_fusion.3), channel_id=1, source_target_pairs={{0,1},{1,0},{2,3},{3,2},{4,5},{5,4},{6,7},{7,6},{8,9},{9,8},{10,11... | collective-permute-start | bytes 921608 | tf_op jit(solution)/shard_map/ppermute | solution.py:461
  472.3 10.2 %collective-permute-start.40 = (bf16[1,1,1,240,640]{4,3,2,1,0:T(8,128)(2,1)S(1)}, bf16[1,1,1,240,640]{4,3,2,1,0:T(8,128)(2,1)S(1)}, u32[]{:S(2)}, u32[]{:S(2)}) collective-permute-start(bf16[1,1,1,240,640]{4,3,2,1,0:T(8,128)(2,1)S(1)} %dynamic-slice_convert_fusion.11), channel_id=1, source_target_pairs={{0,2},{1,3},{2,0},{3,1},{4,6},{5,7},{6,4},{7,5},{8,10},{9,11},{10,... | collective-permute-start | bytes 921608 | tf_op jit(solution)/shard_map/ppermute | solution.py:461
  472.5 21.8 %collective-permute-start.55 = (bf16[1,1,1,240,640]{4,3,2,1,0:T(8,128)(2,1)S(1)}, bf16[1,1,1,240,640]{4,3,2,1,0:T(8,128)(2,1)S(1)}, u32[]{:S(2)}, u32[]{:S(2)}) collective-permute-start(bf16[1,1,1,240,640]{4,3,2,1,0:T(8,128)(2,1)S(1)} %add_convert_fusion.1), channel_id=1, source_target_pairs={{0,2},{1,3},{2,0},{3,1},{4,6},{5,7},{6,4},{7,5},{8,10},{9,11},{10,... | collective-permute-start | bytes 921608 | tf_op jit(solution)/shard_map/ppermute | solution.py:461
  480.0 17.6 %collective-permute-start.49 = (bf16[1,1,1,240,640]{4,3,2,1,0:T(8,128)(2,1)S(1)}, bf16[1,1,1,240,640]{4,3,2,1,0:T(8,128)(2,1)S(1)}, u32[]{:S(2)}, u32[]{:S(2)}) collective-permute-start(bf16[1,1,1,240,640]{4,3,2,1,0:T(8,128)(2,1)S(1)} %add_convert_fusion.2), channel_id=1, source_target_pairs={{0,6},{1,7},{2,4},{3,5},{4,2},{5,3},{6,0},{7,1},{8,14},{9,15},{10,... | collective-permute-start | bytes 921608 | tf_op jit(solution)/shard_map/ppermute | solution.py:461
  482.6 18.4 %collective-permute-start.41 = (bf16[1,1,1,240,640]{4,3,2,1,0:T(8,128)(2,1)S(1)}, bf16[1,1,1,240,640]{4,3,2,1,0:T(8,128)(2,1)S(1)}, u32[]{:S(2)}, u32[]{:S(2)}) collective-permute-start(bf16[1,1,1,240,640]{4,3,2,1,0:T(8,128)(2,1)S(1)} %add_convert_fusion.5), channel_id=1, source_target_pairs={{0,6},{1,7},{2,4},{3,5},{4,2},{5,3},{6,0},{7,1},{8,14},{9,15},{10,... | collective-permute-start | bytes 921608 | tf_op jit(solution)/shard_map/ppermute | solution.py:461
  494.3 8.1 %collective-permute-start.56 = (bf16[1,1,1,240,640]{4,3,2,1,0:T(8,128)(2,1)S(1)}, bf16[1,1,1,240,640]{4,3,2,1,0:T(8,128)(2,1)S(1)}, u32[]{:S(2)}, u32[]{:S(2)}) collective-permute-start(bf16[1,1,1,240,640]{4,3,2,1,0:T(8,128)(2,1)S(1)} %add_convert_fusion), channel_id=1, source_target_pairs={{0,1},{1,0},{2,3},{3,2},{4,5},{5,4},{6,7},{7,6},{8,9},{9,8},{10,11... | collective-permute-start | bytes 921608 | tf_op jit(solution)/shard_map/ppermute | solution.py:461
  497.7 33.2 %collective-permute-start.50 = (bf16[1,1,2,240,640]{4,3,2,1,0:T(8,128)(2,1)S(1)}, bf16[1,1,2,240,640]{4,3,2,1,0:T(8,128)(2,1)S(1)}, u32[]{:S(2)}, u32[]{:S(2)}) collective-permute-start(bf16[1,1,2,240,640]{4,3,2,1,0:T(8,128)(2,1)S(1)} %maximum_select_fusion.22), channel_id=1, source_target_pairs={{0,2},{1,3},{2,0},{3,1},{4,6},{5,7},{6,4},{7,5},{8,10},{9,11},{10,... | collective-permute-start | bytes 1843208 | tf_op jit(solution)/shard_map/ppermute | solution.py:461
  501.1 27.6 %collective-permute-start.42 = (bf16[1,1,1,240,640]{4,3,2,1,0:T(8,128)(2,1)S(1)}, bf16[1,1,1,240,640]{4,3,2,1,0:T(8,128)(2,1)}, u32[]{:S(2)}, u32[]{:S(2)}) collective-permute-start(bf16[1,1,1,240,640]{4,3,2,1,0:T(8,128)(2,1)S(1)} %add_convert_fusion.4), channel_id=1, source_target_pairs={{0,2},{1,3},{2,0},{3,1},{4,6},{5,7},{6,4},{7,5},{8,10},{9,11},{10,... | collective-permute-start | bytes 921608 | tf_op jit(solution)/shard_map/ppermute | solution.py:461
  502.5 31.8 %collective-permute-start.57 = (bf16[1,1,2,240,640]{4,3,2,1,0:T(8,128)(2,1)S(1)}, bf16[1,1,2,240,640]{4,3,2,1,0:T(8,128)(2,1)S(1)}, u32[]{:S(2)}, u32[]{:S(2)}) collective-permute-start(bf16[1,1,2,240,640]{4,3,2,1,0:T(8,128)(2,1)S(1)} %maximum_select_fusion.23), channel_id=1, source_target_pairs={{0,6},{1,7},{2,4},{3,5},{4,2},{5,3},{6,0},{7,1},{8,14},{9,15},{10,... | collective-permute-start | bytes 1843208 | tf_op jit(solution)/shard_map/ppermute | solution.py:461
  529.9 10.2 %collective-permute-start.43 = (bf16[1,1,2,240,640]{4,3,2,1,0:T(8,128)(2,1)S(1)}, bf16[1,1,2,240,640]{4,3,2,1,0:T(8,128)(2,1)S(1)}, u32[]{:S(2)}, u32[]{:S(2)}) collective-permute-start(bf16[1,1,2,240,640]{4,3,2,1,0:T(8,128)(2,1)S(1)} %maximum_select_fusion.21), channel_id=1, source_target_pairs={{0,1},{1,0},{2,3},{3,2},{4,5},{5,4},{6,7},{7,6},{8,9},{9,8},{10,11... | collective-permute-start | bytes 1843208 | tf_op jit(solution)/shard_map/ppermute | solution.py:461
  (35 other events, 154.2 us)

commit v2 on v1

--- a/solution.py
+++ b/solution.py
@@ -1,3 +1,5 @@
+import functools
+
 import jax
 import jax.numpy as jnp
 from jax import lax
@@ -62,34 +64,97 @@
     return pl.BlockSpec((height, width), lambda i: (0, i))
 
 
-def project_kernel(x_ref, w_ref, cos_ref, sin_ref, qkv_ref, h_ref):
-    gain = w_ref[:, 0:1].astype(F32)
+class Weight:
+    def __init__(self, axis, pieces, dim=None, blocks=0):
+        self.axis, self.dim, self.blocks = axis, dim, blocks
+        self.arrays = [array for array, _, _ in pieces]
+        self.places = [(flip, side) for _, flip, side in pieces]
+        shape = list(self.arrays[0].shape)
+        self.size = shape[axis]
+        self.half = shape[1 - axis] // 2
+        shape[axis] *= 4
+        self.shape = tuple(shape)
+
+    def specs(self):
+        return [pl.BlockSpec(memory_space=pl.ANY)] * len(self.arrays)
+
+    def scratch(self):
+        if not self.blocks:
+            return [pltpu.VMEM(self.shape, BF16), pltpu.SemaphoreType.DMA]
+        block = (self.shape[0], self.shape[1] // self.blocks)
+        return [pltpu.VMEM((self.blocks,) + block, BF16), pltpu.SemaphoreType.DMA((self.blocks,))]
+
+    def load(self, where_ref, refs, scratch, sem):
+        wide = self.shape[1] // max(self.blocks, 1)
+        for ref, (flip, side) in zip(refs, self.places):
+            at = (where_ref[0] ^ flip) * self.size
+            other = 0 if side is None else (where_ref[1 + self.dim] ^ side) * self.half
+            row, column = (at, other) if self.axis == 0 else (other, at)
+            rows = pl.ds(pl.multiple_of(row, OWN), ref.shape[0])
+            if not self.blocks:
+                pltpu.make_async_copy(ref, scratch.at[rows, :], sem).start()
+                continue
+            first = column // wide
+            for i in range(ref.shape[1] // wide):
+                pltpu.make_async_copy(
+                    ref.at[:, i * wide:(i + 1) * wide], scratch.at[first + i, rows, :],
+                    sem.at[first + i],
+                ).start()
+
+
+def wait_for(scratch, sem):
+    pltpu.make_async_copy(scratch, scratch, sem).wait()
+
+
+SMEM = pl.BlockSpec(memory_space=pltpu.SMEM)
+
+
+def project_kernel(weights, where_ref, x_ref, cos_ref, sin_ref, *refs):
+    qkv_ref, h_ref, gains_ref, wq, q_sem, wk, k_sem = refs[8:]
+
+    @pl.when(pl.program_id(0) == 0)
+    def _():
+        weights[0].load(where_ref, refs[:4], wq, q_sem)
+        weights[1].load(where_ref, refs[4:8], wk, k_sem)
+        wait_for(wq, q_sem)
+        wait_for(wk, k_sem)
+        gains_ref[...] = wk[:, 2 * KEYS:]
+
+    gain = wk[:, 2 * KEYS:2 * KEYS + 1].astype(F32)
     normal, _ = norm_columns(x_ref[...].astype(F32))
     h = (normal * gain).astype(BF16)
     h_ref[...] = h
     c, s = cos_ref[...], sin_ref[...]
-    out = dot(w_ref[:, GAINS:], h, 0, 0)
-    for head in range(QUERY_HEADS + KEY_VALUE_HEADS):
-        at = head * HEAD_WIDTH
-        a, b = out[at:at + HALF], out[at + HALF:at + HEAD_WIDTH]
-        scale = HEAD_WIDTH ** -0.5 if head < QUERY_HEADS else 1.0
-        qkv_ref[at:at + HALF, :] = ((a * c - b * s) * scale).astype(BF16)
-        qkv_ref[at + HALF:at + HEAD_WIDTH, :] = ((b * c + a * s) * scale).astype(BF16)
-    qkv_ref[D + KEYS:, :] = out[D + KEYS:].astype(BF16)
-
-
-def project(x, w, cos, sin):
+
+    def rotary(out, at, heads, scale):
+        for head in range(heads):
+            low = head * HEAD_WIDTH
+            a, b = out[low:low + HALF], out[low + HALF:low + HEAD_WIDTH]
+            to = at + low
+            qkv_ref[to:to + HALF, :] = ((a * c - b * s) * scale).astype(BF16)
+            qkv_ref[to + HALF:to + HEAD_WIDTH, :] = ((b * c + a * s) * scale).astype(BF16)
+
+    rotary(dot(wq[...], h, 0, 0), 0, QUERY_HEADS, HEAD_WIDTH ** -0.5)
+    out = dot(wk[:, :2 * KEYS], h, 0, 0)
+    rotary(out, D, KEY_VALUE_HEADS, 1.0)
+    qkv_ref[D + KEYS:, :] = out[KEYS:].astype(BF16)
+
+
+def project(where, x, wq, wk, cos, sin):
     rows = x.shape[1]
     return pl.pallas_call(
-        project_kernel,
+        functools.partial(project_kernel, (wq, wk)),
         grid=(rows // TILE,),
-        in_specs=[columns(D, TILE), fixed(w.shape), columns(HALF, TILE), columns(HALF, TILE)],
-        out_specs=[columns(WIDE, TILE), columns(D, TILE)],
-        out_shape=shaped(((WIDE, rows), BF16), ((D, rows), BF16)),
+        in_specs=[SMEM, columns(D, TILE), columns(HALF, TILE), columns(HALF, TILE)]
+        + wq.specs() + wk.specs(),
+        out_specs=[columns(WIDE, TILE), columns(D, TILE),
+                   pl.BlockSpec((D, GAINS), lambda i: (0, 0))],
+        out_shape=shaped(((WIDE, rows), BF16), ((D, rows), BF16), ((D, GAINS), BF16)),
+        scratch_shapes=wq.scratch() + wk.scratch(),
         compiler_params=params(40),
         cost_estimate=cost(2 * rows * D * WIDE, rows * (2 * D + WIDE) * 2 + D * WIDE * 2),
         name="project",
-    )(x, w, cos, sin)
+    )(where, x, cos, sin, *wq.arrays, *wk.arrays)
 
 
 def key_span(block):
@@ -143,49 +208,57 @@
                 lse_ref[kv, i:i + 1, b * QB:(b + 1) * QB] = lse[:, i * QB:(i + 1) * QB]
 
 
-def attend(qkv, segments):
-    seqs, length = segments.shape
-    wide, rows = qkv.shape
-    pairs = seqs * QUERY_HEADS * length * length
+def attend(qkv, segments, at):
+    length = segments.shape[1]
+    wide = qkv.shape[0]
+    pairs = QUERY_HEADS * length * length
     return pl.pallas_call(
         attend_kernel,
-        grid=(seqs,),
+        grid=(1,),
         in_specs=[
-            pl.BlockSpec((wide, length), lambda i: (0, i)),
-            pl.BlockSpec((1, 1, length), lambda i: (i, 0, 0)),
-            pl.BlockSpec((1, length, 1), lambda i: (i, 0, 0)),
+            pl.BlockSpec((wide, length), lambda i: (0, at)),
+            pl.BlockSpec((1, 1, length), lambda i: (at, 0, 0)),
+            pl.BlockSpec((1, length, 1), lambda i: (at, 0, 0)),
         ],
         out_specs=[
-            pl.BlockSpec((D, length), lambda i: (0, i)),
-            pl.BlockSpec((KEY_VALUE_HEADS, 8, length), lambda i: (0, 0, i)),
+            pl.BlockSpec((D, length), lambda i: (0, 0)),
+            pl.BlockSpec((KEY_VALUE_HEADS, 8, length), lambda i: (0, 0, 0)),
         ],
-        out_shape=shaped(((D, rows), BF16), ((KEY_VALUE_HEADS, 8, rows), F32)),
+        out_shape=shaped(((D, length), BF16), ((KEY_VALUE_HEADS, 8, length), F32)),
         scratch_shapes=[pltpu.VMEM((length // QB, 3 * QB, QB), F32)],
-        compiler_params=params(48),
-        cost_estimate=cost(pairs * 256 * 2, rows * (wide + D) * 2, pairs // 2),
+        compiler_params=params(40),
+        cost_estimate=cost(pairs * 256 * 2, length * (wide + D) * 2, pairs // 2),
         name="attend",
     )(qkv, segments[:, None, :], segments[:, :, None])
 
 
-def middle_kernel(x_ref, o_ref, w_ref, gain_ref, x1_ref, h_ref):
-    x1 = x_ref[...].astype(F32) + dot(w_ref[...], o_ref[...], 0, 0)
+def middle_kernel(weight, where_ref, x_ref, o_ref, gain_ref, *refs):
+    x1_ref, h_ref, w, sem = refs[4:]
+
+    @pl.when(pl.program_id(0) == 0)
+    def _():
+        weight.load(where_ref, refs[:4], w, sem)
+        wait_for(w, sem)
+
+    x1 = x_ref[...].astype(F32) + dot(w[...], o_ref[...], 0, 0)
     normal, _ = norm_columns(x1)
     x1_ref[...] = x1
     h_ref[...] = (normal * gain_ref[:, 1:2].astype(F32)).astype(BF16)
 
 
-def middle(x, o, w, gains):
+def middle(where, x, o, w, gains):
     rows = x.shape[1]
     return pl.pallas_call(
-        middle_kernel,
+        functools.partial(middle_kernel, w),
         grid=(rows // TILE,),
-        in_specs=[columns(D, TILE), columns(D, TILE), fixed(w.shape), fixed((D, GAINS))],
+        in_specs=[SMEM, columns(D, TILE), columns(D, TILE), fixed((D, GAINS))] + w.specs(),
         out_specs=[columns(D, TILE), columns(D, TILE)],
         out_shape=shaped(((D, rows), F32), ((D, rows), BF16)),
+        scratch_shapes=w.scratch(),
         compiler_params=params(40),
         cost_estimate=cost(2 * rows * D * D, rows * D * 10),
         name="middle",
-    )(x, o, w, gains)
+    )(where, x, o, gains, *w.arrays)
 
 
 def split_owners(grad, core, keep_ref, send_ref):
@@ -196,16 +269,24 @@
         send_ref[x, 0] = jnp.where(core == 0, b, a).astype(BF16)
 
 
-def feed_forward_kernel(core_ref, h_ref, dy_ref, x1_ref, wg_ref, wu_ref, wd_ref, y_ref, dh_ref,
-                        gg_keep, gg_send, gu_keep, gu_send, gd_keep, gd_send, acc_ref):
+def feed_forward_kernel(weights, where_ref, h_ref, dy_ref, x1_ref, *refs):
+    count = len(weights[0].arrays)
+    (y_ref, dh_ref, gg_keep, gg_send, gu_keep, gu_send, gd_keep, gd_send, acc_ref, *scratch) = (
+        refs[3 * count:]
+    )
     step = pl.program_id(0)
-    core = core_ref[0]
+    core = where_ref[0] & 1
 
     @pl.when(step == 0)
     def _():
+        for i, weight in enumerate(weights):
+            weight.load(where_ref, refs[i * count:(i + 1) * count], *scratch[2 * i:2 * i + 2])
         acc_ref[...] = x1_ref[...]
         dh_ref[...] = jnp.zeros_like(dh_ref)
 
+    wg_ref, wu_ref, wd_ref = (w.at[step] for w in scratch[::2])
+    for w, sem in zip((wg_ref, wu_ref, wd_ref), scratch[1::2]):
+        wait_for(w, sem.at[step])
     h, dy = h_ref[...], dy_ref[...]
     gate = dot(wg_ref[...], h, 0, 0)
     up = dot(wu_ref[...], h, 0, 0)
@@ -235,30 +316,36 @@
         y_ref[...] = acc_ref[...].astype(BF16)
 
 
-def feed_forward(core, h, dy, x1, wg, wu, wd):
-    rows, hidden = h.shape[1], wg.shape[1]
+def feed_forward(where, h, dy, x1, weights):
+    rows, hidden = h.shape[1], weights[0].shape[1]
     steps = hidden // CUT
     part = (2, steps, OWN, CUT)
     by_rows = pl.BlockSpec((2, 1, OWN, CUT), lambda f: (0, f, 0, 0))
     by_columns = pl.BlockSpec((1, steps, OWN, CUT), lambda f: (f // 2, 0, 0, 0))
     return pl.pallas_call(
-        feed_forward_kernel,
+        functools.partial(feed_forward_kernel, weights),
         grid=(steps,),
         in_specs=[
-            pl.BlockSpec(memory_space=pltpu.SMEM),
+            SMEM,
             fixed((D, rows)), fixed((D, rows)), fixed((D, rows)),
-            columns(D, CUT), columns(D, CUT), columns(D, CUT),
-        ],
+        ] + sum((w.specs() for w in weights), []),
         out_specs=[fixed((D, rows)), fixed((D, rows))] + [by_rows] * 4 + [by_columns] * 2,
         out_shape=shaped(((D, rows), BF16), ((D, rows), F32)) + shaped((part, BF16)) * 6,
-        scratch_shapes=[pltpu.VMEM((D, rows), F32)],
+        scratch_shapes=sum((w.scratch() for w in weights), [pltpu.VMEM((D, rows), F32)]),
         compiler_params=params(60),
         cost_estimate=cost(18 * rows * D * hidden, 16 * rows * D + 12 * D * hidden, rows * hidden),
         name="feed_forward",
-    )(core, h, dy, x1, wg, wu, wd)
-
-
-def branch_kernel(dh_ref, x1_ref, dy_ref, gain_ref, w_ref, dx_ref, da_ref, do_ref, gain_grad):
+    )(where, h, dy, x1, *sum((w.arrays for w in weights), []))
+
+
+def branch_kernel(weight, where_ref, dh_ref, x1_ref, dy_ref, gain_ref, *refs):
+    dx_ref, da_ref, do_ref, gain_grad, w, sem = refs[4:]
+    first = pl.program_id(0) == 0
+
+    @pl.when(first)
+    def _():
+        weight.load(where_ref, refs[:4], w, sem)
+
     gain = gain_ref[:, 1:2].astype(F32)
     normal, inverse = norm_columns(x1_ref[...])
     back, part = norm_columns_back(dh_ref[...], normal, inverse, gain)
@@ -266,29 +353,32 @@
     da = dx.astype(BF16)
     dx_ref[...] = dx
     da_ref[...] = da
-    do_ref[...] = dot(w_ref[...], da, 1, 0).astype(BF16)
-
-    @pl.when(pl.program_id(0) == 0)
+
+    @pl.when(first)
     def _():
         gain_grad[...] = part
-
-    @pl.when(pl.program_id(0) > 0)
+        wait_for(w, sem)
+
+    @pl.when(jnp.logical_not(first))
     def _():
         gain_grad[...] += part
 
-
-def branch(dh, x1, dy, gains, w):
+    do_ref[...] = dot(w[...], da, 1, 0).astype(BF16)
+
+
+def branch(where, dh, x1, dy, gains, w):
     rows = dh.shape[1]
     return pl.pallas_call(
-        branch_kernel,
+        functools.partial(branch_kernel, w),
         grid=(rows // TILE,),
-        in_specs=[columns(D, TILE)] * 3 + [fixed((D, GAINS)), fixed(w.shape)],
+        in_specs=[SMEM] + [columns(D, TILE)] * 3 + [fixed((D, GAINS))] + w.specs(),
         out_specs=[columns(D, TILE)] * 3 + [pl.BlockSpec((D, 1), lambda i: (0, 0))],
         out_shape=shaped(((D, rows), F32), ((D, rows), BF16), ((D, rows), BF16), ((D, 1), F32)),
+        scratch_shapes=w.scratch(),
         compiler_params=params(40),
         cost_estimate=cost(2 * rows * D * D, rows * D * 18),
         name="branch",
-    )(dh, x1, dy, gains, w)
+    )(where, dh, x1, dy, gains, *w.arrays)
 
 
 def attend_back_kernel(qkv_ref, o_ref, do_ref, lse_ref, segr_ref, segc_ref, cos_ref, sin_ref,
@@ -329,38 +419,39 @@
             dv_ref[...].astype(BF16))
 
 
-def attend_back(qkv, o, do, lse, segments, cos, sin):
-    seqs, length = segments.shape
-    wide, rows = qkv.shape
-    pairs = seqs * QUERY_HEADS * length * length
+def attend_back(qkv, o, do, lse, segments, cos, sin, at):
+    length = segments.shape[1]
+    wide = qkv.shape[0]
+    pairs = QUERY_HEADS * length * length
+    here = lambda height: pl.BlockSpec((height, length), lambda i: (0, at))
     return pl.pallas_call(
         attend_back_kernel,
-        grid=(seqs,),
+        grid=(1,),
         in_specs=[
-            pl.BlockSpec((wide, length), lambda i: (0, i)),
-            pl.BlockSpec((D, length), lambda i: (0, i)),
-            pl.BlockSpec((D, length), lambda i: (0, i)),
-            pl.BlockSpec((KEY_VALUE_HEADS, 8, length), lambda i: (0, 0, i)),
-            pl.BlockSpec((1, 1, length), lambda i: (i, 0, 0)),
-            pl.BlockSpec((1, length, 1), lambda i: (i, 0, 0)),
-            pl.BlockSpec((HALF, length), lambda i: (0, i)),
-            pl.BlockSpec((HALF, length), lambda i: (0, i)),
+            here(wide),
+            pl.BlockSpec((D, length), lambda i: (0, 0)),
+            here(D),
+            pl.BlockSpec((KEY_VALUE_HEADS, 8, length), lambda i: (0, 0, 0)),
+            pl.BlockSpec((1, 1, length), lambda i: (at, 0, 0)),
+            pl.BlockSpec((1, length, 1), lambda i: (at, 0, 0)),
+            here(HALF),
+            here(HALF),
         ],
-        out_specs=pl.BlockSpec((wide, length), lambda i: (0, i)),
-        out_shape=jax.ShapeDtypeStruct((wide, rows), BF16),
+        out_specs=pl.BlockSpec((wide, length), lambda i: (0, 0)),
+        out_shape=jax.ShapeDtypeStruct((wide, length), BF16),
         scratch_shapes=[
             pltpu.VMEM((length // QB, 3 * QB, QB), F32),
             pltpu.VMEM((HEAD_WIDTH, length), F32),
             pltpu.VMEM((HEAD_WIDTH, length), F32),
         ],
-        compiler_params=params(48),
-        cost_estimate=cost(pairs * 256 * 5, rows * (2 * wide + 2 * D) * 2, pairs // 2),
+        compiler_params=params(40),
+        cost_estimate=cost(pairs * 256 * 5, length * (2 * wide + 2 * D) * 2, pairs // 2),
         name="attend_back",
     )(qkv, o, do, lse, segments[:, None, :], segments[:, :, None], cos, sin)
 
 
-def weight_kernel(core_ref, h_ref, dqkv_ref, o_ref, da_ref, keep_ref, send_ref):
-    core = core_ref[0]
+def weight_kernel(where_ref, h_ref, dqkv_ref, o_ref, da_ref, keep_ref, send_ref):
+    core = where_ref[0] & 1
     step = pl.program_id(0)
 
     @pl.when(step < 2)
@@ -379,50 +470,62 @@
         split_owners(dot(o_ref[...], da_ref[3 * CUT - WIDE:, :], 1, 1), core, keep_ref, send_ref)
 
 
-def weight_grads(core, h, dqkv, o, da):
+def weight_grads(where, h, dqkv, o, da):
     rows = h.shape[1]
     part = pl.BlockSpec((2, 1, OWN, CUT), lambda f: (0, f, 0, 0))
     return pl.pallas_call(
         weight_kernel,
         grid=(4,),
-        in_specs=[pl.BlockSpec(memory_space=pltpu.SMEM), fixed((D, rows)), fixed((WIDE, rows)),
+        in_specs=[SMEM, fixed((D, rows)), fixed((WIDE, rows)),
                   fixed((D, rows)), fixed((D, rows))],
         out_specs=[part, part],
         out_shape=shaped(((2, 4, OWN, CUT), BF16)) * 2,
         compiler_params=params(40),
         cost_estimate=cost(2 * rows * D * (D + WIDE), rows * (3 * D + WIDE) * 2 + D * 5120),
         name="weight_grads",
-    )(core, h, dqkv, o, da)
-
-
-def inputs_kernel(x_ref, dx_ref, w_ref, dqkv_ref, out_ref, gain_grad):
-    gain = w_ref[:, 0:1].astype(F32)
-    dh = dot(w_ref[:, GAINS:], dqkv_ref[...], 1, 0)
+    )(where, h, dqkv, o, da)
+
+
+def inputs_kernel(weights, where_ref, x_ref, dx_ref, dqkv_ref, *refs):
+    out_ref, gain_grad, wq, q_sem, wk, k_sem = refs[8:]
+    first = pl.program_id(0) == 0
+
+    @pl.when(first)
+    def _():
+        weights[0].load(where_ref, refs[:4], wq, q_sem)
+        weights[1].load(where_ref, refs[4:8], wk, k_sem)
+        wait_for(wq, q_sem)
+        wait_for(wk, k_sem)
+
+    gain = wk[:, 2 * KEYS:2 * KEYS + 1].astype(F32)
+    dh = dot(wq[...], dqkv_ref[:D], 1, 0) + dot(wk[:, :2 * KEYS], dqkv_ref[D:], 1, 0)
     normal, inverse = norm_columns(x_ref[...].astype(F32))
     back, part = norm_columns_back(dh, normal, inverse, gain)
     out_ref[...] = (dx_ref[...] + back).astype(BF16)
 
-    @pl.when(pl.program_id(0) == 0)
+    @pl.when(first)
     def _():
         gain_grad[...] = part
 
-    @pl.when(pl.program_id(0) > 0)
+    @pl.when(jnp.logical_not(first))
     def _():
         gain_grad[...] += part
 
 
-def input_grads(x, dx, w, dqkv):
+def input_grads(where, x, dx, wq, wk, dqkv):
     rows = x.shape[1]
     return pl.pallas_call(
-        inputs_kernel,
+        functools.partial(inputs_kernel, (wq, wk)),
         grid=(rows // TILE,),
-        in_specs=[columns(D, TILE), columns(D, TILE), fixed(w.shape), columns(WIDE, TILE)],
+        in_specs=[SMEM, columns(D, TILE), columns(D, TILE), columns(WIDE, TILE)]
+        + wq.specs() + wk.specs(),
         out_specs=[columns(D, TILE), pl.BlockSpec((D, 1), lambda i: (0, 0))],
         out_shape=shaped(((D, rows), BF16), ((D, 1), F32)),
+        scratch_shapes=wq.scratch() + wk.scratch(),
         compiler_params=params(40),
         cost_estimate=cost(2 * rows * D * WIDE, rows * (D * 8 + WIDE * 2) + D * WIDE * 2),
         name="input_grads",
-    )(x, dx, w, dqkv)
+    )(where, x, dx, dqkv, *wq.arrays, *wk.arrays)
 
 
 def tables(segments):
@@ -451,6 +554,7 @@
         self.coordinate[1] = bits[1] ^ bits[2]
         self.coordinate["x"] = group >> 1
         self.coordinate["core"] = group & 1
+        self.me = group
 
     def swap(self, value, dim):
         if dim == "x":
@@ -468,39 +572,76 @@
         )
 
 
-def gather(cube, shard, axis, relay, halves):
-    sibling = cube.swap(shard, "core")
-    if relay is None:
-        across = cube.swap(shard, "x")
-    else:
-        size = shard.shape[halves] // 2
-        part = lax.dynamic_slice_in_dim(shard, cube.coordinate[relay] * size, size, halves)
-        direct = cube.swap(part, "x")
-        across = cube.ordered(relay, direct, cube.swap(direct, relay), halves)
-    diagonal = cube.swap(across, "core")
-    here = cube.ordered("core", shard, sibling, axis)
-    there = cube.ordered("core", across, diagonal, axis)
-    return cube.ordered("x", here, there, axis)
-
-
-def reduce_piece(cube, keep, got, order):
-    rows, wide = keep.shape[2:]
-    total = keep.astype(F32) + got.astype(F32)
-    total = total.reshape(2, 2, 2, rows, wide)
-    cut = [d for d in order if d != "x"]
-    place = {"x": 0, cut[0]: 1, cut[1]: 2}
-    for dim in order:
-        mine = cube.coordinate[dim]
-        other = lax.dynamic_slice_in_dim(total, 1 - mine, 1, place[dim]).astype(BF16)
-        own = lax.dynamic_slice_in_dim(total, mine, 1, place[dim])
-        total = own + cube.swap(other, dim).astype(F32)
-    low = total.astype(BF16)
-    for dim in range(cube.dims):
-        if dim not in cut:
-            low = (low.astype(F32) + cube.swap(low, dim).astype(F32)).astype(BF16)
-    for dim in reversed(cut):
-        low = cube.ordered(dim, low, cube.swap(low, dim), place[dim])
-    return low.reshape(4, rows, wide)
+def rows_of(own, sibling, across, diagonal):
+    pieces = own, sibling, across, diagonal
+    return Weight(0, [(array, flip, None) for flip, array in enumerate(pieces)])
+
+
+class Relay:
+    def __init__(self, cube, shard, axis, first, second):
+        self.cube, self.shard, self.axis, self.dims = cube, shard, axis, (first, second)
+        self.cut = 1 - axis
+        self.size = shard.shape[self.cut] // 4
+        at = 2 * cube.coordinate[second] + cube.coordinate[first]
+        self.quarter = lax.dynamic_slice_in_dim(shard, at * self.size, self.size, self.cut)
+
+    def cross(self, *others):
+        self.direct = self.cube.swap(after(self.quarter, *others), "x")
+        return self.direct
+
+    def hand_on(self, *others):
+        self.handed = self.cube.swap(after(self.direct, *others), self.dims[0])
+        return self.handed
+
+    def finish(self, *others):
+        cube = self.cube
+        handed = after(self.handed, *others)
+        self.half = cube.ordered(self.dims[0], self.direct, handed, self.cut)
+        self.rest = cube.swap(self.half, self.dims[1])
+        self.half_diagonal = cube.swap(self.half, "core")
+        return self.rest
+
+    def weight(self, sibling, *others):
+        rest = after(self.rest, *others)
+        pieces = [
+            (self.shard, 0, None), (sibling, 1, None), (self.half, 2, 0), (rest, 2, 1),
+            (self.half_diagonal, 3, 0), (self.cube.swap(rest, "core"), 3, 1),
+        ]
+        return Weight(self.axis, pieces, self.dims[1], 4)
+
+
+class Reduce:
+    def __init__(self, cube, keep, got, order):
+        rows, wide = keep.shape[2:]
+        self.cube, self.order, self.shape = cube, order, (4, rows, wide)
+
+        self.cut = [d for d in order[:2] if d != "x"][0]
+        self.terms = [t.reshape(2, 2, 2, rows, wide) for t in (keep, got)]
+        self.got = None
+
+    def sum(self):
+        return functools.reduce(jnp.add, [t.astype(F32) for t in self.terms]).astype(BF16)
+
+    def step(self, index, *others):
+        cube, dim = self.cube, self.order[index]
+        if index < 2:
+            mine, axis = cube.coordinate[dim], 0 if dim == "x" else 1
+            take = lambda which: [
+                lax.dynamic_slice_in_dim(t, which, 1, axis) for t in self.terms
+            ]
+            other, self.terms = take(1 - mine), take(mine)
+            send = functools.reduce(jnp.add, [t.astype(F32) for t in other]).astype(BF16)
+            self.got = cube.swap(after(send, *others), dim)
+            self.terms = self.terms + [self.got]
+        elif dim != self.cut:
+            low = after(self.sum(), *others)
+            self.got = cube.swap(low, dim)
+            self.terms = [low, self.got]
+        else:
+            low = after(self.sum(), *others)
+            self.got = cube.swap(low, dim)
+            self.result = cube.ordered(dim, low, self.got, 1).reshape(self.shape)
+        return self.got
 
 
 def per_device(
@@ -519,49 +660,84 @@
     replicas,
 ):
     cube = Cube(replicas)
-    core = cube.coordinate["core"].astype(jnp.int32).reshape(1)
+    where = jnp.stack([cube.me] + [cube.coordinate[i] for i in range(3)]).astype(jnp.int32)
     x, dy = tokens.T, cotangent.T
-    pad = jnp.zeros((attn_gain.shape[0], GAINS - 2), BF16)
-    first = jnp.concatenate(
-        [attn_gain[:, None], ffn_gain[:, None], pad, query_weight, key_weight, value_weight], axis=1
+
+    q_across = cube.swap(query_weight, "x")
+    pad = jnp.zeros((OWN, GAINS - 2), BF16)
+    kv = jnp.concatenate(
+        [key_weight, value_weight, attn_gain[:, None], ffn_gain[:, None], pad], axis=1
     )
-    wqkv = gather(cube, first, 0, None, 1)
-    wo = gather(cube, output_weight, 0, None, 1)
-    wg = gather(cube, w_gate, 0, 0, 1)
-    wu = gather(cube, w_up, 0, 1, 1)
-    wd = gather(cube, w_down.T, 1, 2, 0)
-    gains = wqkv[:, :GAINS]
-
+    kv_across = cube.swap(kv, "x")
+    q_sibling, kv_sibling = cube.swap(query_weight, "core"), cube.swap(kv, "core")
+    q_diagonal, kv_diagonal = cube.swap(q_across, "core"), cube.swap(kv_across, "core")
+    wq = rows_of(query_weight, q_sibling, q_across, q_diagonal)
+    wk = rows_of(kv, kv_sibling, kv_across, kv_diagonal)
     cos, sin = tables(segments)
-    qkv, h = project(x, wqkv, cos, sin)
-    o, lse = attend(qkv, segments)
-    x1, h2 = middle(x, o, wo, gains)
+    relays = [
+        Relay(cube, w_gate, 0, 0, 1), Relay(cube, w_up, 0, 1, 2), Relay(cube, w_down.T, 1, 2, 0)
+    ]
+    direct = [relay.cross(q_across, kv_across) for relay in relays]
+    qkv, h, gains = project(where, x, wq, wk, cos, sin)
+    wo_across = cube.swap(after(output_weight, qkv), "x")
+    siblings = [cube.swap(after(relay.shard, qkv), "core") for relay in relays]
+    wo_sibling = cube.swap(after(output_weight, qkv), "core")
+    o0, lse0 = attend(qkv, segments, 0)
+    qkv1 = after(qkv, o0, wo_sibling, *direct)
+    handed = [relay.hand_on(o0) for relay in relays]
+    o1, lse1 = attend(qkv1, segments, 1)
+    wo_diagonal = cube.swap(after(wo_across, o1), "core")
+    wo = rows_of(output_weight, wo_sibling, wo_across, wo_diagonal)
+    o = jnp.concatenate([o0, after(o1, *handed)], axis=1)
+    rest = [relay.finish(o1) for relay in relays]
+    x1, h2 = middle(where, x, o, wo, gains)
+    weights = [relay.weight(sibling, h2) for relay, sibling in zip(relays, siblings)]
     y, dh2, gg_keep, gg_send, gu_keep, gu_send, gd_keep, gd_send = feed_forward(
-        core, h2, dy, x1, wg, wu, wd
+        where, h2, dy, x1, weights
     )
-    dx1, da, do, ffn_gain_grad = branch(dh2, x1, dy, gains, wo)
-    dqkv = attend_back(qkv, o, do, lse, segments, cos, sin)
-    ga_keep, ga_send = weight_grads(core, h, dqkv, o, da)
-    grad_x, attn_gain_grad = input_grads(x, dx1, wqkv, dqkv)
-
-    gg = reduce_piece(cube, gg_keep, cube.swap(gg_send, "core"), ("x", 0, 1))
-    gu = reduce_piece(cube, gu_keep, cube.swap(gu_send, "core"), (1, "x", 2))
-    gd = reduce_piece(cube, gd_keep, cube.swap(gd_send, "core"), (2, 0, "x"))
+
+    gd_got, gg_got, gu_got = (cube.swap(g, "core") for g in (gd_send, gg_send, gu_send))
+    dx1, da, do, ffn_gain_grad = branch(where, dh2, x1, dy, gains, wo)
+    more = tuple(range(3, cube.dims))
+    orders = [
+        ("x", 0, 1, 2) + more + (0,), (1, "x", 2, 0) + more + (1,), (2, "x", 0, 1) + more + (2,)
+    ]
+    gd = Reduce(cube, gd_keep, gd_got, orders[0])
+    gg = Reduce(cube, gg_keep, gg_got, orders[1])
+    gu = Reduce(cube, gu_keep, gu_got, orders[2])
+    do = after(do, gd_got, gg_got)
+    first = [gd.step(0, da), gg.step(0, da)]
+    dqkv0 = attend_back(qkv, o0, do, lse0, segments, cos, sin, 0)
+    do1 = after(do, dqkv0, gu_got)
+    first.append(gu.step(0, dqkv0))
+    dqkv1 = attend_back(qkv, o1, do1, lse1, segments, cos, sin, 1)
+    dqkv = jnp.concatenate([dqkv0, dqkv1], axis=1)
+    ga_keep, ga_send = weight_grads(where, h, dqkv, o, da)
     ga_got = cube.swap(ga_send, "core")
-    orders = (("x", 0, 1), (1, "x", 2), (2, 0, "x"))
-    size = OWN // len(orders)
-    ga = jnp.concatenate(
-        [
-            reduce_piece(cube, ga_keep[:, :, i * size:(i + 1) * size],
-                         ga_got[:, :, i * size:(i + 1) * size], order)
-            for i, order in enumerate(orders)
-        ],
-        axis=1,
-    )
+    dqkv = after(dqkv, ga_send, *first[:2])
+    second = [gd.step(1, ga_send), gg.step(1, ga_send)]
+    grad_x, attn_gain_grad = input_grads(where, x, dx1, wq, wk, dqkv)
+    second.append(gu.step(1, grad_x))
+    size = OWN // 3
+    cut = lambda g, i: g[:, :, i * size:(i + 1) * size]
+    parts = [
+        Reduce(cube, cut(ga_keep, i), cut(ga_got, i), order) for i, order in enumerate(orders)
+    ]
+    both = jnp.concatenate([attn_gain_grad, ffn_gain_grad], axis=1).T.reshape(-1)
+    ends = ["core", "x"] + list(range(cube.dims))
+    done = second + [ga_got]
+    for index in range(len(orders[0])):
+        now = [part.step(index, *done) for part in parts]
+        if index + 2 < len(orders[0]):
+            now += [piece.step(index + 2, *done) for piece in (gd, gg, gu)]
+        got = cube.swap(after(both, *done), ends[index])
+        both = both + got
+        done = now + [got]
+    for dim in ends[len(orders[0]):]:
+        both = both + cube.swap(both, dim)
+    both = lax.dynamic_slice_in_dim(both.reshape(2, D), cube.me * OWN, OWN, 1)
     flat = lambda g: jnp.swapaxes(g, 0, 1).reshape(OWN, 4 * CUT).astype(F32)
-    ga = flat(ga)
-    both = lax.psum(jnp.concatenate([attn_gain_grad, ffn_gain_grad], axis=1), ("group", "replica"))
-    both = lax.dynamic_slice_in_dim(both, lax.axis_index("group") * OWN, OWN, 0)
+    ga = flat(jnp.concatenate([part.result for part in parts], axis=1))
     return (
         y.T,
         grad_x.T,
@@ -569,11 +745,11 @@
         ga[:, D:D + KEYS],
         ga[:, D + KEYS:WIDE],
         ga[:, WIDE:],
-        flat(gg),
-        flat(gu),
-        gd.reshape(D, CUT).T.astype(F32),
-        both[:, 0],
-        both[:, 1],
+        flat(gg.result),
+        flat(gu.result),
+        gd.result.reshape(D, CUT).T.astype(F32),
+        both[0],
+        both[1],
     )
 
 

time: 553 us -> 533 us (0.964)
  the two profiles are of different devices: /device:TPU:24 before, /device:TPU:0 now
where the time goes in v2:
time: 533 us; the launch traced here: 523 us
  Pallas kernels  158 us (30%)
  waiting for transfers between devices  157 us (29%)
  starting transfers between devices  112 us (21%)
  local copies, waits for them, and re-layouts  49.2 us (9%)
  other arithmetic  44.4 us (8%)
    ppermute x33, waiting for transfers between devices, swap(): lax.ppermute(value, 'replica', [(i, i ^ mask) for i in range(self.count)])  111 us
    ppermute x33, starting transfers between devices, swap(): lax.ppermute(value, 'replica', [(i, i ^ mask) for i in range(self.count)])  93.3 us
    pallas_call x1, Pallas kernels, feed_forward(): pl.pallas_call(functools.partial(feed_forward_kernel, weights), grid=(ste...  81.9 us
    ppermute x13, waiting for transfers between devices, swap(): return lax.ppermute(value, 'group', [(i, i ^ 2) for i in range(4)])  43.7 us
    unnamed x149, local copies, waits for them, and re-layouts  32.4 us
    convert_element_type x12, other arithmetic, step(): functools.reduce(jnp.add, [t.astype(F32) for t in other]).astype(BF16)  18.2 us
    pallas_call x2, Pallas kernels, attend_back(): pl.pallas_call(attend_back_kernel, grid=(1,), in_specs=[here(wide), pl.Bl...  17.1 us
    convert_element_type x18, other arithmetic, sum(): functools.reduce(jnp.add, [t.astype(F32) for t in self.terms]).astype(BF16)  16.3 us
  transfers between devices with their start and end apart: 66, of which 25 were waited for; matrix products, arithmetic and copies ran while one was open for 11% of the time, Pallas kernels for 13%

profile of v2, /device:TPU:0, one launch (start us, length us, event | category | flops | bytes accessed | tf_op | source)
XLA Modules:
  0.0 523.1 jit_solution(1626823346351869319)
XLA Ops:
  4.8 3.0 collective-permute-start.4
  8.7 8.6 %collective-permute-done.4.refs_6_ = bf16[240,768]{1,0:T(8,128)(2,1)} collective-permute-done((bf16[240,768]{1,0:T(8,128)(2,1)S(1)}, bf16[240,768]{1,0:T(8,128)(2,1)}, u32[]{:S(2)}, u32[]{:S(2)}) %collective-permute-start.4) | collective-permute-done | bytes 368672 | tf_op jit(solution)/shard_map/ppermute | solution.py:561
  17.3 9.6 %collective-permute-done.1.refs_2_ = bf16[240,960]{1,0:T(8,128)(2,1)S(1)} collective-permute-done((bf16[240,960]{1,0:T(8,128)(2,1)S(1)}, bf16[240,960]{1,0:T(8,128)(2,1)S(1)}, u32[]{:S(2)}, u32[]{:S(2)}) %collective-permute-start.1) | collective-permute-done | bytes 460832 | tf_op jit(solution)/shard_map/ppermute | solution.py:561
  27.0 1.8 constant_dynamic-slice_fusion.1
  29.4 9.1 %project.1 = (bf16[1600,1024]{1,0:T(8,128)(2,1)S(1)}, bf16[960,1024]{1,0:T(8,128)(2,1)S(1)}, bf16[960,128]{1,0:T(8,128)(2,1)S(1)}) custom-call(s32[4]{0:T(128)S(1)} %pad_add_fusion.where_ref, bf16[960,1024]{1,0:T(8,128)(2,1)S(1)} %bitcast.54, f32[32,1024]{1,0:T(8,128)S(1)} %get-tuple-element.232.cos_ref, f32[32,1024]{1,0:T(8,128)S(1)} %get-tuple-element.231.sin_ref, ...), custom_call_target="tpu_custom_call" | custom-call | flops 3145728000 | bytes 10280960 | tf_op jit(solution)/shard_map/project/pallas_call | solution.py:145
  39.3 1.8 copy-done.33
  42.9 1.7 dynamic-slice_bitcast_fusion
  44.6 1.7 collective-permute-start.8
  46.6 1.7 constant_dynamic-slice_fusion.2
  48.3 1.7 collective-permute-start.7
  50.6 1.9 copy-done.34
  52.6 6.7 %attend.2 = (bf16[960,512]{1,0:T(8,128)(2,1)S(1)}, f32[5,8,512]{2,1,0:T(8,128)S(1)}) custom-call(bf16[1600,1024]{1,0:T(8,128)(2,1)S(1)} %copy-done.34, s32[2,1,512]{2,1,0:T(1,128)S(1)} %broadcast_in_dim.43.segr_ref, s32[2,512,1]{2,1,0:T(8,128)S(1)} %copy.69.segc_ref), custom_call_target="tpu_custom_call" | custom-call | flops 2013265920 | bytes 2621440 | tf_op jit(solution)/shard_map/attend/pallas_call | solution.py:215
  61.6 3.8 collective-permute-start.12
  65.4 2.7 collective-permute-done.7
  68.2 1.8 collective-permute-start.10
  69.9 1.9 copy-done.35
  71.9 6.7 %attend.3 = (bf16[960,512]{1,0:T(8,128)(2,1)S(1)}, f32[5,8,512]{2,1,0:T(8,128)S(1)}) custom-call(bf16[1600,1024]{1,0:T(8,128)(2,1)S(1)} %copy-done.35, s32[2,1,512]{2,1,0:T(1,128)S(1)} %broadcast_in_dim.43.segr_ref, s32[2,512,1]{2,1,0:T(8,128)S(1)} %copy.69.segc_ref), custom_call_target="tpu_custom_call" | custom-call | flops 2013265920 | bytes 2621440 | tf_op jit(solution)/shard_map/attend/pallas_call | solution.py:215
  78.7 1.8 maximum_select_fusion.5.refs_14_
  82.7 3.8 collective-permute-start.20
  87.9 6.6 %collective-permute-done.24.refs_15_ = bf16[480,640]{1,0:T(8,128)(2,1)S(1)} collective-permute-done((bf16[480,640]{1,0:T(8,128)(2,1)S(1)}, bf16[480,640]{1,0:T(8,128)(2,1)S(1)}, u32[]{:S(2)}, u32[]{:S(2)}) %collective-permute-start.24) | collective-permute-done | bytes 614432 | tf_op jit(solution)/shard_map/ppermute | solution.py:565
  95.0 6.3 %collective-permute-done.20.refs_9_ = bf16[240,1280]{1,0:T(8,128)(2,1)S(1)} collective-permute-done((bf16[240,1280]{1,0:T(8,128)(2,1)S(1)}, bf16[240,1280]{1,0:T(8,128)(2,1)S(1)}, u32[]{:S(2)}, u32[]{:S(2)}) %collective-permute-start.20) | collective-permute-done | bytes 614432 | tf_op jit(solution)/shard_map/ppermute | solution.py:565
  101.3 12.4 %collective-permute-done.16.refs_3_ = bf16[240,1280]{1,0:T(8,128)(2,1)S(1)} collective-permute-done((bf16[240,1280]{1,0:T(8,128)(2,1)S(1)}, bf16[240,1280]{1,0:T(8,128)(2,1)S(1)}, u32[]{:S(2)}, u32[]{:S(2)}) %collective-permute-start.16) | collective-permute-done | bytes 614432 | tf_op jit(solution)/shard_map/ppermute | solution.py:565
  114.9 7.1 %middle.1 = (f32[960,1024]{1,0:T(8,128)S(1)}, bf16[960,1024]{1,0:T(8,128)(2,1)S(1)}) custom-call(s32[4]{0:T(128)S(1)} %pad_add_fusion.where_ref, bf16[960,1024]{1,0:T(8,128)(2,1)S(1)} %bitcast.55, bf16[960,1024]{1,0:T(8,128)(2,1)S(1)} %constant_dynamic-update-slice_fusion.o_ref, bf16[960,128]{1,0:T(8,128)(2,1)S(1)} %copy-done.24, bf16[240,960]{1,0:T(8,128)(2,1)} %refs_0_.8, ...), custom_call_target="tpu_custom_call" | custom-call | flops 1887436800 | bytes 9830400 | tf_op jit(solution)/shard_map/middle/pallas_call | solution.py:251
  122.1 1.9 copy-done.2
  130.0 81.9 %feed_forward.1 = (bf16[960,1024]{1,0:T(8,128)(2,1)}, f32[960,1024]{1,0:T(8,128)}, bf16[2,4,240,640]{3,2,1,0:T(8,128)(2,1)}, bf16[2,4,240,640]{3,2,1,0:T(8,128)(...) custom-call(s32[4]{0:T(128)} %copy-done.30, ...), custom_call_target="tpu_custom_call" | custom-call | flops 45298483200 | bytes 45219840 | tf_op jit(solution)/shard_map/feed_forward/pallas_call | solution.py:325
  215.3 9.8 %branch.1 = (f32[960,1024]{1,0:T(8,128)S(1)}, bf16[960,1024]{1,0:T(8,128)(2,1)S(1)}, bf16[960,1024]{1,0:T(8,128)(2,1)S(1)}, f32[960,1]{1,0:T(8,128)S(1)}) custom-call(s32[4]{0:T(128)S(1)} %copy-done.31, f32[960,1024]{1,0:T(8,128)} %get-tuple-element.119.dh_ref, f32[960,1024]{1,0:T(8,128)} %copy-done.2, bf16[960,1024]{1,0:T(8,128)(2,1)S(1)} %bitcast.58, ...), custom_call_target="tpu_custom_call" | custom-call | flops 1887436800 | bytes 17694720 | tf_op jit(solution)/shard_map/branch/pallas_call | solution.py:371
  225.1 1.9 copy-done
  227.1 2.9 add_convert_fusion.1
  229.9 2.0 collective-permute-start.31
  232.0 2.8 add_convert_fusion.2
  234.8 2.4 collective-permute-start.30
  237.2 8.6 %attend_back.2 = bf16[1600,512]{1,0:T(8,128)(2,1)S(1)} custom-call(bf16[1600,1024]{1,0:T(8,128)(2,1)S(1)} %copy-done.36, bf16[960,512]{1,0:T(8,128)(2,1)S(1)} %get-tuple-element.94.o_ref, bf16[960,1024]{1,0:T(8,128)(2,1)S(1)} %get-tuple-element.127.do_ref, f32[5,8,512]{2,1,0:T(8,128)S(1)} %copy-done.40, s32[2,1,512]{2,1,0:T(1,128)S(1)} %broadcast_in_dim.43.segr_ref, ...), custom_call_target="tpu_custom_call" | custom-call | flops 5033164800 | bytes 5242880 | tf_op jit(solution)/shard_map/attend_back/pallas_call | solution.py:427
  245.8 8.5 %attend_back.3 = bf16[1600,512]{1,0:T(8,128)(2,1)S(1)} custom-call(bf16[1600,1024]{1,0:T(8,128)(2,1)S(1)} %copy-done.36, bf16[960,512]{1,0:T(8,128)(2,1)S(1)} %copy-done.11, bf16[960,1024]{1,0:T(8,128)(2,1)S(1)} %get-tuple-element.127.do_ref, f32[5,8,512]{2,1,0:T(8,128)S(1)} %copy-done.42, s32[2,1,512]{2,1,0:T(1,128)S(1)} %broadcast_in_dim.43.segr_ref, ...), custom_call_target="tpu_custom_call" | custom-call | flops 5033164800 | bytes 5242880 | tf_op jit(solution)/shard_map/attend_back/pallas_call | solution.py:427
  256.0 2.8 add_convert_fusion
  260.3 9.2 %weight_grads.1 = (bf16[2,4,240,640]{3,2,1,0:T(8,128)(2,1)S(1)}, bf16[2,4,240,640]{3,2,1,0:T(8,128)(2,1)}) custom-call(s32[4]{0:T(128)S(1)} %copy-done.31, bf16[960,1024]{1,0:T(8,128)(2,1)S(1)} %copy-done.38, bf16[1600,1024]{1,0:T(8,128)(2,1)S(1)} %pad_maximum_fusion.dqkv_ref, bf16[960,1024]{1,0:T(8,128)(2,1)S(1)} %copy-done.13, ...), custom_call_target="tpu_custom_call" | custom-call | flops 5033164800 | bytes 14090240 | tf_op jit(solution)/shard_map/weight_grads/pallas_call | solution.py:476
  272.2 17.3 %collective-permute-done.35 = bf16[2,1,2,240,640]{4,3,2,1,0:T(8,128)(2,1)} collective-permute-done((bf16[2,1,2,240,640]{4,3,2,1,0:T(8,128)(2,1)}, bf16[2,1,2,240,640]{4,3,2,1,0:T(8,128)(2,1)}, u32[]{:S(2)}, u32[]{:S(2)}) %collective-permute-start.35) | collective-permute-done | bytes 1228832 | tf_op jit(solution)/shard_map/ppermute | solution.py:565
  289.5 2.5 add_convert_fusion.12
  292.0 2.1 copy-done.1
  296.1 10.7 %input_grads.1 = (bf16[960,1024]{1,0:T(8,128)(2,1)}, f32[960,1]{1,0:T(8,128)S(1)}) custom-call(s32[4]{0:T(128)S(1)} %copy-done.31, bf16[960,1024]{1,0:T(8,128)(2,1)S(1)} %bitcast.56, f32[960,1024]{1,0:T(8,128)S(1)} %copy-done.1, bf16[1600,1024]{1,0:T(8,128)(2,1)S(1)} %pad_maximum_fusion.dqkv_ref, bf16[240,960]{1,0:T(8,128)(2,1)S(1)} %copy-done.15, ...), custom_call_target="tpu_custom_call" | custom-call | flops 3145728000 | bytes 14213120 | tf_op jit(solution)/shard_map/input_grads/pallas_call | solution.py:517
  307.3 2.0 add_convert_fusion.13
  315.4 8.6 %collective-permute-done.36 = bf16[1,1,2,240,640]{4,3,2,1,0:T(8,128)(2,1)} collective-permute-done((bf16[1,1,2,240,640]{4,3,2,1,0:T(8,128)(2,1)}, bf16[1,1,2,240,640]{4,3,2,1,0:T(8,128)(2,1)}, u32[]{:S(2)}, u32[]{:S(2)}) %collective-permute-start.36) | collective-permute-done | bytes 614432 | tf_op jit(solution)/shard_map/ppermute | solution.py:561
  324.1 2.8 add_convert_fusion.9
  326.8 8.0 %collective-permute-done.34 = bf16[1,1,2,240,640]{4,3,2,1,0:T(8,128)(2,1)} collective-permute-done((bf16[1,1,2,240,640]{4,3,2,1,0:T(8,128)(2,1)S(1)}, bf16[1,1,2,240,640]{4,3,2,1,0:T(8,128)(2,1)}, u32[]{:S(2)}, u32[]{:S(2)}) %collective-permute-start.34) | collective-permute-done | bytes 614432 | tf_op jit(solution)/shard_map/ppermute | solution.py:561
  334.8 2.8 add_convert_fusion.10
  337.6 1.9 fusion.3
  339.7 25.6 %collective-permute-start.38 = (bf16[2,1,2,80,640]{4,3,2,1,0:T(8,128)(2,1)S(1)}, bf16[2,1,2,80,640]{4,3,2,1,0:T(8,128)(2,1)S(1)}, u32[]{:S(2)}, u32[]{:S(2)}) collective-permute-start(bf16[2,1,2,80,640]{4,3,2,1,0:T(8,128)(2,1)S(1)} %add_convert_fusion.16), channel_id=1, source_target_pairs={{0,2},{1,3},{2,0},{3,1},{4,6},{5,7},{6,4},{7,5},{8,10},{9,11},{10,... | collective-permute-start | bytes 1228808 | tf_op jit(solution)/shard_map/ppermute | solution.py:565
  365.3 2.6 add_convert_fusion.11
  369.3 3.0 collective-permute-start.41
  373.7 4.4 collective-permute-start.39
  379.4 4.5 collective-permute-done.37
  385.0 26.4 %collective-permute-done.39 = bf16[2,1,2,80,640]{4,3,2,1,0:T(8,128)(2,1)} collective-permute-done((bf16[2,1,2,80,640]{4,3,2,1,0:T(8,128)(2,1)S(1)}, bf16[2,1,2,80,640]{4,3,2,1,0:T(8,128)(2,1)}, u32[]{:S(2)}, u32[]{:S(2)}) %collective-permute-start.39) | collective-permute-done | bytes 409632 | tf_op jit(solution)/shard_map/ppermute | solution.py:565
  414.2 5.8 %collective-permute-start.49 = (bf16[1,1,2,240,640]{4,3,2,1,0:T(8,128)(2,1)S(1)}, bf16[1,1,2,240,640]{4,3,2,1,0:T(8,128)(2,1)S(1)}, u32[]{:S(2)}, u32[]{:S(2)}) collective-permute-start(bf16[1,1,2,240,640]{4,3,2,1,0:T(8,128)(2,1)S(1)} %add_convert_fusion.6), channel_id=1, source_target_pairs={{0,2},{1,3},{2,0},{3,1},{4,6},{5,7},{6,4},{7,5},{8,10},{9,11},{10,... | collective-permute-start | bytes 1843208 | tf_op jit(solution)/shard_map/ppermute | solution.py:565
  422.0 1.7 collective-permute-start.45
  425.2 2.7 collective-permute-start.47
  430.8 10.0 %collective-permute-done.44 = bf16[1,1,2,80,640]{4,3,2,1,0:T(8,128)(2,1)S(1)} collective-permute-done((bf16[1,1,2,80,640]{4,3,2,1,0:T(8,128)(2,1)S(1)}, bf16[1,1,2,80,640]{4,3,2,1,0:T(8,128)(2,1)S(1)}, u32[]{:S(2)}, u32[]{:S(2)}) %collective-permute-start.44) | collective-permute-done | bytes 204832 | tf_op jit(solution)/shard_map/ppermute | solution.py:565
  442.9 5.8 %collective-permute-done.47 = bf16[1,1,2,240,640]{4,3,2,1,0:T(8,128)(2,1)S(1)} collective-permute-done((bf16[1,1,2,240,640]{4,3,2,1,0:T(8,128)(2,1)S(1)}, bf16[1,1,2,240,640]{4,3,2,1,0:T(8,128)(2,1)S(1)}, u32[]{:S(2)}, u32[]{:S(2)}) %collective-permute-start.47) | collective-permute-done | bytes 614432 | tf_op jit(solution)/shard_map/ppermute | solution.py:565
  451.2 18.8 %collective-permute-start.55 = (bf16[1,1,2,240,640]{4,3,2,1,0:T(8,128)(2,1)S(1)}, bf16[1,1,2,240,640]{4,3,2,1,0:T(8,128)(2,1)S(1)}, u32[]{:S(2)}, u32[]{:S(2)}) collective-permute-start(bf16[1,1,2,240,640]{4,3,2,1,0:T(8,128)(2,1)S(1)} %add_convert_fusion.4), channel_id=1, source_target_pairs={{0,2},{1,3},{2,0},{3,1},{4,6},{5,7},{6,4},{7,5},{8,10},{9,11},{10,... | collective-permute-start | bytes 1843208 | tf_op jit(solution)/shard_map/ppermute | solution.py:565
  471.6 13.3 %collective-permute-done.52 = bf16[1,1,2,80,640]{4,3,2,1,0:T(8,128)(2,1)S(1)} collective-permute-done((bf16[1,1,2,80,640]{4,3,2,1,0:T(8,128)(2,1)S(1)}, bf16[1,1,2,80,640]{4,3,2,1,0:T(8,128)(2,1)S(1)}, u32[]{:S(2)}, u32[]{:S(2)}) %collective-permute-start.52) | collective-permute-done | bytes 204832 | tf_op jit(solution)/shard_map/ppermute | solution.py:565
  487.1 5.4 %collective-permute-done.53 = bf16[1,1,2,80,640]{4,3,2,1,0:T(8,128)(2,1)S(1)} collective-permute-done((bf16[1,1,2,80,640]{4,3,2,1,0:T(8,128)(2,1)S(1)}, bf16[1,1,2,80,640]{4,3,2,1,0:T(8,128)(2,1)S(1)}, u32[]{:S(2)}, u32[]{:S(2)}) %collective-permute-start.53) | collective-permute-done | bytes 204832 | tf_op jit(solution)/shard_map/ppermute | solution.py:565
  495.7 2.2 collective-permute-start.58
  498.2 1.7 convert_bitcast_fusion
  506.1 1.9 collective-permute-done.60
  510.0 2.3 collective-permute-start.64
  515.9 2.3 collective-permute-done.64
  (306 shorter events, 82.7 us)
Async XLA Ops:
  4.8 12.5 %collective-permute-start.4 = (bf16[240,768]{1,0:T(8,128)(2,1)S(1)}, bf16[240,768]{1,0:T(8,128)(2,1)}, u32[]{:S(2)}, u32[]{:S(2)}) collective-permute-start(bf16[240,768]{1,0:T(8,128)(2,1)S(1)} %concatenate.93.refs_4_), channel_id=1, source_target_pairs={{0,16},{8,24},{16,0},{24,8},{1,17},{9,25},{17,1},{25,9},{2,18},{10... | collective-permute-start | bytes 1105928 | tf_op jit(solution)/shard_map/ppermute | solution.py:561
  7.8 21.6 %collective-permute-start.3 = (bf16[240,768]{1,0:T(8,128)(2,1)S(1)}, bf16[240,768]{1,0:T(8,128)(2,1)}, u32[]{:S(2)}, u32[]{:S(2)}) collective-permute-start(bf16[240,768]{1,0:T(8,128)(2,1)S(1)} %concatenate.93.refs_4_), channel_id=1, source_target_pairs={{0,8},{8,0},{16,24},{24,16},{1,9},{9,1},{17,25},{25,17},{2,10},{10... | collective-permute-start | bytes 1105928 | tf_op jit(solution)/shard_map/ppermute | solution.py:563
  7.8 19.1 %collective-permute-start.1 = (bf16[240,960]{1,0:T(8,128)(2,1)S(1)}, bf16[240,960]{1,0:T(8,128)(2,1)S(1)}, u32[]{:S(2)}, u32[]{:S(2)}) collective-permute-start(bf16[240,960]{1,0:T(8,128)(2,1)S(1)} %copy-done.14), channel_id=1, source_target_pairs={{0,16},{8,24},{16,0},{24,8},{1,17},{9,25},{17,1},{25,9},{2,18},{10... | collective-permute-start | bytes 1382408 | tf_op jit(solution)/shard_map/ppermute | solution.py:561
  8.0 21.4 %collective-permute-start = (bf16[240,960]{1,0:T(8,128)(2,1)S(1)}, bf16[240,960]{1,0:T(8,128)(2,1)}, u32[]{:S(2)}, u32[]{:S(2)}) collective-permute-start(bf16[240,960]{1,0:T(8,128)(2,1)S(1)} %copy-done.14), channel_id=1, source_target_pairs={{0,8},{8,0},{16,24},{24,16},{1,9},{9,1},{17,25},{25,17},{2,10},{10... | collective-permute-start | bytes 1382408 | tf_op jit(solution)/shard_map/ppermute | solution.py:563
  17.3 12.1 %collective-permute-start.5 = (bf16[240,768]{1,0:T(8,128)(2,1)}, bf16[240,768]{1,0:T(8,128)(2,1)}, u32[]{:S(2)}, u32[]{:S(2)}) collective-permute-start(bf16[240,768]{1,0:T(8,128)(2,1)} %collective-permute-done.4.refs_6_), channel_id=1, source_target_pairs={{0,8},{8,0},{16,24},{24,16},{1,9},{9,1},{17,25},{25,17},{2,10},{10... | collective-permute-start | bytes 1105928 | tf_op jit(solution)/shard_map/ppermute | solution.py:563
  42.4 27.5 %collective-permute-start.6 = (bf16[240,960]{1,0:T(8,128)(2,1)}, bf16[240,960]{1,0:T(8,128)(2,1)}, u32[]{:S(2)}, u32[]{:S(2)}) collective-permute-start(bf16[240,960]{1,0:T(8,128)(2,1)} %refs_0_.8), channel_id=1, source_target_pairs={{0,8},{8,0},{16,24},{24,16},{1,9},{9,1},{17,25},{25,17},{2,10},{10... | collective-permute-start | bytes 1382408 | tf_op jit(solution)/shard_map/ppermute | solution.py:563
  44.6 20.9 %collective-permute-start.8 = (bf16[240,640]{1,0:T(8,128)(2,1)}, bf16[240,640]{1,0:T(8,128)(2,1)}, u32[]{:S(2)}, u32[]{:S(2)}) collective-permute-start(bf16[240,640]{1,0:T(8,128)(2,1)} %constant_dynamic-slice_fusion.1), channel_id=1, source_target_pairs={{0,16},{8,24},{16,0},{24,8},{1,17},{9,25},{17,1},{25,9},{2,18},{10... | collective-permute-start | bytes 921608 | tf_op jit(solution)/shard_map/ppermute | solution.py:561
  46.3 15.3 %collective-permute-start.9 = (bf16[240,640]{1,0:T(8,128)(2,1)}, bf16[240,640]{1,0:T(8,128)(2,1)}, u32[]{:S(2)}, u32[]{:S(2)}) collective-permute-start(bf16[240,640]{1,0:T(8,128)(2,1)} %dynamic-slice_bitcast_fusion), channel_id=1, source_target_pairs={{0,16},{8,24},{16,0},{24,8},{1,17},{9,25},{17,1},{25,9},{2,18},{10... | collective-permute-start | bytes 921608 | tf_op jit(solution)/shard_map/ppermute | solution.py:561
  48.3 19.9 %collective-permute-start.7 = (bf16[240,640]{1,0:T(8,128)(2,1)}, bf16[240,640]{1,0:T(8,128)(2,1)}, u32[]{:S(2)}, u32[]{:S(2)}) collective-permute-start(bf16[240,640]{1,0:T(8,128)(2,1)} %constant_dynamic-slice_fusion.2), channel_id=1, source_target_pairs={{0,16},{8,24},{16,0},{24,8},{1,17},{9,25},{17,1},{25,9},{2,18},{10... | collective-permute-start | bytes 921608 | tf_op jit(solution)/shard_map/ppermute | solution.py:561
  50.3 30.5 %collective-permute-start.13 = (bf16[240,960]{1,0:T(8,128)(2,1)}, bf16[240,960]{1,0:T(8,128)(2,1)}, u32[]{:S(2)}, u32[]{:S(2)}) collective-permute-start(bf16[240,960]{1,0:T(8,128)(2,1)} %refs_0_.8), channel_id=1, source_target_pairs={{0,16},{8,24},{16,0},{24,8},{1,17},{9,25},{17,1},{25,9},{2,18},{10... | collective-permute-start | bytes 1382408 | tf_op jit(solution)/shard_map/ppermute | solution.py:561
  61.6 17.0 %collective-permute-start.12 = (bf16[240,640]{1,0:T(8,128)(2,1)}, bf16[240,640]{1,0:T(8,128)(2,1)}, u32[]{:S(2)}, u32[]{:S(2)}) collective-permute-start(bf16[240,640]{1,0:T(8,128)(2,1)} %collective-permute-done.9), channel_id=1, source_target_pairs={{0,6},{1,7},{2,4},{3,5},{4,2},{5,3},{6,0},{7,1},{8,14},{9,15},{10,... | collective-permute-start | bytes 921608 | tf_op jit(solution)/shard_map/ppermute | solution.py:565
  65.4 15.9 %collective-permute-start.11 = (bf16[240,640]{1,0:T(8,128)(2,1)}, bf16[240,640]{1,0:T(8,128)(2,1)S(1)}, u32[]{:S(2)}, u32[]{:S(2)}) collective-permute-start(bf16[240,640]{1,0:T(8,128)(2,1)} %collective-permute-done.8), channel_id=1, source_target_pairs={{0,2},{1,3},{2,0},{3,1},{4,6},{5,7},{6,4},{7,5},{8,10},{9,11},{10,... | collective-permute-start | bytes 921608 | tf_op jit(solution)/shard_map/ppermute | solution.py:565
  68.2 18.3 %collective-permute-start.10 = (bf16[240,640]{1,0:T(8,128)(2,1)}, bf16[240,640]{1,0:T(8,128)(2,1)S(1)}, u32[]{:S(2)}, u32[]{:S(2)}) collective-permute-start(bf16[240,640]{1,0:T(8,128)(2,1)} %collective-permute-done.7), channel_id=1, source_target_pairs={{0,1},{1,0},{2,3},{3,2},{4,5},{5,4},{6,7},{7,6},{8,9},{9,8},{10,11... | collective-permute-start | bytes 921608 | tf_op jit(solution)/shard_map/ppermute | solution.py:565
  80.5 14.0 %collective-permute-start.24 = (bf16[480,640]{1,0:T(8,128)(2,1)S(1)}, bf16[480,640]{1,0:T(8,128)(2,1)S(1)}, u32[]{:S(2)}, u32[]{:S(2)}) collective-permute-start(bf16[480,640]{1,0:T(8,128)(2,1)S(1)} %maximum_select_fusion.5.refs_14_), channel_id=1, source_target_pairs={{0,1},{1,0},{2,3},{3,2},{4,5},{5,4},{6,7},{7,6},{8,9},{9,8},{10,11... | collective-permute-start | bytes 1843208 | tf_op jit(solution)/shard_map/ppermute | solution.py:565
  80.8 13.7 %collective-permute-start.25 = (bf16[480,640]{1,0:T(8,128)(2,1)S(1)}, bf16[480,640]{1,0:T(8,128)(2,1)S(1)}, u32[]{:S(2)}, u32[]{:S(2)}) collective-permute-start(bf16[480,640]{1,0:T(8,128)(2,1)S(1)} %maximum_select_fusion.5.refs_14_), channel_id=1, source_target_pairs={{0,8},{8,0},{16,24},{24,16},{1,9},{9,1},{17,25},{25,17},{2,10},{10... | collective-permute-start | bytes 1843208 | tf_op jit(solution)/shard_map/ppermute | solution.py:563
  80.8 7.0 %collective-permute-start.14 = (bf16[240,960]{1,0:T(8,128)(2,1)}, bf16[240,960]{1,0:T(8,128)(2,1)S(1)}, u32[]{:S(2)}, u32[]{:S(2)}) collective-permute-start(bf16[240,960]{1,0:T(8,128)(2,1)} %collective-permute-done.13.refs_2_), channel_id=1, source_target_pairs={{0,8},{8,0},{16,24},{24,16},{1,9},{9,1},{17,25},{25,17},{2,10},{10... | collective-permute-start | bytes 1382408 | tf_op jit(solution)/shard_map/ppermute | solution.py:563
  82.7 18.6 %collective-permute-start.20 = (bf16[240,1280]{1,0:T(8,128)(2,1)S(1)}, bf16[240,1280]{1,0:T(8,128)(2,1)S(1)}, u32[]{:S(2)}, u32[]{:S(2)}) collective-permute-start(bf16[240,1280]{1,0:T(8,128)(2,1)S(1)} %maximum_select_fusion.4.refs_8_), channel_id=1, source_target_pairs={{0,6},{1,7},{2,4},{3,5},{4,2},{5,3},{6,0},{7,1},{8,14},{9,15},{10,... | collective-permute-start | bytes 1843208 | tf_op jit(solution)/shard_map/ppermute | solution.py:565
  87.7 26.1 %collective-permute-start.16 = (bf16[240,1280]{1,0:T(8,128)(2,1)S(1)}, bf16[240,1280]{1,0:T(8,128)(2,1)S(1)}, u32[]{:S(2)}, u32[]{:S(2)}) collective-permute-start(bf16[240,1280]{1,0:T(8,128)(2,1)S(1)} %maximum_select_fusion.3.refs_2_), channel_id=1, source_target_pairs={{0,2},{1,3},{2,0},{3,1},{4,6},{5,7},{6,4},{7,5},{8,10},{9,11},{10,... | collective-permute-start | bytes 1843208 | tf_op jit(solution)/shard_map/ppermute | solution.py:565
  87.8 38.1 %collective-permute-start.23 = (bf16[960,640]{1,0:T(8,128)(2,1)S(1)}, bf16[960,640]{1,0:T(8,128)(2,1)S(1)}, u32[]{:S(2)}, u32[]{:S(2)}) collective-permute-start(bf16[960,640]{1,0:T(8,128)(2,1)S(1)} %bitcast.97), channel_id=1, source_target_pairs={{0,8},{8,0},{16,24},{24,16},{1,9},{9,1},{17,25},{25,17},{2,10},{10... | collective-permute-start | bytes 3686408 | tf_op jit(solution)/shard_map/ppermute | solution.py:563
  94.5 31.9 %collective-permute-start.15 = (bf16[240,2560]{1,0:T(8,128)(2,1)S(1)}, bf16[240,2560]{1,0:T(8,128)(2,1)S(1)}, u32[]{:S(2)}, u32[]{:S(2)}) collective-permute-start(bf16[240,2560]{1,0:T(8,128)(2,1)S(1)} %copy-done.55), channel_id=1, source_target_pairs={{0,8},{8,0},{16,24},{24,16},{1,9},{9,1},{17,25},{25,17},{2,10},{10... | collective-permute-start | bytes 3686408 | tf_op jit(solution)/shard_map/ppermute | solution.py:563
  94.5 30.8 %collective-permute-start.21 = (bf16[240,1280]{1,0:T(8,128)(2,1)S(1)}, bf16[240,1280]{1,0:T(8,128)(2,1)S(1)}, u32[]{:S(2)}, u32[]{:S(2)}) collective-permute-start(bf16[240,1280]{1,0:T(8,128)(2,1)S(1)} %maximum_select_fusion.4.refs_8_), channel_id=1, source_target_pairs={{0,8},{8,0},{16,24},{24,16},{1,9},{9,1},{17,25},{25,17},{2,10},{10... | collective-permute-start | bytes 1843208 | tf_op jit(solution)/shard_map/ppermute | solution.py:563
  101.3 24.5 %collective-permute-start.17 = (bf16[240,1280]{1,0:T(8,128)(2,1)S(1)}, bf16[240,1280]{1,0:T(8,128)(2,1)}, u32[]{:S(2)}, u32[]{:S(2)}) collective-permute-start(bf16[240,1280]{1,0:T(8,128)(2,1)S(1)} %maximum_select_fusion.3.refs_2_), channel_id=1, source_target_pairs={{0,8},{8,0},{16,24},{24,16},{1,9},{9,1},{17,25},{25,17},{2,10},{10... | collective-permute-start | bytes 1843208 | tf_op jit(solution)/shard_map/ppermute | solution.py:563
  113.8 12.6 %collective-permute-start.19 = (bf16[240,2560]{1,0:T(8,128)(2,1)S(1)}, bf16[240,2560]{1,0:T(8,128)(2,1)S(1)}, u32[]{:S(2)}, u32[]{:S(2)}) collective-permute-start(bf16[240,2560]{1,0:T(8,128)(2,1)S(1)} %copy-done.56), channel_id=1, source_target_pairs={{0,8},{8,0},{16,24},{24,16},{1,9},{9,1},{17,25},{25,17},{2,10},{10... | collective-permute-start | bytes 3686408 | tf_op jit(solution)/shard_map/ppermute | solution.py:563
  125.8 2.5 collective-permute-start.22
  125.9 3.3 collective-permute-start.18
  211.9 15.1 %collective-permute-start.28 = (bf16[2,4,240,640]{3,2,1,0:T(8,128)(2,1)}, bf16[2,4,240,640]{3,2,1,0:T(8,128)(2,1)}, u32[]{:S(2)}, u32[]{:S(2)}) collective-permute-start(bf16[2,4,240,640]{3,2,1,0:T(8,128)(2,1)} %get-tuple-element.123), channel_id=1, source_target_pairs={{0,8},{8,0},{16,24},{24,16},{1,9},{9,1},{17,25},{25,17},{2,10},{10... | collective-permute-start | bytes 7372808 | tf_op jit(solution)/shard_map/ppermute | solution.py:563
  212.8 19.2 %collective-permute-start.27 = (bf16[2,4,240,640]{3,2,1,0:T(8,128)(2,1)}, bf16[2,4,240,640]{3,2,1,0:T(8,128)(2,1)}, u32[]{:S(2)}, u32[]{:S(2)}) collective-permute-start(bf16[2,4,240,640]{3,2,1,0:T(8,128)(2,1)} %get-tuple-element.122), channel_id=1, source_target_pairs={{0,8},{8,0},{16,24},{24,16},{1,9},{9,1},{17,25},{25,17},{2,10},{10... | collective-permute-start | bytes 7372808 | tf_op jit(solution)/shard_map/ppermute | solution.py:563
  212.9 32.9 %collective-permute-start.29 = (bf16[2,4,240,640]{3,2,1,0:T(8,128)(2,1)}, bf16[2,4,240,640]{3,2,1,0:T(8,128)(2,1)}, u32[]{:S(2)}, u32[]{:S(2)}) collective-permute-start(bf16[2,4,240,640]{3,2,1,0:T(8,128)(2,1)} %get-tuple-element.126), channel_id=1, source_target_pairs={{0,8},{8,0},{16,24},{24,16},{1,9},{9,1},{17,25},{25,17},{2,10},{10... | collective-permute-start | bytes 7372808 | tf_op jit(solution)/shard_map/ppermute | solution.py:563
  229.9 42.2 %collective-permute-start.31 = (bf16[2,1,2,240,640]{4,3,2,1,0:T(8,128)(2,1)}, bf16[2,1,2,240,640]{4,3,2,1,0:T(8,128)(2,1)}, u32[]{:S(2)}, u32[]{:S(2)}) collective-permute-start(bf16[2,1,2,240,640]{4,3,2,1,0:T(8,128)(2,1)} %add_convert_fusion.1), channel_id=1, source_target_pairs={{0,2},{1,3},{2,0},{3,1},{4,6},{5,7},{6,4},{7,5},{8,10},{9,11},{10,... | collective-permute-start | bytes 3686408 | tf_op jit(solution)/shard_map/ppermute | solution.py:565
  234.8 37.4 %collective-permute-start.30 = (bf16[1,2,2,240,640]{4,3,2,1,0:T(8,128)(2,1)}, bf16[1,2,2,240,640]{4,3,2,1,0:T(8,128)(2,1)}, u32[]{:S(2)}, u32[]{:S(2)}) collective-permute-start(bf16[1,2,2,240,640]{4,3,2,1,0:T(8,128)(2,1)} %add_convert_fusion.2), channel_id=1, source_target_pairs={{0,16},{8,24},{16,0},{24,8},{1,17},{9,25},{17,1},{25,9},{2,18},{10... | collective-permute-start | bytes 3686408 | tf_op jit(solution)/shard_map/ppermute | solution.py:561
  258.8 30.7 %collective-permute-start.35 = (bf16[2,1,2,240,640]{4,3,2,1,0:T(8,128)(2,1)}, bf16[2,1,2,240,640]{4,3,2,1,0:T(8,128)(2,1)}, u32[]{:S(2)}, u32[]{:S(2)}) collective-permute-start(bf16[2,1,2,240,640]{4,3,2,1,0:T(8,128)(2,1)} %add_convert_fusion), channel_id=1, source_target_pairs={{0,6},{1,7},{2,4},{3,5},{4,2},{5,3},{6,0},{7,1},{8,14},{9,15},{10,... | collective-permute-start | bytes 3686408 | tf_op jit(solution)/shard_map/ppermute | solution.py:565
  270.9 66.6 %collective-permute-start.32 = (bf16[2,4,240,640]{3,2,1,0:T(8,128)(2,1)}, bf16[2,4,240,640]{3,2,1,0:T(8,128)(2,1)}, u32[]{:S(2)}, u32[]{:S(2)}) collective-permute-start(bf16[2,4,240,640]{3,2,1,0:T(8,128)(2,1)} %get-tuple-element.131), channel_id=1, source_target_pairs={{0,8},{8,0},{16,24},{24,16},{1,9},{9,1},{17,25},{25,17},{2,10},{10... | collective-permute-start | bytes 7372808 | tf_op jit(solution)/shard_map/ppermute | solution.py:563
  306.9 17.2 %collective-permute-start.36 = (bf16[1,1,2,240,640]{4,3,2,1,0:T(8,128)(2,1)}, bf16[1,1,2,240,640]{4,3,2,1,0:T(8,128)(2,1)}, u32[]{:S(2)}, u32[]{:S(2)}) collective-permute-start(bf16[1,1,2,240,640]{4,3,2,1,0:T(8,128)(2,1)} %add_convert_fusion.12), channel_id=1, source_target_pairs={{0,16},{8,24},{16,0},{24,8},{1,17},{9,25},{17,1},{25,9},{2,18},{10... | collective-permute-start | bytes 1843208 | tf_op jit(solution)/shard_map/ppermute | solution.py:561
  309.4 25.4 %collective-permute-start.34 = (bf16[1,1,2,240,640]{4,3,2,1,0:T(8,128)(2,1)S(1)}, bf16[1,1,2,240,640]{4,3,2,1,0:T(8,128)(2,1)}, u32[]{:S(2)}, u32[]{:S(2)}) collective-permute-start(bf16[1,1,2,240,640]{4,3,2,1,0:T(8,128)(2,1)S(1)} %add_convert_fusion.13), channel_id=1, source_target_pairs={{0,16},{8,24},{16,0},{24,8},{1,17},{9,25},{17,1},{25,9},{2,18},{10... | collective-permute-start | bytes 1843208 | tf_op jit(solution)/shard_map/ppermute | solution.py:561
  313.8 25.8 %collective-permute-start.33 = (bf16[1,1,2,240,640]{4,3,2,1,0:T(8,128)(2,1)S(1)}, bf16[1,1,2,240,640]{4,3,2,1,0:T(8,128)(2,1)S(1)}, u32[]{:S(2)}, u32[]{:S(2)}) collective-permute-start(bf16[1,1,2,240,640]{4,3,2,1,0:T(8,128)(2,1)S(1)} %add_convert_fusion.14), channel_id=1, source_target_pairs={{0,1},{1,0},{2,3},{3,2},{4,5},{5,4},{6,7},{7,6},{8,9},{9,8},{10,11... | collective-permute-start | bytes 1843208 | tf_op jit(solution)/shard_map/ppermute | solution.py:565
  339.7 33.3 %collective-permute-start.38 = (bf16[2,1,2,80,640]{4,3,2,1,0:T(8,128)(2,1)S(1)}, bf16[2,1,2,80,640]{4,3,2,1,0:T(8,128)(2,1)S(1)}, u32[]{:S(2)}, u32[]{:S(2)}) collective-permute-start(bf16[2,1,2,80,640]{4,3,2,1,0:T(8,128)(2,1)S(1)} %add_convert_fusion.16), channel_id=1, source_target_pairs={{0,2},{1,3},{2,0},{3,1},{4,6},{5,7},{6,4},{7,5},{8,10},{9,11},{10,... | collective-permute-start | bytes 1228808 | tf_op jit(solution)/shard_map/ppermute | solution.py:565
  367.8 4.6 collective-permute-start.43
  367.8 44.6 %collective-permute-start.42 = (bf16[1,1,2,240,640]{4,3,2,1,0:T(8,128)(2,1)}, bf16[1,1,2,240,640]{4,3,2,1,0:T(8,128)(2,1)}, u32[]{:S(2)}, u32[]{:S(2)}) collective-permute-start(bf16[1,1,2,240,640]{4,3,2,1,0:T(8,128)(2,1)} %add_convert_fusion.9), channel_id=1, source_target_pairs={{0,1},{1,0},{2,3},{3,2},{4,5},{5,4},{6,7},{7,6},{8,9},{9,8},{10,11... | collective-permute-start | bytes 1843208 | tf_op jit(solution)/shard_map/ppermute | solution.py:565
  369.3 43.1 %collective-permute-start.41 = (bf16[1,1,2,240,640]{4,3,2,1,0:T(8,128)(2,1)}, bf16[1,1,2,240,640]{4,3,2,1,0:T(8,128)(2,1)}, u32[]{:S(2)}, u32[]{:S(2)}) collective-permute-start(bf16[1,1,2,240,640]{4,3,2,1,0:T(8,128)(2,1)} %add_convert_fusion.10), channel_id=1, source_target_pairs={{0,6},{1,7},{2,4},{3,5},{4,2},{5,3},{6,0},{7,1},{8,14},{9,15},{10,... | collective-permute-start | bytes 1843208 | tf_op jit(solution)/shard_map/ppermute | solution.py:565
  372.4 40.1 %collective-permute-start.40 = (bf16[1,1,2,240,640]{4,3,2,1,0:T(8,128)(2,1)}, bf16[1,1,2,240,640]{4,3,2,1,0:T(8,128)(2,1)}, u32[]{:S(2)}, u32[]{:S(2)}) collective-permute-start(bf16[1,1,2,240,640]{4,3,2,1,0:T(8,128)(2,1)} %add_convert_fusion.11), channel_id=1, source_target_pairs={{0,2},{1,3},{2,0},{3,1},{4,6},{5,7},{6,4},{7,5},{8,10},{9,11},{10,... | collective-permute-start | bytes 1843208 | tf_op jit(solution)/shard_map/ppermute | solution.py:565
  372.5 11.5 %collective-permute-start.37 = (bf16[1,2,2,80,640]{4,3,2,1,0:T(8,128)(2,1)S(1)}, bf16[1,2,2,80,640]{4,3,2,1,0:T(8,128)(2,1)}, u32[]{:S(2)}, u32[]{:S(2)}) collective-permute-start(bf16[1,2,2,80,640]{4,3,2,1,0:T(8,128)(2,1)S(1)} %add_convert_fusion.17), channel_id=1, source_target_pairs={{0,16},{8,24},{16,0},{24,8},{1,17},{9,25},{17,1},{25,9},{2,18},{10... | collective-permute-start | bytes 1228808 | tf_op jit(solution)/shard_map/ppermute | solution.py:561
  373.7 37.7 %collective-permute-start.39 = (bf16[2,1,2,80,640]{4,3,2,1,0:T(8,128)(2,1)S(1)}, bf16[2,1,2,80,640]{4,3,2,1,0:T(8,128)(2,1)}, u32[]{:S(2)}, u32[]{:S(2)}) collective-permute-start(bf16[2,1,2,80,640]{4,3,2,1,0:T(8,128)(2,1)S(1)} %add_convert_fusion.15), channel_id=1, source_target_pairs={{0,6},{1,7},{2,4},{3,5},{4,2},{5,3},{6,0},{7,1},{8,14},{9,15},{10,... | collective-permute-start | bytes 1228808 | tf_op jit(solution)/shard_map/ppermute | solution.py:565
  412.4 15.4 %collective-permute-start.50 = (f32[1920]{0:T(1024)S(1)}, f32[1920]{0:T(1024)S(1)}, u32[]{:S(2)}, u32[]{:S(2)}) collective-permute-start(f32[1920]{0:T(1024)S(1)} %add.427), channel_id=1, source_target_pairs={{0,16},{8,24},{16,0},{24,8},{1,17},{9,25},{17,1},{25,9},{2,18},{10... | collective-permute-start | bytes 23048 | tf_op jit(solution)/shard_map/ppermute | solution.py:561
  414.2 28.7 %collective-permute-start.49 = (bf16[1,1,2,240,640]{4,3,2,1,0:T(8,128)(2,1)S(1)}, bf16[1,1,2,240,640]{4,3,2,1,0:T(8,128)(2,1)S(1)}, u32[]{:S(2)}, u32[]{:S(2)}) collective-permute-start(bf16[1,1,2,240,640]{4,3,2,1,0:T(8,128)(2,1)S(1)} %add_convert_fusion.6), channel_id=1, source_target_pairs={{0,2},{1,3},{2,0},{3,1},{4,6},{5,7},{6,4},{7,5},{8,10},{9,11},{10,... | collective-permute-start | bytes 1843208 | tf_op jit(solution)/shard_map/ppermute | solution.py:565
  421.4 21.5 %collective-permute-start.48 = (bf16[1,1,2,240,640]{4,3,2,1,0:T(8,128)(2,1)S(1)}, bf16[1,1,2,240,640]{4,3,2,1,0:T(8,128)(2,1)S(1)}, u32[]{:S(2)}, u32[]{:S(2)}) collective-permute-start(bf16[1,1,2,240,640]{4,3,2,1,0:T(8,128)(2,1)S(1)} %add_convert_fusion.7), channel_id=1, source_target_pairs={{0,1},{1,0},{2,3},{3,2},{4,5},{5,4},{6,7},{7,6},{8,9},{9,8},{10,11... | collective-permute-start | bytes 1843208 | tf_op jit(solution)/shard_map/ppermute | solution.py:565
  422.0 7.4 %collective-permute-start.45 = (bf16[1,1,2,80,640]{4,3,2,1,0:T(8,128)(2,1)S(1)}, bf16[1,1,2,80,640]{4,3,2,1,0:T(8,128)(2,1)S(1)}, u32[]{:S(2)}, u32[]{:S(2)}) collective-permute-start(bf16[1,1,2,80,640]{4,3,2,1,0:T(8,128)(2,1)S(1)} %add_convert_fusion.27), channel_id=1, source_target_pairs={{0,16},{8,24},{16,0},{24,8},{1,17},{9,25},{17,1},{25,9},{2,18},{10... | collective-permute-start | bytes 614408 | tf_op jit(solution)/shard_map/ppermute | solution.py:561
  425.2 23.6 %collective-permute-start.47 = (bf16[1,1,2,240,640]{4,3,2,1,0:T(8,128)(2,1)S(1)}, bf16[1,1,2,240,640]{4,3,2,1,0:T(8,128)(2,1)S(1)}, u32[]{:S(2)}, u32[]{:S(2)}) collective-permute-start(bf16[1,1,2,240,640]{4,3,2,1,0:T(8,128)(2,1)S(1)} %add_convert_fusion.8), channel_id=1, source_target_pairs={{0,6},{1,7},{2,4},{3,5},{4,2},{5,3},{6,0},{7,1},{8,14},{9,15},{10,... | collective-permute-start | bytes 1843208 | tf_op jit(solution)/shard_map/ppermute | solution.py:565
  427.9 12.9 %collective-permute-start.44 = (bf16[1,1,2,80,640]{4,3,2,1,0:T(8,128)(2,1)S(1)}, bf16[1,1,2,80,640]{4,3,2,1,0:T(8,128)(2,1)S(1)}, u32[]{:S(2)}, u32[]{:S(2)}) collective-permute-start(bf16[1,1,2,80,640]{4,3,2,1,0:T(8,128)(2,1)S(1)} %add_convert_fusion.29), channel_id=1, source_target_pairs={{0,1},{1,0},{2,3},{3,2},{4,5},{5,4},{6,7},{7,6},{8,9},{9,8},{10,11... | collective-permute-start | bytes 614408 | tf_op jit(solution)/shard_map/ppermute | solution.py:565
  429.4 12.5 %collective-permute-start.46 = (bf16[1,1,2,80,640]{4,3,2,1,0:T(8,128)(2,1)S(1)}, bf16[1,1,2,80,640]{4,3,2,1,0:T(8,128)(2,1)S(1)}, u32[]{:S(2)}, u32[]{:S(2)}) collective-permute-start(bf16[1,1,2,80,640]{4,3,2,1,0:T(8,128)(2,1)S(1)} %add_convert_fusion.26), channel_id=1, source_target_pairs={{0,16},{8,24},{16,0},{24,8},{1,17},{9,25},{17,1},{25,9},{2,18},{10... | collective-permute-start | bytes 614408 | tf_op jit(solution)/shard_map/ppermute | solution.py:561
  448.8 22.8 %collective-permute-start.57 = (f32[1920]{0:T(1024)S(1)}, f32[1920]{0:T(1024)S(1)}, u32[]{:S(2)}, u32[]{:S(2)}) collective-permute-start(f32[1920]{0:T(1024)S(1)} %add.438), channel_id=1, source_target_pairs={{0,1},{1,0},{2,3},{3,2},{4,5},{5,4},{6,7},{7,6},{8,9},{9,8},{10,11... | collective-permute-start | bytes 23048 | tf_op jit(solution)/shard_map/ppermute | solution.py:565
  449.5 43.1 %collective-permute-start.56 = (bf16[1,1,2,240,640]{4,3,2,1,0:T(8,128)(2,1)S(1)}, bf16[1,1,2,240,640]{4,3,2,1,0:T(8,128)(2,1)S(1)}, u32[]{:S(2)}, u32[]{:S(2)}) collective-permute-start(bf16[1,1,2,240,640]{4,3,2,1,0:T(8,128)(2,1)S(1)} %add_convert_fusion.3), channel_id=1, source_target_pairs={{0,6},{1,7},{2,4},{3,5},{4,2},{5,3},{6,0},{7,1},{8,14},{9,15},{10,... | collective-permute-start | bytes 1843208 | tf_op jit(solution)/shard_map/ppermute | solution.py:565
  451.2 41.4 %collective-permute-start.55 = (bf16[1,1,2,240,640]{4,3,2,1,0:T(8,128)(2,1)S(1)}, bf16[1,1,2,240,640]{4,3,2,1,0:T(8,128)(2,1)S(1)}, u32[]{:S(2)}, u32[]{:S(2)}) collective-permute-start(bf16[1,1,2,240,640]{4,3,2,1,0:T(8,128)(2,1)S(1)} %add_convert_fusion.4), channel_id=1, source_target_pairs={{0,2},{1,3},{2,0},{3,1},{4,6},{5,7},{6,4},{7,5},{8,10},{9,11},{10,... | collective-permute-start | bytes 1843208 | tf_op jit(solution)/shard_map/ppermute | solution.py:565
  470.0 15.0 %collective-permute-start.52 = (bf16[1,1,2,80,640]{4,3,2,1,0:T(8,128)(2,1)S(1)}, bf16[1,1,2,80,640]{4,3,2,1,0:T(8,128)(2,1)S(1)}, u32[]{:S(2)}, u32[]{:S(2)}) collective-permute-start(bf16[1,1,2,80,640]{4,3,2,1,0:T(8,128)(2,1)S(1)} %add_convert_fusion.24), channel_id=1, source_target_pairs={{0,6},{1,7},{2,4},{3,5},{4,2},{5,3},{6,0},{7,1},{8,14},{9,15},{10,... | collective-permute-start | bytes 614408 | tf_op jit(solution)/shard_map/ppermute | solution.py:565
  471.0 21.5 %collective-permute-start.54 = (bf16[1,1,2,240,640]{4,3,2,1,0:T(8,128)(2,1)S(1)}, bf16[1,1,2,240,640]{4,3,2,1,0:T(8,128)(2,1)S(1)}, u32[]{:S(2)}, u32[]{:S(2)}) collective-permute-start(bf16[1,1,2,240,640]{4,3,2,1,0:T(8,128)(2,1)S(1)} %add_convert_fusion.5), channel_id=1, source_target_pairs={{0,1},{1,0},{2,3},{3,2},{4,5},{5,4},{6,7},{7,6},{8,9},{9,8},{10,11... | collective-permute-start | bytes 1843208 | tf_op jit(solution)/shard_map/ppermute | solution.py:565
  471.6 15.4 %collective-permute-start.51 = (bf16[1,1,2,80,640]{4,3,2,1,0:T(8,128)(2,1)S(1)}, bf16[1,1,2,80,640]{4,3,2,1,0:T(8,128)(2,1)S(1)}, u32[]{:S(2)}, u32[]{:S(2)}) collective-permute-start(bf16[1,1,2,80,640]{4,3,2,1,0:T(8,128)(2,1)S(1)} %add_convert_fusion.28), channel_id=1, source_target_pairs={{0,2},{1,3},{2,0},{3,1},{4,6},{5,7},{6,4},{7,5},{8,10},{9,11},{10,... | collective-permute-start | bytes 614408 | tf_op jit(solution)/shard_map/ppermute | solution.py:565
  485.0 7.5 %collective-permute-start.53 = (bf16[1,1,2,80,640]{4,3,2,1,0:T(8,128)(2,1)S(1)}, bf16[1,1,2,80,640]{4,3,2,1,0:T(8,128)(2,1)S(1)}, u32[]{:S(2)}, u32[]{:S(2)}) collective-permute-start(bf16[1,1,2,80,640]{4,3,2,1,0:T(8,128)(2,1)S(1)} %add_convert_fusion.23), channel_id=1, source_target_pairs={{0,1},{1,0},{2,3},{3,2},{4,5},{5,4},{6,7},{7,6},{8,9},{9,8},{10,11... | collective-permute-start | bytes 614408 | tf_op jit(solution)/shard_map/ppermute | solution.py:565
  492.6 13.5 %collective-permute-start.61 = (f32[1920]{0:T(1024)S(1)}, f32[1920]{0:T(1024)S(1)}, u32[]{:S(2)}, u32[]{:S(2)}) collective-permute-start(f32[1920]{0:T(1024)S(1)} %add.442), channel_id=1, source_target_pairs={{0,2},{1,3},{2,0},{3,1},{4,6},{5,7},{6,4},{7,5},{8,10},{9,11},{10,... | collective-permute-start | bytes 23048 | tf_op jit(solution)/shard_map/ppermute | solution.py:565
  494.1 12.0 %collective-permute-start.59 = (bf16[1,1,2,80,640]{4,3,2,1,0:T(8,128)(2,1)S(1)}, bf16[1,1,2,80,640]{4,3,2,1,0:T(8,128)(2,1)S(1)}, u32[]{:S(2)}, u32[]{:S(2)}) collective-permute-start(bf16[1,1,2,80,640]{4,3,2,1,0:T(8,128)(2,1)S(1)} %add_convert_fusion.21), channel_id=1, source_target_pairs={{0,1},{1,0},{2,3},{3,2},{4,5},{5,4},{6,7},{7,6},{8,9},{9,8},{10,11... | collective-permute-start | bytes 614408 | tf_op jit(solution)/shard_map/ppermute | solution.py:565
  495.7 10.4 %collective-permute-start.58 = (bf16[1,1,2,80,640]{4,3,2,1,0:T(8,128)(2,1)S(1)}, bf16[1,1,2,80,640]{4,3,2,1,0:T(8,128)(2,1)S(1)}, u32[]{:S(2)}, u32[]{:S(2)}) collective-permute-start(bf16[1,1,2,80,640]{4,3,2,1,0:T(8,128)(2,1)S(1)} %add_convert_fusion.25), channel_id=1, source_target_pairs={{0,6},{1,7},{2,4},{3,5},{4,2},{5,3},{6,0},{7,1},{8,14},{9,15},{10,... | collective-permute-start | bytes 614408 | tf_op jit(solution)/shard_map/ppermute | solution.py:565
  497.9 10.1 %collective-permute-start.60 = (bf16[1,1,2,80,640]{4,3,2,1,0:T(8,128)(2,1)S(1)}, bf16[1,1,2,80,640]{4,3,2,1,0:T(8,128)(2,1)S(1)}, u32[]{:S(2)}, u32[]{:S(2)}) collective-permute-start(bf16[1,1,2,80,640]{4,3,2,1,0:T(8,128)(2,1)S(1)} %add_convert_fusion.20), channel_id=1, source_target_pairs={{0,2},{1,3},{2,0},{3,1},{4,6},{5,7},{6,4},{7,5},{8,10},{9,11},{10,... | collective-permute-start | bytes 614408 | tf_op jit(solution)/shard_map/ppermute | solution.py:565
  508.0 5.4 %collective-permute-start.65 = (f32[1920]{0:T(1024)S(1)}, f32[1920]{0:T(1024)S(1)}, u32[]{:S(2)}, u32[]{:S(2)}) collective-permute-start(f32[1920]{0:T(1024)S(1)} %add.445), channel_id=1, source_target_pairs={{0,6},{1,7},{2,4},{3,5},{4,2},{5,3},{6,0},{7,1},{8,14},{9,15},{10,... | collective-permute-start | bytes 23048 | tf_op jit(solution)/shard_map/ppermute | solution.py:565
  509.5 5.8 %collective-permute-start.62 = (bf16[1,1,2,80,640]{4,3,2,1,0:T(8,128)(2,1)S(1)}, bf16[1,1,2,80,640]{4,3,2,1,0:T(8,128)(2,1)S(1)}, u32[]{:S(2)}, u32[]{:S(2)}) collective-permute-start(bf16[1,1,2,80,640]{4,3,2,1,0:T(8,128)(2,1)S(1)} %add_convert_fusion.22), channel_id=1, source_target_pairs={{0,1},{1,0},{2,3},{3,2},{4,5},{5,4},{6,7},{7,6},{8,9},{9,8},{10,11... | collective-permute-start | bytes 614408 | tf_op jit(solution)/shard_map/ppermute | solution.py:565
  509.8 5.8 %collective-permute-start.63 = (bf16[1,1,2,80,640]{4,3,2,1,0:T(8,128)(2,1)S(1)}, bf16[1,1,2,80,640]{4,3,2,1,0:T(8,128)(2,1)S(1)}, u32[]{:S(2)}, u32[]{:S(2)}) collective-permute-start(bf16[1,1,2,80,640]{4,3,2,1,0:T(8,128)(2,1)S(1)} %add_convert_fusion.19), channel_id=1, source_target_pairs={{0,2},{1,3},{2,0},{3,1},{4,6},{5,7},{6,4},{7,5},{8,10},{9,11},{10,... | collective-permute-start | bytes 614408 | tf_op jit(solution)/shard_map/ppermute | solution.py:565
  510.0 8.2 %collective-permute-start.64 = (bf16[1,1,2,80,640]{4,3,2,1,0:T(8,128)(2,1)S(1)}, bf16[1,1,2,80,640]{4,3,2,1,0:T(8,128)(2,1)S(1)}, u32[]{:S(2)}, u32[]{:S(2)}) collective-permute-start(bf16[1,1,2,80,640]{4,3,2,1,0:T(8,128)(2,1)S(1)} %add_convert_fusion.18), channel_id=1, source_target_pairs={{0,6},{1,7},{2,4},{3,5},{4,2},{5,3},{6,0},{7,1},{8,14},{9,15},{10,... | collective-permute-start | bytes 614408 | tf_op jit(solution)/shard_map/ppermute | solution.py:565
  (72 other events, 899.9 us)

commit v3 on v2

--- a/solution.py
+++ b/solution.py
@@ -37,8 +37,8 @@
     )
 
 
-def cost(flops, moved, exps=0):
-    return pl.CostEstimate(flops=flops, bytes_accessed=moved, transcendentals=exps)
+def cost(*_):
+    return pl.CostEstimate(flops=1, bytes_accessed=1, transcendentals=0)
 
 
 def shaped(*shape_type):
@@ -261,21 +261,10 @@
     )(where, x, o, gains, *w.arrays)
 
 
-def split_owners(grad, core, keep_ref, send_ref):
-    for x in range(2):
-        a = grad[2 * x * OWN:(2 * x + 1) * OWN]
-        b = grad[(2 * x + 1) * OWN:(2 * x + 2) * OWN]
-        keep_ref[x, 0] = jnp.where(core == 0, a, b).astype(BF16)
-        send_ref[x, 0] = jnp.where(core == 0, b, a).astype(BF16)
-
-
 def feed_forward_kernel(weights, where_ref, h_ref, dy_ref, x1_ref, *refs):
     count = len(weights[0].arrays)
-    (y_ref, dh_ref, gg_keep, gg_send, gu_keep, gu_send, gd_keep, gd_send, acc_ref, *scratch) = (
-        refs[3 * count:]
-    )
+    y_ref, dh_ref, hid_ref, dgate_ref, dup_ref, acc_ref, *scratch = refs[3 * count:]
     step = pl.program_id(0)
-    core = where_ref[0] & 1
 
     @pl.when(step == 0)
     def _():
@@ -296,19 +285,10 @@
     hid = (silu * up).astype(BF16)
     dgate = (dhid * up * (sig + silu * (1.0 - sig))).astype(BF16)
     dup = (dhid * silu).astype(BF16)
+    hid_ref[...] = hid
+    dgate_ref[...] = dgate
+    dup_ref[...] = dup
     acc_ref[...] += dot(wd_ref[...], hid, 1, 0)
-    split_owners(dot(h, dgate, 1, 1), core, gg_keep, gg_send)
-    split_owners(dot(h, dup, 1, 1), core, gu_keep, gu_send)
-    down = dot(dy, hid, 1, 1).astype(BF16).reshape(4, OWN, CUT)
-
-    @pl.when(step % 2 == core)
-    def _():
-        gd_keep[0] = down
-
-    @pl.when(step % 2 != core)
-    def _():
-        gd_send[0] = down
-
     dh_ref[...] += dot(wg_ref[...], dgate, 1, 0) + dot(wu_ref[...], dup, 1, 0)
 
     @pl.when(step == pl.num_programs(0) - 1)
@@ -318,24 +298,70 @@
 
 def feed_forward(where, h, dy, x1, weights):
     rows, hidden = h.shape[1], weights[0].shape[1]
-    steps = hidden // CUT
-    part = (2, steps, OWN, CUT)
-    by_rows = pl.BlockSpec((2, 1, OWN, CUT), lambda f: (0, f, 0, 0))
-    by_columns = pl.BlockSpec((1, steps, OWN, CUT), lambda f: (f // 2, 0, 0, 0))
+    block = pl.BlockSpec((CUT, rows), lambda f: (f, 0))
     return pl.pallas_call(
         functools.partial(feed_forward_kernel, weights),
-        grid=(steps,),
-        in_specs=[
-            SMEM,
-            fixed((D, rows)), fixed((D, rows)), fixed((D, rows)),
-        ] + sum((w.specs() for w in weights), []),
-        out_specs=[fixed((D, rows)), fixed((D, rows))] + [by_rows] * 4 + [by_columns] * 2,
-        out_shape=shaped(((D, rows), BF16), ((D, rows), F32)) + shaped((part, BF16)) * 6,
+        grid=(hidden // CUT,),
+        in_specs=[SMEM, fixed((D, rows)), fixed((D, rows)), fixed((D, rows))]
+        + sum((w.specs() for w in weights), []),
+        out_specs=[fixed((D, rows)), fixed((D, rows))] + [block] * 3,
+        out_shape=shaped(((D, rows), BF16), ((D, rows), F32)) + shaped(((hidden, rows), BF16)) * 3,
         scratch_shapes=sum((w.scratch() for w in weights), [pltpu.VMEM((D, rows), F32)]),
         compiler_params=params(60),
-        cost_estimate=cost(18 * rows * D * hidden, 16 * rows * D + 12 * D * hidden, rows * hidden),
+        cost_estimate=cost(),
         name="feed_forward",
     )(where, h, dy, x1, *sum((w.arrays for w in weights), []))
+
+
+def split_owners(grad, where_ref, put):
+    core, x_here = where_ref[0] & 1, where_ref[0] >> 1
+    for x in range(2):
+        a = grad[2 * x * OWN:(2 * x + 1) * OWN].astype(BF16)
+        b = grad[(2 * x + 1) * OWN:(2 * x + 2) * OWN].astype(BF16)
+        put(x_here ^ x, jnp.where(core == 0, a, b), jnp.where(core == 0, b, a))
+
+
+def row_grads_kernel(where_ref, a_ref, b_ref, keep_ref, send_ref):
+    def put(x, keep, send):
+        keep_ref[x, 0] = keep
+        send_ref[x, 0] = send
+
+    split_owners(dot(a_ref[...], b_ref[...], 1, 1), where_ref, put)
+
+
+def column_grads_kernel(dim, where_ref, a_ref, b_ref, keep_ref, send_ref):
+    grad = dot(a_ref[...], b_ref[...], 1, 1).astype(BF16)
+    here = (pl.program_id(0) & 1) == (where_ref[0] & 1)
+
+    def put(ref):
+        for i in range(4):
+            ref[0, (2 * where_ref[1 + dim]) ^ i] = grad[i * OWN:(i + 1) * OWN]
+
+    pl.when(here)(lambda: put(keep_ref))
+    pl.when(jnp.logical_not(here))(lambda: put(send_ref))
+
+
+def ffn_grads(where, a, b, dim, by_columns):
+    rows = a.shape[1]
+    if by_columns:
+        kernel = functools.partial(column_grads_kernel, dim)
+        out = pl.BlockSpec((1, 4, OWN, CUT), lambda f, at: ((f >> 1) ^ (at[0] >> 1), 0, 0, 0))
+    else:
+        kernel = row_grads_kernel
+        out = pl.BlockSpec((2, 1, OWN, CUT), lambda f, at: (0, f ^ (2 * at[1 + dim]), 0, 0))
+    return pl.pallas_call(
+        kernel,
+        grid_spec=pltpu.PrefetchScalarGridSpec(
+            num_scalar_prefetch=1,
+            grid=(b.shape[0] // CUT,),
+            in_specs=[fixed((D, rows)), pl.BlockSpec((CUT, rows), lambda f, at: (f, 0))],
+            out_specs=[out, out],
+        ),
+        out_shape=shaped(((2, 4, OWN, CUT), BF16)) * 2,
+        compiler_params=params(40),
+        cost_estimate=cost(),
+        name="ffn_grads",
+    )(where, a, b)
 
 
 def branch_kernel(weight, where_ref, dh_ref, x1_ref, dy_ref, gain_ref, *refs):
@@ -450,38 +476,38 @@
     )(qkv, o, do, lse, segments[:, None, :], segments[:, :, None], cos, sin)
 
 
-def weight_kernel(where_ref, h_ref, dqkv_ref, o_ref, da_ref, keep_ref, send_ref):
-    core = where_ref[0] & 1
-    step = pl.program_id(0)
-
-    @pl.when(step < 2)
-    def _():
-        rows = pl.ds(pl.multiple_of(step * CUT, CUT), CUT)
-        split_owners(dot(h_ref[...], dqkv_ref[rows, :], 1, 1), core, keep_ref, send_ref)
-
-    @pl.when(step == 2)
-    def _():
-        left = dot(h_ref[...], dqkv_ref[2 * CUT:, :], 1, 1)
-        right = dot(o_ref[...], da_ref[:3 * CUT - WIDE, :], 1, 1)
-        split_owners(jnp.concatenate([left, right], axis=1), core, keep_ref, send_ref)
-
-    @pl.when(step == 3)
-    def _():
-        split_owners(dot(o_ref[...], da_ref[3 * CUT - WIDE:, :], 1, 1), core, keep_ref, send_ref)
+PIECES = ((0, 128), (128, OWN))
+
+
+def weight_kernel(where_ref, h_ref, dqkv_ref, o_ref, da_ref, *out_refs):
+    def store(block, grad):
+        def put(x, keep, send):
+            for i, (low, high) in enumerate(PIECES):
+                at = block ^ (2 * where_ref[1 + i])
+                out_refs[2 * i][x, at] = keep[low:high]
+                out_refs[2 * i + 1][x, at] = send[low:high]
+
+        split_owners(grad, where_ref, put)
+
+    store(0, dot(h_ref[...], dqkv_ref[:CUT, :], 1, 1))
+    store(1, dot(h_ref[...], dqkv_ref[CUT:2 * CUT, :], 1, 1))
+    left = dot(h_ref[...], dqkv_ref[2 * CUT:, :], 1, 1)
+    right = dot(o_ref[...], da_ref[:3 * CUT - WIDE, :], 1, 1)
+    store(2, jnp.concatenate([left, right], axis=1))
+    store(3, dot(o_ref[...], da_ref[3 * CUT - WIDE:, :], 1, 1))
 
 
 def weight_grads(where, h, dqkv, o, da):
     rows = h.shape[1]
-    part = pl.BlockSpec((2, 1, OWN, CUT), lambda f: (0, f, 0, 0))
+    shapes = [(2, 4, high - low, CUT) for low, high in PIECES for _ in range(2)]
     return pl.pallas_call(
         weight_kernel,
-        grid=(4,),
-        in_specs=[SMEM, fixed((D, rows)), fixed((WIDE, rows)),
-                  fixed((D, rows)), fixed((D, rows))],
-        out_specs=[part, part],
-        out_shape=shaped(((2, 4, OWN, CUT), BF16)) * 2,
-        compiler_params=params(40),
-        cost_estimate=cost(2 * rows * D * (D + WIDE), rows * (3 * D + WIDE) * 2 + D * 5120),
+        grid=(1,),
+        in_specs=[SMEM, fixed((D, rows)), fixed((WIDE, rows)), fixed((D, rows)), fixed((D, rows))],
+        out_specs=[fixed(shape) for shape in shapes],
+        out_shape=shaped(*((shape, BF16) for shape in shapes)),
+        compiler_params=params(48),
+        cost_estimate=cost(),
         name="weight_grads",
     )(where, h, dqkv, o, da)
 
@@ -614,34 +640,40 @@
     def __init__(self, cube, keep, got, order):
         rows, wide = keep.shape[2:]
         self.cube, self.order, self.shape = cube, order, (4, rows, wide)
-
         self.cut = [d for d in order[:2] if d != "x"][0]
         self.terms = [t.reshape(2, 2, 2, rows, wide) for t in (keep, got)]
-        self.got = None
-
-    def sum(self):
-        return functools.reduce(jnp.add, [t.astype(F32) for t in self.terms]).astype(BF16)
-
-    def step(self, index, *others):
-        cube, dim = self.cube, self.order[index]
-        if index < 2:
-            mine, axis = cube.coordinate[dim], 0 if dim == "x" else 1
-            take = lambda which: [
-                lax.dynamic_slice_in_dim(t, which, 1, axis) for t in self.terms
-            ]
-            other, self.terms = take(1 - mine), take(mine)
-            send = functools.reduce(jnp.add, [t.astype(F32) for t in other]).astype(BF16)
-            self.got = cube.swap(after(send, *others), dim)
+        self.index = 0
+
+    def sum(self, terms):
+        return functools.reduce(jnp.add, [t.astype(F32) for t in terms]).astype(BF16)
+
+    def ready(self, *others):
+        dim = self.order[self.index]
+        self.terms[-1] = after(self.terms[-1], *others)
+        if self.index < 2:
+            axis = 0 if dim == "x" else 1
+            take = lambda i: [lax.slice_in_dim(t, i, i + 1, axis=axis) for t in self.terms]
+            self.send, self.terms = self.sum(take(1)), take(0)
+        else:
+            self.send = self.sum(self.terms)
+            self.terms = [self.send]
+        return self.send
+
+    def swap(self):
+        dim = self.order[self.index]
+        self.got = self.cube.swap(self.send, dim)
+        self.index += 1
+        if self.index == len(self.order):
+            self.result = self.cube.ordered(dim, self.send, self.got, 1).reshape(self.shape)
+        elif self.index > 2:
+            self.terms = [self.send, self.got]
+        else:
             self.terms = self.terms + [self.got]
-        elif dim != self.cut:
-            low = after(self.sum(), *others)
-            self.got = cube.swap(low, dim)
-            self.terms = [low, self.got]
-        else:
-            low = after(self.sum(), *others)
-            self.got = cube.swap(low, dim)
-            self.result = cube.ordered(dim, low, self.got, 1).reshape(self.shape)
         return self.got
+
+    def step(self, *others):
+        self.ready(*others)
+        return self.swap()
 
 
 def per_device(
@@ -692,47 +724,57 @@
     rest = [relay.finish(o1) for relay in relays]
     x1, h2 = middle(where, x, o, wo, gains)
     weights = [relay.weight(sibling, h2) for relay, sibling in zip(relays, siblings)]
-    y, dh2, gg_keep, gg_send, gu_keep, gu_send, gd_keep, gd_send = feed_forward(
-        where, h2, dy, x1, weights
-    )
-
-    gd_got, gg_got, gu_got = (cube.swap(g, "core") for g in (gd_send, gg_send, gu_send))
-    dx1, da, do, ffn_gain_grad = branch(where, dh2, x1, dy, gains, wo)
+    y, dh2, hid, dgate, dup = feed_forward(where, h2, dy, x1, weights)
+
     more = tuple(range(3, cube.dims))
     orders = [
         ("x", 0, 1, 2) + more + (0,), (1, "x", 2, 0) + more + (1,), (2, "x", 0, 1) + more + (2,)
     ]
-    gd = Reduce(cube, gd_keep, gd_got, orders[0])
-    gg = Reduce(cube, gg_keep, gg_got, orders[1])
-    gu = Reduce(cube, gu_keep, gu_got, orders[2])
-    do = after(do, gd_got, gg_got)
-    first = [gd.step(0, da), gg.step(0, da)]
-    dqkv0 = attend_back(qkv, o0, do, lse0, segments, cos, sin, 0)
-    do1 = after(do, dqkv0, gu_got)
-    first.append(gu.step(0, dqkv0))
+    core = lambda value: cube.swap(value, "core")
+    gd_keep, gd_send = ffn_grads(where, dy, hid, 0, True)
+    gd = Reduce(cube, gd_keep, core(gd_send), orders[0])
+    gg_keep, gg_send = ffn_grads(where, h2, after(dgate, gd_send), 1, False)
+    gg = Reduce(cube, gg_keep, core(gg_send), orders[1])
+    gd.ready(gg_send)
+    gu_keep, gu_send = ffn_grads(where, h2, after(dup, gd.send), 2, False)
+    gd.swap()
+    gu = Reduce(cube, gu_keep, core(gu_send), orders[2])
+    gg.ready(gu_send)
+    dx1, da, do, ffn_gain_grad = branch(where, after(dh2, gg.send), x1, dy, gains, wo)
+    gg.swap()
+    gu.ready(da)
+    do0 = after(do, gu.send)
+    gu.swap()
+    dqkv0 = attend_back(qkv, o0, do0, lse0, segments, cos, sin, 0)
+    gd.ready(dqkv0)
+    do1 = after(do, dqkv0, gd.send)
+    gd.swap()
     dqkv1 = attend_back(qkv, o1, do1, lse1, segments, cos, sin, 1)
-    dqkv = jnp.concatenate([dqkv0, dqkv1], axis=1)
-    ga_keep, ga_send = weight_grads(where, h, dqkv, o, da)
-    ga_got = cube.swap(ga_send, "core")
-    dqkv = after(dqkv, ga_send, *first[:2])
-    second = [gd.step(1, ga_send), gg.step(1, ga_send)]
+    gg.ready(dqkv1)
+    dqkv = after(jnp.concatenate([dqkv0, dqkv1], axis=1), gg.send)
+    gg.swap()
+    parts = []
+    weight_parts = weight_grads(where, h, dqkv, o, da)
+    for i in range(len(PIECES)):
+        keep, send = weight_parts[2 * i:2 * i + 2]
+        parts.append(Reduce(cube, keep, core(send), orders[i]))
+    gu.ready(send)
+    gd.ready(send)
+    dqkv = after(dqkv, gu.send, gd.send)
+    gu.swap()
+    gd.swap()
     grad_x, attn_gain_grad = input_grads(where, x, dx1, wq, wk, dqkv)
-    second.append(gu.step(1, grad_x))
-    size = OWN // 3
-    cut = lambda g, i: g[:, :, i * size:(i + 1) * size]
-    parts = [
-        Reduce(cube, cut(ga_keep, i), cut(ga_got, i), order) for i, order in enumerate(orders)
-    ]
     both = jnp.concatenate([attn_gain_grad, ffn_gain_grad], axis=1).T.reshape(-1)
     ends = ["core", "x"] + list(range(cube.dims))
-    done = second + [ga_got]
-    for index in range(len(orders[0])):
-        now = [part.step(index, *done) for part in parts]
-        if index + 2 < len(orders[0]):
-            now += [piece.step(index + 2, *done) for piece in (gd, gg, gu)]
-        got = cube.swap(after(both, *done), ends[index])
-        both = both + got
-        done = now + [got]
+    swaps = [gg, parts[0], gu, parts[1], gd]
+    token = grad_x
+    for round_of in range(len(orders[0])):
+        before = token
+        for piece in swaps:
+            if piece.index < len(piece.order):
+                token = piece.ready(token)
+                piece.swap()
+        both = both + after(cube.swap(after(both, before), ends[round_of]), token)
     for dim in ends[len(orders[0]):]:
         both = both + cube.swap(both, dim)
     both = lax.dynamic_slice_in_dim(both.reshape(2, D), cube.me * OWN, OWN, 1)

time: 533 us -> 468 us (0.88)
  waiting for transfers between devices: 157 us -> 99.7 us
  starting transfers between devices: 112 us -> 95.2 us
  local copies, waits for them, and re-layouts: 49.2 us -> 64.8 us
    ppermute x33 -> x29, waiting for transfers between devices: 111 us -> 75.8 us  [swap(): lax.ppermute(value, 'replica', [(i, i ^ mask) for i in range(self.count)])]
    ppermute x13 -> x12, waiting for transfers between devices: 43.7 us -> 20.8 us  [swap(): return lax.ppermute(value, 'group', [(i, i ^ 2) for i in range(4)])]
    ppermute x33 -> x29, starting transfers between devices: 93.3 us -> 74.8 us  [swap(): lax.ppermute(value, 'replica', [(i, i ^ mask) for i in range(self.count)])]
    unnamed x149 -> x183, local copies, waits for them, and re-layouts: 32.4 us -> 48.3 us
    convert_element_type x30 -> x24, other arithmetic: 34.6 us -> 29.7 us  [sum(): functools.reduce(jnp.add, [t.astype(F32) for t in terms]).astype(BF16)]
    pallas_call x2 -> x5, Pallas kernels: 91.1 us -> 88 us  [the longest x1 50.4 us: feed_forward(): pl.pallas_call(functools.partial(feed_forward_kernel, weights), grid=(hid...]
    ppermute x13 -> x12, starting transfers between devices: 14.1 us -> 16.2 us  [swap(): return lax.ppermute(value, 'group', [(i, i ^ 2) for i in range(4)])]
  transfers between devices with their start and end apart: 66 -> 62, of which waited for: 25 -> 16; matrix products, arithmetic and copies ran while one was open for 11% -> 12% of each run, Pallas kernels for 13% -> 21%
where the time goes in v3:
time: 468 us; the launch traced here: 460 us
  Pallas kernels  157 us (34%)
  waiting for transfers between devices  99.7 us (21%)
  starting transfers between devices  95.2 us (20%)
  local copies, waits for them, and re-layouts  64.8 us (14%)
  other arithmetic  41.2 us (9%)
    ppermute x29, waiting for transfers between devices, swap(): lax.ppermute(value, 'replica', [(i, i ^ mask) for i in range(self.count)])  75.8 us
    ppermute x29, starting transfers between devices, swap(): lax.ppermute(value, 'replica', [(i, i ^ mask) for i in range(self.count)])  74.8 us
    pallas_call x1, Pallas kernels, feed_forward(): pl.pallas_call(functools.partial(feed_forward_kernel, weights), grid=(hid...  50.4 us
    unnamed x183, local copies, waits for them, and re-layouts  48.3 us
    convert_element_type x24, other arithmetic, sum(): functools.reduce(jnp.add, [t.astype(F32) for t in terms]).astype(BF16)  29.7 us
    pallas_call x3, Pallas kernels, ffn_grads(): pl.pallas_call(kernel, grid_spec=pltpu.PrefetchScalarGridSpec(num_scalar_...  25.9 us
    ppermute x12, waiting for transfers between devices, swap(): return lax.ppermute(value, 'group', [(i, i ^ 2) for i in range(4)])  20.8 us
    pallas_call x2, Pallas kernels, attend_back(): pl.pallas_call(attend_back_kernel, grid=(1,), in_specs=[here(wide), pl.Bl...  17.3 us
  transfers between devices with their start and end apart: 62, of which 16 were waited for; matrix products, arithmetic and copies ran while one was open for 12% of the time, Pallas kernels for 21%

profile of v3, /device:TPU:0, one launch (start us, length us, event | category | flops | bytes accessed | tf_op | source)
XLA Modules:
  0.0 459.7 jit_solution(4436773526254923604)
XLA Ops:
  4.6 3.0 collective-permute-start.4
  8.6 8.5 %collective-permute-done.4.refs_6_ = bf16[240,768]{1,0:T(8,128)(2,1)S(1)} collective-permute-done((bf16[240,768]{1,0:T(8,128)(2,1)S(1)}, bf16[240,768]{1,0:T(8,128)(2,1)S(1)}, u32[]{:S(2)}, u32[]{:S(2)}) %collective-permute-start.4) | collective-permute-done | bytes 368672 | tf_op jit(solution)/shard_map/ppermute | solution.py:587
  17.1 9.7 %collective-permute-done.1.refs_2_ = bf16[240,960]{1,0:T(8,128)(2,1)S(1)} collective-permute-done((bf16[240,960]{1,0:T(8,128)(2,1)S(1)}, bf16[240,960]{1,0:T(8,128)(2,1)S(1)}, u32[]{:S(2)}, u32[]{:S(2)}) %collective-permute-start.1) | collective-permute-done | bytes 460832 | tf_op jit(solution)/shard_map/ppermute | solution.py:587
  27.3 1.7 dynamic-slice_bitcast_fusion
  29.0 1.7 collective-permute-start.9
  30.8 1.7 constant_dynamic-slice_fusion.1
  43.9 9.8 %project.1 = (bf16[1600,1024]{1,0:T(8,128)(2,1)S(1)}, bf16[960,1024]{1,0:T(8,128)(2,1)S(1)}, bf16[960,128]{1,0:T(8,128)(2,1)S(1)}) custom-call(s32[4]{0:T(128)S(1)} %pad_add_fusion.where_ref, bf16[960,1024]{1,0:T(8,128)(2,1)S(1)} %bitcast.55, f32[32,1024]{1,0:T(8,128)S(1)} %get-tuple-element.248.cos_ref, f32[32,1024]{1,0:T(8,128)S(1)} %get-tuple-element.247.sin_ref, ...), custom_call_target="tpu_custom_call" | custom-call | flops 1 | bytes 1 | tf_op jit(solution)/shard_map/project/pallas_call | solution.py:145
  55.6 1.7 collective-permute-start.13
  57.3 1.7 constant_dynamic-slice_fusion.2
  61.4 6.7 %attend.2 = (bf16[960,512]{1,0:T(8,128)(2,1)S(1)}, f32[5,8,512]{2,1,0:T(8,128)S(1)}) custom-call(bf16[1600,1024]{1,0:T(8,128)(2,1)S(1)} %get-tuple-element.108.qkv_ref, s32[2,1,512]{2,1,0:T(1,128)S(1)} %broadcast_in_dim.43.segr_ref, s32[2,512,1]{2,1,0:T(8,128)S(1)} %copy-done.9), custom_call_target="tpu_custom_call" | custom-call | flops 1 | bytes 1 | tf_op jit(solution)/shard_map/attend/pallas_call | solution.py:215
  69.8 3.8 collective-permute-start.12
  73.6 2.5 collective-permute-done.7
  76.1 1.7 collective-permute-start.10
  78.9 6.7 %attend.3 = (bf16[960,512]{1,0:T(8,128)(2,1)S(1)}, f32[5,8,512]{2,1,0:T(8,128)S(1)}) custom-call(bf16[1600,1024]{1,0:T(8,128)(2,1)S(1)} %get-tuple-element.108.qkv_ref, s32[2,1,512]{2,1,0:T(1,128)S(1)} %broadcast_in_dim.43.segr_ref, s32[2,512,1]{2,1,0:T(8,128)S(1)} %copy-done.10), custom_call_target="tpu_custom_call" | custom-call | flops 1 | bytes 1 | tf_op jit(solution)/shard_map/attend/pallas_call | solution.py:215
  86.3 1.8 maximum_select_fusion.6.refs_14_
  90.4 3.9 collective-permute-start.20
  95.7 7.7 %collective-permute-done.24.refs_15_ = bf16[480,640]{1,0:T(8,128)(2,1)S(1)} collective-permute-done((bf16[480,640]{1,0:T(8,128)(2,1)S(1)}, bf16[480,640]{1,0:T(8,128)(2,1)S(1)}, u32[]{:S(2)}, u32[]{:S(2)}) %collective-permute-start.24) | collective-permute-done | bytes 614432 | tf_op jit(solution)/shard_map/ppermute | solution.py:591
  103.9 5.1 %collective-permute-done.20.refs_9_ = bf16[240,1280]{1,0:T(8,128)(2,1)S(1)} collective-permute-done((bf16[240,1280]{1,0:T(8,128)(2,1)S(1)}, bf16[240,1280]{1,0:T(8,128)(2,1)S(1)}, u32[]{:S(2)}, u32[]{:S(2)}) %collective-permute-start.20) | collective-permute-done | bytes 614432 | tf_op jit(solution)/shard_map/ppermute | solution.py:591
  109.9 11.7 %collective-permute-done.16.refs_3_ = bf16[240,1280]{1,0:T(8,128)(2,1)S(1)} collective-permute-done((bf16[240,1280]{1,0:T(8,128)(2,1)S(1)}, bf16[240,1280]{1,0:T(8,128)(2,1)S(1)}, u32[]{:S(2)}, u32[]{:S(2)}) %collective-permute-start.16) | collective-permute-done | bytes 614432 | tf_op jit(solution)/shard_map/ppermute | solution.py:591
  124.9 7.1 %middle.1 = (f32[960,1024]{1,0:T(8,128)S(1)}, bf16[960,1024]{1,0:T(8,128)(2,1)S(1)}) custom-call(s32[4]{0:T(128)S(1)} %pad_add_fusion.where_ref, bf16[960,1024]{1,0:T(8,128)(2,1)S(1)} %bitcast.56, bf16[960,1024]{1,0:T(8,128)(2,1)S(1)} %constant_dynamic-update-slice_fusion.o_ref, bf16[960,128]{1,0:T(8,128)(2,1)S(1)} %copy-done.53, bf16[240,960]{1,0:T(8,128)(2,1)} %refs_0_.8, ...), custom_call_target="tpu_custom_call" | custom-call | flops 1 | bytes 1 | tf_op jit(solution)/shard_map/middle/pallas_call | solution.py:251
  133.3 1.9 copy-done.8
  140.7 50.4 %feed_forward.1 = (bf16[960,1024]{1,0:T(8,128)(2,1)}, f32[960,1024]{1,0:T(8,128)}, bf16[2560,1024]{1,0:T(8,128)(2,1)}, bf16[2560,1024]{1,0:T(8,128)(2,1)}, bf16[2560,1024]{1,0:T(8,128)(2,1)}) custom-call(s32[4]{0:T(128)} %copy-done.61, bf16[960,1024]{1,0:T(8,128)(2,1)} %copy-done.4, bf16[960,1024]{1,0:T(8,128)(2,1)} %bitcast.58, f32[960,1024]{1,0:T(8,128)} %copy-done.8, ...), custom_call_target="tpu_custom_call" | custom-call | flops 1 | bytes 1 | tf_op jit(solution)/shard_map/feed_forward/pallas_call | solution.py:302
  192.6 2.5 copy-done.14
  195.1 9.1 %ffn_grads.3 = (bf16[2,4,240,640]{3,2,1,0:T(8,128)(2,1)S(1)}, bf16[2,4,240,640]{3,2,1,0:T(8,128)(2,1)}) custom-call(s32[4]{0:T(128)S(1)} %copy-done.62, bf16[960,1024]{1,0:T(8,128)(2,1)S(1)} %bitcast.59, bf16[2560,1024]{1,0:T(8,128)(2,1)S(1)} %copy-done.14), custom_call_target="tpu_custom_call" | custom-call | flops 1 | bytes 1 | tf_op jit(solution)/shard_map/ffn_grads/pallas_call | solution.py:352
  205.0 2.5 copy-done.13
  207.5 8.6 %ffn_grads.4 = (bf16[2,4,240,640]{3,2,1,0:T(8,128)(2,1)S(1)}, bf16[2,4,240,640]{3,2,1,0:T(8,128)(2,1)}) custom-call(s32[4]{0:T(128)S(1)} %copy-done.62, bf16[960,1024]{1,0:T(8,128)(2,1)S(1)} %copy-done.5, bf16[2560,1024]{1,0:T(8,128)(2,1)S(1)} %copy-done.13), custom_call_target="tpu_custom_call" | custom-call | flops 1 | bytes 1 | tf_op jit(solution)/shard_map/ffn_grads/pallas_call | solution.py:352
  217.8 3.1 fusion
  220.9 8.2 %ffn_grads.5 = (bf16[2,4,240,640]{3,2,1,0:T(8,128)(2,1)S(1)}, bf16[2,4,240,640]{3,2,1,0:T(8,128)(2,1)S(1)}) custom-call(s32[4]{0:T(128)S(1)} %copy-done.62, bf16[960,1024]{1,0:T(8,128)(2,1)S(1)} %copy-done.5, bf16[2560,1024]{1,0:T(8,128)(2,1)S(1)} %bitcast.62), custom_call_target="tpu_custom_call" | custom-call | flops 1 | bytes 1 | tf_op jit(solution)/shard_map/ffn_grads/pallas_call | solution.py:352
  229.7 2.7 collective-permute-start.30
  233.7 1.7 collective-permute-start.31
  235.4 9.7 %branch.1 = (f32[960,1024]{1,0:T(8,128)S(1)}, bf16[960,1024]{1,0:T(8,128)(2,1)S(1)}, bf16[960,1024]{1,0:T(8,128)(2,1)S(1)}, f32[960,1]{1,0:T(8,128)S(1)}) custom-call(s32[4]{0:T(128)S(1)} %copy-done.62, f32[960,1024]{1,0:T(8,128)} %get-tuple-element.141.dh_ref, f32[960,1024]{1,0:T(8,128)} %copy-done.8, bf16[960,1024]{1,0:T(8,128)(2,1)S(1)} %bitcast.60, ...), custom_call_target="tpu_custom_call" | custom-call | flops 1 | bytes 1 | tf_op jit(solution)/shard_map/branch/pallas_call | solution.py:397
  245.1 1.9 copy-done.15
  247.1 3.6 add_convert_fusion
  250.7 2.9 collective-permute-start.32
  253.6 8.6 %attend_back.2 = bf16[1600,512]{1,0:T(8,128)(2,1)S(1)} custom-call(bf16[1600,1024]{1,0:T(8,128)(2,1)S(1)} %get-tuple-element.108.qkv_ref, bf16[960,512]{1,0:T(8,128)(2,1)S(1)} %copy-done.19, bf16[960,1024]{1,0:T(8,128)(2,1)S(1)} %get-tuple-element.150.do_ref, f32[5,8,512]{2,1,0:T(8,128)S(1)} %copy-done.58, s32[2,1,512]{2,1,0:T(1,128)S(1)} %broadcast_in_dim.43.segr_ref, ...), custom_call_target="tpu_custom_call" | custom-call | flops 1 | bytes 1 | tf_op jit(solution)/shard_map/attend_back/pallas_call | solution.py:453
  262.2 2.4 add_convert_fusion.13
  266.2 8.8 %attend_back.3 = bf16[1600,512]{1,0:T(8,128)(2,1)S(1)} custom-call(bf16[1600,1024]{1,0:T(8,128)(2,1)S(1)} %get-tuple-element.108.qkv_ref, bf16[960,512]{1,0:T(8,128)(2,1)S(1)} %copy-done.21, bf16[960,1024]{1,0:T(8,128)(2,1)S(1)} %get-tuple-element.150.do_ref, f32[5,8,512]{2,1,0:T(8,128)S(1)} %copy-done.60, s32[2,1,512]{2,1,0:T(1,128)S(1)} %broadcast_in_dim.43.segr_ref, ...), custom_call_target="tpu_custom_call" | custom-call | flops 1 | bytes 1 | tf_op jit(solution)/shard_map/attend_back/pallas_call | solution.py:453
  275.0 2.3 pad_maximum_fusion.dqkv_ref
  277.3 2.1 add_convert_fusion.12
  279.4 11.7 %weight_grads.1 = (bf16[2,4,128,640]{3,2,1,0:T(8,128)(2,1)S(1)}, bf16[2,4,128,640]{3,2,1,0:T(8,128)(2,1)}, bf16[2,4,112,640]{3,2,1,0:T(8,128)(2,1)S(1)}, bf16[2,4,112,640]{3,2,1,0:T(8,128)(2,1)S(1)}) custom-call(s32[4]{0:T(128)S(1)} %copy-done.62, bf16[960,1024]{1,0:T(8,128)(2,1)} %copy-done.29, bf16[1600,1024]{1,0:T(8,128)(2,1)} %pad_maximum_fusion.dqkv_ref, ...), custom_call_target="tpu_custom_call" | custom-call | flops 1 | bytes 1 | tf_op jit(solution)/shard_map/weight_grads/pallas_call | solution.py:503
  294.7 2.6 fusion.5
  297.7 4.0 add_convert_fusion.10
  301.6 1.7 collective-permute-start.40
  303.3 8.8 %collective-permute-start.38 = (bf16[1,1,2,240,640]{4,3,2,1,0:T(8,128)(2,1)}, bf16[1,1,2,240,640]{4,3,2,1,0:T(8,128)(2,1)}, u32[]{:S(2)}, u32[]{:S(2)}) collective-permute-start(bf16[1,1,2,240,640]{4,3,2,1,0:T(8,128)(2,1)} %get-tuple-element.249), channel_id=1, source_target_pairs={{0,2},{1,3},{2,0},{3,1},{4,6},{5,7},{6,4},{7,5},{8,10},{9,11},{10,... | collective-permute-start | bytes 1843208 | tf_op jit(solution)/shard_map/ppermute | solution.py:591
  312.2 2.1 copy-done.16
  314.3 11.5 %input_grads.1 = (bf16[960,1024]{1,0:T(8,128)(2,1)}, f32[960,1]{1,0:T(8,128)S(1)}) custom-call(s32[4]{0:T(128)S(1)} %copy-done.62, bf16[960,1024]{1,0:T(8,128)(2,1)S(1)} %bitcast.57, f32[960,1024]{1,0:T(8,128)S(1)} %copy-done.16, bf16[1600,1024]{1,0:T(8,128)(2,1)S(1)} %copy-done, bf16[240,960]{1,0:T(8,128)(2,1)S(1)} %copy-done.33, ...), custom_call_target="tpu_custom_call" | custom-call | flops 1 | bytes 1 | tf_op jit(solution)/shard_map/input_grads/pallas_call | solution.py:543
  326.1 1.8 add_convert_fusion.9
  328.0 1.8 collective-permute-start.37
  332.5 1.9 add_convert_fusion.8
  338.7 2.3 collective-permute-start.43
  340.9 5.6 %collective-permute-done.37 = bf16[1,1,2,240,640]{4,3,2,1,0:T(8,128)(2,1)S(1)} collective-permute-done((bf16[1,1,2,240,640]{4,3,2,1,0:T(8,128)(2,1)S(1)}, bf16[1,1,2,240,640]{4,3,2,1,0:T(8,128)(2,1)S(1)}, u32[]{:S(2)}, u32[]{:S(2)}) %collective-permute-start.37) | collective-permute-done | bytes 614432 | tf_op jit(solution)/shard_map/ppermute | solution.py:591
  352.0 6.9 %collective-permute-done.44 = bf16[2,1,2,112,640]{4,3,2,1,0:T(8,128)(2,1)S(1)} collective-permute-done((bf16[2,1,2,112,640]{4,3,2,1,0:T(8,128)(2,1)S(1)}, bf16[2,1,2,112,640]{4,3,2,1,0:T(8,128)(2,1)S(1)}, u32[]{:S(2)}, u32[]{:S(2)}) %collective-permute-start.44) | collective-permute-done | bytes 573472 | tf_op jit(solution)/shard_map/ppermute | solution.py:591
  358.9 4.1 collective-permute-start.48
  364.1 8.0 %collective-permute-done.43 = bf16[1,1,2,240,640]{4,3,2,1,0:T(8,128)(2,1)S(1)} collective-permute-done((bf16[1,1,2,240,640]{4,3,2,1,0:T(8,128)(2,1)S(1)}, bf16[1,1,2,240,640]{4,3,2,1,0:T(8,128)(2,1)S(1)}, u32[]{:S(2)}, u32[]{:S(2)}) %collective-permute-start.43) | collective-permute-done | bytes 614432 | tf_op jit(solution)/shard_map/ppermute | solution.py:591
  376.0 11.7 %collective-permute-start.54 = (bf16[1,1,2,240,640]{4,3,2,1,0:T(8,128)(2,1)S(1)}, bf16[1,1,2,240,640]{4,3,2,1,0:T(8,128)(2,1)S(1)}, u32[]{:S(2)}, u32[]{:S(2)}) collective-permute-start(bf16[1,1,2,240,640]{4,3,2,1,0:T(8,128)(2,1)S(1)} %add_convert_fusion.3), channel_id=1, source_target_pairs={{0,2},{1,3},{2,0},{3,1},{4,6},{5,7},{6,4},{7,5},{8,10},{9,11},{10,... | collective-permute-start | bytes 1843208 | tf_op jit(solution)/shard_map/ppermute | solution.py:591
  389.1 1.7 collective-permute-start.55
  391.9 2.2 collective-permute-start.50
  394.1 14.9 %collective-permute-done.46 = bf16[1,1,2,128,640]{4,3,2,1,0:T(8,128)(2,1)S(1)} collective-permute-done((bf16[1,1,2,128,640]{4,3,2,1,0:T(8,128)(2,1)S(1)}, bf16[1,1,2,128,640]{4,3,2,1,0:T(8,128)(2,1)S(1)}, u32[]{:S(2)}, u32[]{:S(2)}) %collective-permute-start.46) | collective-permute-done | bytes 327712 | tf_op jit(solution)/shard_map/ppermute | solution.py:591
  409.0 2.5 collective-permute-start.60
  411.6 1.7 collective-permute-start.49
  413.8 1.7 convert_bitcast_fusion
  415.5 15.1 %collective-permute-done.50 = bf16[1,1,2,112,640]{4,3,2,1,0:T(8,128)(2,1)S(1)} collective-permute-done((bf16[1,1,2,112,640]{4,3,2,1,0:T(8,128)(2,1)S(1)}, bf16[1,1,2,112,640]{4,3,2,1,0:T(8,128)(2,1)S(1)}, u32[]{:S(2)}, u32[]{:S(2)}) %collective-permute-start.50) | collective-permute-done | bytes 286752 | tf_op jit(solution)/shard_map/ppermute | solution.py:591
  435.0 2.2 collective-permute-start.61
  438.6 11.3 %collective-permute-start.53 = (bf16[1,1,2,112,640]{4,3,2,1,0:T(8,128)(2,1)S(1)}, bf16[1,1,2,112,640]{4,3,2,1,0:T(8,128)(2,1)S(1)}, u32[]{:S(2)}, u32[]{:S(2)}) collective-permute-start(bf16[1,1,2,112,640]{4,3,2,1,0:T(8,128)(2,1)S(1)} %add_convert_fusion.19), channel_id=1, source_target_pairs={{0,2},{1,3},{2,0},{3,1},{4,6},{5,7},{6,4},{7,5},{8,10},{9,11},{10,... | collective-permute-start | bytes 860168 | tf_op jit(solution)/shard_map/ppermute | solution.py:591
  (328 shorter events, 86.4 us)
Async XLA Ops:
  4.6 12.4 %collective-permute-start.4 = (bf16[240,768]{1,0:T(8,128)(2,1)S(1)}, bf16[240,768]{1,0:T(8,128)(2,1)S(1)}, u32[]{:S(2)}, u32[]{:S(2)}) collective-permute-start(bf16[240,768]{1,0:T(8,128)(2,1)S(1)} %concatenate.83.refs_4_), channel_id=1, source_target_pairs={{0,16},{8,24},{16,0},{24,8},{1,17},{9,25},{17,1},{25,9},{2,18},{10... | collective-permute-start | bytes 1105928 | tf_op jit(solution)/shard_map/ppermute | solution.py:587
  7.6 24.9 %collective-permute-start.3 = (bf16[240,768]{1,0:T(8,128)(2,1)S(1)}, bf16[240,768]{1,0:T(8,128)(2,1)S(1)}, u32[]{:S(2)}, u32[]{:S(2)}) collective-permute-start(bf16[240,768]{1,0:T(8,128)(2,1)S(1)} %concatenate.83.refs_4_), channel_id=1, source_target_pairs={{0,8},{8,0},{16,24},{24,16},{1,9},{9,1},{17,25},{25,17},{2,10},{10... | collective-permute-start | bytes 1105928 | tf_op jit(solution)/shard_map/ppermute | solution.py:589
  7.7 19.1 %collective-permute-start.1 = (bf16[240,960]{1,0:T(8,128)(2,1)S(1)}, bf16[240,960]{1,0:T(8,128)(2,1)S(1)}, u32[]{:S(2)}, u32[]{:S(2)}) collective-permute-start(bf16[240,960]{1,0:T(8,128)(2,1)S(1)} %copy-done.31), channel_id=1, source_target_pairs={{0,16},{8,24},{16,0},{24,8},{1,17},{9,25},{17,1},{25,9},{2,18},{10... | collective-permute-start | bytes 1382408 | tf_op jit(solution)/shard_map/ppermute | solution.py:587
  7.8 25.8 %collective-permute-start = (bf16[240,960]{1,0:T(8,128)(2,1)S(1)}, bf16[240,960]{1,0:T(8,128)(2,1)S(1)}, u32[]{:S(2)}, u32[]{:S(2)}) collective-permute-start(bf16[240,960]{1,0:T(8,128)(2,1)S(1)} %copy-done.31), channel_id=1, source_target_pairs={{0,8},{8,0},{16,24},{24,16},{1,9},{9,1},{17,25},{25,17},{2,10},{10... | collective-permute-start | bytes 1382408 | tf_op jit(solution)/shard_map/ppermute | solution.py:589
  17.1 17.4 %collective-permute-start.5 = (bf16[240,768]{1,0:T(8,128)(2,1)S(1)}, bf16[240,768]{1,0:T(8,128)(2,1)}, u32[]{:S(2)}, u32[]{:S(2)}) collective-permute-start(bf16[240,768]{1,0:T(8,128)(2,1)S(1)} %collective-permute-done.4.refs_6_), channel_id=1, source_target_pairs={{0,8},{8,0},{16,24},{24,16},{1,9},{9,1},{17,25},{25,17},{2,10},{10... | collective-permute-start | bytes 1105928 | tf_op jit(solution)/shard_map/ppermute | solution.py:589
  26.8 7.7 %collective-permute-start.2 = (bf16[240,960]{1,0:T(8,128)(2,1)S(1)}, bf16[240,960]{1,0:T(8,128)(2,1)S(1)}, u32[]{:S(2)}, u32[]{:S(2)}) collective-permute-start(bf16[240,960]{1,0:T(8,128)(2,1)S(1)} %collective-permute-done.1.refs_2_), channel_id=1, source_target_pairs={{0,8},{8,0},{16,24},{24,16},{1,9},{9,1},{17,25},{25,17},{2,10},{10... | collective-permute-start | bytes 1382408 | tf_op jit(solution)/shard_map/ppermute | solution.py:589
  29.0 40.7 %collective-permute-start.9 = (bf16[240,640]{1,0:T(8,128)(2,1)}, bf16[240,640]{1,0:T(8,128)(2,1)}, u32[]{:S(2)}, u32[]{:S(2)}) collective-permute-start(bf16[240,640]{1,0:T(8,128)(2,1)} %dynamic-slice_bitcast_fusion), channel_id=1, source_target_pairs={{0,16},{8,24},{16,0},{24,8},{1,17},{9,25},{17,1},{25,9},{2,18},{10... | collective-permute-start | bytes 921608 | tf_op jit(solution)/shard_map/ppermute | solution.py:587
  33.3 40.3 %collective-permute-start.8 = (bf16[240,640]{1,0:T(8,128)(2,1)}, bf16[240,640]{1,0:T(8,128)(2,1)}, u32[]{:S(2)}, u32[]{:S(2)}) collective-permute-start(bf16[240,640]{1,0:T(8,128)(2,1)} %constant_dynamic-slice_fusion.1), channel_id=1, source_target_pairs={{0,16},{8,24},{16,0},{24,8},{1,17},{9,25},{17,1},{25,9},{2,18},{10... | collective-permute-start | bytes 921608 | tf_op jit(solution)/shard_map/ppermute | solution.py:587
  55.6 22.3 %collective-permute-start.6 = (bf16[240,960]{1,0:T(8,128)(2,1)}, bf16[240,960]{1,0:T(8,128)(2,1)}, u32[]{:S(2)}, u32[]{:S(2)}) collective-permute-start(bf16[240,960]{1,0:T(8,128)(2,1)} %refs_0_.8), channel_id=1, source_target_pairs={{0,8},{8,0},{16,24},{24,16},{1,9},{9,1},{17,25},{25,17},{2,10},{10... | collective-permute-start | bytes 1382408 | tf_op jit(solution)/shard_map/ppermute | solution.py:589
  55.6 32.9 %collective-permute-start.13 = (bf16[240,960]{1,0:T(8,128)(2,1)}, bf16[240,960]{1,0:T(8,128)(2,1)}, u32[]{:S(2)}, u32[]{:S(2)}) collective-permute-start(bf16[240,960]{1,0:T(8,128)(2,1)} %refs_0_.8), channel_id=1, source_target_pairs={{0,16},{8,24},{16,0},{24,8},{1,17},{9,25},{17,1},{25,9},{2,18},{10... | collective-permute-start | bytes 1382408 | tf_op jit(solution)/shard_map/ppermute | solution.py:587
  59.0 17.1 %collective-permute-start.7 = (bf16[240,640]{1,0:T(8,128)(2,1)}, bf16[240,640]{1,0:T(8,128)(2,1)}, u32[]{:S(2)}, u32[]{:S(2)}) collective-permute-start(bf16[240,640]{1,0:T(8,128)(2,1)} %constant_dynamic-slice_fusion.2), channel_id=1, source_target_pairs={{0,16},{8,24},{16,0},{24,8},{1,17},{9,25},{17,1},{25,9},{2,18},{10... | collective-permute-start | bytes 921608 | tf_op jit(solution)/shard_map/ppermute | solution.py:587
  69.8 16.6 %collective-permute-start.12 = (bf16[240,640]{1,0:T(8,128)(2,1)}, bf16[240,640]{1,0:T(8,128)(2,1)}, u32[]{:S(2)}, u32[]{:S(2)}) collective-permute-start(bf16[240,640]{1,0:T(8,128)(2,1)} %collective-permute-done.9), channel_id=1, source_target_pairs={{0,6},{1,7},{2,4},{3,5},{4,2},{5,3},{6,0},{7,1},{8,14},{9,15},{10,... | collective-permute-start | bytes 921608 | tf_op jit(solution)/shard_map/ppermute | solution.py:591
  73.6 15.4 %collective-permute-start.11 = (bf16[240,640]{1,0:T(8,128)(2,1)}, bf16[240,640]{1,0:T(8,128)(2,1)}, u32[]{:S(2)}, u32[]{:S(2)}) collective-permute-start(bf16[240,640]{1,0:T(8,128)(2,1)} %collective-permute-done.8), channel_id=1, source_target_pairs={{0,2},{1,3},{2,0},{3,1},{4,6},{5,7},{6,4},{7,5},{8,10},{9,11},{10,... | collective-permute-start | bytes 921608 | tf_op jit(solution)/shard_map/ppermute | solution.py:591
  76.1 18.2 %collective-permute-start.10 = (bf16[240,640]{1,0:T(8,128)(2,1)}, bf16[240,640]{1,0:T(8,128)(2,1)S(1)}, u32[]{:S(2)}, u32[]{:S(2)}) collective-permute-start(bf16[240,640]{1,0:T(8,128)(2,1)} %collective-permute-done.7), channel_id=1, source_target_pairs={{0,1},{1,0},{2,3},{3,2},{4,5},{5,4},{6,7},{7,6},{8,9},{9,8},{10,11... | collective-permute-start | bytes 921608 | tf_op jit(solution)/shard_map/ppermute | solution.py:591
  88.1 15.3 %collective-permute-start.24 = (bf16[480,640]{1,0:T(8,128)(2,1)S(1)}, bf16[480,640]{1,0:T(8,128)(2,1)S(1)}, u32[]{:S(2)}, u32[]{:S(2)}) collective-permute-start(bf16[480,640]{1,0:T(8,128)(2,1)S(1)} %maximum_select_fusion.6.refs_14_), channel_id=1, source_target_pairs={{0,1},{1,0},{2,3},{3,2},{4,5},{5,4},{6,7},{7,6},{8,9},{9,8},{10,11... | collective-permute-start | bytes 1843208 | tf_op jit(solution)/shard_map/ppermute | solution.py:591
  88.5 14.9 %collective-permute-start.25 = (bf16[480,640]{1,0:T(8,128)(2,1)S(1)}, bf16[480,640]{1,0:T(8,128)(2,1)S(1)}, u32[]{:S(2)}, u32[]{:S(2)}) collective-permute-start(bf16[480,640]{1,0:T(8,128)(2,1)S(1)} %maximum_select_fusion.6.refs_14_), channel_id=1, source_target_pairs={{0,8},{8,0},{16,24},{24,16},{1,9},{9,1},{17,25},{25,17},{2,10},{10... | collective-permute-start | bytes 1843208 | tf_op jit(solution)/shard_map/ppermute | solution.py:589
  88.5 7.1 %collective-permute-start.14 = (bf16[240,960]{1,0:T(8,128)(2,1)}, bf16[240,960]{1,0:T(8,128)(2,1)S(1)}, u32[]{:S(2)}, u32[]{:S(2)}) collective-permute-start(bf16[240,960]{1,0:T(8,128)(2,1)} %collective-permute-done.13.refs_2_), channel_id=1, source_target_pairs={{0,8},{8,0},{16,24},{24,16},{1,9},{9,1},{17,25},{25,17},{2,10},{10... | collective-permute-start | bytes 1382408 | tf_op jit(solution)/shard_map/ppermute | solution.py:589
  90.4 18.6 %collective-permute-start.20 = (bf16[240,1280]{1,0:T(8,128)(2,1)S(1)}, bf16[240,1280]{1,0:T(8,128)(2,1)S(1)}, u32[]{:S(2)}, u32[]{:S(2)}) collective-permute-start(bf16[240,1280]{1,0:T(8,128)(2,1)S(1)} %maximum_select_fusion.5.refs_8_), channel_id=1, source_target_pairs={{0,6},{1,7},{2,4},{3,5},{4,2},{5,3},{6,0},{7,1},{8,14},{9,15},{10,... | collective-permute-start | bytes 1843208 | tf_op jit(solution)/shard_map/ppermute | solution.py:591
  95.5 26.1 %collective-permute-start.16 = (bf16[240,1280]{1,0:T(8,128)(2,1)S(1)}, bf16[240,1280]{1,0:T(8,128)(2,1)S(1)}, u32[]{:S(2)}, u32[]{:S(2)}) collective-permute-start(bf16[240,1280]{1,0:T(8,128)(2,1)S(1)} %maximum_select_fusion.4.refs_2_), channel_id=1, source_target_pairs={{0,2},{1,3},{2,0},{3,1},{4,6},{5,7},{6,4},{7,5},{8,10},{9,11},{10,... | collective-permute-start | bytes 1843208 | tf_op jit(solution)/shard_map/ppermute | solution.py:591
  95.6 40.7 %collective-permute-start.23 = (bf16[960,640]{1,0:T(8,128)(2,1)S(1)}, bf16[960,640]{1,0:T(8,128)(2,1)S(1)}, u32[]{:S(2)}, u32[]{:S(2)}) collective-permute-start(bf16[960,640]{1,0:T(8,128)(2,1)S(1)} %bitcast.91), channel_id=1, source_target_pairs={{0,8},{8,0},{16,24},{24,16},{1,9},{9,1},{17,25},{25,17},{2,10},{10... | collective-permute-start | bytes 3686408 | tf_op jit(solution)/shard_map/ppermute | solution.py:589
  103.4 33.3 %collective-permute-start.15 = (bf16[240,2560]{1,0:T(8,128)(2,1)S(1)}, bf16[240,2560]{1,0:T(8,128)(2,1)S(1)}, u32[]{:S(2)}, u32[]{:S(2)}) collective-permute-start(bf16[240,2560]{1,0:T(8,128)(2,1)S(1)} %copy-done.71), channel_id=1, source_target_pairs={{0,8},{8,0},{16,24},{24,16},{1,9},{9,1},{17,25},{25,17},{2,10},{10... | collective-permute-start | bytes 3686408 | tf_op jit(solution)/shard_map/ppermute | solution.py:589
  103.4 32.3 %collective-permute-start.21 = (bf16[240,1280]{1,0:T(8,128)(2,1)S(1)}, bf16[240,1280]{1,0:T(8,128)(2,1)}, u32[]{:S(2)}, u32[]{:S(2)}) collective-permute-start(bf16[240,1280]{1,0:T(8,128)(2,1)S(1)} %maximum_select_fusion.5.refs_8_), channel_id=1, source_target_pairs={{0,8},{8,0},{16,24},{24,16},{1,9},{9,1},{17,25},{25,17},{2,10},{10... | collective-permute-start | bytes 1843208 | tf_op jit(solution)/shard_map/ppermute | solution.py:589
  109.0 27.2 %collective-permute-start.17 = (bf16[240,1280]{1,0:T(8,128)(2,1)S(1)}, bf16[240,1280]{1,0:T(8,128)(2,1)}, u32[]{:S(2)}, u32[]{:S(2)}) collective-permute-start(bf16[240,1280]{1,0:T(8,128)(2,1)S(1)} %maximum_select_fusion.4.refs_2_), channel_id=1, source_target_pairs={{0,8},{8,0},{16,24},{24,16},{1,9},{9,1},{17,25},{25,17},{2,10},{10... | collective-permute-start | bytes 1843208 | tf_op jit(solution)/shard_map/ppermute | solution.py:589
  122.4 14.3 %collective-permute-start.19 = (bf16[240,2560]{1,0:T(8,128)(2,1)S(1)}, bf16[240,2560]{1,0:T(8,128)(2,1)S(1)}, u32[]{:S(2)}, u32[]{:S(2)}) collective-permute-start(bf16[240,2560]{1,0:T(8,128)(2,1)S(1)} %copy-done.72), channel_id=1, source_target_pairs={{0,8},{8,0},{16,24},{24,16},{1,9},{9,1},{17,25},{25,17},{2,10},{10... | collective-permute-start | bytes 3686408 | tf_op jit(solution)/shard_map/ppermute | solution.py:589
  135.7 2.2 collective-permute-start.26
  136.2 2.8 collective-permute-start.22
  136.3 3.5 collective-permute-start.18
  140.7 50.4 %copy-start.62 = (s32[4]{0:T(128)S(1)}, s32[4]{0:T(128)}, u32[]{:S(2)}) copy-start(s32[4]{0:T(128)} %copy-done.61) | copy-start | bytes 52
  204.2 13.6 %collective-permute-start.28 = (bf16[2,4,240,640]{3,2,1,0:T(8,128)(2,1)}, bf16[2,4,240,640]{3,2,1,0:T(8,128)(2,1)}, u32[]{:S(2)}, u32[]{:S(2)}) collective-permute-start(bf16[2,4,240,640]{3,2,1,0:T(8,128)(2,1)} %get-tuple-element.131), channel_id=1, source_target_pairs={{0,8},{8,0},{16,24},{24,16},{1,9},{9,1},{17,25},{25,17},{2,10},{10... | collective-permute-start | bytes 7372808 | tf_op jit(solution)/shard_map/ppermute | solution.py:589
  217.5 14.8 %collective-permute-start.27 = (bf16[2,4,240,640]{3,2,1,0:T(8,128)(2,1)}, bf16[2,4,240,640]{3,2,1,0:T(8,128)(2,1)S(1)}, u32[]{:S(2)}, u32[]{:S(2)}) collective-permute-start(bf16[2,4,240,640]{3,2,1,0:T(8,128)(2,1)} %get-tuple-element.134), channel_id=1, source_target_pairs={{0,8},{8,0},{16,24},{24,16},{1,9},{9,1},{17,25},{25,17},{2,10},{10... | collective-permute-start | bytes 7372808 | tf_op jit(solution)/shard_map/ppermute | solution.py:589
  229.1 17.9 %collective-permute-start.29 = (bf16[2,4,240,640]{3,2,1,0:T(8,128)(2,1)S(1)}, bf16[2,4,240,640]{3,2,1,0:T(8,128)(2,1)}, u32[]{:S(2)}, u32[]{:S(2)}) collective-permute-start(bf16[2,4,240,640]{3,2,1,0:T(8,128)(2,1)S(1)} %get-tuple-element.139), channel_id=1, source_target_pairs={{0,8},{8,0},{16,24},{24,16},{1,9},{9,1},{17,25},{25,17},{2,10},{10... | collective-permute-start | bytes 7372808 | tf_op jit(solution)/shard_map/ppermute | solution.py:589
  229.7 32.5 %collective-permute-start.30 = (bf16[1,2,2,240,640]{4,3,2,1,0:T(8,128)(2,1)}, bf16[1,2,2,240,640]{4,3,2,1,0:T(8,128)(2,1)}, u32[]{:S(2)}, u32[]{:S(2)}) collective-permute-start(bf16[1,2,2,240,640]{4,3,2,1,0:T(8,128)(2,1)} %fusion), channel_id=1, source_target_pairs={{0,16},{8,24},{16,0},{24,8},{1,17},{9,25},{17,1},{25,9},{2,18},{10... | collective-permute-start | bytes 3686408 | tf_op jit(solution)/shard_map/ppermute | solution.py:587
  232.4 44.9 %copy-start.70 = (bf16[2,4,240,640]{3,2,1,0:T(8,128)(2,1)}, bf16[2,4,240,640]{3,2,1,0:T(8,128)(2,1)S(1)}, u32[]{:S(2)}) copy-start(bf16[2,4,240,640]{3,2,1,0:T(8,128)(2,1)S(1)} %collective-permute-done.27) | copy-start | bytes 7372804
  233.7 41.3 %collective-permute-start.31 = (bf16[2,1,2,240,640]{4,3,2,1,0:T(8,128)(2,1)}, bf16[2,1,2,240,640]{4,3,2,1,0:T(8,128)(2,1)}, u32[]{:S(2)}, u32[]{:S(2)}) collective-permute-start(bf16[2,1,2,240,640]{4,3,2,1,0:T(8,128)(2,1)} %add_convert_fusion.1), channel_id=1, source_target_pairs={{0,2},{1,3},{2,0},{3,1},{4,6},{5,7},{6,4},{7,5},{8,10},{9,11},{10,... | collective-permute-start | bytes 3686408 | tf_op jit(solution)/shard_map/ppermute | solution.py:591
  250.7 47.0 %collective-permute-start.32 = (bf16[2,1,2,240,640]{4,3,2,1,0:T(8,128)(2,1)}, bf16[2,1,2,240,640]{4,3,2,1,0:T(8,128)(2,1)}, u32[]{:S(2)}, u32[]{:S(2)}) collective-permute-start(bf16[2,1,2,240,640]{4,3,2,1,0:T(8,128)(2,1)} %add_convert_fusion), channel_id=1, source_target_pairs={{0,6},{1,7},{2,4},{3,5},{4,2},{5,3},{6,0},{7,1},{8,14},{9,15},{10,... | collective-permute-start | bytes 3686408 | tf_op jit(solution)/shard_map/ppermute | solution.py:591
  264.7 33.0 %collective-permute-start.33 = (bf16[1,1,2,240,640]{4,3,2,1,0:T(8,128)(2,1)}, bf16[1,1,2,240,640]{4,3,2,1,0:T(8,128)(2,1)}, u32[]{:S(2)}, u32[]{:S(2)}) collective-permute-start(bf16[1,1,2,240,640]{4,3,2,1,0:T(8,128)(2,1)} %add_convert_fusion.13), channel_id=1, source_target_pairs={{0,1},{1,0},{2,3},{3,2},{4,5},{5,4},{6,7},{7,6},{8,9},{9,8},{10,11... | collective-permute-start | bytes 1843208 | tf_op jit(solution)/shard_map/ppermute | solution.py:591
  294.2 33.7 %collective-permute-start.34 = (bf16[2,4,128,640]{3,2,1,0:T(8,128)(2,1)}, bf16[2,4,128,640]{3,2,1,0:T(8,128)(2,1)}, u32[]{:S(2)}, u32[]{:S(2)}) collective-permute-start(bf16[2,4,128,640]{3,2,1,0:T(8,128)(2,1)} %get-tuple-element.161), channel_id=1, source_target_pairs={{0,8},{8,0},{16,24},{24,16},{1,9},{9,1},{17,25},{25,17},{2,10},{10... | collective-permute-start | bytes 3932168 | tf_op jit(solution)/shard_map/ppermute | solution.py:589
  294.4 31.7 %collective-permute-start.35 = (bf16[1,1,2,240,640]{4,3,2,1,0:T(8,128)(2,1)}, bf16[1,1,2,240,640]{4,3,2,1,0:T(8,128)(2,1)}, u32[]{:S(2)}, u32[]{:S(2)}) collective-permute-start(bf16[1,1,2,240,640]{4,3,2,1,0:T(8,128)(2,1)} %add_convert_fusion.12), channel_id=1, source_target_pairs={{0,16},{8,24},{16,0},{24,8},{1,17},{9,25},{17,1},{25,9},{2,18},{10... | collective-permute-start | bytes 1843208 | tf_op jit(solution)/shard_map/ppermute | solution.py:587
  297.3 37.1 %collective-permute-start.39 = (bf16[2,4,112,640]{3,2,1,0:T(8,128)(2,1)}, bf16[2,4,112,640]{3,2,1,0:T(8,128)(2,1)}, u32[]{:S(2)}, u32[]{:S(2)}) collective-permute-start(bf16[2,4,112,640]{3,2,1,0:T(8,128)(2,1)} %copy-done.63), channel_id=1, source_target_pairs={{0,8},{8,0},{16,24},{24,16},{1,9},{9,1},{17,25},{25,17},{2,10},{10... | collective-permute-start | bytes 3440648 | tf_op jit(solution)/shard_map/ppermute | solution.py:589
  301.6 29.4 %collective-permute-start.40 = (bf16[1,1,2,240,640]{4,3,2,1,0:T(8,128)(2,1)}, bf16[1,1,2,240,640]{4,3,2,1,0:T(8,128)(2,1)}, u32[]{:S(2)}, u32[]{:S(2)}) collective-permute-start(bf16[1,1,2,240,640]{4,3,2,1,0:T(8,128)(2,1)} %get-tuple-element.250), channel_id=1, source_target_pairs={{0,16},{8,24},{16,0},{24,8},{1,17},{9,25},{17,1},{25,9},{2,18},{10... | collective-permute-start | bytes 1843208 | tf_op jit(solution)/shard_map/ppermute | solution.py:587
  303.3 33.8 %collective-permute-start.38 = (bf16[1,1,2,240,640]{4,3,2,1,0:T(8,128)(2,1)}, bf16[1,1,2,240,640]{4,3,2,1,0:T(8,128)(2,1)}, u32[]{:S(2)}, u32[]{:S(2)}) collective-permute-start(bf16[1,1,2,240,640]{4,3,2,1,0:T(8,128)(2,1)} %get-tuple-element.249), channel_id=1, source_target_pairs={{0,2},{1,3},{2,0},{3,1},{4,6},{5,7},{6,4},{7,5},{8,10},{9,11},{10,... | collective-permute-start | bytes 1843208 | tf_op jit(solution)/shard_map/ppermute | solution.py:591
  326.1 12.6 %collective-permute-start.57 = (f32[1920]{0:T(1024)S(1)}, f32[1920]{0:T(1024)S(1)}, u32[]{:S(2)}, u32[]{:S(2)}) collective-permute-start(f32[1920]{0:T(1024)S(1)} %reshape.221), channel_id=1, source_target_pairs={{0,8},{8,0},{16,24},{24,16},{1,9},{9,1},{17,25},{25,17},{2,10},{10... | collective-permute-start | bytes 23048 | tf_op jit(solution)/shard_map/ppermute | solution.py:589
  328.0 18.6 %collective-permute-start.37 = (bf16[1,1,2,240,640]{4,3,2,1,0:T(8,128)(2,1)S(1)}, bf16[1,1,2,240,640]{4,3,2,1,0:T(8,128)(2,1)S(1)}, u32[]{:S(2)}, u32[]{:S(2)}) collective-permute-start(bf16[1,1,2,240,640]{4,3,2,1,0:T(8,128)(2,1)S(1)} %add_convert_fusion.9), channel_id=1, source_target_pairs={{0,6},{1,7},{2,4},{3,5},{4,2},{5,3},{6,0},{7,1},{8,14},{9,15},{10,... | collective-permute-start | bytes 1843208 | tf_op jit(solution)/shard_map/ppermute | solution.py:591
  331.0 17.1 %collective-permute-start.36 = (bf16[1,2,2,128,640]{4,3,2,1,0:T(8,128)(2,1)S(1)}, bf16[1,2,2,128,640]{4,3,2,1,0:T(8,128)(2,1)S(1)}, u32[]{:S(2)}, u32[]{:S(2)}) collective-permute-start(bf16[1,2,2,128,640]{4,3,2,1,0:T(8,128)(2,1)S(1)} %fusion.1), channel_id=1, source_target_pairs={{0,16},{8,24},{16,0},{24,8},{1,17},{9,25},{17,1},{25,9},{2,18},{10... | collective-permute-start | bytes 1966088 | tf_op jit(solution)/shard_map/ppermute | solution.py:587
  334.4 16.4 %collective-permute-start.45 = (bf16[1,1,2,240,640]{4,3,2,1,0:T(8,128)(2,1)S(1)}, bf16[1,1,2,240,640]{4,3,2,1,0:T(8,128)(2,1)S(1)}, u32[]{:S(2)}, u32[]{:S(2)}) collective-permute-start(bf16[1,1,2,240,640]{4,3,2,1,0:T(8,128)(2,1)S(1)} %add_convert_fusion.8), channel_id=1, source_target_pairs={{0,1},{1,0},{2,3},{3,2},{4,5},{5,4},{6,7},{7,6},{8,9},{9,8},{10,11... | collective-permute-start | bytes 1843208 | tf_op jit(solution)/shard_map/ppermute | solution.py:591
  337.2 21.7 %collective-permute-start.44 = (bf16[2,1,2,112,640]{4,3,2,1,0:T(8,128)(2,1)S(1)}, bf16[2,1,2,112,640]{4,3,2,1,0:T(8,128)(2,1)S(1)}, u32[]{:S(2)}, u32[]{:S(2)}) collective-permute-start(bf16[2,1,2,112,640]{4,3,2,1,0:T(8,128)(2,1)S(1)} %add_convert_fusion.14), channel_id=1, source_target_pairs={{0,2},{1,3},{2,0},{3,1},{4,6},{5,7},{6,4},{7,5},{8,10},{9,11},{10,... | collective-permute-start | bytes 1720328 | tf_op jit(solution)/shard_map/ppermute | solution.py:591
  338.7 33.4 %collective-permute-start.43 = (bf16[1,1,2,240,640]{4,3,2,1,0:T(8,128)(2,1)S(1)}, bf16[1,1,2,240,640]{4,3,2,1,0:T(8,128)(2,1)S(1)}, u32[]{:S(2)}, u32[]{:S(2)}) collective-permute-start(bf16[1,1,2,240,640]{4,3,2,1,0:T(8,128)(2,1)S(1)} %add_convert_fusion.7), channel_id=1, source_target_pairs={{0,6},{1,7},{2,4},{3,5},{4,2},{5,3},{6,0},{7,1},{8,14},{9,15},{10,... | collective-permute-start | bytes 1843208 | tf_op jit(solution)/shard_map/ppermute | solution.py:591
  346.6 27.1 %collective-permute-start.58 = (f32[1920]{0:T(1024)S(1)}, f32[1920]{0:T(1024)S(1)}, u32[]{:S(2)}, u32[]{:S(2)}) collective-permute-start(f32[1920]{0:T(1024)S(1)} %add.202), channel_id=1, source_target_pairs={{0,16},{8,24},{16,0},{24,8},{1,17},{9,25},{17,1},{25,9},{2,18},{10... | collective-permute-start | bytes 23048 | tf_op jit(solution)/shard_map/ppermute | solution.py:587
  348.2 27.1 %collective-permute-start.42 = (bf16[1,1,2,240,640]{4,3,2,1,0:T(8,128)(2,1)S(1)}, bf16[1,1,2,240,640]{4,3,2,1,0:T(8,128)(2,1)S(1)}, u32[]{:S(2)}, u32[]{:S(2)}) collective-permute-start(bf16[1,1,2,240,640]{4,3,2,1,0:T(8,128)(2,1)S(1)} %add_convert_fusion.6), channel_id=1, source_target_pairs={{0,1},{1,0},{2,3},{3,2},{4,5},{5,4},{6,7},{7,6},{8,9},{9,8},{10,11... | collective-permute-start | bytes 1843208 | tf_op jit(solution)/shard_map/ppermute | solution.py:591
  350.9 25.1 %collective-permute-start.41 = (bf16[1,1,2,128,640]{4,3,2,1,0:T(8,128)(2,1)S(1)}, bf16[1,1,2,128,640]{4,3,2,1,0:T(8,128)(2,1)S(1)}, u32[]{:S(2)}, u32[]{:S(2)}) collective-permute-start(bf16[1,1,2,128,640]{4,3,2,1,0:T(8,128)(2,1)S(1)} %add_convert_fusion.18), channel_id=1, source_target_pairs={{0,1},{1,0},{2,3},{3,2},{4,5},{5,4},{6,7},{7,6},{8,9},{9,8},{10,11... | collective-permute-start | bytes 983048 | tf_op jit(solution)/shard_map/ppermute | solution.py:591
  358.9 29.9 %collective-permute-start.48 = (bf16[1,1,2,240,640]{4,3,2,1,0:T(8,128)(2,1)S(1)}, bf16[1,1,2,240,640]{4,3,2,1,0:T(8,128)(2,1)S(1)}, u32[]{:S(2)}, u32[]{:S(2)}) collective-permute-start(bf16[1,1,2,240,640]{4,3,2,1,0:T(8,128)(2,1)S(1)} %add_convert_fusion.5), channel_id=1, source_target_pairs={{0,2},{1,3},{2,0},{3,1},{4,6},{5,7},{6,4},{7,5},{8,10},{9,11},{10,... | collective-permute-start | bytes 1843208 | tf_op jit(solution)/shard_map/ppermute | solution.py:591
  372.1 17.0 %collective-permute-start.47 = (bf16[1,1,2,112,640]{4,3,2,1,0:T(8,128)(2,1)S(1)}, bf16[1,1,2,112,640]{4,3,2,1,0:T(8,128)(2,1)S(1)}, u32[]{:S(2)}, u32[]{:S(2)}) collective-permute-start(bf16[1,1,2,112,640]{4,3,2,1,0:T(8,128)(2,1)S(1)} %add_convert_fusion.22), channel_id=1, source_target_pairs={{0,16},{8,24},{16,0},{24,8},{1,17},{9,25},{17,1},{25,9},{2,18},{10... | collective-permute-start | bytes 860168 | tf_op jit(solution)/shard_map/ppermute | solution.py:587
  373.7 37.9 %collective-permute-start.56 = (bf16[1,1,2,240,640]{4,3,2,1,0:T(8,128)(2,1)S(1)}, bf16[1,1,2,240,640]{4,3,2,1,0:T(8,128)(2,1)S(1)}, u32[]{:S(2)}, u32[]{:S(2)}) collective-permute-start(bf16[1,1,2,240,640]{4,3,2,1,0:T(8,128)(2,1)S(1)} %add_convert_fusion.4), channel_id=1, source_target_pairs={{0,1},{1,0},{2,3},{3,2},{4,5},{5,4},{6,7},{7,6},{8,9},{9,8},{10,11... | collective-permute-start | bytes 1843208 | tf_op jit(solution)/shard_map/ppermute | solution.py:591
  375.3 16.6 %collective-permute-start.59 = (f32[1920]{0:T(1024)S(1)}, f32[1920]{0:T(1024)S(1)}, u32[]{:S(2)}, u32[]{:S(2)}) collective-permute-start(f32[1920]{0:T(1024)S(1)} %add.203), channel_id=1, source_target_pairs={{0,1},{1,0},{2,3},{3,2},{4,5},{5,4},{6,7},{7,6},{8,9},{9,8},{10,11... | collective-permute-start | bytes 23048 | tf_op jit(solution)/shard_map/ppermute | solution.py:591
  376.0 37.6 %collective-permute-start.54 = (bf16[1,1,2,240,640]{4,3,2,1,0:T(8,128)(2,1)S(1)}, bf16[1,1,2,240,640]{4,3,2,1,0:T(8,128)(2,1)S(1)}, u32[]{:S(2)}, u32[]{:S(2)}) collective-permute-start(bf16[1,1,2,240,640]{4,3,2,1,0:T(8,128)(2,1)S(1)} %add_convert_fusion.3), channel_id=1, source_target_pairs={{0,2},{1,3},{2,0},{3,1},{4,6},{5,7},{6,4},{7,5},{8,10},{9,11},{10,... | collective-permute-start | bytes 1843208 | tf_op jit(solution)/shard_map/ppermute | solution.py:591
  388.8 20.2 %collective-permute-start.46 = (bf16[1,1,2,128,640]{4,3,2,1,0:T(8,128)(2,1)S(1)}, bf16[1,1,2,128,640]{4,3,2,1,0:T(8,128)(2,1)S(1)}, u32[]{:S(2)}, u32[]{:S(2)}) collective-permute-start(bf16[1,1,2,128,640]{4,3,2,1,0:T(8,128)(2,1)S(1)} %add_convert_fusion.17), channel_id=1, source_target_pairs={{0,2},{1,3},{2,0},{3,1},{4,6},{5,7},{6,4},{7,5},{8,10},{9,11},{10,... | collective-permute-start | bytes 983048 | tf_op jit(solution)/shard_map/ppermute | solution.py:591
  389.1 61.6 %collective-permute-start.55 = (bf16[1,1,2,240,640]{4,3,2,1,0:T(8,128)(2,1)S(1)}, bf16[1,1,2,240,640]{4,3,2,1,0:T(8,128)(2,1)S(1)}, u32[]{:S(2)}, u32[]{:S(2)}) collective-permute-start(bf16[1,1,2,240,640]{4,3,2,1,0:T(8,128)(2,1)S(1)} %add_convert_fusion.2), channel_id=1, source_target_pairs={{0,6},{1,7},{2,4},{3,5},{4,2},{5,3},{6,0},{7,1},{8,14},{9,15},{10,... | collective-permute-start | bytes 1843208 | tf_op jit(solution)/shard_map/ppermute | solution.py:591
  391.9 38.6 %collective-permute-start.50 = (bf16[1,1,2,112,640]{4,3,2,1,0:T(8,128)(2,1)S(1)}, bf16[1,1,2,112,640]{4,3,2,1,0:T(8,128)(2,1)S(1)}, u32[]{:S(2)}, u32[]{:S(2)}) collective-permute-start(bf16[1,1,2,112,640]{4,3,2,1,0:T(8,128)(2,1)S(1)} %add_convert_fusion.21), channel_id=1, source_target_pairs={{0,6},{1,7},{2,4},{3,5},{4,2},{5,3},{6,0},{7,1},{8,14},{9,15},{10,... | collective-permute-start | bytes 860168 | tf_op jit(solution)/shard_map/ppermute | solution.py:591
  409.0 26.0 %collective-permute-start.60 = (f32[1920]{0:T(1024)S(1)}, f32[1920]{0:T(1024)S(1)}, u32[]{:S(2)}, u32[]{:S(2)}) collective-permute-start(f32[1920]{0:T(1024)S(1)} %add.204), channel_id=1, source_target_pairs={{0,2},{1,3},{2,0},{3,1},{4,6},{5,7},{6,4},{7,5},{8,10},{9,11},{10,... | collective-permute-start | bytes 23048 | tf_op jit(solution)/shard_map/ppermute | solution.py:591
  411.6 25.6 %collective-permute-start.49 = (bf16[1,1,2,128,640]{4,3,2,1,0:T(8,128)(2,1)S(1)}, bf16[1,1,2,128,640]{4,3,2,1,0:T(8,128)(2,1)S(1)}, u32[]{:S(2)}, u32[]{:S(2)}) collective-permute-start(bf16[1,1,2,128,640]{4,3,2,1,0:T(8,128)(2,1)S(1)} %add_convert_fusion.16), channel_id=1, source_target_pairs={{0,6},{1,7},{2,4},{3,5},{4,2},{5,3},{6,0},{7,1},{8,14},{9,15},{10,... | collective-permute-start | bytes 983048 | tf_op jit(solution)/shard_map/ppermute | solution.py:591
  430.7 7.9 %collective-permute-start.52 = (bf16[1,1,2,112,640]{4,3,2,1,0:T(8,128)(2,1)S(1)}, bf16[1,1,2,112,640]{4,3,2,1,0:T(8,128)(2,1)S(1)}, u32[]{:S(2)}, u32[]{:S(2)}) collective-permute-start(bf16[1,1,2,112,640]{4,3,2,1,0:T(8,128)(2,1)S(1)} %add_convert_fusion.20), channel_id=1, source_target_pairs={{0,1},{1,0},{2,3},{3,2},{4,5},{5,4},{6,7},{7,6},{8,9},{9,8},{10,11... | collective-permute-start | bytes 860168 | tf_op jit(solution)/shard_map/ppermute | solution.py:591
  435.0 14.9 %collective-permute-start.61 = (f32[1920]{0:T(1024)S(1)}, f32[1920]{0:T(1024)S(1)}, u32[]{:S(2)}, u32[]{:S(2)}) collective-permute-start(f32[1920]{0:T(1024)S(1)} %add.205), channel_id=1, source_target_pairs={{0,6},{1,7},{2,4},{3,5},{4,2},{5,3},{6,0},{7,1},{8,14},{9,15},{10,... | collective-permute-start | bytes 23048 | tf_op jit(solution)/shard_map/ppermute | solution.py:591
  437.3 16.4 %collective-permute-start.51 = (bf16[1,1,2,128,640]{4,3,2,1,0:T(8,128)(2,1)S(1)}, bf16[1,1,2,128,640]{4,3,2,1,0:T(8,128)(2,1)S(1)}, u32[]{:S(2)}, u32[]{:S(2)}) collective-permute-start(bf16[1,1,2,128,640]{4,3,2,1,0:T(8,128)(2,1)S(1)} %add_convert_fusion.15), channel_id=1, source_target_pairs={{0,1},{1,0},{2,3},{3,2},{4,5},{5,4},{6,7},{7,6},{8,9},{9,8},{10,11... | collective-permute-start | bytes 983048 | tf_op jit(solution)/shard_map/ppermute | solution.py:591
  438.6 15.9 %collective-permute-start.53 = (bf16[1,1,2,112,640]{4,3,2,1,0:T(8,128)(2,1)S(1)}, bf16[1,1,2,112,640]{4,3,2,1,0:T(8,128)(2,1)S(1)}, u32[]{:S(2)}, u32[]{:S(2)}) collective-permute-start(bf16[1,1,2,112,640]{4,3,2,1,0:T(8,128)(2,1)S(1)} %add_convert_fusion.19), channel_id=1, source_target_pairs={{0,2},{1,3},{2,0},{3,1},{4,6},{5,7},{6,4},{7,5},{8,10},{9,11},{10,... | collective-permute-start | bytes 860168 | tf_op jit(solution)/shard_map/ppermute | solution.py:591
  (85 other events, 724.1 us)

commit v4 on v3

--- a/solution.py
+++ b/solution.py
@@ -76,7 +76,7 @@
         self.shape = tuple(shape)
 
     def specs(self):
-        return [pl.BlockSpec(memory_space=pl.ANY)] * len(self.arrays)
+        return [pl.BlockSpec(memory_space=pltpu.HBM)] * len(self.arrays)
 
     def scratch(self):
         if not self.blocks:
@@ -151,7 +151,7 @@
                    pl.BlockSpec((D, GAINS), lambda i: (0, 0))],
         out_shape=shaped(((WIDE, rows), BF16), ((D, rows), BF16), ((D, GAINS), BF16)),
         scratch_shapes=wq.scratch() + wk.scratch(),
-        compiler_params=params(40),
+        compiler_params=params(60),
         cost_estimate=cost(2 * rows * D * WIDE, rows * (2 * D + WIDE) * 2 + D * WIDE * 2),
         name="project",
     )(where, x, cos, sin, *wq.arrays, *wk.arrays)
@@ -186,7 +186,9 @@
     return jnp.concatenate([one] * SHARE, axis=1)
 
 
-def attend_kernel(qkv_ref, segr_ref, segc_ref, o_ref, lse_ref, bias_ref):
+def attend_kernel(qkv_ref, segr_ref, segc_ref, *refs):
+    o_ref, lse_ref, done_ref, bias_ref = refs[-4:]
+    done_ref[...] = jnp.zeros_like(done_ref)
     length = qkv_ref.shape[1]
     make_bias(bias_ref, segr_ref.at[0], segc_ref.at[0], length)
 
@@ -208,10 +210,12 @@
                 lse_ref[kv, i:i + 1, b * QB:(b + 1) * QB] = lse[:, i * QB:(i + 1) * QB]
 
 
-def attend(qkv, segments, at):
-    length = segments.shape[1]
-    wide = qkv.shape[0]
-    pairs = QUERY_HEADS * length * length
+DONE = jax.ShapeDtypeStruct((8, GAINS), F32)
+
+
+def attend(qkv, segments, at, before=()):
+    seqs, length = segments.shape
+    wide, rows = qkv.shape
     return pl.pallas_call(
         attend_kernel,
         grid=(1,),
@@ -219,17 +223,19 @@
             pl.BlockSpec((wide, length), lambda i: (0, at)),
             pl.BlockSpec((1, 1, length), lambda i: (at, 0, 0)),
             pl.BlockSpec((1, length, 1), lambda i: (at, 0, 0)),
+        ] + [pl.BlockSpec(memory_space=pltpu.HBM)] * len(before),
+        out_specs=[
+            pl.BlockSpec((D, length), lambda i: (0, at)),
+            pl.BlockSpec((KEY_VALUE_HEADS, 8, length), lambda i: (0, 0, at)),
+            fixed(DONE.shape),
         ],
-        out_specs=[
-            pl.BlockSpec((D, length), lambda i: (0, 0)),
-            pl.BlockSpec((KEY_VALUE_HEADS, 8, length), lambda i: (0, 0, 0)),
-        ],
-        out_shape=shaped(((D, length), BF16), ((KEY_VALUE_HEADS, 8, length), F32)),
+        out_shape=shaped(((D, rows), BF16), ((KEY_VALUE_HEADS, 8, rows), F32)) + [DONE],
+        input_output_aliases={3 + i: i for i in range(len(before))},
         scratch_shapes=[pltpu.VMEM((length // QB, 3 * QB, QB), F32)],
-        compiler_params=params(40),
-        cost_estimate=cost(pairs * 256 * 2, length * (wide + D) * 2, pairs // 2),
+        compiler_params=params(60),
+        cost_estimate=cost(),
         name="attend",
-    )(qkv, segments[:, None, :], segments[:, :, None])
+    )(qkv, segments[:, None, :], segments[:, :, None], *before)
 
 
 def middle_kernel(weight, where_ref, x_ref, o_ref, gain_ref, *refs):
@@ -255,7 +261,7 @@
         out_specs=[columns(D, TILE), columns(D, TILE)],
         out_shape=shaped(((D, rows), F32), ((D, rows), BF16)),
         scratch_shapes=w.scratch(),
-        compiler_params=params(40),
+        compiler_params=params(60),
         cost_estimate=cost(2 * rows * D * D, rows * D * 10),
         name="middle",
     )(where, x, o, gains, *w.arrays)
@@ -358,7 +364,7 @@
             out_specs=[out, out],
         ),
         out_shape=shaped(((2, 4, OWN, CUT), BF16)) * 2,
-        compiler_params=params(40),
+        compiler_params=params(60),
         cost_estimate=cost(),
         name="ffn_grads",
     )(where, a, b)
@@ -401,14 +407,16 @@
         out_specs=[columns(D, TILE)] * 3 + [pl.BlockSpec((D, 1), lambda i: (0, 0))],
         out_shape=shaped(((D, rows), F32), ((D, rows), BF16), ((D, rows), BF16), ((D, 1), F32)),
         scratch_shapes=w.scratch(),
-        compiler_params=params(40),
+        compiler_params=params(60),
         cost_estimate=cost(2 * rows * D * D, rows * D * 18),
         name="branch",
     )(where, dh, x1, dy, gains, *w.arrays)
 
 
 def attend_back_kernel(qkv_ref, o_ref, do_ref, lse_ref, segr_ref, segc_ref, cos_ref, sin_ref,
-                       out_ref, bias_ref, dk_ref, dv_ref):
+                       *refs):
+    out_ref, done_ref, bias_ref, dk_ref, dv_ref = refs[-5:]
+    done_ref[...] = jnp.zeros_like(done_ref)
     length = qkv_ref.shape[1]
     make_bias(bias_ref, segr_ref.at[0], segc_ref.at[0], length)
 
@@ -445,35 +453,35 @@
             dv_ref[...].astype(BF16))
 
 
-def attend_back(qkv, o, do, lse, segments, cos, sin, at):
+def attend_back(qkv, o, do, lse, segments, cos, sin, at, before=()):
     length = segments.shape[1]
-    wide = qkv.shape[0]
-    pairs = QUERY_HEADS * length * length
+    wide, rows = qkv.shape
     here = lambda height: pl.BlockSpec((height, length), lambda i: (0, at))
     return pl.pallas_call(
         attend_back_kernel,
         grid=(1,),
         in_specs=[
             here(wide),
-            pl.BlockSpec((D, length), lambda i: (0, 0)),
             here(D),
-            pl.BlockSpec((KEY_VALUE_HEADS, 8, length), lambda i: (0, 0, 0)),
+            here(D),
+            pl.BlockSpec((KEY_VALUE_HEADS, 8, length), lambda i: (0, 0, at)),
             pl.BlockSpec((1, 1, length), lambda i: (at, 0, 0)),
             pl.BlockSpec((1, length, 1), lambda i: (at, 0, 0)),
             here(HALF),
             here(HALF),
-        ],
-        out_specs=pl.BlockSpec((wide, length), lambda i: (0, 0)),
-        out_shape=jax.ShapeDtypeStruct((wide, length), BF16),
+        ] + [pl.BlockSpec(memory_space=pltpu.HBM)] * len(before),
+        out_specs=[here(wide), fixed(DONE.shape)],
+        out_shape=shaped(((wide, rows), BF16)) + [DONE],
+        input_output_aliases={8 + i: i for i in range(len(before))},
         scratch_shapes=[
             pltpu.VMEM((length // QB, 3 * QB, QB), F32),
             pltpu.VMEM((HEAD_WIDTH, length), F32),
             pltpu.VMEM((HEAD_WIDTH, length), F32),
         ],
-        compiler_params=params(40),
-        cost_estimate=cost(pairs * 256 * 5, length * (2 * wide + 2 * D) * 2, pairs // 2),
+        compiler_params=params(60),
+        cost_estimate=cost(),
         name="attend_back",
-    )(qkv, o, do, lse, segments[:, None, :], segments[:, :, None], cos, sin)
+    )(qkv, o, do, lse, segments[:, None, :], segments[:, :, None], cos, sin, *before)
 
 
 PIECES = ((0, 128), (128, OWN))
@@ -506,7 +514,7 @@
         in_specs=[SMEM, fixed((D, rows)), fixed((WIDE, rows)), fixed((D, rows)), fixed((D, rows))],
         out_specs=[fixed(shape) for shape in shapes],
         out_shape=shaped(*((shape, BF16) for shape in shapes)),
-        compiler_params=params(48),
+        compiler_params=params(60),
         cost_estimate=cost(),
         name="weight_grads",
     )(where, h, dqkv, o, da)
@@ -548,7 +556,7 @@
         out_specs=[columns(D, TILE), pl.BlockSpec((D, 1), lambda i: (0, 0))],
         out_shape=shaped(((D, rows), BF16), ((D, 1), F32)),
         scratch_shapes=wq.scratch() + wk.scratch(),
-        compiler_params=params(40),
+        compiler_params=params(60),
         cost_estimate=cost(2 * rows * D * WIDE, rows * (D * 8 + WIDE * 2) + D * WIDE * 2),
         name="input_grads",
     )(where, x, dx, dqkv, *wq.arrays, *wk.arrays)
@@ -695,34 +703,34 @@
     where = jnp.stack([cube.me] + [cube.coordinate[i] for i in range(3)]).astype(jnp.int32)
     x, dy = tokens.T, cotangent.T
 
+    core = lambda value: cube.swap(value, "core")
     q_across = cube.swap(query_weight, "x")
     pad = jnp.zeros((OWN, GAINS - 2), BF16)
     kv = jnp.concatenate(
         [key_weight, value_weight, attn_gain[:, None], ffn_gain[:, None], pad], axis=1
     )
-    kv_across = cube.swap(kv, "x")
-    q_sibling, kv_sibling = cube.swap(query_weight, "core"), cube.swap(kv, "core")
-    q_diagonal, kv_diagonal = cube.swap(q_across, "core"), cube.swap(kv_across, "core")
-    wq = rows_of(query_weight, q_sibling, q_across, q_diagonal)
-    wk = rows_of(kv, kv_sibling, kv_across, kv_diagonal)
-    cos, sin = tables(segments)
+    kv_across = cube.swap(after(kv, q_across), "x")
     relays = [
         Relay(cube, w_gate, 0, 0, 1), Relay(cube, w_up, 0, 1, 2), Relay(cube, w_down.T, 1, 2, 0)
     ]
+    q_sibling, kv_sibling, wo_sibling = core(query_weight), core(kv), core(output_weight)
+    siblings = [core(relay.shard) for relay in relays]
+    cos, sin = tables(segments)
+    early = [relay.quarter for relay in relays] + [cos, sin, q_sibling, kv_sibling, wo_sibling]
+    q_across, kv_across = lax.optimization_barrier((q_across, kv_across, *early, *siblings))[:2]
+    q_diagonal, kv_diagonal = core(q_across), core(kv_across)
     direct = [relay.cross(q_across, kv_across) for relay in relays]
+    wq = rows_of(query_weight, q_sibling, q_across, q_diagonal)
+    wk = rows_of(kv, kv_sibling, kv_across, kv_diagonal)
     qkv, h, gains = project(where, x, wq, wk, cos, sin)
-    wo_across = cube.swap(after(output_weight, qkv), "x")
-    siblings = [cube.swap(after(relay.shard, qkv), "core") for relay in relays]
-    wo_sibling = cube.swap(after(output_weight, qkv), "core")
-    o0, lse0 = attend(qkv, segments, 0)
-    qkv1 = after(qkv, o0, wo_sibling, *direct)
-    handed = [relay.hand_on(o0) for relay in relays]
-    o1, lse1 = attend(qkv1, segments, 1)
-    wo_diagonal = cube.swap(after(wo_across, o1), "core")
+    *first, done0 = attend(qkv, segments, 0)
+    handed = [relay.hand_on(done0) for relay in relays]
+    wo_across = cube.swap(after(output_weight, done0, *direct), "x")
+    o, lse, done1 = attend(after(qkv, done0, *direct), segments, 1, first)
+    rest = [relay.finish(done1) for relay in relays]
+    wo_diagonal = core(after(wo_across, done1))
     wo = rows_of(output_weight, wo_sibling, wo_across, wo_diagonal)
-    o = jnp.concatenate([o0, after(o1, *handed)], axis=1)
-    rest = [relay.finish(o1) for relay in relays]
-    x1, h2 = middle(where, x, o, wo, gains)
+    x1, h2 = middle(where, x, after(o, *[relay.half for relay in relays]), wo, gains)
     weights = [relay.weight(sibling, h2) for relay, sibling in zip(relays, siblings)]
     y, dh2, hid, dgate, dup = feed_forward(where, h2, dy, x1, weights)
 
@@ -730,7 +738,6 @@
     orders = [
         ("x", 0, 1, 2) + more + (0,), (1, "x", 2, 0) + more + (1,), (2, "x", 0, 1) + more + (2,)
     ]
-    core = lambda value: cube.swap(value, "core")
     gd_keep, gd_send = ffn_grads(where, dy, hid, 0, True)
     gd = Reduce(cube, gd_keep, core(gd_send), orders[0])
     gg_keep, gg_send = ffn_grads(where, h2, after(dgate, gd_send), 1, False)
@@ -743,30 +750,33 @@
     dx1, da, do, ffn_gain_grad = branch(where, after(dh2, gg.send), x1, dy, gains, wo)
     gg.swap()
     gu.ready(da)
-    do0 = after(do, gu.send)
+    gd.ready(da)
+    do0 = after(do, gu.send, gd.send)
     gu.swap()
-    dqkv0 = attend_back(qkv, o0, do0, lse0, segments, cos, sin, 0)
-    gd.ready(dqkv0)
-    do1 = after(do, dqkv0, gd.send)
     gd.swap()
-    dqkv1 = attend_back(qkv, o1, do1, lse1, segments, cos, sin, 1)
-    gg.ready(dqkv1)
-    dqkv = after(jnp.concatenate([dqkv0, dqkv1], axis=1), gg.send)
+    *first, done0 = attend_back(qkv, o, do0, lse, segments, cos, sin, 0)
+    gg.ready(done0)
+    gd.ready(done0)
+    do1 = after(do, done0, gg.send, gd.send)
     gg.swap()
+    gd.swap()
+    dqkv, done1 = attend_back(qkv, o, do1, lse, segments, cos, sin, 1, first)
+    swaps = [gd, gg, gu]
+    dqkv = after(dqkv, *[piece.ready(done1) for piece in swaps])
+    for piece in swaps:
+        piece.swap()
     parts = []
     weight_parts = weight_grads(where, h, dqkv, o, da)
     for i in range(len(PIECES)):
         keep, send = weight_parts[2 * i:2 * i + 2]
         parts.append(Reduce(cube, keep, core(send), orders[i]))
-    gu.ready(send)
-    gd.ready(send)
-    dqkv = after(dqkv, gu.send, gd.send)
-    gu.swap()
-    gd.swap()
+    dqkv = after(dqkv, *[part.ready(weight_parts[0]) for part in parts])
+    for part in parts:
+        part.swap()
     grad_x, attn_gain_grad = input_grads(where, x, dx1, wq, wk, dqkv)
+    swaps = [gu, gg, parts[0], gd, parts[1]]
     both = jnp.concatenate([attn_gain_grad, ffn_gain_grad], axis=1).T.reshape(-1)
     ends = ["core", "x"] + list(range(cube.dims))
-    swaps = [gg, parts[0], gu, parts[1], gd]
     token = grad_x
     for round_of in range(len(orders[0])):
         before = token

time: 468 us -> 466 us (level)
  local copies, waits for them, and re-layouts: 64.8 us -> 29.5 us
  Pallas kernels: 157 us -> 180 us
  waiting for transfers between devices: 99.7 us -> 114 us
  starting transfers between devices: 95.2 us -> 89.4 us
    unnamed x183 -> x60, local copies, waits for them, and re-layouts: 48.3 us -> 12.4 us
    ppermute x29, waiting for transfers between devices: 75.8 us -> 85.4 us  [swap(): lax.ppermute(value, 'replica', [(i, i ^ mask) for i in range(self.count)])]
    pallas_call x3, Pallas kernels: 25.9 us -> 33.7 us  [ffn_grads(): pl.pallas_call(kernel, grid_spec=pltpu.PrefetchScalarGridSpec(num_scalar_...]
    ppermute x29, starting transfers between devices: 74.8 us -> 67.7 us  [swap(): lax.ppermute(value, 'replica', [(i, i ^ mask) for i in range(self.count)])]
    pallas_call x2, Pallas kernels: 17.3 us -> 23.8 us  [attend_back(): pl.pallas_call(attend_back_kernel, grid=(1,), in_specs=[here(wide), here(...]
    pallas_call x2, Pallas kernels: 13.5 us -> 18.3 us  [attend(): pl.pallas_call(attend_kernel, grid=(1,), in_specs=[pl.BlockSpec((wide, le...]
    convert_element_type x24 -> x25, other arithmetic: 29.7 us -> 33.6 us  [sum(): functools.reduce(jnp.add, [t.astype(F32) for t in terms]).astype(BF16)]
  transfers between devices with their start and end apart: 62 -> 62, of which waited for: 16 -> 18; matrix products, arithmetic and copies ran while one was open for 12% -> 13% of each run, Pallas kernels for 21% -> 23%
where the time goes in v4:
time: 466 us; the launch traced here: 458 us
  Pallas kernels  180 us (39%)
  waiting for transfers between devices  114 us (24%)
  starting transfers between devices  89.4 us (19%)
  other arithmetic  43.5 us (9%)
  local copies, waits for them, and re-layouts  29.5 us (6%)
    ppermute x29, waiting for transfers between devices, swap(): lax.ppermute(value, 'replica', [(i, i ^ mask) for i in range(self.count)])  85.4 us
    ppermute x29, starting transfers between devices, swap(): lax.ppermute(value, 'replica', [(i, i ^ mask) for i in range(self.count)])  67.7 us
    pallas_call x1, Pallas kernels, feed_forward(): pl.pallas_call(functools.partial(feed_forward_kernel, weights), grid=(hid...  50.4 us
    pallas_call x3, Pallas kernels, ffn_grads(): pl.pallas_call(kernel, grid_spec=pltpu.PrefetchScalarGridSpec(num_scalar_...  33.7 us
    convert_element_type x25, other arithmetic, sum(): functools.reduce(jnp.add, [t.astype(F32) for t in terms]).astype(BF16)  33.6 us
    ppermute x12, waiting for transfers between devices, swap(): return lax.ppermute(value, 'group', [(i, i ^ 2) for i in range(4)])  24.5 us
    pallas_call x2, Pallas kernels, attend_back(): pl.pallas_call(attend_back_kernel, grid=(1,), in_specs=[here(wide), here(...  23.8 us
    pallas_call x2, Pallas kernels, attend(): pl.pallas_call(attend_kernel, grid=(1,), in_specs=[pl.BlockSpec((wide, le...  18.3 us
  transfers between devices with their start and end apart: 62, of which 18 were waited for; matrix products, arithmetic and copies ran while one was open for 13% of the time, Pallas kernels for 23%

profile of v4, /device:TPU:0, one launch (start us, length us, event | category | flops | bytes accessed | tf_op | source)
XLA Modules:
  0.0 458.0 jit_solution(3836229377861486636)
XLA Ops:
  0.7 3.0 collective-permute-start.1
  8.7 1.9 dynamic-slice_bitcast_fusion
  10.5 4.6 collective-permute-done.1.refs_2_
  16.9 1.8 collective-permute-start.2
  18.7 1.9 constant_dynamic-slice_fusion.1
  21.9 5.9 %collective-permute-done.2.refs_6_ = bf16[240,768]{1,0:T(8,128)(2,1)S(1)} collective-permute-done((bf16[240,768]{1,0:T(8,128)(2,1)S(1)}, bf16[240,768]{1,0:T(8,128)(2,1)S(1)}, u32[]{:S(2)}, u32[]{:S(2)}) %collective-permute-start.2) | collective-permute-done | bytes 368672 | tf_op jit(solution)/shard_map/ppermute | solution.py:595
  29.1 1.7 collective-permute-start.12
  31.1 1.7 collective-permute-start.10
  35.8 9.4 %project.1 = (bf16[1600,1024]{1,0:T(8,128)(2,1)}, bf16[960,1024]{1,0:T(8,128)(2,1)}, bf16[960,128]{1,0:T(8,128)(2,1)}) custom-call(s32[4]{0:T(128)} %pad_add_fusion.where_ref, bf16[960,1024]{1,0:T(8,128)(2,1)} %bitcast.55, f32[32,1024]{1,0:T(8,128)} %get-tuple-element.260.cos_ref, f32[32,1024]{1,0:T(8,128)} %get-tuple-element.259.sin_ref, ...), custom_call_target="tpu_custom_call" | custom-call | flops 1 | bytes 1 | tf_op jit(solution)/shard_map/project/pallas_call | solution.py:145
  45.3 9.2 %attend.2 = (bf16[960,1024]{1,0:T(8,128)(2,1)}, f32[5,8,1024]{2,1,0:T(8,128)}, f32[8,128]{1,0:T(8,128)}) custom-call(bf16[1600,1024]{1,0:T(8,128)(2,1)} %get-tuple-element.116.qkv_ref, s32[2,1,512]{2,1,0:T(1,128)} %broadcast_in_dim.43.segr_ref, s32[2,512,1]{2,1,0:T(8,128)} %copy.69.segc_ref), custom_call_target="tpu_custom_call" | custom-call | flops 1 | bytes 1 | tf_op jit(solution)/shard_map/attend/pallas_call | solution.py:219
  54.5 3.6 collective-permute-start.15
  58.1 1.6 collective-permute-start.13
  60.2 9.2 %attend.3 = (bf16[960,1024]{1,0:T(8,128)(2,1)}, f32[5,8,1024]{2,1,0:T(8,128)}, f32[8,128]{1,0:T(8,128)}) custom-call(bf16[1600,1024]{1,0:T(8,128)(2,1)} %get-tuple-element.116.qkv_ref, s32[2,1,512]{2,1,0:T(1,128)} %broadcast_in_dim.43.segr_ref, s32[2,512,1]{2,1,0:T(8,128)} %copy.69.segc_ref, ...), custom_call_target="tpu_custom_call", output_to_operand_aliasing={{0}: (3, {}), {1}: (4, {})} | custom-call | flops 1 | bytes 1 | tf_op jit(solution)/shard_map/attend/pallas_call | solution.py:219
  69.4 2.2 collective-permute-done.14
  72.8 1.6 collective-permute-start.24
  75.7 1.8 collective-permute-start.21
  79.4 2.2 collective-permute-done.17.refs_3_
  82.4 8.6 %middle.1 = (f32[960,1024]{1,0:T(8,128)}, bf16[960,1024]{1,0:T(8,128)(2,1)}) custom-call(s32[4]{0:T(128)} %pad_add_fusion.where_ref, bf16[960,1024]{1,0:T(8,128)(2,1)} %bitcast.56, bf16[960,1024]{1,0:T(8,128)(2,1)} %get-tuple-element.127.o_ref, bf16[960,128]{1,0:T(8,128)(2,1)} %get-tuple-element.128.gain_ref, bf16[240,960]{1,0:T(8,128)(2,1)} %refs_0_.8, ...), custom_call_target="tpu_custom_call" | custom-call | flops 1 | bytes 1 | tf_op jit(solution)/shard_map/middle/pallas_call | solution.py:257
  91.2 3.1 collective-permute-done.21.refs_9_
  94.4 11.5 %collective-permute-done.18.refs_3_ = bf16[240,1280]{1,0:T(8,128)(2,1)} collective-permute-done((bf16[240,1280]{1,0:T(8,128)(2,1)S(1)}, bf16[240,1280]{1,0:T(8,128)(2,1)}, u32[]{:S(2)}, u32[]{:S(2)}) %collective-permute-start.18) | collective-permute-done | bytes 614432 | tf_op jit(solution)/shard_map/ppermute | solution.py:599
  109.9 50.4 %feed_forward.1 = (bf16[960,1024]{1,0:T(8,128)(2,1)}, f32[960,1024]{1,0:T(8,128)}, bf16[2560,1024]{1,0:T(8,128)(2,1)}, bf16[2560,1024]{1,0:T(8,128)(2,1)}, bf16[2560,1024]{1,0:T(8,128)(2,1)}) custom-call(s32[4]{0:T(128)} %pad_add_fusion.where_ref, bf16[960,1024]{1,0:T(8,128)(2,1)} %get-tuple-element.131.h_ref.a_ref, bf16[960,1024]{1,0:T(8,128)(2,1)} %bitcast.58, ...), custom_call_target="tpu_custom_call" | custom-call | flops 1 | bytes 1 | tf_op jit(solution)/shard_map/feed_forward/pallas_call | solution.py:308
  160.3 11.9 %ffn_grads.3 = (bf16[2,4,240,640]{3,2,1,0:T(8,128)(2,1)}, bf16[2,4,240,640]{3,2,1,0:T(8,128)(2,1)}) custom-call(s32[4]{0:T(128)} %pad_add_fusion.where_ref, bf16[960,1024]{1,0:T(8,128)(2,1)} %bitcast.59, bf16[2560,1024]{1,0:T(8,128)(2,1)} %get-tuple-element.139.b_ref), custom_call_target="tpu_custom_call" | custom-call | flops 1 | bytes 1 | tf_op jit(solution)/shard_map/ffn_grads/pallas_call | solution.py:358
  172.8 10.7 %ffn_grads.4 = (bf16[2,4,240,640]{3,2,1,0:T(8,128)(2,1)}, bf16[2,4,240,640]{3,2,1,0:T(8,128)(2,1)}) custom-call(s32[4]{0:T(128)} %pad_add_fusion.where_ref, bf16[960,1024]{1,0:T(8,128)(2,1)} %get-tuple-element.131.h_ref.a_ref, bf16[2560,1024]{1,0:T(8,128)(2,1)} %get-tuple-element.141.b_ref), custom_call_target="tpu_custom_call" | custom-call | flops 1 | bytes 1 | tf_op jit(solution)/shard_map/ffn_grads/pallas_call | solution.py:358
  183.5 1.9 fusion.4
  187.2 11.0 %ffn_grads.5 = (bf16[2,4,240,640]{3,2,1,0:T(8,128)(2,1)}, bf16[2,4,240,640]{3,2,1,0:T(8,128)(2,1)}) custom-call(s32[4]{0:T(128)} %pad_add_fusion.where_ref, bf16[960,1024]{1,0:T(8,128)(2,1)} %get-tuple-element.131.h_ref.a_ref, bf16[2560,1024]{1,0:T(8,128)(2,1)} %get-tuple-element.147.b_ref), custom_call_target="tpu_custom_call" | custom-call | flops 1 | bytes 1 | tf_op jit(solution)/shard_map/ffn_grads/pallas_call | solution.py:358
  198.7 1.7 collective-permute-start.30
  200.4 2.6 add_convert_fusion.1
  203.1 10.9 %branch.1 = (f32[960,1024]{1,0:T(8,128)}, bf16[960,1024]{1,0:T(8,128)(2,1)}, bf16[960,1024]{1,0:T(8,128)(2,1)}, f32[960,1]{1,0:T(8,128)}) custom-call(s32[4]{0:T(128)} %pad_add_fusion.where_ref, f32[960,1024]{1,0:T(8,128)} %get-tuple-element.150.dh_ref, f32[960,1024]{1,0:T(8,128)} %get-tuple-element.132.x1_ref, bf16[960,1024]{1,0:T(8,128)(2,1)} %bitcast.60, ...), custom_call_target="tpu_custom_call" | custom-call | flops 1 | bytes 1 | tf_op jit(solution)/shard_map/branch/pallas_call | solution.py:403
  214.0 14.0 %collective-permute-done.30 = bf16[1,2,2,240,640]{4,3,2,1,0:T(8,128)(2,1)} collective-permute-done((bf16[1,2,2,240,640]{4,3,2,1,0:T(8,128)(2,1)}, bf16[1,2,2,240,640]{4,3,2,1,0:T(8,128)(2,1)}, u32[]{:S(2)}, u32[]{:S(2)}) %collective-permute-start.30) | collective-permute-done | bytes 1228832 | tf_op jit(solution)/shard_map/ppermute | solution.py:595
  228.0 2.5 add_convert_fusion.13
  230.9 2.6 add_convert_fusion
  233.6 1.9 collective-permute-start.35
  235.5 11.8 %attend_back.2 = (bf16[1600,1024]{1,0:T(8,128)(2,1)}, f32[8,128]{1,0:T(8,128)}) custom-call(bf16[1600,1024]{1,0:T(8,128)(2,1)} %get-tuple-element.116.qkv_ref, bf16[960,1024]{1,0:T(8,128)(2,1)} %get-tuple-element.127.o_ref, bf16[960,1024]{1,0:T(8,128)(2,1)} %get-tuple-element.162.do_ref, f32[5,8,1024]{2,1,0:T(8,128)} %get-tuple-element.158.lse_ref, ...), custom_call_target="tpu_custom_call" | custom-call | flops 1 | bytes 1 | tf_op jit(solution)/shard_map/attend_back/pallas_call | solution.py:460
  247.2 2.5 add_convert_fusion.12
  250.4 2.6 add_convert_fusion.11
  253.7 12.0 %attend_back.3 = (bf16[1600,1024]{1,0:T(8,128)(2,1)}, f32[8,128]{1,0:T(8,128)}) custom-call(bf16[1600,1024]{1,0:T(8,128)(2,1)} %get-tuple-element.116.qkv_ref, bf16[960,1024]{1,0:T(8,128)(2,1)} %get-tuple-element.127.o_ref, bf16[960,1024]{1,0:T(8,128)(2,1)} %get-tuple-element.162.do_ref, ...), custom_call_target="tpu_custom_call", output_to_operand_aliasing={{0}: (8, {})} | custom-call | flops 1 | bytes 1 | tf_op jit(solution)/shard_map/attend_back/pallas_call | solution.py:460
  265.8 11.1 %collective-permute-done.33 = bf16[1,1,2,240,640]{4,3,2,1,0:T(8,128)(2,1)} collective-permute-done((bf16[1,1,2,240,640]{4,3,2,1,0:T(8,128)(2,1)}, bf16[1,1,2,240,640]{4,3,2,1,0:T(8,128)(2,1)}, u32[]{:S(2)}, u32[]{:S(2)}) %collective-permute-start.33) | collective-permute-done | bytes 614432 | tf_op jit(solution)/shard_map/ppermute | solution.py:599
  278.2 2.8 add_convert_fusion.9
  281.0 2.3 add_convert_fusion.8
  283.3 13.0 %weight_grads.1 = (bf16[2,4,128,640]{3,2,1,0:T(8,128)(2,1)}, bf16[2,4,128,640]{3,2,1,0:T(8,128)(2,1)}, bf16[2,4,112,640]{3,2,1,0:T(8,128)(2,1)}, bf16[2,4,112,640]{3,2,1,0:T(8,128)(2,1)}) custom-call(s32[4]{0:T(128)} %pad_add_fusion.where_ref, bf16[960,1024]{1,0:T(8,128)(2,1)} %get-tuple-element.170.h_ref, bf16[1600,1024]{1,0:T(8,128)(2,1)} %get-tuple-element.177.dqkv_ref, ...), custom_call_target="tpu_custom_call" | custom-call | flops 1 | bytes 1 | tf_op jit(solution)/shard_map/weight_grads/pallas_call | solution.py:511
  297.0 2.4 collective-permute-start.39
  300.8 1.8 collective-permute-start.40
  304.2 2.0 add_convert_fusion.14
  306.2 5.2 %collective-permute-start.44 = (bf16[2,1,2,112,640]{4,3,2,1,0:T(8,128)(2,1)}, bf16[2,1,2,112,640]{4,3,2,1,0:T(8,128)(2,1)}, u32[]{:S(2)}, u32[]{:S(2)}) collective-permute-start(bf16[2,1,2,112,640]{4,3,2,1,0:T(8,128)(2,1)} %add_convert_fusion.14), channel_id=1, source_target_pairs={{0,2},{1,3},{2,0},{3,1},{4,6},{5,7},{6,4},{7,5},{8,10},{9,11},{10,... | collective-permute-start | bytes 1720328 | tf_op jit(solution)/shard_map/ppermute | solution.py:599
  312.5 1.7 collective-permute-start.38
  314.2 11.4 %input_grads.1 = (bf16[960,1024]{1,0:T(8,128)(2,1)}, f32[960,1]{1,0:T(8,128)}) custom-call(s32[4]{0:T(128)} %pad_add_fusion.where_ref, bf16[960,1024]{1,0:T(8,128)(2,1)} %bitcast.57, f32[960,1024]{1,0:T(8,128)} %get-tuple-element.151.dx_ref, bf16[1600,1024]{1,0:T(8,128)(2,1)} %get-tuple-element.177.dqkv_ref, bf16[240,960]{1,0:T(8,128)(2,1)} %refs_0_.9, ...), custom_call_target="tpu_custom_call" | custom-call | flops 1 | bytes 1 | tf_op jit(solution)/shard_map/input_grads/pallas_call | solution.py:551
  327.0 1.9 add_convert_fusion.7
  336.2 4.0 collective-permute-done.44
  342.9 1.8 collective-permute-start.48
  346.1 12.7 %collective-permute-done.42 = bf16[1,1,2,240,640]{4,3,2,1,0:T(8,128)(2,1)S(1)} collective-permute-done((bf16[1,1,2,240,640]{4,3,2,1,0:T(8,128)(2,1)S(1)}, bf16[1,1,2,240,640]{4,3,2,1,0:T(8,128)(2,1)S(1)}, u32[]{:S(2)}, u32[]{:S(2)}) %collective-permute-start.42) | collective-permute-done | bytes 614432 | tf_op jit(solution)/shard_map/ppermute | solution.py:599
  358.8 12.8 %collective-permute-start.47 = (bf16[1,1,2,240,640]{4,3,2,1,0:T(8,128)(2,1)S(1)}, bf16[1,1,2,240,640]{4,3,2,1,0:T(8,128)(2,1)S(1)}, u32[]{:S(2)}, u32[]{:S(2)}) collective-permute-start(bf16[1,1,2,240,640]{4,3,2,1,0:T(8,128)(2,1)S(1)} %add_convert_fusion.4), channel_id=1, source_target_pairs={{0,2},{1,3},{2,0},{3,1},{4,6},{5,7},{6,4},{7,5},{8,10},{9,11},{10,... | collective-permute-start | bytes 1843208 | tf_op jit(solution)/shard_map/ppermute | solution.py:599
  371.7 6.9 %collective-permute-start.54 = (bf16[1,1,2,240,640]{4,3,2,1,0:T(8,128)(2,1)S(1)}, bf16[1,1,2,240,640]{4,3,2,1,0:T(8,128)(2,1)S(1)}, u32[]{:S(2)}, u32[]{:S(2)}) collective-permute-start(bf16[1,1,2,240,640]{4,3,2,1,0:T(8,128)(2,1)S(1)} %add_convert_fusion.3), channel_id=1, source_target_pairs={{0,2},{1,3},{2,0},{3,1},{4,6},{5,7},{6,4},{7,5},{8,10},{9,11},{10,... | collective-permute-start | bytes 1843208 | tf_op jit(solution)/shard_map/ppermute | solution.py:599
  381.0 2.4 collective-permute-start.50
  385.2 1.7 convert_bitcast_fusion
  387.0 1.8 collective-permute-start.55
  388.9 17.2 %collective-permute-done.46 = bf16[1,1,2,128,640]{4,3,2,1,0:T(8,128)(2,1)S(1)} collective-permute-done((bf16[1,1,2,128,640]{4,3,2,1,0:T(8,128)(2,1)S(1)}, bf16[1,1,2,128,640]{4,3,2,1,0:T(8,128)(2,1)S(1)}, u32[]{:S(2)}, u32[]{:S(2)}) %collective-permute-start.46) | collective-permute-done | bytes 327712 | tf_op jit(solution)/shard_map/ppermute | solution.py:599
  406.1 2.4 collective-permute-start.49
  408.5 6.6 %collective-permute-done.50 = bf16[1,1,2,112,640]{4,3,2,1,0:T(8,128)(2,1)S(1)} collective-permute-done((bf16[1,1,2,112,640]{4,3,2,1,0:T(8,128)(2,1)S(1)}, bf16[1,1,2,112,640]{4,3,2,1,0:T(8,128)(2,1)S(1)}, u32[]{:S(2)}, u32[]{:S(2)}) %collective-permute-start.50) | collective-permute-done | bytes 286752 | tf_op jit(solution)/shard_map/ppermute | solution.py:599
  415.2 1.6 collective-permute-start.52
  417.2 15.3 %collective-permute-done.49 = bf16[1,1,2,128,640]{4,3,2,1,0:T(8,128)(2,1)S(1)} collective-permute-done((bf16[1,1,2,128,640]{4,3,2,1,0:T(8,128)(2,1)S(1)}, bf16[1,1,2,128,640]{4,3,2,1,0:T(8,128)(2,1)S(1)}, u32[]{:S(2)}, u32[]{:S(2)}) %collective-permute-start.49) | collective-permute-done | bytes 327712 | tf_op jit(solution)/shard_map/ppermute | solution.py:599
  435.4 1.6 copy.83
  438.6 8.9 %collective-permute-start.53 = (bf16[1,1,2,112,640]{4,3,2,1,0:T(8,128)(2,1)S(1)}, bf16[1,1,2,112,640]{4,3,2,1,0:T(8,128)(2,1)S(1)}, u32[]{:S(2)}, u32[]{:S(2)}) collective-permute-start(bf16[1,1,2,112,640]{4,3,2,1,0:T(8,128)(2,1)S(1)} %add_convert_fusion.19), channel_id=1, source_target_pairs={{0,2},{1,3},{2,0},{3,1},{4,6},{5,7},{6,4},{7,5},{8,10},{9,11},{10,... | collective-permute-start | bytes 860168 | tf_op jit(solution)/shard_map/ppermute | solution.py:599
  449.7 1.6 copy.84
  454.0 1.6 fusion.2
  (202 shorter events, 62.3 us)
Async XLA Ops:
  0.7 14.4 %collective-permute-start.1 = (bf16[240,960]{1,0:T(8,128)(2,1)}, bf16[240,960]{1,0:T(8,128)(2,1)S(1)}, u32[]{:S(2)}, u32[]{:S(2)}) collective-permute-start(bf16[240,960]{1,0:T(8,128)(2,1)} %refs_0_.9), channel_id=1, source_target_pairs={{0,16},{8,24},{16,0},{24,8},{1,17},{9,25},{17,1},{25,9},{2,18},{10... | collective-permute-start | bytes 1382408 | tf_op jit(solution)/shard_map/ppermute | solution.py:595
  3.7 24.1 %collective-permute-start.7 = (bf16[960,640]{1,0:T(8,128)(2,1)}, bf16[960,640]{1,0:T(8,128)(2,1)}, u32[]{:S(2)}, u32[]{:S(2)}) collective-permute-start(bf16[960,640]{1,0:T(8,128)(2,1)} %bitcast.85), channel_id=1, source_target_pairs={{0,8},{8,0},{16,24},{24,16},{1,9},{9,1},{17,25},{25,17},{2,10},{10... | collective-permute-start | bytes 3686408 | tf_op jit(solution)/shard_map/ppermute | solution.py:597
  3.7 24.1 %collective-permute-start.5 = (bf16[240,2560]{1,0:T(8,128)(2,1)}, bf16[240,2560]{1,0:T(8,128)(2,1)}, u32[]{:S(2)}, u32[]{:S(2)}) collective-permute-start(bf16[240,2560]{1,0:T(8,128)(2,1)} %refs_0_.7), channel_id=1, source_target_pairs={{0,8},{8,0},{16,24},{24,16},{1,9},{9,1},{17,25},{25,17},{2,10},{10... | collective-permute-start | bytes 3686408 | tf_op jit(solution)/shard_map/ppermute | solution.py:597
  4.2 23.6 %collective-permute-start.6 = (bf16[240,2560]{1,0:T(8,128)(2,1)}, bf16[240,2560]{1,0:T(8,128)(2,1)}, u32[]{:S(2)}, u32[]{:S(2)}) collective-permute-start(bf16[240,2560]{1,0:T(8,128)(2,1)} %refs_6_.1), channel_id=1, source_target_pairs={{0,8},{8,0},{16,24},{24,16},{1,9},{9,1},{17,25},{25,17},{2,10},{10... | collective-permute-start | bytes 3686408 | tf_op jit(solution)/shard_map/ppermute | solution.py:597
  4.2 12.8 %collective-permute-start = (bf16[240,960]{1,0:T(8,128)(2,1)}, bf16[240,960]{1,0:T(8,128)(2,1)S(1)}, u32[]{:S(2)}, u32[]{:S(2)}) collective-permute-start(bf16[240,960]{1,0:T(8,128)(2,1)} %refs_0_.9), channel_id=1, source_target_pairs={{0,8},{8,0},{16,24},{24,16},{1,9},{9,1},{17,25},{25,17},{2,10},{10... | collective-permute-start | bytes 1382408 | tf_op jit(solution)/shard_map/ppermute | solution.py:597
  8.7 25.8 %copy-start = (bf16[240,768]{1,0:T(8,128)(2,1)}, bf16[240,768]{1,0:T(8,128)(2,1)S(1)}, u32[]{:S(2)}) copy-start(bf16[240,768]{1,0:T(8,128)(2,1)S(1)} %concatenate.77.refs_4_) | copy-start | bytes 1105924
  15.1 1.7 collective-permute-start.3
  16.8 5.1 %collective-permute-start.4 = (bf16[240,960]{1,0:T(8,128)(2,1)S(1)}, bf16[240,960]{1,0:T(8,128)(2,1)S(1)}, u32[]{:S(2)}, u32[]{:S(2)}) collective-permute-start(bf16[240,960]{1,0:T(8,128)(2,1)S(1)} %copy-done.8), channel_id=1, source_target_pairs={{0,8},{8,0},{16,24},{24,16},{1,9},{9,1},{17,25},{25,17},{2,10},{10... | collective-permute-start | bytes 1382408 | tf_op jit(solution)/shard_map/ppermute | solution.py:597
  16.9 10.9 %collective-permute-start.2 = (bf16[240,768]{1,0:T(8,128)(2,1)S(1)}, bf16[240,768]{1,0:T(8,128)(2,1)S(1)}, u32[]{:S(2)}, u32[]{:S(2)}) collective-permute-start(bf16[240,768]{1,0:T(8,128)(2,1)S(1)} %concatenate.77.refs_4_), channel_id=1, source_target_pairs={{0,16},{8,24},{16,0},{24,8},{1,17},{9,25},{17,1},{25,9},{2,18},{10... | collective-permute-start | bytes 1105928 | tf_op jit(solution)/shard_map/ppermute | solution.py:595
  21.9 23.4 %copy-start.12 = (bf16[240,960]{1,0:T(8,128)(2,1)}, bf16[240,960]{1,0:T(8,128)(2,1)S(1)}, u32[]{:S(2)}) copy-start(bf16[240,960]{1,0:T(8,128)(2,1)S(1)} %collective-permute-done.4.refs_1_) | copy-start | bytes 1382404
  28.5 6.5 %collective-permute-start.8 = (bf16[240,960]{1,0:T(8,128)(2,1)S(1)}, bf16[240,960]{1,0:T(8,128)(2,1)S(1)}, u32[]{:S(2)}, u32[]{:S(2)}) collective-permute-start(bf16[240,960]{1,0:T(8,128)(2,1)S(1)} %collective-permute-done.1.refs_2_), channel_id=1, source_target_pairs={{0,8},{8,0},{16,24},{24,16},{1,9},{9,1},{17,25},{25,17},{2,10},{10... | collective-permute-start | bytes 1382408 | tf_op jit(solution)/shard_map/ppermute | solution.py:597
  28.5 6.5 %collective-permute-start.9 = (bf16[240,768]{1,0:T(8,128)(2,1)}, bf16[240,768]{1,0:T(8,128)(2,1)}, u32[]{:S(2)}, u32[]{:S(2)}) collective-permute-start(bf16[240,768]{1,0:T(8,128)(2,1)} %copy-done.16), channel_id=1, source_target_pairs={{0,8},{8,0},{16,24},{24,16},{1,9},{9,1},{17,25},{25,17},{2,10},{10... | collective-permute-start | bytes 1105928 | tf_op jit(solution)/shard_map/ppermute | solution.py:597
  29.1 25.4 %collective-permute-start.12 = (bf16[240,640]{1,0:T(8,128)(2,1)}, bf16[240,640]{1,0:T(8,128)(2,1)}, u32[]{:S(2)}, u32[]{:S(2)}) collective-permute-start(bf16[240,640]{1,0:T(8,128)(2,1)} %dynamic-slice_bitcast_fusion), channel_id=1, source_target_pairs={{0,16},{8,24},{16,0},{24,8},{1,17},{9,25},{17,1},{25,9},{2,18},{10... | collective-permute-start | bytes 921608 | tf_op jit(solution)/shard_map/ppermute | solution.py:595
  30.8 27.3 %collective-permute-start.11 = (bf16[240,640]{1,0:T(8,128)(2,1)}, bf16[240,640]{1,0:T(8,128)(2,1)}, u32[]{:S(2)}, u32[]{:S(2)}) collective-permute-start(bf16[240,640]{1,0:T(8,128)(2,1)} %get-tuple-element.114), channel_id=1, source_target_pairs={{0,16},{8,24},{16,0},{24,8},{1,17},{9,25},{17,1},{25,9},{2,18},{10... | collective-permute-start | bytes 921608 | tf_op jit(solution)/shard_map/ppermute | solution.py:595
  31.1 27.0 %collective-permute-start.10 = (bf16[240,640]{1,0:T(8,128)(2,1)}, bf16[240,640]{1,0:T(8,128)(2,1)}, u32[]{:S(2)}, u32[]{:S(2)}) collective-permute-start(bf16[240,640]{1,0:T(8,128)(2,1)} %get-tuple-element.113), channel_id=1, source_target_pairs={{0,16},{8,24},{16,0},{24,8},{1,17},{9,25},{17,1},{25,9},{2,18},{10... | collective-permute-start | bytes 921608 | tf_op jit(solution)/shard_map/ppermute | solution.py:595
  54.5 14.9 %collective-permute-start.15 = (bf16[240,640]{1,0:T(8,128)(2,1)}, bf16[240,640]{1,0:T(8,128)(2,1)S(1)}, u32[]{:S(2)}, u32[]{:S(2)}) collective-permute-start(bf16[240,640]{1,0:T(8,128)(2,1)} %collective-permute-done.12), channel_id=1, source_target_pairs={{0,6},{1,7},{2,4},{3,5},{4,2},{5,3},{6,0},{7,1},{8,14},{9,15},{10,... | collective-permute-start | bytes 921608 | tf_op jit(solution)/shard_map/ppermute | solution.py:599
  58.1 13.5 %collective-permute-start.14 = (bf16[240,640]{1,0:T(8,128)(2,1)}, bf16[240,640]{1,0:T(8,128)(2,1)S(1)}, u32[]{:S(2)}, u32[]{:S(2)}) collective-permute-start(bf16[240,640]{1,0:T(8,128)(2,1)} %collective-permute-done.11), channel_id=1, source_target_pairs={{0,2},{1,3},{2,0},{3,1},{4,6},{5,7},{6,4},{7,5},{8,10},{9,11},{10,... | collective-permute-start | bytes 921608 | tf_op jit(solution)/shard_map/ppermute | solution.py:599
  58.1 13.5 %collective-permute-start.13 = (bf16[240,640]{1,0:T(8,128)(2,1)}, bf16[240,640]{1,0:T(8,128)(2,1)S(1)}, u32[]{:S(2)}, u32[]{:S(2)}) collective-permute-start(bf16[240,640]{1,0:T(8,128)(2,1)} %collective-permute-done.10), channel_id=1, source_target_pairs={{0,1},{1,0},{2,3},{3,2},{4,5},{5,4},{6,7},{7,6},{8,9},{9,8},{10,11... | collective-permute-start | bytes 921608 | tf_op jit(solution)/shard_map/ppermute | solution.py:599
  59.7 19.2 %collective-permute-start.16 = (bf16[240,960]{1,0:T(8,128)(2,1)S(1)}, bf16[240,960]{1,0:T(8,128)(2,1)S(1)}, u32[]{:S(2)}, u32[]{:S(2)}) collective-permute-start(bf16[240,960]{1,0:T(8,128)(2,1)S(1)} %copy-done.8), channel_id=1, source_target_pairs={{0,16},{8,24},{16,0},{24,8},{1,17},{9,25},{17,1},{25,9},{2,18},{10... | collective-permute-start | bytes 1382408 | tf_op jit(solution)/shard_map/ppermute | solution.py:595
  72.8 18.2 %collective-permute-start.24 = (bf16[480,640]{1,0:T(8,128)(2,1)S(1)}, bf16[480,640]{1,0:T(8,128)(2,1)S(1)}, u32[]{:S(2)}, u32[]{:S(2)}) collective-permute-start(bf16[480,640]{1,0:T(8,128)(2,1)S(1)} %maximum_select_fusion.6.refs_14_), channel_id=1, source_target_pairs={{0,1},{1,0},{2,3},{3,2},{4,5},{5,4},{6,7},{7,6},{8,9},{9,8},{10,11... | collective-permute-start | bytes 1843208 | tf_op jit(solution)/shard_map/ppermute | solution.py:599
  75.7 18.7 %collective-permute-start.21 = (bf16[240,1280]{1,0:T(8,128)(2,1)S(1)}, bf16[240,1280]{1,0:T(8,128)(2,1)}, u32[]{:S(2)}, u32[]{:S(2)}) collective-permute-start(bf16[240,1280]{1,0:T(8,128)(2,1)S(1)} %maximum_select_fusion.5.refs_8_), channel_id=1, source_target_pairs={{0,6},{1,7},{2,4},{3,5},{4,2},{5,3},{6,0},{7,1},{8,14},{9,15},{10,... | collective-permute-start | bytes 1843208 | tf_op jit(solution)/shard_map/ppermute | solution.py:599
  78.7 27.2 %collective-permute-start.18 = (bf16[240,1280]{1,0:T(8,128)(2,1)S(1)}, bf16[240,1280]{1,0:T(8,128)(2,1)}, u32[]{:S(2)}, u32[]{:S(2)}) collective-permute-start(bf16[240,1280]{1,0:T(8,128)(2,1)S(1)} %maximum_select_fusion.4.refs_2_), channel_id=1, source_target_pairs={{0,2},{1,3},{2,0},{3,1},{4,6},{5,7},{6,4},{7,5},{8,10},{9,11},{10,... | collective-permute-start | bytes 1843208 | tf_op jit(solution)/shard_map/ppermute | solution.py:599
  78.8 27.1 %collective-permute-start.25 = (bf16[480,640]{1,0:T(8,128)(2,1)S(1)}, bf16[480,640]{1,0:T(8,128)(2,1)}, u32[]{:S(2)}, u32[]{:S(2)}) collective-permute-start(bf16[480,640]{1,0:T(8,128)(2,1)S(1)} %maximum_select_fusion.6.refs_14_), channel_id=1, source_target_pairs={{0,8},{8,0},{16,24},{24,16},{1,9},{9,1},{17,25},{25,17},{2,10},{10... | collective-permute-start | bytes 1843208 | tf_op jit(solution)/shard_map/ppermute | solution.py:597
  78.9 2.7 collective-permute-start.17
  81.6 24.8 %collective-permute-start.22 = (bf16[240,1280]{1,0:T(8,128)(2,1)S(1)}, bf16[240,1280]{1,0:T(8,128)(2,1)}, u32[]{:S(2)}, u32[]{:S(2)}) collective-permute-start(bf16[240,1280]{1,0:T(8,128)(2,1)S(1)} %maximum_select_fusion.5.refs_8_), channel_id=1, source_target_pairs={{0,8},{8,0},{16,24},{24,16},{1,9},{9,1},{17,25},{25,17},{2,10},{10... | collective-permute-start | bytes 1843208 | tf_op jit(solution)/shard_map/ppermute | solution.py:597
  91.0 15.4 %collective-permute-start.19 = (bf16[240,1280]{1,0:T(8,128)(2,1)S(1)}, bf16[240,1280]{1,0:T(8,128)(2,1)S(1)}, u32[]{:S(2)}, u32[]{:S(2)}) collective-permute-start(bf16[240,1280]{1,0:T(8,128)(2,1)S(1)} %maximum_select_fusion.4.refs_2_), channel_id=1, source_target_pairs={{0,8},{8,0},{16,24},{24,16},{1,9},{9,1},{17,25},{25,17},{2,10},{10... | collective-permute-start | bytes 1843208 | tf_op jit(solution)/shard_map/ppermute | solution.py:597
  94.4 12.1 %collective-permute-start.26 = (bf16[480,640]{1,0:T(8,128)(2,1)S(1)}, bf16[480,640]{1,0:T(8,128)(2,1)S(1)}, u32[]{:S(2)}, u32[]{:S(2)}) collective-permute-start(bf16[480,640]{1,0:T(8,128)(2,1)S(1)} %collective-permute-done.24.refs_15_), channel_id=1, source_target_pairs={{0,8},{8,0},{16,24},{24,16},{1,9},{9,1},{17,25},{25,17},{2,10},{10... | collective-permute-start | bytes 1843208 | tf_op jit(solution)/shard_map/ppermute | solution.py:597
  105.9 2.2 collective-permute-start.23
  105.9 3.1 collective-permute-start.20
  172.2 13.2 %collective-permute-start.28 = (bf16[2,4,240,640]{3,2,1,0:T(8,128)(2,1)}, bf16[2,4,240,640]{3,2,1,0:T(8,128)(2,1)S(1)}, u32[]{:S(2)}, u32[]{:S(2)}) collective-permute-start(bf16[2,4,240,640]{3,2,1,0:T(8,128)(2,1)} %get-tuple-element.140), channel_id=1, source_target_pairs={{0,8},{8,0},{16,24},{24,16},{1,9},{9,1},{17,25},{25,17},{2,10},{10... | collective-permute-start | bytes 7372808 | tf_op jit(solution)/shard_map/ppermute | solution.py:597
  183.5 16.9 %collective-permute-start.27 = (bf16[2,4,240,640]{3,2,1,0:T(8,128)(2,1)}, bf16[2,4,240,640]{3,2,1,0:T(8,128)(2,1)}, u32[]{:S(2)}, u32[]{:S(2)}) collective-permute-start(bf16[2,4,240,640]{3,2,1,0:T(8,128)(2,1)} %get-tuple-element.143), channel_id=1, source_target_pairs={{0,8},{8,0},{16,24},{24,16},{1,9},{9,1},{17,25},{25,17},{2,10},{10... | collective-permute-start | bytes 7372808 | tf_op jit(solution)/shard_map/ppermute | solution.py:597
  198.2 32.7 %collective-permute-start.29 = (bf16[2,4,240,640]{3,2,1,0:T(8,128)(2,1)}, bf16[2,4,240,640]{3,2,1,0:T(8,128)(2,1)}, u32[]{:S(2)}, u32[]{:S(2)}) collective-permute-start(bf16[2,4,240,640]{3,2,1,0:T(8,128)(2,1)} %get-tuple-element.148), channel_id=1, source_target_pairs={{0,8},{8,0},{16,24},{24,16},{1,9},{9,1},{17,25},{25,17},{2,10},{10... | collective-permute-start | bytes 7372808 | tf_op jit(solution)/shard_map/ppermute | solution.py:597
  198.7 29.3 %collective-permute-start.30 = (bf16[1,2,2,240,640]{4,3,2,1,0:T(8,128)(2,1)}, bf16[1,2,2,240,640]{4,3,2,1,0:T(8,128)(2,1)}, u32[]{:S(2)}, u32[]{:S(2)}) collective-permute-start(bf16[1,2,2,240,640]{4,3,2,1,0:T(8,128)(2,1)} %fusion), channel_id=1, source_target_pairs={{0,16},{8,24},{16,0},{24,8},{1,17},{9,25},{17,1},{25,9},{2,18},{10... | collective-permute-start | bytes 3686408 | tf_op jit(solution)/shard_map/ppermute | solution.py:595
  203.1 44.2 %collective-permute-start.31 = (bf16[2,1,2,240,640]{4,3,2,1,0:T(8,128)(2,1)}, bf16[2,1,2,240,640]{4,3,2,1,0:T(8,128)(2,1)}, u32[]{:S(2)}, u32[]{:S(2)}) collective-permute-start(bf16[2,1,2,240,640]{4,3,2,1,0:T(8,128)(2,1)} %add_convert_fusion.1), channel_id=1, source_target_pairs={{0,2},{1,3},{2,0},{3,1},{4,6},{5,7},{6,4},{7,5},{8,10},{9,11},{10,... | collective-permute-start | bytes 3686408 | tf_op jit(solution)/shard_map/ppermute | solution.py:599
  230.4 16.8 %collective-permute-start.32 = (bf16[1,1,2,240,640]{4,3,2,1,0:T(8,128)(2,1)}, bf16[1,1,2,240,640]{4,3,2,1,0:T(8,128)(2,1)}, u32[]{:S(2)}, u32[]{:S(2)}) collective-permute-start(bf16[1,1,2,240,640]{4,3,2,1,0:T(8,128)(2,1)} %add_convert_fusion.13), channel_id=1, source_target_pairs={{0,1},{1,0},{2,3},{3,2},{4,5},{5,4},{6,7},{7,6},{8,9},{9,8},{10,11... | collective-permute-start | bytes 1843208 | tf_op jit(solution)/shard_map/ppermute | solution.py:599
  233.6 47.4 %collective-permute-start.35 = (bf16[2,1,2,240,640]{4,3,2,1,0:T(8,128)(2,1)}, bf16[2,1,2,240,640]{4,3,2,1,0:T(8,128)(2,1)}, u32[]{:S(2)}, u32[]{:S(2)}) collective-permute-start(bf16[2,1,2,240,640]{4,3,2,1,0:T(8,128)(2,1)} %add_convert_fusion), channel_id=1, source_target_pairs={{0,6},{1,7},{2,4},{3,5},{4,2},{5,3},{6,0},{7,1},{8,14},{9,15},{10,... | collective-permute-start | bytes 3686408 | tf_op jit(solution)/shard_map/ppermute | solution.py:599
  249.7 16.0 %collective-permute-start.34 = (bf16[1,1,2,240,640]{4,3,2,1,0:T(8,128)(2,1)}, bf16[1,1,2,240,640]{4,3,2,1,0:T(8,128)(2,1)}, u32[]{:S(2)}, u32[]{:S(2)}) collective-permute-start(bf16[1,1,2,240,640]{4,3,2,1,0:T(8,128)(2,1)} %add_convert_fusion.12), channel_id=1, source_target_pairs={{0,16},{8,24},{16,0},{24,8},{1,17},{9,25},{17,1},{25,9},{2,18},{10... | collective-permute-start | bytes 1843208 | tf_op jit(solution)/shard_map/ppermute | solution.py:595
  252.9 23.9 %collective-permute-start.33 = (bf16[1,1,2,240,640]{4,3,2,1,0:T(8,128)(2,1)}, bf16[1,1,2,240,640]{4,3,2,1,0:T(8,128)(2,1)}, u32[]{:S(2)}, u32[]{:S(2)}) collective-permute-start(bf16[1,1,2,240,640]{4,3,2,1,0:T(8,128)(2,1)} %add_convert_fusion.11), channel_id=1, source_target_pairs={{0,2},{1,3},{2,0},{3,1},{4,6},{5,7},{6,4},{7,5},{8,10},{9,11},{10,... | collective-permute-start | bytes 1843208 | tf_op jit(solution)/shard_map/ppermute | solution.py:599
  296.3 7.8 %collective-permute-start.37 = (bf16[2,4,112,640]{3,2,1,0:T(8,128)(2,1)}, bf16[2,4,112,640]{3,2,1,0:T(8,128)(2,1)}, u32[]{:S(2)}, u32[]{:S(2)}) collective-permute-start(bf16[2,4,112,640]{3,2,1,0:T(8,128)(2,1)} %get-tuple-element.175), channel_id=1, source_target_pairs={{0,8},{8,0},{16,24},{24,16},{1,9},{9,1},{17,25},{25,17},{2,10},{10... | collective-permute-start | bytes 3440648 | tf_op jit(solution)/shard_map/ppermute | solution.py:597
  296.3 15.2 %collective-permute-start.36 = (bf16[2,4,128,640]{3,2,1,0:T(8,128)(2,1)}, bf16[2,4,128,640]{3,2,1,0:T(8,128)(2,1)S(1)}, u32[]{:S(2)}, u32[]{:S(2)}) collective-permute-start(bf16[2,4,128,640]{3,2,1,0:T(8,128)(2,1)} %get-tuple-element.172), channel_id=1, source_target_pairs={{0,8},{8,0},{16,24},{24,16},{1,9},{9,1},{17,25},{25,17},{2,10},{10... | collective-permute-start | bytes 3932168 | tf_op jit(solution)/shard_map/ppermute | solution.py:597
  297.0 31.9 %collective-permute-start.39 = (bf16[1,1,2,240,640]{4,3,2,1,0:T(8,128)(2,1)S(1)}, bf16[1,1,2,240,640]{4,3,2,1,0:T(8,128)(2,1)}, u32[]{:S(2)}, u32[]{:S(2)}) collective-permute-start(bf16[1,1,2,240,640]{4,3,2,1,0:T(8,128)(2,1)S(1)} %copy-done.7), channel_id=1, source_target_pairs={{0,6},{1,7},{2,4},{3,5},{4,2},{5,3},{6,0},{7,1},{8,14},{9,15},{10,... | collective-permute-start | bytes 1843208 | tf_op jit(solution)/shard_map/ppermute | solution.py:599
  299.3 34.1 %collective-permute-start.45 = (bf16[1,1,2,240,640]{4,3,2,1,0:T(8,128)(2,1)S(1)}, bf16[1,1,2,240,640]{4,3,2,1,0:T(8,128)(2,1)}, u32[]{:S(2)}, u32[]{:S(2)}) collective-permute-start(bf16[1,1,2,240,640]{4,3,2,1,0:T(8,128)(2,1)S(1)} %add_convert_fusion.10), channel_id=1, source_target_pairs={{0,6},{1,7},{2,4},{3,5},{4,2},{5,3},{6,0},{7,1},{8,14},{9,15},{10,... | collective-permute-start | bytes 1843208 | tf_op jit(solution)/shard_map/ppermute | solution.py:599
  300.8 26.1 %collective-permute-start.40 = (bf16[1,1,2,240,640]{4,3,2,1,0:T(8,128)(2,1)}, bf16[1,1,2,240,640]{4,3,2,1,0:T(8,128)(2,1)}, u32[]{:S(2)}, u32[]{:S(2)}) collective-permute-start(bf16[1,1,2,240,640]{4,3,2,1,0:T(8,128)(2,1)} %add_convert_fusion.8), channel_id=1, source_target_pairs={{0,16},{8,24},{16,0},{24,8},{1,17},{9,25},{17,1},{25,9},{2,18},{10... | collective-permute-start | bytes 1843208 | tf_op jit(solution)/shard_map/ppermute | solution.py:595
  306.2 34.0 %collective-permute-start.44 = (bf16[2,1,2,112,640]{4,3,2,1,0:T(8,128)(2,1)}, bf16[2,1,2,112,640]{4,3,2,1,0:T(8,128)(2,1)}, u32[]{:S(2)}, u32[]{:S(2)}) collective-permute-start(bf16[2,1,2,112,640]{4,3,2,1,0:T(8,128)(2,1)} %add_convert_fusion.14), channel_id=1, source_target_pairs={{0,2},{1,3},{2,0},{3,1},{4,6},{5,7},{6,4},{7,5},{8,10},{9,11},{10,... | collective-permute-start | bytes 1720328 | tf_op jit(solution)/shard_map/ppermute | solution.py:599
  312.5 19.2 %collective-permute-start.38 = (bf16[1,2,2,128,640]{4,3,2,1,0:T(8,128)(2,1)}, bf16[1,2,2,128,640]{4,3,2,1,0:T(8,128)(2,1)}, u32[]{:S(2)}, u32[]{:S(2)}) collective-permute-start(bf16[1,2,2,128,640]{4,3,2,1,0:T(8,128)(2,1)} %fusion.1), channel_id=1, source_target_pairs={{0,16},{8,24},{16,0},{24,8},{1,17},{9,25},{17,1},{25,9},{2,18},{10... | collective-permute-start | bytes 1966088 | tf_op jit(solution)/shard_map/ppermute | solution.py:595
  326.9 16.0 %collective-permute-start.57 = (f32[1920]{0:T(1024)S(1)}, f32[1920]{0:T(1024)S(1)}, u32[]{:S(2)}, u32[]{:S(2)}) collective-permute-start(f32[1920]{0:T(1024)S(1)} %reshape.221), channel_id=1, source_target_pairs={{0,8},{8,0},{16,24},{24,16},{1,9},{9,1},{17,25},{25,17},{2,10},{10... | collective-permute-start | bytes 23048 | tf_op jit(solution)/shard_map/ppermute | solution.py:597
  328.9 16.7 %collective-permute-start.43 = (bf16[1,1,2,240,640]{4,3,2,1,0:T(8,128)(2,1)S(1)}, bf16[1,1,2,240,640]{4,3,2,1,0:T(8,128)(2,1)S(1)}, u32[]{:S(2)}, u32[]{:S(2)}) collective-permute-start(bf16[1,1,2,240,640]{4,3,2,1,0:T(8,128)(2,1)S(1)} %add_convert_fusion.7), channel_id=1, source_target_pairs={{0,1},{1,0},{2,3},{3,2},{4,5},{5,4},{6,7},{7,6},{8,9},{9,8},{10,11... | collective-permute-start | bytes 1843208 | tf_op jit(solution)/shard_map/ppermute | solution.py:599
  331.7 27.1 %collective-permute-start.42 = (bf16[1,1,2,240,640]{4,3,2,1,0:T(8,128)(2,1)S(1)}, bf16[1,1,2,240,640]{4,3,2,1,0:T(8,128)(2,1)S(1)}, u32[]{:S(2)}, u32[]{:S(2)}) collective-permute-start(bf16[1,1,2,240,640]{4,3,2,1,0:T(8,128)(2,1)S(1)} %add_convert_fusion.6), channel_id=1, source_target_pairs={{0,1},{1,0},{2,3},{3,2},{4,5},{5,4},{6,7},{7,6},{8,9},{9,8},{10,11... | collective-permute-start | bytes 1843208 | tf_op jit(solution)/shard_map/ppermute | solution.py:599
  333.4 38.3 %collective-permute-start.41 = (bf16[1,1,2,128,640]{4,3,2,1,0:T(8,128)(2,1)S(1)}, bf16[1,1,2,128,640]{4,3,2,1,0:T(8,128)(2,1)S(1)}, u32[]{:S(2)}, u32[]{:S(2)}) collective-permute-start(bf16[1,1,2,128,640]{4,3,2,1,0:T(8,128)(2,1)S(1)} %add_convert_fusion.18), channel_id=1, source_target_pairs={{0,1},{1,0},{2,3},{3,2},{4,5},{5,4},{6,7},{7,6},{8,9},{9,8},{10,11... | collective-permute-start | bytes 983048 | tf_op jit(solution)/shard_map/ppermute | solution.py:599
  340.2 43.2 %collective-permute-start.56 = (bf16[1,1,2,240,640]{4,3,2,1,0:T(8,128)(2,1)S(1)}, bf16[1,1,2,240,640]{4,3,2,1,0:T(8,128)(2,1)S(1)}, u32[]{:S(2)}, u32[]{:S(2)}) collective-permute-start(bf16[1,1,2,240,640]{4,3,2,1,0:T(8,128)(2,1)S(1)} %add_convert_fusion.5), channel_id=1, source_target_pairs={{0,1},{1,0},{2,3},{3,2},{4,5},{5,4},{6,7},{7,6},{8,9},{9,8},{10,11... | collective-permute-start | bytes 1843208 | tf_op jit(solution)/shard_map/ppermute | solution.py:599
  342.9 36.8 %collective-permute-start.48 = (bf16[1,1,2,112,640]{4,3,2,1,0:T(8,128)(2,1)S(1)}, bf16[1,1,2,112,640]{4,3,2,1,0:T(8,128)(2,1)S(1)}, u32[]{:S(2)}, u32[]{:S(2)}) collective-permute-start(bf16[1,1,2,112,640]{4,3,2,1,0:T(8,128)(2,1)S(1)} %add_convert_fusion.22), channel_id=1, source_target_pairs={{0,16},{8,24},{16,0},{24,8},{1,17},{9,25},{17,1},{25,9},{2,18},{10... | collective-permute-start | bytes 860168 | tf_op jit(solution)/shard_map/ppermute | solution.py:595
  345.6 35.4 %collective-permute-start.58 = (f32[1920]{0:T(1024)S(1)}, f32[1920]{0:T(1024)S(1)}, u32[]{:S(2)}, u32[]{:S(2)}) collective-permute-start(f32[1920]{0:T(1024)S(1)} %add.202), channel_id=1, source_target_pairs={{0,16},{8,24},{16,0},{24,8},{1,17},{9,25},{17,1},{25,9},{2,18},{10... | collective-permute-start | bytes 23048 | tf_op jit(solution)/shard_map/ppermute | solution.py:595
  358.8 28.1 %collective-permute-start.47 = (bf16[1,1,2,240,640]{4,3,2,1,0:T(8,128)(2,1)S(1)}, bf16[1,1,2,240,640]{4,3,2,1,0:T(8,128)(2,1)S(1)}, u32[]{:S(2)}, u32[]{:S(2)}) collective-permute-start(bf16[1,1,2,240,640]{4,3,2,1,0:T(8,128)(2,1)S(1)} %add_convert_fusion.4), channel_id=1, source_target_pairs={{0,2},{1,3},{2,0},{3,1},{4,6},{5,7},{6,4},{7,5},{8,10},{9,11},{10,... | collective-permute-start | bytes 1843208 | tf_op jit(solution)/shard_map/ppermute | solution.py:599
  371.7 45.1 %collective-permute-start.54 = (bf16[1,1,2,240,640]{4,3,2,1,0:T(8,128)(2,1)S(1)}, bf16[1,1,2,240,640]{4,3,2,1,0:T(8,128)(2,1)S(1)}, u32[]{:S(2)}, u32[]{:S(2)}) collective-permute-start(bf16[1,1,2,240,640]{4,3,2,1,0:T(8,128)(2,1)S(1)} %add_convert_fusion.3), channel_id=1, source_target_pairs={{0,2},{1,3},{2,0},{3,1},{4,6},{5,7},{6,4},{7,5},{8,10},{9,11},{10,... | collective-permute-start | bytes 1843208 | tf_op jit(solution)/shard_map/ppermute | solution.py:599
  379.7 26.3 %collective-permute-start.46 = (bf16[1,1,2,128,640]{4,3,2,1,0:T(8,128)(2,1)S(1)}, bf16[1,1,2,128,640]{4,3,2,1,0:T(8,128)(2,1)S(1)}, u32[]{:S(2)}, u32[]{:S(2)}) collective-permute-start(bf16[1,1,2,128,640]{4,3,2,1,0:T(8,128)(2,1)S(1)} %add_convert_fusion.17), channel_id=1, source_target_pairs={{0,2},{1,3},{2,0},{3,1},{4,6},{5,7},{6,4},{7,5},{8,10},{9,11},{10,... | collective-permute-start | bytes 983048 | tf_op jit(solution)/shard_map/ppermute | solution.py:599
  381.0 34.2 %collective-permute-start.50 = (bf16[1,1,2,112,640]{4,3,2,1,0:T(8,128)(2,1)S(1)}, bf16[1,1,2,112,640]{4,3,2,1,0:T(8,128)(2,1)S(1)}, u32[]{:S(2)}, u32[]{:S(2)}) collective-permute-start(bf16[1,1,2,112,640]{4,3,2,1,0:T(8,128)(2,1)S(1)} %add_convert_fusion.21), channel_id=1, source_target_pairs={{0,6},{1,7},{2,4},{3,5},{4,2},{5,3},{6,0},{7,1},{8,14},{9,15},{10,... | collective-permute-start | bytes 860168 | tf_op jit(solution)/shard_map/ppermute | solution.py:599
  383.4 33.6 %collective-permute-start.59 = (f32[1920]{0:T(1024)S(1)}, f32[1920]{0:T(1024)S(1)}, u32[]{:S(2)}, u32[]{:S(2)}) collective-permute-start(f32[1920]{0:T(1024)S(1)} %add.203), channel_id=1, source_target_pairs={{0,1},{1,0},{2,3},{3,2},{4,5},{5,4},{6,7},{7,6},{8,9},{9,8},{10,11... | collective-permute-start | bytes 23048 | tf_op jit(solution)/shard_map/ppermute | solution.py:599
  387.0 61.2 %collective-permute-start.55 = (bf16[1,1,2,240,640]{4,3,2,1,0:T(8,128)(2,1)S(1)}, bf16[1,1,2,240,640]{4,3,2,1,0:T(8,128)(2,1)S(1)}, u32[]{:S(2)}, u32[]{:S(2)}) collective-permute-start(bf16[1,1,2,240,640]{4,3,2,1,0:T(8,128)(2,1)S(1)} %add_convert_fusion.2), channel_id=1, source_target_pairs={{0,6},{1,7},{2,4},{3,5},{4,2},{5,3},{6,0},{7,1},{8,14},{9,15},{10,... | collective-permute-start | bytes 1843208 | tf_op jit(solution)/shard_map/ppermute | solution.py:599
  406.1 26.3 %collective-permute-start.49 = (bf16[1,1,2,128,640]{4,3,2,1,0:T(8,128)(2,1)S(1)}, bf16[1,1,2,128,640]{4,3,2,1,0:T(8,128)(2,1)S(1)}, u32[]{:S(2)}, u32[]{:S(2)}) collective-permute-start(bf16[1,1,2,128,640]{4,3,2,1,0:T(8,128)(2,1)S(1)} %add_convert_fusion.16), channel_id=1, source_target_pairs={{0,6},{1,7},{2,4},{3,5},{4,2},{5,3},{6,0},{7,1},{8,14},{9,15},{10,... | collective-permute-start | bytes 983048 | tf_op jit(solution)/shard_map/ppermute | solution.py:599
  415.2 17.3 %collective-permute-start.52 = (bf16[1,1,2,112,640]{4,3,2,1,0:T(8,128)(2,1)S(1)}, bf16[1,1,2,112,640]{4,3,2,1,0:T(8,128)(2,1)S(1)}, u32[]{:S(2)}, u32[]{:S(2)}) collective-permute-start(bf16[1,1,2,112,640]{4,3,2,1,0:T(8,128)(2,1)S(1)} %add_convert_fusion.20), channel_id=1, source_target_pairs={{0,1},{1,0},{2,3},{3,2},{4,5},{5,4},{6,7},{7,6},{8,9},{9,8},{10,11... | collective-permute-start | bytes 860168 | tf_op jit(solution)/shard_map/ppermute | solution.py:599
  417.1 15.6 %collective-permute-start.60 = (f32[1920]{0:T(1024)S(1)}, f32[1920]{0:T(1024)S(1)}, u32[]{:S(2)}, u32[]{:S(2)}) collective-permute-start(f32[1920]{0:T(1024)S(1)} %add.204), channel_id=1, source_target_pairs={{0,2},{1,3},{2,0},{3,1},{4,6},{5,7},{6,4},{7,5},{8,10},{9,11},{10,... | collective-permute-start | bytes 23048 | tf_op jit(solution)/shard_map/ppermute | solution.py:599
  432.7 14.8 %collective-permute-start.61 = (f32[1920]{0:T(1024)S(1)}, f32[1920]{0:T(1024)S(1)}, u32[]{:S(2)}, u32[]{:S(2)}) collective-permute-start(f32[1920]{0:T(1024)S(1)} %add.205), channel_id=1, source_target_pairs={{0,6},{1,7},{2,4},{3,5},{4,2},{5,3},{6,0},{7,1},{8,14},{9,15},{10,... | collective-permute-start | bytes 23048 | tf_op jit(solution)/shard_map/ppermute | solution.py:599
  437.1 15.4 %collective-permute-start.51 = (bf16[1,1,2,128,640]{4,3,2,1,0:T(8,128)(2,1)S(1)}, bf16[1,1,2,128,640]{4,3,2,1,0:T(8,128)(2,1)S(1)}, u32[]{:S(2)}, u32[]{:S(2)}) collective-permute-start(bf16[1,1,2,128,640]{4,3,2,1,0:T(8,128)(2,1)S(1)} %add_convert_fusion.15), channel_id=1, source_target_pairs={{0,1},{1,0},{2,3},{3,2},{4,5},{5,4},{6,7},{7,6},{8,9},{9,8},{10,11... | collective-permute-start | bytes 983048 | tf_op jit(solution)/shard_map/ppermute | solution.py:599
  438.6 13.5 %collective-permute-start.53 = (bf16[1,1,2,112,640]{4,3,2,1,0:T(8,128)(2,1)S(1)}, bf16[1,1,2,112,640]{4,3,2,1,0:T(8,128)(2,1)S(1)}, u32[]{:S(2)}, u32[]{:S(2)}) collective-permute-start(bf16[1,1,2,112,640]{4,3,2,1,0:T(8,128)(2,1)S(1)} %add_convert_fusion.19), channel_id=1, source_target_pairs={{0,2},{1,3},{2,0},{3,1},{4,6},{5,7},{6,4},{7,5},{8,10},{9,11},{10,... | collective-permute-start | bytes 860168 | tf_op jit(solution)/shard_map/ppermute | solution.py:599
  (24 other events, 200.2 us)

commit v5 on v4

--- a/solution.py
+++ b/solution.py
@@ -319,6 +319,10 @@
     )(where, h, dy, x1, *sum((w.arrays for w in weights), []))
 
 
+def block_here(where_ref):
+    return 2 * where_ref[1] + where_ref[2]
+
+
 def split_owners(grad, where_ref, put):
     core, x_here = where_ref[0] & 1, where_ref[0] >> 1
     for x in range(2):
@@ -335,26 +339,26 @@
     split_owners(dot(a_ref[...], b_ref[...], 1, 1), where_ref, put)
 
 
-def column_grads_kernel(dim, where_ref, a_ref, b_ref, keep_ref, send_ref):
+def column_grads_kernel(where_ref, a_ref, b_ref, keep_ref, send_ref):
     grad = dot(a_ref[...], b_ref[...], 1, 1).astype(BF16)
     here = (pl.program_id(0) & 1) == (where_ref[0] & 1)
 
     def put(ref):
         for i in range(4):
-            ref[0, (2 * where_ref[1 + dim]) ^ i] = grad[i * OWN:(i + 1) * OWN]
+            ref[0, block_here(where_ref) ^ i] = grad[i * OWN:(i + 1) * OWN]
 
     pl.when(here)(lambda: put(keep_ref))
     pl.when(jnp.logical_not(here))(lambda: put(send_ref))
 
 
-def ffn_grads(where, a, b, dim, by_columns):
+def ffn_grads(where, a, b, by_columns):
     rows = a.shape[1]
     if by_columns:
-        kernel = functools.partial(column_grads_kernel, dim)
+        kernel = column_grads_kernel
         out = pl.BlockSpec((1, 4, OWN, CUT), lambda f, at: ((f >> 1) ^ (at[0] >> 1), 0, 0, 0))
     else:
         kernel = row_grads_kernel
-        out = pl.BlockSpec((2, 1, OWN, CUT), lambda f, at: (0, f ^ (2 * at[1 + dim]), 0, 0))
+        out = pl.BlockSpec((2, 1, OWN, CUT), lambda f, at: (0, f ^ block_here(at), 0, 0))
     return pl.pallas_call(
         kernel,
         grid_spec=pltpu.PrefetchScalarGridSpec(
@@ -491,7 +495,7 @@
     def store(block, grad):
         def put(x, keep, send):
             for i, (low, high) in enumerate(PIECES):
-                at = block ^ (2 * where_ref[1 + i])
+                at = block ^ block_here(where_ref)
                 out_refs[2 * i][x, at] = keep[low:high]
                 out_refs[2 * i + 1][x, at] = send[low:high]
 
@@ -581,11 +585,8 @@
     def __init__(self, count):
         self.count = count
         self.dims = count.bit_length() - 1
-        self.masks = [1, 2, 6] + [1 << i for i in range(3, self.dims)]
         replica, group = lax.axis_index("replica"), lax.axis_index("group")
-        bits = [(replica >> i) & 1 for i in range(self.dims)]
-        self.coordinate = {i: bits[i] for i in range(self.dims)}
-        self.coordinate[1] = bits[1] ^ bits[2]
+        self.coordinate = {i: (replica >> i) & 1 for i in range(self.dims)}
         self.coordinate["x"] = group >> 1
         self.coordinate["core"] = group & 1
         self.me = group
@@ -595,8 +596,7 @@
             return lax.ppermute(value, "group", [(i, i ^ 2) for i in range(4)])
         if dim == "core":
             return lax.ppermute(value, "group", [(i, i ^ 1) for i in range(4)])
-        mask = self.masks[dim]
-        return lax.ppermute(value, "replica", [(i, i ^ mask) for i in range(self.count)])
+        return lax.ppermute(value, "replica", [(i, i ^ (1 << dim)) for i in range(self.count)])
 
     def ordered(self, dim, mine, other, axis):
         return jnp.where(
@@ -645,43 +645,43 @@
 
 
 class Reduce:
-    def __init__(self, cube, keep, got, order):
+    def __init__(self, cube, keep, got, halves, gathers):
         rows, wide = keep.shape[2:]
-        self.cube, self.order, self.shape = cube, order, (4, rows, wide)
-        self.cut = [d for d in order[:2] if d != "x"][0]
+        self.cube, self.shape = cube, (4, rows, wide)
+        self.order = halves + tuple(range(2, cube.dims)) + gathers
+        self.place = {"x": 0, 0: 1, 1: 2}
         self.terms = [t.reshape(2, 2, 2, rows, wide) for t in (keep, got)]
         self.index = 0
 
     def sum(self, terms):
+        if len(terms) == 1:
+            return terms[0]
         return functools.reduce(jnp.add, [t.astype(F32) for t in terms]).astype(BF16)
 
     def ready(self, *others):
         dim = self.order[self.index]
         self.terms[-1] = after(self.terms[-1], *others)
-        if self.index < 2:
-            axis = 0 if dim == "x" else 1
+        if self.index < 3:
+            axis = self.place[dim]
             take = lambda i: [lax.slice_in_dim(t, i, i + 1, axis=axis) for t in self.terms]
             self.send, self.terms = self.sum(take(1)), take(0)
         else:
             self.send = self.sum(self.terms)
-            self.terms = [self.send]
         return self.send
 
     def swap(self):
         dim = self.order[self.index]
-        self.got = self.cube.swap(self.send, dim)
+        got = self.cube.swap(self.send, dim)
         self.index += 1
-        if self.index == len(self.order):
-            self.result = self.cube.ordered(dim, self.send, self.got, 1).reshape(self.shape)
-        elif self.index > 2:
-            self.terms = [self.send, self.got]
+        if self.index <= 3:
+            self.terms = self.terms + [got]
+        elif self.index <= len(self.order) - 2:
+            self.terms = [self.send, got]
         else:
-            self.terms = self.terms + [self.got]
-        return self.got
-
-    def step(self, *others):
-        self.ready(*others)
-        return self.swap()
+            self.terms = [self.cube.ordered(dim, self.send, got, self.place[dim])]
+
+    def result(self):
+        return self.terms[0].reshape(self.shape)
 
 
 def per_device(
@@ -711,7 +711,7 @@
     )
     kv_across = cube.swap(after(kv, q_across), "x")
     relays = [
-        Relay(cube, w_gate, 0, 0, 1), Relay(cube, w_up, 0, 1, 2), Relay(cube, w_down.T, 1, 2, 0)
+        Relay(cube, w_gate, 0, 0, 1), Relay(cube, w_up, 0, 1, 0), Relay(cube, w_down.T, 1, 0, 1)
     ]
     q_sibling, kv_sibling, wo_sibling = core(query_weight), core(kv), core(output_weight)
     siblings = [core(relay.shard) for relay in relays]
@@ -734,32 +734,24 @@
     weights = [relay.weight(sibling, h2) for relay, sibling in zip(relays, siblings)]
     y, dh2, hid, dgate, dup = feed_forward(where, h2, dy, x1, weights)
 
-    more = tuple(range(3, cube.dims))
-    orders = [
-        ("x", 0, 1, 2) + more + (0,), (1, "x", 2, 0) + more + (1,), (2, "x", 0, 1) + more + (2,)
-    ]
-    gd_keep, gd_send = ffn_grads(where, dy, hid, 0, True)
-    gd = Reduce(cube, gd_keep, core(gd_send), orders[0])
-    gg_keep, gg_send = ffn_grads(where, h2, after(dgate, gd_send), 1, False)
-    gg = Reduce(cube, gg_keep, core(gg_send), orders[1])
+    gd_keep, gd_send = ffn_grads(where, dy, hid, True)
+    gd = Reduce(cube, gd_keep, core(gd_send), ("x", 0, 1), (1, 0))
+    gg_keep, gg_send = ffn_grads(where, h2, after(dgate, gd_send), False)
+    gg = Reduce(cube, gg_keep, core(gg_send), (0, "x", 1), (0, 1))
     gd.ready(gg_send)
-    gu_keep, gu_send = ffn_grads(where, h2, after(dup, gd.send), 2, False)
+    gu_keep, gu_send = ffn_grads(where, h2, after(dup, gd.send), False)
     gd.swap()
-    gu = Reduce(cube, gu_keep, core(gu_send), orders[2])
+    gu = Reduce(cube, gu_keep, core(gu_send), (1, 0, "x"), (1, 0))
     gg.ready(gu_send)
     dx1, da, do, ffn_gain_grad = branch(where, after(dh2, gg.send), x1, dy, gains, wo)
     gg.swap()
     gu.ready(da)
-    gd.ready(da)
-    do0 = after(do, gu.send, gd.send)
+    do0 = after(do, gu.send)
     gu.swap()
+    *first, done0 = attend_back(qkv, o, do0, lse, segments, cos, sin, 0)
+    do1 = after(do, done0, *[piece.ready(done0) for piece in (gd, gg)])
     gd.swap()
-    *first, done0 = attend_back(qkv, o, do0, lse, segments, cos, sin, 0)
-    gg.ready(done0)
-    gd.ready(done0)
-    do1 = after(do, done0, gg.send, gd.send)
     gg.swap()
-    gd.swap()
     dqkv, done1 = attend_back(qkv, o, do1, lse, segments, cos, sin, 1, first)
     swaps = [gd, gg, gu]
     dqkv = after(dqkv, *[piece.ready(done1) for piece in swaps])
@@ -767,29 +759,30 @@
         piece.swap()
     parts = []
     weight_parts = weight_grads(where, h, dqkv, o, da)
-    for i in range(len(PIECES)):
+    for i, halves in enumerate((("x", 0, 1), (0, "x", 1))):
         keep, send = weight_parts[2 * i:2 * i + 2]
-        parts.append(Reduce(cube, keep, core(send), orders[i]))
+        parts.append(Reduce(cube, keep, core(send), halves, (1 - i, i)))
     dqkv = after(dqkv, *[part.ready(weight_parts[0]) for part in parts])
     for part in parts:
         part.swap()
     grad_x, attn_gain_grad = input_grads(where, x, dx1, wq, wk, dqkv)
-    swaps = [gu, gg, parts[0], gd, parts[1]]
+    swaps = [gd, gg, gu] + parts
     both = jnp.concatenate([attn_gain_grad, ffn_gain_grad], axis=1).T.reshape(-1)
     ends = ["core", "x"] + list(range(cube.dims))
     token = grad_x
-    for round_of in range(len(orders[0])):
+    while any(piece.index < len(piece.order) for piece in swaps):
         before = token
         for piece in swaps:
             if piece.index < len(piece.order):
                 token = piece.ready(token)
                 piece.swap()
-        both = both + after(cube.swap(after(both, before), ends[round_of]), token)
-    for dim in ends[len(orders[0]):]:
+        if ends:
+            both = both + after(cube.swap(after(both, before), ends.pop(0)), token)
+    for dim in ends:
         both = both + cube.swap(both, dim)
     both = lax.dynamic_slice_in_dim(both.reshape(2, D), cube.me * OWN, OWN, 1)
-    flat = lambda g: jnp.swapaxes(g, 0, 1).reshape(OWN, 4 * CUT).astype(F32)
-    ga = flat(jnp.concatenate([part.result for part in parts], axis=1))
+    flat = lambda g: jnp.concatenate([g[i] for i in range(4)], axis=1)
+    ga = jnp.concatenate([flat(part.result()) for part in parts], axis=0).astype(F32)
     return (
         y.T,
         grad_x.T,
@@ -797,9 +790,9 @@
         ga[:, D:D + KEYS],
         ga[:, D + KEYS:WIDE],
         ga[:, WIDE:],
-        flat(gg.result),
-        flat(gu.result),
-        gd.result.reshape(D, CUT).T.astype(F32),
+        flat(gg.result()).astype(F32),
+        flat(gu.result()).astype(F32),
+        gd.result().reshape(D, CUT).T.astype(F32),
         both[0],
         both[1],
     )

time: 466 us -> 431 us (0.925)
  starting transfers between devices: 89.4 us -> 59.1 us
  other arithmetic: 43.5 us -> 52.7 us
  local copies, waits for them, and re-layouts: 29.5 us -> 21.9 us
  waiting for transfers between devices: 114 us -> 108 us
    ppermute x29 -> x34, starting transfers between devices: 67.7 us -> 38.2 us  [swap(): lax.ppermute(value, 'replica', [(i, i ^ 1 << dim) for i in range(self.cou...]
    ppermute x12, waiting for transfers between devices: 24.5 us -> 14 us  [swap(): return lax.ppermute(value, 'group', [(i, i ^ 2) for i in range(4)])]
    select_n x8 -> x13, other arithmetic: 4.71 us -> 9.71 us  [ordered(): jnp.where(self.coordinate[dim] == 0, jnp.concatenate([mine, other], axis=...]
    ppermute x29 -> x34, waiting for transfers between devices: 85.4 us -> 88.3 us  [swap(): lax.ppermute(value, 'replica', [(i, i ^ 1 << dim) for i in range(self.cou...]
    unnamed x60 -> x61, local copies, waits for them, and re-layouts: 12.4 us -> 9.59 us
  transfers between devices with their start and end apart: 62 -> 67, of which waited for: 18 -> 23; matrix products, arithmetic and copies ran while one was open for 13% -> 15% of each run, Pallas kernels for 23% -> 25%
where the time goes in v5:
time: 431 us; the launch traced here: 422 us
  Pallas kernels  179 us (42%)
  waiting for transfers between devices  108 us (25%)
  starting transfers between devices  59.1 us (14%)
  other arithmetic  52.7 us (12%)
  local copies, waits for them, and re-layouts  21.9 us (5%)
    ppermute x34, waiting for transfers between devices, swap(): lax.ppermute(value, 'replica', [(i, i ^ 1 << dim) for i in range(self.cou...  88.3 us
    pallas_call x1, Pallas kernels, feed_forward(): pl.pallas_call(functools.partial(feed_forward_kernel, weights), grid=(hid...  50.1 us
    ppermute x34, starting transfers between devices, swap(): lax.ppermute(value, 'replica', [(i, i ^ 1 << dim) for i in range(self.cou...  38.2 us
    convert_element_type x25, other arithmetic, sum(): functools.reduce(jnp.add, [t.astype(F32) for t in terms]).astype(BF16)  34 us
    pallas_call x3, Pallas kernels, ffn_grads(): pl.pallas_call(kernel, grid_spec=pltpu.PrefetchScalarGridSpec(num_scalar_...  33.8 us
    pallas_call x2, Pallas kernels, attend_back(): pl.pallas_call(attend_back_kernel, grid=(1,), in_specs=[here(wide), here(...  23.8 us
    pallas_call x2, Pallas kernels, attend(): pl.pallas_call(attend_kernel, grid=(1,), in_specs=[pl.BlockSpec((wide, le...  18.3 us
    ppermute x12, starting transfers between devices, swap(): return lax.ppermute(value, 'group', [(i, i ^ 2) for i in range(4)])  15.9 us
  transfers between devices with their start and end apart: 67, of which 23 were waited for; matrix products, arithmetic and copies ran while one was open for 15% of the time, Pallas kernels for 25%

profile of v5, /device:TPU:0, one launch (start us, length us, event | category | flops | bytes accessed | tf_op | source)
XLA Modules:
  0.0 422.3 jit_solution(16454186678989494278)
XLA Ops:
  0.7 3.0 collective-permute-start.1
  9.8 5.3 %collective-permute-done.1.refs_2_ = bf16[240,960]{1,0:T(8,128)(2,1)S(1)} collective-permute-done((bf16[240,960]{1,0:T(8,128)(2,1)}, bf16[240,960]{1,0:T(8,128)(2,1)S(1)}, u32[]{:S(2)}, u32[]{:S(2)}) %collective-permute-start.1) | collective-permute-done | bytes 460832 | tf_op jit(solution)/shard_map/ppermute | solution.py:596
  16.9 1.8 collective-permute-start.2
  18.7 1.9 constant_dynamic-slice_fusion.1
  21.9 5.9 %collective-permute-done.2.refs_6_ = bf16[240,768]{1,0:T(8,128)(2,1)S(1)} collective-permute-done((bf16[240,768]{1,0:T(8,128)(2,1)S(1)}, bf16[240,768]{1,0:T(8,128)(2,1)S(1)}, u32[]{:S(2)}, u32[]{:S(2)}) %collective-permute-start.2) | collective-permute-done | bytes 368672 | tf_op jit(solution)/shard_map/ppermute | solution.py:596
  29.0 1.7 collective-permute-start.12
  31.1 1.7 collective-permute-start.10
  35.8 9.5 %project.1 = (bf16[1600,1024]{1,0:T(8,128)(2,1)}, bf16[960,1024]{1,0:T(8,128)(2,1)}, bf16[960,128]{1,0:T(8,128)(2,1)}) custom-call(s32[4]{0:T(128)} %pad_add_fusion.where_ref, bf16[960,1024]{1,0:T(8,128)(2,1)} %bitcast.74, f32[32,1024]{1,0:T(8,128)} %get-tuple-element.284.cos_ref, f32[32,1024]{1,0:T(8,128)} %get-tuple-element.283.sin_ref, ...), custom_call_target="tpu_custom_call" | custom-call | flops 1 | bytes 1 | tf_op jit(solution)/shard_map/project/pallas_call | solution.py:145
  45.3 9.1 %attend.2 = (bf16[960,1024]{1,0:T(8,128)(2,1)}, f32[5,8,1024]{2,1,0:T(8,128)}, f32[8,128]{1,0:T(8,128)}) custom-call(bf16[1600,1024]{1,0:T(8,128)(2,1)} %get-tuple-element.121.qkv_ref, s32[2,1,512]{2,1,0:T(1,128)} %broadcast_in_dim.43.segr_ref, s32[2,512,1]{2,1,0:T(8,128)} %copy.57.segc_ref), custom_call_target="tpu_custom_call" | custom-call | flops 1 | bytes 1 | tf_op jit(solution)/shard_map/attend/pallas_call | solution.py:219
  54.5 1.5 collective-permute-start.15
  56.0 1.6 collective-permute-start.14
  58.6 9.2 %attend.3 = (bf16[960,1024]{1,0:T(8,128)(2,1)}, f32[5,8,1024]{2,1,0:T(8,128)}, f32[8,128]{1,0:T(8,128)}) custom-call(bf16[1600,1024]{1,0:T(8,128)(2,1)} %get-tuple-element.121.qkv_ref, s32[2,1,512]{2,1,0:T(1,128)} %broadcast_in_dim.43.segr_ref, s32[2,512,1]{2,1,0:T(8,128)} %copy.57.segc_ref, ...), custom_call_target="tpu_custom_call", output_to_operand_aliasing={{0}: (3, {}), {1}: (4, {})} | custom-call | flops 1 | bytes 1 | tf_op jit(solution)/shard_map/attend/pallas_call | solution.py:219
  67.8 1.8 collective-permute-done.13
  70.8 1.7 collective-permute-start.24
  73.7 1.6 collective-permute-start.21
  77.5 2.2 collective-permute-done.17.refs_3_
  80.6 8.5 %middle.1 = (f32[960,1024]{1,0:T(8,128)}, bf16[960,1024]{1,0:T(8,128)(2,1)}) custom-call(s32[4]{0:T(128)} %pad_add_fusion.where_ref, bf16[960,1024]{1,0:T(8,128)(2,1)} %bitcast.75, bf16[960,1024]{1,0:T(8,128)(2,1)} %get-tuple-element.132.o_ref, bf16[960,128]{1,0:T(8,128)(2,1)} %get-tuple-element.133.gain_ref, bf16[240,960]{1,0:T(8,128)(2,1)} %refs_0_.8, ...), custom_call_target="tpu_custom_call" | custom-call | flops 1 | bytes 1 | tf_op jit(solution)/shard_map/middle/pallas_call | solution.py:257
  89.7 8.4 %collective-permute-done.18.refs_3_ = bf16[240,1280]{1,0:T(8,128)(2,1)} collective-permute-done((bf16[240,1280]{1,0:T(8,128)(2,1)S(1)}, bf16[240,1280]{1,0:T(8,128)(2,1)}, u32[]{:S(2)}, u32[]{:S(2)}) %collective-permute-start.18) | collective-permute-done | bytes 614432 | tf_op jit(solution)/shard_map/ppermute | solution.py:599
  102.1 50.1 %feed_forward.1 = (bf16[960,1024]{1,0:T(8,128)(2,1)}, f32[960,1024]{1,0:T(8,128)}, bf16[2560,1024]{1,0:T(8,128)(2,1)}, bf16[2560,1024]{1,0:T(8,128)(2,1)}, bf16[2560,1024]{1,0:T(8,128)(2,1)}) custom-call(s32[4]{0:T(128)} %pad_add_fusion.where_ref, bf16[960,1024]{1,0:T(8,128)(2,1)} %get-tuple-element.136.h_ref.a_ref, bf16[960,1024]{1,0:T(8,128)(2,1)} %bitcast.77, ...), custom_call_target="tpu_custom_call" | custom-call | flops 1 | bytes 1 | tf_op jit(solution)/shard_map/feed_forward/pallas_call | solution.py:308
  152.3 11.9 %ffn_grads.3 = (bf16[2,4,240,640]{3,2,1,0:T(8,128)(2,1)}, bf16[2,4,240,640]{3,2,1,0:T(8,128)(2,1)}) custom-call(s32[4]{0:T(128)} %pad_add_fusion.where_ref, bf16[960,1024]{1,0:T(8,128)(2,1)} %bitcast.78, bf16[2560,1024]{1,0:T(8,128)(2,1)} %get-tuple-element.144.b_ref), custom_call_target="tpu_custom_call" | custom-call | flops 1 | bytes 1 | tf_op jit(solution)/shard_map/ffn_grads/pallas_call | solution.py:362
  164.8 10.7 %ffn_grads.4 = (bf16[2,4,240,640]{3,2,1,0:T(8,128)(2,1)}, bf16[2,4,240,640]{3,2,1,0:T(8,128)(2,1)}) custom-call(s32[4]{0:T(128)} %pad_add_fusion.where_ref, bf16[960,1024]{1,0:T(8,128)(2,1)} %get-tuple-element.136.h_ref.a_ref, bf16[2560,1024]{1,0:T(8,128)(2,1)} %get-tuple-element.146.b_ref), custom_call_target="tpu_custom_call" | custom-call | flops 1 | bytes 1 | tf_op jit(solution)/shard_map/ffn_grads/pallas_call | solution.py:362
  175.6 1.9 fusion.2
  177.4 1.6 fusion
  179.0 11.2 %ffn_grads.5 = (bf16[2,4,240,640]{3,2,1,0:T(8,128)(2,1)}, bf16[2,4,240,640]{3,2,1,0:T(8,128)(2,1)}) custom-call(s32[4]{0:T(128)} %pad_add_fusion.where_ref, bf16[960,1024]{1,0:T(8,128)(2,1)} %get-tuple-element.136.h_ref.a_ref, bf16[2560,1024]{1,0:T(8,128)(2,1)} %get-tuple-element.152.b_ref), custom_call_target="tpu_custom_call" | custom-call | flops 1 | bytes 1 | tf_op jit(solution)/shard_map/ffn_grads/pallas_call | solution.py:362
  190.7 3.0 add_convert_fusion.1
  193.7 2.1 collective-permute-start.31
  196.9 10.9 %branch.1 = (f32[960,1024]{1,0:T(8,128)}, bf16[960,1024]{1,0:T(8,128)(2,1)}, bf16[960,1024]{1,0:T(8,128)(2,1)}, f32[960,1]{1,0:T(8,128)}) custom-call(s32[4]{0:T(128)} %pad_add_fusion.where_ref, f32[960,1024]{1,0:T(8,128)} %get-tuple-element.155.dh_ref, f32[960,1024]{1,0:T(8,128)} %get-tuple-element.137.x1_ref, bf16[960,1024]{1,0:T(8,128)(2,1)} %bitcast.79, ...), custom_call_target="tpu_custom_call" | custom-call | flops 1 | bytes 1 | tf_op jit(solution)/shard_map/branch/pallas_call | solution.py:407
  207.8 3.0 add_convert_fusion
  210.8 1.6 collective-permute-start.34
  212.4 11.8 %attend_back.2 = (bf16[1600,1024]{1,0:T(8,128)(2,1)}, f32[8,128]{1,0:T(8,128)}) custom-call(bf16[1600,1024]{1,0:T(8,128)(2,1)} %get-tuple-element.121.qkv_ref, bf16[960,1024]{1,0:T(8,128)(2,1)} %get-tuple-element.132.o_ref, bf16[960,1024]{1,0:T(8,128)(2,1)} %get-tuple-element.166.do_ref, f32[5,8,1024]{2,1,0:T(8,128)} %get-tuple-element.162.lse_ref, ...), custom_call_target="tpu_custom_call" | custom-call | flops 1 | bytes 1 | tf_op jit(solution)/shard_map/attend_back/pallas_call | solution.py:464
  224.2 1.7 add_convert_fusion.3
  226.8 2.3 add_convert_fusion.4
  230.2 12.0 %attend_back.3 = (bf16[1600,1024]{1,0:T(8,128)(2,1)}, f32[8,128]{1,0:T(8,128)}) custom-call(bf16[1600,1024]{1,0:T(8,128)(2,1)} %get-tuple-element.121.qkv_ref, bf16[960,1024]{1,0:T(8,128)(2,1)} %get-tuple-element.132.o_ref, bf16[960,1024]{1,0:T(8,128)(2,1)} %get-tuple-element.166.do_ref, ...), custom_call_target="tpu_custom_call", output_to_operand_aliasing={{0}: (8, {})} | custom-call | flops 1 | bytes 1 | tf_op jit(solution)/shard_map/attend_back/pallas_call | solution.py:464
  242.3 2.1 collective-permute-done.32
  244.4 2.2 add_convert_fusion.14
  246.6 1.9 add_convert_fusion.15
  248.5 2.5 add_convert_fusion.2
  251.1 12.8 %weight_grads.1 = (bf16[2,4,128,640]{3,2,1,0:T(8,128)(2,1)}, bf16[2,4,128,640]{3,2,1,0:T(8,128)(2,1)}, bf16[2,4,112,640]{3,2,1,0:T(8,128)(2,1)}, bf16[2,4,112,640]{3,2,1,0:T(8,128)(2,1)}) custom-call(s32[4]{0:T(128)} %pad_add_fusion.where_ref, bf16[960,1024]{1,0:T(8,128)(2,1)} %get-tuple-element.174.h_ref, bf16[1600,1024]{1,0:T(8,128)(2,1)} %get-tuple-element.181.dqkv_ref, ...), custom_call_target="tpu_custom_call" | custom-call | flops 1 | bytes 1 | tf_op jit(solution)/shard_map/weight_grads/pallas_call | solution.py:515
  267.4 1.5 fusion.3
  269.0 2.0 add_convert_fusion.5
  274.5 11.4 %input_grads.1 = (bf16[960,1024]{1,0:T(8,128)(2,1)}, f32[960,1]{1,0:T(8,128)}) custom-call(s32[4]{0:T(128)} %pad_add_fusion.where_ref, bf16[960,1024]{1,0:T(8,128)(2,1)} %bitcast.76, f32[960,1024]{1,0:T(8,128)} %get-tuple-element.156.dx_ref, bf16[1600,1024]{1,0:T(8,128)(2,1)} %get-tuple-element.181.dqkv_ref, bf16[240,960]{1,0:T(8,128)(2,1)} %refs_0_.9, ...), custom_call_target="tpu_custom_call" | custom-call | flops 1 | bytes 1 | tf_op jit(solution)/shard_map/input_grads/pallas_call | solution.py:555
  286.6 1.4 add_convert_fusion.13
  288.1 2.6 collective-permute-start.44
  298.3 1.7 collective-permute-start.50
  300.0 11.9 %collective-permute-done.44 = bf16[1,1,1,240,640]{4,3,2,1,0:T(8,128)(2,1)S(1)} collective-permute-done((bf16[1,1,1,240,640]{4,3,2,1,0:T(8,128)(2,1)S(1)}, bf16[1,1,1,240,640]{4,3,2,1,0:T(8,128)(2,1)S(1)}, u32[]{:S(2)}, u32[]{:S(2)}) %collective-permute-start.44) | collective-permute-done | bytes 307232 | tf_op jit(solution)/shard_map/ppermute | solution.py:599
  312.1 5.3 %collective-permute-done.43 = bf16[1,1,1,240,640]{4,3,2,1,0:T(8,128)(2,1)S(1)} collective-permute-done((bf16[1,1,1,240,640]{4,3,2,1,0:T(8,128)(2,1)S(1)}, bf16[1,1,1,240,640]{4,3,2,1,0:T(8,128)(2,1)S(1)}, u32[]{:S(2)}, u32[]{:S(2)}) %collective-permute-start.43) | collective-permute-done | bytes 307232 | tf_op jit(solution)/shard_map/ppermute | solution.py:599
  318.3 1.4 add_convert_fusion.8
  319.8 6.1 %collective-permute-done.49 = bf16[1,1,1,240,640]{4,3,2,1,0:T(8,128)(2,1)S(1)} collective-permute-done((bf16[1,1,1,240,640]{4,3,2,1,0:T(8,128)(2,1)S(1)}, bf16[1,1,1,240,640]{4,3,2,1,0:T(8,128)(2,1)S(1)}, u32[]{:S(2)}, u32[]{:S(2)}) %collective-permute-start.49) | collective-permute-done | bytes 307232 | tf_op jit(solution)/shard_map/ppermute | solution.py:599
  331.9 3.3 collective-permute-done.47
  335.4 3.3 collective-permute-done.46
  339.9 1.9 collective-permute-done.53
  344.0 23.5 %collective-permute-done.52 = bf16[1,1,1,240,640]{4,3,2,1,0:T(8,128)(2,1)S(1)} collective-permute-done((bf16[1,1,1,240,640]{4,3,2,1,0:T(8,128)(2,1)S(1)}, bf16[1,1,1,240,640]{4,3,2,1,0:T(8,128)(2,1)S(1)}, u32[]{:S(2)}, u32[]{:S(2)}) %collective-permute-start.52) | collective-permute-done | bytes 307232 | tf_op jit(solution)/shard_map/ppermute | solution.py:599
  370.8 2.7 collective-permute-done.63
  374.8 2.3 collective-permute-done.64
  377.2 2.0 collective-permute-start.65
  382.1 2.2 collective-permute-start.66
  386.8 2.0 collective-permute-start.58
  390.0 1.7 maximum_convert_fusion.1
  391.7 4.4 %collective-permute-done.61 = bf16[1,1,2,240,640]{4,3,2,1,0:T(8,128)(2,1)} collective-permute-done((bf16[1,1,2,240,640]{4,3,2,1,0:T(8,128)(2,1)S(1)}, bf16[1,1,2,240,640]{4,3,2,1,0:T(8,128)(2,1)}, u32[]{:S(2)}, u32[]{:S(2)}) %collective-permute-start.61) | collective-permute-done | bytes 614432 | tf_op jit(solution)/shard_map/ppermute | solution.py:599
  396.1 1.5 maximum_select_fusion.2
  397.6 1.7 convert_bitcast_fusion
  400.5 12.6 %collective-permute-done.56 = bf16[1,1,2,128,640]{4,3,2,1,0:T(8,128)(2,1)} collective-permute-done((bf16[1,1,2,128,640]{4,3,2,1,0:T(8,128)(2,1)S(1)}, bf16[1,1,2,128,640]{4,3,2,1,0:T(8,128)(2,1)}, u32[]{:S(2)}, u32[]{:S(2)}) %collective-permute-start.56) | collective-permute-done | bytes 327712 | tf_op jit(solution)/shard_map/ppermute | solution.py:599
  418.7 1.5 maximum_select_fusion.1
  420.3 1.7 maximum_convert_fusion.2
  (219 shorter events, 72.9 us)
Async XLA Ops:
  0.7 14.4 %collective-permute-start.1 = (bf16[240,960]{1,0:T(8,128)(2,1)}, bf16[240,960]{1,0:T(8,128)(2,1)S(1)}, u32[]{:S(2)}, u32[]{:S(2)}) collective-permute-start(bf16[240,960]{1,0:T(8,128)(2,1)} %refs_0_.9), channel_id=1, source_target_pairs={{0,16},{8,24},{16,0},{24,8},{1,17},{9,25},{17,1},{25,9},{2,18},{10... | collective-permute-start | bytes 1382408 | tf_op jit(solution)/shard_map/ppermute | solution.py:596
  3.7 24.1 %collective-permute-start.7 = (bf16[960,640]{1,0:T(8,128)(2,1)}, bf16[960,640]{1,0:T(8,128)(2,1)}, u32[]{:S(2)}, u32[]{:S(2)}) collective-permute-start(bf16[960,640]{1,0:T(8,128)(2,1)} %bitcast.100), channel_id=1, source_target_pairs={{0,8},{8,0},{16,24},{24,16},{1,9},{9,1},{17,25},{25,17},{2,10},{10... | collective-permute-start | bytes 3686408 | tf_op jit(solution)/shard_map/ppermute | solution.py:598
  3.7 24.1 %collective-permute-start.5 = (bf16[240,2560]{1,0:T(8,128)(2,1)}, bf16[240,2560]{1,0:T(8,128)(2,1)}, u32[]{:S(2)}, u32[]{:S(2)}) collective-permute-start(bf16[240,2560]{1,0:T(8,128)(2,1)} %refs_0_.7), channel_id=1, source_target_pairs={{0,8},{8,0},{16,24},{24,16},{1,9},{9,1},{17,25},{25,17},{2,10},{10... | collective-permute-start | bytes 3686408 | tf_op jit(solution)/shard_map/ppermute | solution.py:598
  4.2 23.6 %collective-permute-start.6 = (bf16[240,2560]{1,0:T(8,128)(2,1)}, bf16[240,2560]{1,0:T(8,128)(2,1)}, u32[]{:S(2)}, u32[]{:S(2)}) collective-permute-start(bf16[240,2560]{1,0:T(8,128)(2,1)} %refs_6_.1), channel_id=1, source_target_pairs={{0,8},{8,0},{16,24},{24,16},{1,9},{9,1},{17,25},{25,17},{2,10},{10... | collective-permute-start | bytes 3686408 | tf_op jit(solution)/shard_map/ppermute | solution.py:598
  4.2 12.8 %collective-permute-start = (bf16[240,960]{1,0:T(8,128)(2,1)}, bf16[240,960]{1,0:T(8,128)(2,1)S(1)}, u32[]{:S(2)}, u32[]{:S(2)}) collective-permute-start(bf16[240,960]{1,0:T(8,128)(2,1)} %refs_0_.9), channel_id=1, source_target_pairs={{0,8},{8,0},{16,24},{24,16},{1,9},{9,1},{17,25},{25,17},{2,10},{10... | collective-permute-start | bytes 1382408 | tf_op jit(solution)/shard_map/ppermute | solution.py:598
  16.8 5.1 %collective-permute-start.4 = (bf16[240,960]{1,0:T(8,128)(2,1)S(1)}, bf16[240,960]{1,0:T(8,128)(2,1)S(1)}, u32[]{:S(2)}, u32[]{:S(2)}) collective-permute-start(bf16[240,960]{1,0:T(8,128)(2,1)S(1)} %copy-done.4), channel_id=1, source_target_pairs={{0,8},{8,0},{16,24},{24,16},{1,9},{9,1},{17,25},{25,17},{2,10},{10... | collective-permute-start | bytes 1382408 | tf_op jit(solution)/shard_map/ppermute | solution.py:598
  16.9 10.9 %collective-permute-start.2 = (bf16[240,768]{1,0:T(8,128)(2,1)S(1)}, bf16[240,768]{1,0:T(8,128)(2,1)S(1)}, u32[]{:S(2)}, u32[]{:S(2)}) collective-permute-start(bf16[240,768]{1,0:T(8,128)(2,1)S(1)} %concatenate.199.refs_4_), channel_id=1, source_target_pairs={{0,16},{8,24},{16,0},{24,8},{1,17},{9,25},{17,1},{25,9},{2,18},{10... | collective-permute-start | bytes 1105928 | tf_op jit(solution)/shard_map/ppermute | solution.py:596
  28.5 6.5 %collective-permute-start.8 = (bf16[240,960]{1,0:T(8,128)(2,1)S(1)}, bf16[240,960]{1,0:T(8,128)(2,1)S(1)}, u32[]{:S(2)}, u32[]{:S(2)}) collective-permute-start(bf16[240,960]{1,0:T(8,128)(2,1)S(1)} %collective-permute-done.1.refs_2_), channel_id=1, source_target_pairs={{0,8},{8,0},{16,24},{24,16},{1,9},{9,1},{17,25},{25,17},{2,10},{10... | collective-permute-start | bytes 1382408 | tf_op jit(solution)/shard_map/ppermute | solution.py:598
  28.5 6.5 %collective-permute-start.9 = (bf16[240,768]{1,0:T(8,128)(2,1)}, bf16[240,768]{1,0:T(8,128)(2,1)}, u32[]{:S(2)}, u32[]{:S(2)}) collective-permute-start(bf16[240,768]{1,0:T(8,128)(2,1)} %copy-done.12), channel_id=1, source_target_pairs={{0,8},{8,0},{16,24},{24,16},{1,9},{9,1},{17,25},{25,17},{2,10},{10... | collective-permute-start | bytes 1105928 | tf_op jit(solution)/shard_map/ppermute | solution.py:598
  29.0 25.4 %collective-permute-start.12 = (bf16[240,640]{1,0:T(8,128)(2,1)S(1)}, bf16[240,640]{1,0:T(8,128)(2,1)}, u32[]{:S(2)}, u32[]{:S(2)}) collective-permute-start(bf16[240,640]{1,0:T(8,128)(2,1)S(1)} %dynamic-slice_bitcast_fusion), channel_id=1, source_target_pairs={{0,16},{8,24},{16,0},{24,8},{1,17},{9,25},{17,1},{25,9},{2,18},{10... | collective-permute-start | bytes 921608 | tf_op jit(solution)/shard_map/ppermute | solution.py:596
  30.8 25.2 %collective-permute-start.11 = (bf16[240,640]{1,0:T(8,128)(2,1)}, bf16[240,640]{1,0:T(8,128)(2,1)}, u32[]{:S(2)}, u32[]{:S(2)}) collective-permute-start(bf16[240,640]{1,0:T(8,128)(2,1)} %get-tuple-element.119), channel_id=1, source_target_pairs={{0,16},{8,24},{16,0},{24,8},{1,17},{9,25},{17,1},{25,9},{2,18},{10... | collective-permute-start | bytes 921608 | tf_op jit(solution)/shard_map/ppermute | solution.py:596
  31.1 26.5 %collective-permute-start.10 = (bf16[240,640]{1,0:T(8,128)(2,1)}, bf16[240,640]{1,0:T(8,128)(2,1)}, u32[]{:S(2)}, u32[]{:S(2)}) collective-permute-start(bf16[240,640]{1,0:T(8,128)(2,1)} %get-tuple-element.118), channel_id=1, source_target_pairs={{0,16},{8,24},{16,0},{24,8},{1,17},{9,25},{17,1},{25,9},{2,18},{10... | collective-permute-start | bytes 921608 | tf_op jit(solution)/shard_map/ppermute | solution.py:596
  54.5 13.3 %collective-permute-start.15 = (bf16[240,640]{1,0:T(8,128)(2,1)}, bf16[240,640]{1,0:T(8,128)(2,1)S(1)}, u32[]{:S(2)}, u32[]{:S(2)}) collective-permute-start(bf16[240,640]{1,0:T(8,128)(2,1)} %collective-permute-done.12), channel_id=1, source_target_pairs={{0,1},{1,0},{2,3},{3,2},{4,5},{5,4},{6,7},{7,6},{8,9},{9,8},{10,11... | collective-permute-start | bytes 921608 | tf_op jit(solution)/shard_map/ppermute | solution.py:599
  56.0 11.8 %collective-permute-start.14 = (bf16[240,640]{1,0:T(8,128)(2,1)}, bf16[240,640]{1,0:T(8,128)(2,1)S(1)}, u32[]{:S(2)}, u32[]{:S(2)}) collective-permute-start(bf16[240,640]{1,0:T(8,128)(2,1)} %collective-permute-done.11), channel_id=1, source_target_pairs={{0,2},{1,3},{2,0},{3,1},{4,6},{5,7},{6,4},{7,5},{8,10},{9,11},{10,... | collective-permute-start | bytes 921608 | tf_op jit(solution)/shard_map/ppermute | solution.py:599
  57.6 12.0 %collective-permute-start.13 = (bf16[240,640]{1,0:T(8,128)(2,1)}, bf16[240,640]{1,0:T(8,128)(2,1)S(1)}, u32[]{:S(2)}, u32[]{:S(2)}) collective-permute-start(bf16[240,640]{1,0:T(8,128)(2,1)} %collective-permute-done.10), channel_id=1, source_target_pairs={{0,1},{1,0},{2,3},{3,2},{4,5},{5,4},{6,7},{7,6},{8,9},{9,8},{10,11... | collective-permute-start | bytes 921608 | tf_op jit(solution)/shard_map/ppermute | solution.py:599
  58.1 19.0 %collective-permute-start.16 = (bf16[240,960]{1,0:T(8,128)(2,1)S(1)}, bf16[240,960]{1,0:T(8,128)(2,1)S(1)}, u32[]{:S(2)}, u32[]{:S(2)}) collective-permute-start(bf16[240,960]{1,0:T(8,128)(2,1)S(1)} %copy-done.4), channel_id=1, source_target_pairs={{0,16},{8,24},{16,0},{24,8},{1,17},{9,25},{17,1},{25,9},{2,18},{10... | collective-permute-start | bytes 1382408 | tf_op jit(solution)/shard_map/ppermute | solution.py:596
  70.8 18.3 %collective-permute-start.24 = (bf16[480,640]{1,0:T(8,128)(2,1)S(1)}, bf16[480,640]{1,0:T(8,128)(2,1)S(1)}, u32[]{:S(2)}, u32[]{:S(2)}) collective-permute-start(bf16[480,640]{1,0:T(8,128)(2,1)S(1)} %maximum_select_fusion.6.refs_14_), channel_id=1, source_target_pairs={{0,2},{1,3},{2,0},{3,1},{4,6},{5,7},{6,4},{7,5},{8,10},{9,11},{10,... | collective-permute-start | bytes 1843208 | tf_op jit(solution)/shard_map/ppermute | solution.py:599
  73.7 15.7 %collective-permute-start.21 = (bf16[240,1280]{1,0:T(8,128)(2,1)S(1)}, bf16[240,1280]{1,0:T(8,128)(2,1)}, u32[]{:S(2)}, u32[]{:S(2)}) collective-permute-start(bf16[240,1280]{1,0:T(8,128)(2,1)S(1)} %maximum_select_fusion.5.refs_8_), channel_id=1, source_target_pairs={{0,1},{1,0},{2,3},{3,2},{4,5},{5,4},{6,7},{7,6},{8,9},{9,8},{10,11... | collective-permute-start | bytes 1843208 | tf_op jit(solution)/shard_map/ppermute | solution.py:599
  76.5 21.7 %collective-permute-start.18 = (bf16[240,1280]{1,0:T(8,128)(2,1)S(1)}, bf16[240,1280]{1,0:T(8,128)(2,1)}, u32[]{:S(2)}, u32[]{:S(2)}) collective-permute-start(bf16[240,1280]{1,0:T(8,128)(2,1)S(1)} %maximum_select_fusion.4.refs_2_), channel_id=1, source_target_pairs={{0,2},{1,3},{2,0},{3,1},{4,6},{5,7},{6,4},{7,5},{8,10},{9,11},{10,... | collective-permute-start | bytes 1843208 | tf_op jit(solution)/shard_map/ppermute | solution.py:599
  77.0 21.2 %collective-permute-start.25 = (bf16[480,640]{1,0:T(8,128)(2,1)S(1)}, bf16[480,640]{1,0:T(8,128)(2,1)}, u32[]{:S(2)}, u32[]{:S(2)}) collective-permute-start(bf16[480,640]{1,0:T(8,128)(2,1)S(1)} %maximum_select_fusion.6.refs_14_), channel_id=1, source_target_pairs={{0,8},{8,0},{16,24},{24,16},{1,9},{9,1},{17,25},{25,17},{2,10},{10... | collective-permute-start | bytes 1843208 | tf_op jit(solution)/shard_map/ppermute | solution.py:598
  77.0 2.7 collective-permute-start.17
  79.8 18.9 %collective-permute-start.22 = (bf16[240,1280]{1,0:T(8,128)(2,1)S(1)}, bf16[240,1280]{1,0:T(8,128)(2,1)}, u32[]{:S(2)}, u32[]{:S(2)}) collective-permute-start(bf16[240,1280]{1,0:T(8,128)(2,1)S(1)} %maximum_select_fusion.5.refs_8_), channel_id=1, source_target_pairs={{0,8},{8,0},{16,24},{24,16},{1,9},{9,1},{17,25},{25,17},{2,10},{10... | collective-permute-start | bytes 1843208 | tf_op jit(solution)/shard_map/ppermute | solution.py:598
  89.2 9.5 %collective-permute-start.19 = (bf16[240,1280]{1,0:T(8,128)(2,1)S(1)}, bf16[240,1280]{1,0:T(8,128)(2,1)S(1)}, u32[]{:S(2)}, u32[]{:S(2)}) collective-permute-start(bf16[240,1280]{1,0:T(8,128)(2,1)S(1)} %maximum_select_fusion.4.refs_2_), channel_id=1, source_target_pairs={{0,8},{8,0},{16,24},{24,16},{1,9},{9,1},{17,25},{25,17},{2,10},{10... | collective-permute-start | bytes 1843208 | tf_op jit(solution)/shard_map/ppermute | solution.py:598
  89.4 9.3 %collective-permute-start.26 = (bf16[480,640]{1,0:T(8,128)(2,1)S(1)}, bf16[480,640]{1,0:T(8,128)(2,1)S(1)}, u32[]{:S(2)}, u32[]{:S(2)}) collective-permute-start(bf16[480,640]{1,0:T(8,128)(2,1)S(1)} %collective-permute-done.24.refs_15_), channel_id=1, source_target_pairs={{0,8},{8,0},{16,24},{24,16},{1,9},{9,1},{17,25},{25,17},{2,10},{10... | collective-permute-start | bytes 1843208 | tf_op jit(solution)/shard_map/ppermute | solution.py:598
  98.2 3.1 collective-permute-start.20
  164.1 13.3 %collective-permute-start.28 = (bf16[2,4,240,640]{3,2,1,0:T(8,128)(2,1)}, bf16[2,4,240,640]{3,2,1,0:T(8,128)(2,1)}, u32[]{:S(2)}, u32[]{:S(2)}) collective-permute-start(bf16[2,4,240,640]{3,2,1,0:T(8,128)(2,1)} %get-tuple-element.145), channel_id=1, source_target_pairs={{0,8},{8,0},{16,24},{24,16},{1,9},{9,1},{17,25},{25,17},{2,10},{10... | collective-permute-start | bytes 7372808 | tf_op jit(solution)/shard_map/ppermute | solution.py:598
  175.5 15.2 %collective-permute-start.27 = (bf16[2,4,240,640]{3,2,1,0:T(8,128)(2,1)}, bf16[2,4,240,640]{3,2,1,0:T(8,128)(2,1)}, u32[]{:S(2)}, u32[]{:S(2)}) collective-permute-start(bf16[2,4,240,640]{3,2,1,0:T(8,128)(2,1)} %get-tuple-element.148), channel_id=1, source_target_pairs={{0,8},{8,0},{16,24},{24,16},{1,9},{9,1},{17,25},{25,17},{2,10},{10... | collective-permute-start | bytes 7372808 | tf_op jit(solution)/shard_map/ppermute | solution.py:598
  190.2 17.6 %collective-permute-start.29 = (bf16[2,4,240,640]{3,2,1,0:T(8,128)(2,1)}, bf16[2,4,240,640]{3,2,1,0:T(8,128)(2,1)}, u32[]{:S(2)}, u32[]{:S(2)}) collective-permute-start(bf16[2,4,240,640]{3,2,1,0:T(8,128)(2,1)} %get-tuple-element.153), channel_id=1, source_target_pairs={{0,8},{8,0},{16,24},{24,16},{1,9},{9,1},{17,25},{25,17},{2,10},{10... | collective-permute-start | bytes 7372808 | tf_op jit(solution)/shard_map/ppermute | solution.py:598
  193.7 30.4 %collective-permute-start.31 = (bf16[2,1,2,240,640]{4,3,2,1,0:T(8,128)(2,1)}, bf16[2,1,2,240,640]{4,3,2,1,0:T(8,128)(2,1)}, u32[]{:S(2)}, u32[]{:S(2)}) collective-permute-start(bf16[2,1,2,240,640]{4,3,2,1,0:T(8,128)(2,1)} %add_convert_fusion.1), channel_id=1, source_target_pairs={{0,1},{1,0},{2,3},{3,2},{4,5},{5,4},{6,7},{7,6},{8,9},{9,8},{10,11... | collective-permute-start | bytes 3686408 | tf_op jit(solution)/shard_map/ppermute | solution.py:599
  195.8 30.0 %collective-permute-start.30 = (bf16[1,2,2,240,640]{4,3,2,1,0:T(8,128)(2,1)S(1)}, bf16[1,2,2,240,640]{4,3,2,1,0:T(8,128)(2,1)}, u32[]{:S(2)}, u32[]{:S(2)}) collective-permute-start(bf16[1,2,2,240,640]{4,3,2,1,0:T(8,128)(2,1)S(1)} %fusion), channel_id=1, source_target_pairs={{0,16},{8,24},{16,0},{24,8},{1,17},{9,25},{17,1},{25,9},{2,18},{10... | collective-permute-start | bytes 3686408 | tf_op jit(solution)/shard_map/ppermute | solution.py:596
  210.8 37.7 %collective-permute-start.34 = (bf16[2,2,1,240,640]{4,3,2,1,0:T(8,128)(2,1)}, bf16[2,2,1,240,640]{4,3,2,1,0:T(8,128)(2,1)}, u32[]{:S(2)}, u32[]{:S(2)}) collective-permute-start(bf16[2,2,1,240,640]{4,3,2,1,0:T(8,128)(2,1)} %add_convert_fusion), channel_id=1, source_target_pairs={{0,2},{1,3},{2,0},{3,1},{4,6},{5,7},{6,4},{7,5},{8,10},{9,11},{10,... | collective-permute-start | bytes 3686408 | tf_op jit(solution)/shard_map/ppermute | solution.py:599
  225.9 16.4 %collective-permute-start.33 = (bf16[1,1,2,240,640]{4,3,2,1,0:T(8,128)(2,1)S(1)}, bf16[1,1,2,240,640]{4,3,2,1,0:T(8,128)(2,1)S(1)}, u32[]{:S(2)}, u32[]{:S(2)}) collective-permute-start(bf16[1,1,2,240,640]{4,3,2,1,0:T(8,128)(2,1)S(1)} %add_convert_fusion.3), channel_id=1, source_target_pairs={{0,16},{8,24},{16,0},{24,8},{1,17},{9,25},{17,1},{25,9},{2,18},{10... | collective-permute-start | bytes 1843208 | tf_op jit(solution)/shard_map/ppermute | solution.py:596
  229.1 15.2 %collective-permute-start.32 = (bf16[1,1,2,240,640]{4,3,2,1,0:T(8,128)(2,1)}, bf16[1,1,2,240,640]{4,3,2,1,0:T(8,128)(2,1)S(1)}, u32[]{:S(2)}, u32[]{:S(2)}) collective-permute-start(bf16[1,1,2,240,640]{4,3,2,1,0:T(8,128)(2,1)} %add_convert_fusion.4), channel_id=1, source_target_pairs={{0,1},{1,0},{2,3},{3,2},{4,5},{5,4},{6,7},{7,6},{8,9},{9,8},{10,11... | collective-permute-start | bytes 1843208 | tf_op jit(solution)/shard_map/ppermute | solution.py:599
  263.9 5.0 %collective-permute-start.36 = (bf16[2,4,112,640]{3,2,1,0:T(8,128)(2,1)}, bf16[2,4,112,640]{3,2,1,0:T(8,128)(2,1)}, u32[]{:S(2)}, u32[]{:S(2)}) collective-permute-start(bf16[2,4,112,640]{3,2,1,0:T(8,128)(2,1)} %get-tuple-element.179), channel_id=1, source_target_pairs={{0,8},{8,0},{16,24},{24,16},{1,9},{9,1},{17,25},{25,17},{2,10},{10... | collective-permute-start | bytes 3440648 | tf_op jit(solution)/shard_map/ppermute | solution.py:598
  263.9 8.5 %collective-permute-start.35 = (bf16[2,4,128,640]{3,2,1,0:T(8,128)(2,1)}, bf16[2,4,128,640]{3,2,1,0:T(8,128)(2,1)S(1)}, u32[]{:S(2)}, u32[]{:S(2)}) collective-permute-start(bf16[2,4,128,640]{3,2,1,0:T(8,128)(2,1)} %get-tuple-element.176), channel_id=1, source_target_pairs={{0,8},{8,0},{16,24},{24,16},{1,9},{9,1},{17,25},{25,17},{2,10},{10... | collective-permute-start | bytes 3932168 | tf_op jit(solution)/shard_map/ppermute | solution.py:598
  264.6 21.3 %collective-permute-start.40 = (bf16[1,1,1,240,640]{4,3,2,1,0:T(8,128)(2,1)}, bf16[1,1,1,240,640]{4,3,2,1,0:T(8,128)(2,1)S(1)}, u32[]{:S(2)}, u32[]{:S(2)}) collective-permute-start(bf16[1,1,1,240,640]{4,3,2,1,0:T(8,128)(2,1)} %add_convert_fusion.15), channel_id=1, source_target_pairs={{0,2},{1,3},{2,0},{3,1},{4,6},{5,7},{6,4},{7,5},{8,10},{9,11},{10,... | collective-permute-start | bytes 921608 | tf_op jit(solution)/shard_map/ppermute | solution.py:599
  265.4 25.3 %collective-permute-start.39 = (bf16[1,1,1,240,640]{4,3,2,1,0:T(8,128)(2,1)}, bf16[1,1,1,240,640]{4,3,2,1,0:T(8,128)(2,1)S(1)}, u32[]{:S(2)}, u32[]{:S(2)}) collective-permute-start(bf16[1,1,1,240,640]{4,3,2,1,0:T(8,128)(2,1)} %add_convert_fusion.14), channel_id=1, source_target_pairs={{0,2},{1,3},{2,0},{3,1},{4,6},{5,7},{6,4},{7,5},{8,10},{9,11},{10,... | collective-permute-start | bytes 921608 | tf_op jit(solution)/shard_map/ppermute | solution.py:599
  266.6 26.0 %collective-permute-start.38 = (bf16[2,1,1,240,640]{4,3,2,1,0:T(8,128)(2,1)}, bf16[2,1,1,240,640]{4,3,2,1,0:T(8,128)(2,1)}, u32[]{:S(2)}, u32[]{:S(2)}) collective-permute-start(bf16[2,1,1,240,640]{4,3,2,1,0:T(8,128)(2,1)} %add_convert_fusion.2), channel_id=1, source_target_pairs={{0,1},{1,0},{2,3},{3,2},{4,5},{5,4},{6,7},{7,6},{8,9},{9,8},{10,11... | collective-permute-start | bytes 1843208 | tf_op jit(solution)/shard_map/ppermute | solution.py:599
  271.1 26.1 %collective-permute-start.45 = (bf16[2,1,2,112,640]{4,3,2,1,0:T(8,128)(2,1)}, bf16[2,1,2,112,640]{4,3,2,1,0:T(8,128)(2,1)}, u32[]{:S(2)}, u32[]{:S(2)}) collective-permute-start(bf16[2,1,2,112,640]{4,3,2,1,0:T(8,128)(2,1)} %add_convert_fusion.5), channel_id=1, source_target_pairs={{0,1},{1,0},{2,3},{3,2},{4,5},{5,4},{6,7},{7,6},{8,9},{9,8},{10,11... | collective-permute-start | bytes 1720328 | tf_op jit(solution)/shard_map/ppermute | solution.py:599
  273.5 21.7 %collective-permute-start.37 = (bf16[1,2,2,128,640]{4,3,2,1,0:T(8,128)(2,1)}, bf16[1,2,2,128,640]{4,3,2,1,0:T(8,128)(2,1)}, u32[]{:S(2)}, u32[]{:S(2)}) collective-permute-start(bf16[1,2,2,128,640]{4,3,2,1,0:T(8,128)(2,1)} %fusion.1), channel_id=1, source_target_pairs={{0,16},{8,24},{16,0},{24,8},{1,17},{9,25},{17,1},{25,9},{2,18},{10... | collective-permute-start | bytes 1966088 | tf_op jit(solution)/shard_map/ppermute | solution.py:596
  288.1 23.9 %collective-permute-start.44 = (bf16[1,1,1,240,640]{4,3,2,1,0:T(8,128)(2,1)S(1)}, bf16[1,1,1,240,640]{4,3,2,1,0:T(8,128)(2,1)S(1)}, u32[]{:S(2)}, u32[]{:S(2)}) collective-permute-start(bf16[1,1,1,240,640]{4,3,2,1,0:T(8,128)(2,1)S(1)} %add_convert_fusion.13), channel_id=1, source_target_pairs={{0,4},{1,5},{2,6},{3,7},{4,0},{5,1},{6,2},{7,3},{8,12},{9,13},{10,... | collective-permute-start | bytes 921608 | tf_op jit(solution)/shard_map/ppermute | solution.py:599
  292.3 25.2 %collective-permute-start.43 = (bf16[1,1,1,240,640]{4,3,2,1,0:T(8,128)(2,1)S(1)}, bf16[1,1,1,240,640]{4,3,2,1,0:T(8,128)(2,1)S(1)}, u32[]{:S(2)}, u32[]{:S(2)}) collective-permute-start(bf16[1,1,1,240,640]{4,3,2,1,0:T(8,128)(2,1)S(1)} %add_convert_fusion.12), channel_id=1, source_target_pairs={{0,4},{1,5},{2,6},{3,7},{4,0},{5,1},{6,2},{7,3},{8,12},{9,13},{10,... | collective-permute-start | bytes 921608 | tf_op jit(solution)/shard_map/ppermute | solution.py:599
  294.1 24.2 %collective-permute-start.42 = (bf16[1,1,1,240,640]{4,3,2,1,0:T(8,128)(2,1)S(1)}, bf16[1,1,1,240,640]{4,3,2,1,0:T(8,128)(2,1)S(1)}, u32[]{:S(2)}, u32[]{:S(2)}) collective-permute-start(bf16[1,1,1,240,640]{4,3,2,1,0:T(8,128)(2,1)S(1)} %add_convert_fusion.11), channel_id=1, source_target_pairs={{0,16},{8,24},{16,0},{24,8},{1,17},{9,25},{17,1},{25,9},{2,18},{10... | collective-permute-start | bytes 921608 | tf_op jit(solution)/shard_map/ppermute | solution.py:596
  296.3 29.9 %collective-permute-start.41 = (bf16[1,1,2,128,640]{4,3,2,1,0:T(8,128)(2,1)S(1)}, bf16[1,1,2,128,640]{4,3,2,1,0:T(8,128)(2,1)S(1)}, u32[]{:S(2)}, u32[]{:S(2)}) collective-permute-start(bf16[1,1,2,128,640]{4,3,2,1,0:T(8,128)(2,1)S(1)} %add_convert_fusion.6), channel_id=1, source_target_pairs={{0,1},{1,0},{2,3},{3,2},{4,5},{5,4},{6,7},{7,6},{8,9},{9,8},{10,11... | collective-permute-start | bytes 983048 | tf_op jit(solution)/shard_map/ppermute | solution.py:599
  298.3 30.4 %collective-permute-start.50 = (bf16[1,1,2,112,640]{4,3,2,1,0:T(8,128)(2,1)S(1)}, bf16[1,1,2,112,640]{4,3,2,1,0:T(8,128)(2,1)S(1)}, u32[]{:S(2)}, u32[]{:S(2)}) collective-permute-start(bf16[1,1,2,112,640]{4,3,2,1,0:T(8,128)(2,1)S(1)} %add_convert_fusion.16), channel_id=1, source_target_pairs={{0,16},{8,24},{16,0},{24,8},{1,17},{9,25},{17,1},{25,9},{2,18},{10... | collective-permute-start | bytes 860168 | tf_op jit(solution)/shard_map/ppermute | solution.py:596
  312.0 13.9 %collective-permute-start.49 = (bf16[1,1,1,240,640]{4,3,2,1,0:T(8,128)(2,1)S(1)}, bf16[1,1,1,240,640]{4,3,2,1,0:T(8,128)(2,1)S(1)}, u32[]{:S(2)}, u32[]{:S(2)}) collective-permute-start(bf16[1,1,1,240,640]{4,3,2,1,0:T(8,128)(2,1)S(1)} %add_convert_fusion.10), channel_id=1, source_target_pairs={{0,2},{1,3},{2,0},{3,1},{4,6},{5,7},{6,4},{7,5},{8,10},{9,11},{10,... | collective-permute-start | bytes 921608 | tf_op jit(solution)/shard_map/ppermute | solution.py:599
  317.5 8.5 %collective-permute-start.48 = (bf16[1,1,1,240,640]{4,3,2,1,0:T(8,128)(2,1)S(1)}, bf16[1,1,1,240,640]{4,3,2,1,0:T(8,128)(2,1)S(1)}, u32[]{:S(2)}, u32[]{:S(2)}) collective-permute-start(bf16[1,1,1,240,640]{4,3,2,1,0:T(8,128)(2,1)S(1)} %add_convert_fusion.9), channel_id=1, source_target_pairs={{0,1},{1,0},{2,3},{3,2},{4,5},{5,4},{6,7},{7,6},{8,9},{9,8},{10,11... | collective-permute-start | bytes 921608 | tf_op jit(solution)/shard_map/ppermute | solution.py:599
  319.7 15.5 %collective-permute-start.47 = (bf16[1,1,1,240,640]{4,3,2,1,0:T(8,128)(2,1)S(1)}, bf16[1,1,1,240,640]{4,3,2,1,0:T(8,128)(2,1)S(1)}, u32[]{:S(2)}, u32[]{:S(2)}) collective-permute-start(bf16[1,1,1,240,640]{4,3,2,1,0:T(8,128)(2,1)S(1)} %add_convert_fusion.8), channel_id=1, source_target_pairs={{0,4},{1,5},{2,6},{3,7},{4,0},{5,1},{6,2},{7,3},{8,12},{9,13},{10,... | collective-permute-start | bytes 921608 | tf_op jit(solution)/shard_map/ppermute | solution.py:599
  327.3 11.4 %collective-permute-start.46 = (bf16[1,1,1,128,640]{4,3,2,1,0:T(8,128)(2,1)S(1)}, bf16[1,1,1,128,640]{4,3,2,1,0:T(8,128)(2,1)S(1)}, u32[]{:S(2)}, u32[]{:S(2)}) collective-permute-start(bf16[1,1,1,128,640]{4,3,2,1,0:T(8,128)(2,1)S(1)} %add_convert_fusion.19), channel_id=1, source_target_pairs={{0,2},{1,3},{2,0},{3,1},{4,6},{5,7},{6,4},{7,5},{8,10},{9,11},{10,... | collective-permute-start | bytes 491528 | tf_op jit(solution)/shard_map/ppermute | solution.py:599
  329.8 12.0 %collective-permute-start.53 = (bf16[1,1,1,112,640]{4,3,2,1,0:T(8,128)(2,1)S(1)}, bf16[1,1,1,112,640]{4,3,2,1,0:T(8,128)(2,1)S(1)}, u32[]{:S(2)}, u32[]{:S(2)}) collective-permute-start(bf16[1,1,1,112,640]{4,3,2,1,0:T(8,128)(2,1)S(1)} %add_convert_fusion.22), channel_id=1, source_target_pairs={{0,2},{1,3},{2,0},{3,1},{4,6},{5,7},{6,4},{7,5},{8,10},{9,11},{10,... | collective-permute-start | bytes 430088 | tf_op jit(solution)/shard_map/ppermute | solution.py:599
  330.5 59.0 %collective-permute-start.59 = (bf16[1,2,1,240,640]{4,3,2,1,0:T(8,128)(2,1)S(1)}, bf16[1,2,1,240,640]{4,3,2,1,0:T(8,128)(2,1)S(1)}, u32[]{:S(2)}, u32[]{:S(2)}) collective-permute-start(bf16[1,2,1,240,640]{4,3,2,1,0:T(8,128)(2,1)S(1)} %maximum_select_fusion.7), channel_id=1, source_target_pairs={{0,2},{1,3},{2,0},{3,1},{4,6},{5,7},{6,4},{7,5},{8,10},{9,11},{10,... | collective-permute-start | bytes 1843208 | tf_op jit(solution)/shard_map/ppermute | solution.py:599
  335.3 32.2 %collective-permute-start.52 = (bf16[1,1,1,240,640]{4,3,2,1,0:T(8,128)(2,1)S(1)}, bf16[1,1,1,240,640]{4,3,2,1,0:T(8,128)(2,1)S(1)}, u32[]{:S(2)}, u32[]{:S(2)}) collective-permute-start(bf16[1,1,1,240,640]{4,3,2,1,0:T(8,128)(2,1)S(1)} %add_convert_fusion.7), channel_id=1, source_target_pairs={{0,2},{1,3},{2,0},{3,1},{4,6},{5,7},{6,4},{7,5},{8,10},{9,11},{10,... | collective-permute-start | bytes 921608 | tf_op jit(solution)/shard_map/ppermute | solution.py:599
  339.8 27.8 %collective-permute-start.51 = (bf16[1,1,1,128,640]{4,3,2,1,0:T(8,128)(2,1)S(1)}, bf16[1,1,1,128,640]{4,3,2,1,0:T(8,128)(2,1)S(1)}, u32[]{:S(2)}, u32[]{:S(2)}) collective-permute-start(bf16[1,1,1,128,640]{4,3,2,1,0:T(8,128)(2,1)S(1)} %add_convert_fusion.18), channel_id=1, source_target_pairs={{0,4},{1,5},{2,6},{3,7},{4,0},{5,1},{6,2},{7,3},{8,12},{9,13},{10,... | collective-permute-start | bytes 491528 | tf_op jit(solution)/shard_map/ppermute | solution.py:599
  342.9 24.9 %collective-permute-start.55 = (bf16[1,1,1,112,640]{4,3,2,1,0:T(8,128)(2,1)S(1)}, bf16[1,1,1,112,640]{4,3,2,1,0:T(8,128)(2,1)S(1)}, u32[]{:S(2)}, u32[]{:S(2)}) collective-permute-start(bf16[1,1,1,112,640]{4,3,2,1,0:T(8,128)(2,1)S(1)} %add_convert_fusion.21), channel_id=1, source_target_pairs={{0,4},{1,5},{2,6},{3,7},{4,0},{5,1},{6,2},{7,3},{8,12},{9,13},{10,... | collective-permute-start | bytes 430088 | tf_op jit(solution)/shard_map/ppermute | solution.py:599
  367.7 16.7 %collective-permute-start.54 = (bf16[1,1,1,128,640]{4,3,2,1,0:T(8,128)(2,1)S(1)}, bf16[1,1,1,128,640]{4,3,2,1,0:T(8,128)(2,1)S(1)}, u32[]{:S(2)}, u32[]{:S(2)}) collective-permute-start(bf16[1,1,1,128,640]{4,3,2,1,0:T(8,128)(2,1)S(1)} %add_convert_fusion.17), channel_id=1, source_target_pairs={{0,2},{1,3},{2,0},{3,1},{4,6},{5,7},{6,4},{7,5},{8,10},{9,11},{10,... | collective-permute-start | bytes 491528 | tf_op jit(solution)/shard_map/ppermute | solution.py:599
  367.8 14.3 %collective-permute-start.57 = (bf16[1,1,1,112,640]{4,3,2,1,0:T(8,128)(2,1)S(1)}, bf16[1,1,1,112,640]{4,3,2,1,0:T(8,128)(2,1)S(1)}, u32[]{:S(2)}, u32[]{:S(2)}) collective-permute-start(bf16[1,1,1,112,640]{4,3,2,1,0:T(8,128)(2,1)S(1)} %add_convert_fusion.20), channel_id=1, source_target_pairs={{0,1},{1,0},{2,3},{3,2},{4,5},{5,4},{6,7},{7,6},{8,9},{9,8},{10,11... | collective-permute-start | bytes 430088 | tf_op jit(solution)/shard_map/ppermute | solution.py:599
  369.9 3.7 collective-permute-start.63
  373.5 3.7 collective-permute-start.64
  377.2 3.7 collective-permute-start.65
  379.2 16.9 %collective-permute-start.61 = (bf16[1,1,2,240,640]{4,3,2,1,0:T(8,128)(2,1)S(1)}, bf16[1,1,2,240,640]{4,3,2,1,0:T(8,128)(2,1)}, u32[]{:S(2)}, u32[]{:S(2)}) collective-permute-start(bf16[1,1,2,240,640]{4,3,2,1,0:T(8,128)(2,1)S(1)} %maximum_select_fusion.8), channel_id=1, source_target_pairs={{0,1},{1,0},{2,3},{3,2},{4,5},{5,4},{6,7},{7,6},{8,9},{9,8},{10,11... | collective-permute-start | bytes 1843208 | tf_op jit(solution)/shard_map/ppermute | solution.py:599
  380.8 37.9 %collective-permute-start.60 = (bf16[1,1,2,240,640]{4,3,2,1,0:T(8,128)(2,1)S(1)}, bf16[1,1,2,240,640]{4,3,2,1,0:T(8,128)(2,1)}, u32[]{:S(2)}, u32[]{:S(2)}) collective-permute-start(bf16[1,1,2,240,640]{4,3,2,1,0:T(8,128)(2,1)S(1)} %maximum_select_fusion.9), channel_id=1, source_target_pairs={{0,1},{1,0},{2,3},{3,2},{4,5},{5,4},{6,7},{7,6},{8,9},{9,8},{10,11... | collective-permute-start | bytes 1843208 | tf_op jit(solution)/shard_map/ppermute | solution.py:599
  382.1 4.7 %collective-permute-start.66 = (f32[1920]{0:T(1024)S(1)}, f32[1920]{0:T(1024)S(1)}, u32[]{:S(2)}, u32[]{:S(2)}) collective-permute-start(f32[1920]{0:T(1024)S(1)} %add.262), channel_id=1, source_target_pairs={{0,4},{1,5},{2,6},{3,7},{4,0},{5,1},{6,2},{7,3},{8,12},{9,13},{10,... | collective-permute-start | bytes 23048 | tf_op jit(solution)/shard_map/ppermute | solution.py:599
  384.5 28.6 %collective-permute-start.56 = (bf16[1,1,2,128,640]{4,3,2,1,0:T(8,128)(2,1)S(1)}, bf16[1,1,2,128,640]{4,3,2,1,0:T(8,128)(2,1)}, u32[]{:S(2)}, u32[]{:S(2)}) collective-permute-start(bf16[1,1,2,128,640]{4,3,2,1,0:T(8,128)(2,1)S(1)} %maximum_select_fusion.11), channel_id=1, source_target_pairs={{0,1},{1,0},{2,3},{3,2},{4,5},{5,4},{6,7},{7,6},{8,9},{9,8},{10,11... | collective-permute-start | bytes 983048 | tf_op jit(solution)/shard_map/ppermute | solution.py:599
  386.8 12.5 %collective-permute-start.58 = (bf16[1,2,1,112,640]{4,3,2,1,0:T(8,128)(2,1)S(1)}, bf16[1,2,1,112,640]{4,3,2,1,0:T(8,128)(2,1)}, u32[]{:S(2)}, u32[]{:S(2)}) collective-permute-start(bf16[1,2,1,112,640]{4,3,2,1,0:T(8,128)(2,1)S(1)} %maximum_select_fusion.12), channel_id=1, source_target_pairs={{0,2},{1,3},{2,0},{3,1},{4,6},{5,7},{6,4},{7,5},{8,10},{9,11},{10,... | collective-permute-start | bytes 860168 | tf_op jit(solution)/shard_map/ppermute | solution.py:599
  (31 other events, 256.9 us)
